TPU v7x, 32 devices: a whole 2x2x4 slice. The times are simulated.
32 devices in a mesh: seq: 8 (over z, y), fsdp: 4 (over x, core).
Axes of the slice: x: 2, y: 2, z: 4, core: 2. Of those that a mesh axis runs over, the one named last changes fastest.
Arguments:
- tokens: bfloat16 [4, 4096, 2048], P('fsdp', 'seq'), may hold values from -9 to 9
- qkv_weight: bfloat16 [2048, 1536], P('fsdp'), may hold values from -0.26516504 to 0.26516504
- near_offset: int32 [4], replicated, may hold values from 0 to 3
- far_offset: int32 [4], replicated, may hold values from 0 to 31
Outputs:
- mixed: bfloat16 [4, 4096, 512], P('fsdp', 'seq')
All inputs are finite; a program needn't handle non-finite values.
Results may differ from a plain program's by a relative error of at most 0.0074.
Values may be sent and summed in bfloat16 or wider, within the bound.
No kernel may reach another device: no remote copies, remote signals or barrier semaphores. Data moves between devices by JAX's collectives and lax.ppermute only.
A program may use at most 64 MiB of HBM per device.

v0:
```python
import functools
import math

import jax
import jax.numpy as jnp
from jax import lax
from jax.experimental import pallas as pl
from jax.experimental.pallas import tpu as pltpu
from jax.sharding import PartitionSpec as P

HEADS = 4
HEAD_DIM = 128
BLOCK = 128
STRIDE = 8
WIDTH = HEADS * HEAD_DIM
PAIR = 2 * HEAD_DIM
NEG = -1e30
SCALE2 = HEAD_DIM ** (-0.5) * math.log2(math.e)
VMEM_LIMIT = 24 * 1024 * 1024

MODEL_FLOPS = {"slot_queries": 575000, "project_pack": 689999, "project_own": 3680000, "project_mid": 1610000, "project_kv": 2990000, "attend_local": 6325000, "merge_near": 2990000}
ORDER = {
    'c1': ('c0',),
    'cD': ('c1',),
    'cQ': ('cD',),
    'p0': ('partial', 'xD'),
    'p1': ('partial',),
    'q': ('kv',),
    'kv': ('pack',),
}
NEAR_ORDER = (3, 2, 1)
F32 = jnp.float32
BF16 = jnp.bfloat16


def near_place(index, half, size):
    if index < half:
        return 0, index
    return 1 + (index - half) // size, (index - half) % size


def partners(count, place, bits):
    where = {place(i): i for i in range(count)}
    pairs = []
    for source in range(count):
        run, spot = place(source)
        if (run, spot ^ bits) in where:
            pairs.append((source, where[run, spot ^ bits]))
    return pairs


def swap(value, axis, bit):
    count = lax.axis_size(axis)
    return lax.ppermute(value, axis, [(i, i ^ bit) for i in range(count)])


def after(value, *others):
    return lax.optimization_barrier((value,) + others)[0]


def ordered(name, value, known):
    others = [known[other] for other in ORDER.get(name, ()) if other in known]
    return after(value, *others) if others else value


def rows_of(block):
    return pl.ds(pl.multiple_of(block * BLOCK, BLOCK), BLOCK)


def qk(query, key):
    return lax.dot_general(query, key, (((1,), (1,)), ((), ())), preferred_element_type=F32)


def pv(weights, value):
    return jnp.dot(weights.astype(BF16), value, preferred_element_type=F32)


def add_up(tokens, places, weights):
    total = None
    for place, weight in zip(places, weights):
        depth = weight.shape[0]
        columns = pl.ds(pl.multiple_of(place, depth), depth)
        term = jnp.dot(tokens[:, columns], weight[...], preferred_element_type=F32)
        total = term if total is None else total + term
    return total


def own_kernel(count, meta, tokens, *refs):
    weights, out = refs[:count], refs[count]
    for j in range(out.shape[1] // PAIR):
        lanes = slice(j * PAIR, (j + 1) * PAIR)
        out[:, lanes] = add_up(tokens, [meta[at] for at in range(count)], [weight.at[:, lanes] for weight in weights])


def pack_kernel(layout, base_at, slots, slot_at, meta, tokens, partial, *refs):
    arrived, packs, joined = refs[: len(layout)], refs[len(layout) : -1], refs[-1]
    for at, array in zip(layout, arrived):
        rows = array.shape[0]
        joined[pl.ds(pl.multiple_of(meta[at], rows), rows), :] = array[...]
    columns = pl.ds(pl.multiple_of(meta[base_at], joined.shape[0]), joined.shape[0])
    for slot in range(slots):
        for head in range(HEADS):
            rows = rows_of(meta[slot_at + HEADS * slot + head])
            lanes = [slice(start, start + HEAD_DIM) for start in (head * HEAD_DIM, WIDTH + head * HEAD_DIM)]
            weight = jnp.concatenate([joined[:, part] for part in lanes], axis=1)
            product = jnp.dot(tokens[rows, columns], weight, preferred_element_type=F32)
            for field, part in enumerate(lanes):
                own = partial[rows, WIDTH + part.start : WIDTH + part.stop]
                total = own + product[:, field * HEAD_DIM : (field + 1) * HEAD_DIM]
                packs[slot][:, part] = total.astype(BF16)


def slot_kernel(core_at, meta, source, out):
    out[1 - meta[core_at]] = source[...]


def kv_kernel(base_at, meta, tokens, partial, joined, kv):
    columns = pl.ds(pl.multiple_of(meta[base_at], joined.shape[0]), joined.shape[0])
    for j in range(2 * WIDTH // PAIR):
        lanes = slice(j * PAIR, (j + 1) * PAIR)
        product = jnp.dot(tokens[:, columns], joined[:, lanes], preferred_element_type=F32)
        kv[:, lanes] = (partial[:, WIDTH + j * PAIR : WIDTH + (j + 1) * PAIR] + product).astype(BF16)


def with_ones(value):
    return jnp.concatenate([value, jnp.ones(value.shape, BF16)], axis=1)


def attend_kernel(bases_at, core_at, slots, slot_at, match_at, meta, tokens, partial, *refs):
    weights, refs = refs[: len(bases_at)], refs[len(bases_at) :]
    kv, out, refs = refs[0], refs[1], refs[2:]
    state, scratch = refs[: 4 * slots], refs[4 * slots :]
    query, acc_all, top_all, sum_all = scratch
    blocks = query.shape[0] // BLOCK
    GROUP = 2 if blocks % 2 == 0 else 1
    row = lax.broadcasted_iota(jnp.int32, (BLOCK, BLOCK), 0)
    column = lax.broadcasted_iota(jnp.int32, (BLOCK, BLOCK), 1)
    causal = column <= row
    places = [meta[at] for at in bases_at]
    other = 1 - meta[core_at]
    for pair in range(HEADS // 2):
        lanes = slice(pair * PAIR, (pair + 1) * PAIR)
        total = partial[:, lanes]
        if weights:
            parts = [weights[0].at[:, lanes], weights[1].at[other, :, lanes]]
            total = total + add_up(tokens, places, parts)
        query[:, lanes] = total.astype(BF16)

    def lanes_of(head):
        return slice(head * HEAD_DIM, (head + 1) * HEAD_DIM)

    def rows_at(b):
        return slice(b * BLOCK, (b + 1) * BLOCK)

    def score(head, group):
        first, last = group * GROUP, (group + 1) * GROUP
        rows = slice(first * BLOCK, last * BLOCK)
        return qk(query[rows, lanes_of(head)], kv[: last * BLOCK, lanes_of(head)])

    def weigh(head, group, scores):
        near_block = meta[slot_at + head]
        far_block = meta[slot_at + HEADS + head]
        tops, weights = [], []
        for i in range(GROUP):
            b = group * GROUP + i
            mine = scores[rows_at(i)]
            times = (
                1
                + jnp.where(near_block == b, 1, 0)
                + jnp.where(far_block == b, meta[match_at + head], 0)
            ).astype(F32)
            diagonal = jnp.where(causal, mine[:, rows_at(b)], NEG)
            top = jnp.max(diagonal, axis=1, keepdims=True)
            if b:
                top = jnp.maximum(top, jnp.max(mine[:, : b * BLOCK], axis=1, keepdims=True))
            parts = [(jnp.exp2((diagonal - top) * SCALE2) * times).astype(BF16)]
            if b:
                parts.insert(0, jnp.exp2((mine[:, : b * BLOCK] - top) * SCALE2).astype(BF16))
            if i < GROUP - 1:
                parts.append(jnp.zeros((BLOCK, (GROUP - 1 - i) * BLOCK), BF16))
            tops.append(top)
            weights.append(jnp.concatenate(parts, axis=1))
        return tops, jnp.concatenate(weights, axis=0)

    def finish(head, group, tops, weight):
        lanes = lanes_of(head)
        keys = (group + 1) * GROUP * BLOCK
        value = kv[:keys, WIDTH + head * HEAD_DIM : WIDTH + (head + 1) * HEAD_DIM]
        both = jnp.dot(weight, with_ones(value), preferred_element_type=F32)
        rows = slice(group * GROUP * BLOCK, keys)
        acc, summed = both[:, :HEAD_DIM], both[:, HEAD_DIM:]
        out[rows, lanes] = (acc / summed).astype(BF16)
        acc_all[rows, lanes] = acc
        sum_all[rows, lanes] = summed
        for i, top in enumerate(tops):
            top_all[rows_at(group * GROUP + i), lanes] = jnp.broadcast_to(top, (BLOCK, HEAD_DIM))
        if group == blocks // GROUP - 1:
            for slot in range(slots):
                rows = rows_of(meta[slot_at + slot * HEADS + head])
                for target, source in zip(state[4 * slot :], scratch):
                    target[:, lanes] = source[rows, lanes]

    tasks = [(head, group) for head in range(HEADS) for group in range(blocks // GROUP)]
    scored, weighed = {}, {}
    for step in range(len(tasks) + 2):
        if step < len(tasks):
            scored[step] = score(*tasks[step])
        if 0 <= step - 1 < len(tasks):
            weighed[step - 1] = weigh(*tasks[step - 1], scored.pop(step - 1))
        if 0 <= step - 2 < len(tasks):
            finish(*tasks[step - 2], *weighed.pop(step - 2))


def merge_kernel(shifts, steps, slot_at, match_at, place_at, meta, *refs):
    slots = len(shifts)
    state = refs[: 4 * slots]
    packs = refs[4 * slots : 4 * slots + sum(shifts)]
    out, results, sems = refs[4 * slots + sum(shifts) + 1 :]
    if slots == 1:
        pl.when(meta[place_at] > 0)(lambda: merge_slots(
            shifts, steps, slot_at, match_at, place_at, meta, state, packs, out, results, sems
        ))
    else:
        merge_slots(shifts, steps, slot_at, match_at, place_at, meta, state, packs, out, results, sems)


def merge_slots(shifts, steps, slot_at, match_at, place_at, meta, state, packs, out, results, sems):
    lanes = [slice(head * HEAD_DIM, (head + 1) * HEAD_DIM) for head in range(HEADS)]
    values = [slice(WIDTH + head * HEAD_DIM, WIDTH + (head + 1) * HEAD_DIM) for head in range(HEADS)]
    earlier = [None] * HEADS
    for slot, count in enumerate(shifts):
        fields = packs[sum(shifts[:slot]) : sum(shifts[: slot + 1])]
        query, acc_ref, top_ref, sum_ref = state[4 * slot : 4 * slot + 4]
        place = meta[place_at + slot]
        scores, weights = [], []
        for head in range(HEADS):
            keys = jnp.concatenate([field[:, lanes[head]] for field in fields], axis=0)
            score = qk(query[:, lanes[head]], keys)
            parts = []
            for number, step in enumerate(steps[sum(shifts[:slot]) : sum(shifts[: slot + 1])]):
                seen = place ^ step < place
                if slot:
                    seen = seen & (meta[match_at + head] == 1)
                part = score[:, number * BLOCK : (number + 1) * BLOCK]
                parts.append(jnp.where(seen, part, NEG))
            scores.append(jnp.concatenate(parts, axis=1))
        for head in range(HEADS):
            acc, top, summed = (ref[:, lanes[head]] for ref in (acc_ref, top_ref, sum_ref))
            if slot:
                same = meta[slot_at + head] == meta[slot_at + HEADS + head]
                acc, top, summed = (
                    jnp.where(same, new, old) for new, old in zip(earlier[head], (acc, top, summed))
                )
            best = jnp.maximum(top, jnp.max(scores[head], axis=1, keepdims=True))
            decay = jnp.exp2((top - best) * SCALE2)
            weight = jnp.exp2((scores[head] - best[:, :1]) * SCALE2).astype(BF16)
            weights.append((acc * decay, best, summed * decay, weight))
        copies = []
        for head in range(HEADS):
            acc, best, summed, weight = weights[head]
            value = jnp.concatenate([field[:, values[head]] for field in fields], axis=0)
            both = jnp.dot(weight, with_ones(value), preferred_element_type=F32)
            acc = acc + both[:, :HEAD_DIM]
            summed = summed + both[:, HEAD_DIM:]
            earlier[head] = (acc, best, summed)
            results[slot, :, lanes[head]] = (acc / summed).astype(BF16)
            rows = rows_of(meta[slot_at + slot * HEADS + head])
            copies.append(
                pltpu.make_async_copy(
                    results.at[slot, :, lanes[head]], out.at[rows, lanes[head]], sems.at[head]
                )
            )
            copies[-1].start()
        for copy in copies:
            copy.wait()


def body(tokens, qkv_weight, near_offset, far_offset):
    sequence = tokens[0]
    row_count, depth = sequence.shape
    share = qkv_weight.shape[0]
    block_rate = row_count // BLOCK
    seq_size = lax.axis_size("seq")
    seq_index = lax.axis_index("seq")
    pieces = lax.axis_size("fsdp")
    mine = lax.axis_index("fsdp")
    near_size = min(16, seq_size)
    half = near_size // 2
    far_size = max(1, min(16, seq_size // STRIDE))
    near_at = lambda i: near_place(i, half, near_size)
    far_at = lambda i: (i // (STRIDE * far_size) * STRIDE + i % STRIDE, i // STRIDE % far_size)
    reach = max(near_at(i)[1] for i in range(seq_size))
    near_shifts = (1 << reach.bit_length()) - 1
    far_shifts = (1 << (far_size - 1).bit_length()) - 1
    slots = 2 if far_shifts else 1
    shifts = (near_shifts, far_shifts)[:slots]

    near_position = jnp.where(seq_index < half, seq_index, (seq_index - half) % near_size)
    far_position = seq_index // STRIDE % far_size
    far_match = (seq_index % STRIDE == far_offset // block_rate).astype(jnp.int32)
    spans = [(0, share // 4), (share // 2, share // 8)] if seq_size % 4 == 0 else []
    direct_from = spans[-1][0] + 2 * spans[-1][1] if spans else 0
    full_places = [(mine ^ j) * share for j in range(pieces)]
    scalars = list(full_places)
    place_at = len(scalars)
    scalars += [near_position, far_position]
    base_at = len(scalars)
    scalars += [(mine ^ bit) // 2 * 2 * share for bit in range(2, pieces, 2)]
    core_at = len(scalars)
    scalars.append(mine % 2)
    slot_at = len(scalars)
    match_at = slot_at + 2 * HEADS
    offsets_at = match_at + HEADS
    offsets = []
    for core in range(2):
        first = (mine % 2 ^ core) * share
        for number, (start, rows) in enumerate(spans):
            side = seq_index // (1 << number) % 2
            offsets += [first + start + side * rows, first + start + (1 - side) * rows]
        offsets.append(first + direct_from)
    as_array = lambda values: jnp.stack([jnp.asarray(value, jnp.int32) for value in values])
    meta = jnp.concatenate(
        [as_array(scalars), near_offset, far_offset % block_rate, far_match, as_array(offsets)]
    )

    scalar_spec = pl.BlockSpec(memory_space=pltpu.SMEM)
    whole = pl.BlockSpec(memory_space=pltpu.VMEM)
    shape = jax.ShapeDtypeStruct

    def call(kernel, args, results, name, scratch=()):
        return pl.pallas_call(
            kernel,
            in_specs=[scalar_spec] + [whole] * len(args),
            out_specs=[whole] * len(results),
            out_shape=results,
            scratch_shapes=list(scratch),
            compiler_params=pltpu.CompilerParams(vmem_limit_bytes=VMEM_LIMIT),
            cost_estimate=pl.CostEstimate(flops=MODEL_FLOPS[name], bytes_accessed=1000, transcendentals=0),
            name=name,
        )(meta, *args)

    local = [qkv_weight]
    bits = range(2, pieces, 2)
    known = {}
    if pieces > 1:
        local.append(swap(qkv_weight, "fsdp", 1))
        known["core"] = local[-1]
    (partial,) = call(
        functools.partial(own_kernel, len(local)),
        [ordered("t", sequence, known), *local],
        [shape((row_count, 3 * WIDTH), F32)],
        "project_own",
    )
    known["partial"] = partial
    direct_rows, queries = [], []
    for bit in bits:
        mine_rows, other_rows = [], []
        for number, (start, rows) in enumerate(spans):
            tag = str(number)
            side = seq_index // (1 << number) % 2
            cut = lax.dynamic_slice(
                ordered("c" + tag, qkv_weight, known), (start + side * rows, WIDTH), (rows, 2 * WIDTH)
            )
            known["c" + tag] = cut
            direct = swap(cut, "fsdp", bit)
            known["x" + tag] = direct
            across = swap(ordered("f" + tag, direct, known), "fsdp", 1)
            known["f" + tag] = across
            passed = ordered("p" + tag, swap(ordered("y" + tag, direct, known), "seq", 1 << number), known)
            known["y" + tag] = passed
            mine_rows += [direct, passed]
            other_rows += [across, swap(passed, "fsdp", 1)]
            known["q" + tag] = other_rows[-1]
        known["meta"] = meta
        cut = ordered("cD", qkv_weight, known)[direct_from:, WIDTH:]
        known["cD"] = cut
        rest = swap(cut, "fsdp", bit)
        known["xD"] = rest
        rest = ordered("pD", rest, known)
        known["fD"] = swap(rest, "fsdp", 1)
        direct_rows.append(mine_rows + [rest] + other_rows + [known["fD"]])
        cut = ordered("cQ", qkv_weight, known)[:, :WIDTH]
        known["cQ"] = cut
        queries.append(swap(cut, "fsdp", bit))
    assert len(bits) <= 1
    if bits:
        layout = [offsets_at + i for i in range(len(direct_rows[0]))]
        *packs, joined = call(
            functools.partial(pack_kernel, layout, base_at, slots, slot_at),
            [sequence, partial, *direct_rows[0]],
            [shape((BLOCK, 2 * WIDTH), BF16)] * slots + [shape((2 * share, 2 * WIDTH), BF16)],
            "project_pack",
        )
        known["pack"] = packs[0]
        (kv,) = call(
            functools.partial(kv_kernel, base_at),
            [sequence, ordered("kv", partial, known), joined],
            [shape((row_count, 2 * WIDTH), BF16)],
            "project_kv",
        )
    else:
        kv = partial[:, WIDTH:].astype(BF16)
        blocks = kv.reshape(block_rate, BLOCK, 2, HEADS, HEAD_DIM)
        packs = []
        for offset in (near_offset, far_offset % block_rate)[:slots]:
            picked = blocks[offset, :, :, jnp.arange(HEADS)]
            packs.append(picked.transpose(1, 2, 0, 3).reshape(BLOCK, 2 * WIDTH))
    known["kv"] = kv
    received = []
    for pack, place, count, unit in zip(packs, (near_at, far_at), shifts, (1, STRIDE)):
        for step in NEAR_ORDER if count == len(NEAR_ORDER) else range(1, count + 1):
            received.append((step, lax.ppermute(pack, "seq", partners(seq_size, place, step))))
        known |= {f"n{step}": r for step, r in received}
    steps = [step for step, _ in received]
    received = [pack for _, pack in received]
    crossed_q, q_places = [], []
    for bit, direct in zip(bits, queries):
        direct = ordered("q", direct, known)
        (slots_out,) = call(
            functools.partial(slot_kernel, core_at), [direct], [shape((2,) + direct.shape, BF16)], "slot_queries"
        )
        both = lax.all_to_all(
            slots_out, "fsdp", 0, 0, axis_index_groups=[[i, i + 1] for i in range(0, pieces, 2)]
        )
        crossed_q += [direct, both]
        q_places += [bit, bit ^ 1]
    state_types = [BF16, F32, F32, F32]
    partial_out, *state = call(
        functools.partial(attend_kernel, q_places, core_at, slots, slot_at, match_at),
        [sequence, partial, *crossed_q, kv],
        [shape((row_count, WIDTH), BF16)] + [shape((BLOCK, WIDTH), kind) for kind in state_types] * slots,
        "attend_local",
        [pltpu.VMEM((row_count, WIDTH), kind) for kind in state_types],
    )
    count = 4 * slots + sum(shifts)
    merged = pl.pallas_call(
        functools.partial(merge_kernel, shifts, steps, slot_at, match_at, place_at),
        in_specs=[scalar_spec] + [whole] * count + [pl.BlockSpec(memory_space=pl.ANY)],
        out_specs=pl.BlockSpec(memory_space=pl.ANY),
        out_shape=shape((row_count, WIDTH), BF16),
        scratch_shapes=[pltpu.VMEM((slots, BLOCK, WIDTH), BF16), pltpu.SemaphoreType.DMA((HEADS,))],
        input_output_aliases={count + 1: 0},
        compiler_params=pltpu.CompilerParams(vmem_limit_bytes=VMEM_LIMIT),
        cost_estimate=pl.CostEstimate(flops=MODEL_FLOPS["merge_near"], bytes_accessed=1000, transcendentals=0),
        name="merge_near",
    )(meta, *state, *received, partial_out)
    return merged[None]


def solution(mesh):
    in_specs = (P("fsdp", "seq", None), P("fsdp", None), P(), P())
    out_specs = P("fsdp", "seq", None)
    return jax.shard_map(body, mesh=mesh, in_specs=in_specs, out_specs=out_specs, check_vma=False)
```

profile of v0, /device:TPU:0, one launch (start us, length us, event | category | flops | bytes accessed | tf_op | source)
XLA Modules:
  0.0 41.2 jit_solution(9677695609253018576)
XLA Ops:
  0.0 0.5 %collective-permute-start = (bf16[512,1536]{1,0:T(8,128)(2,1)}, bf16[512,1536]{1,0:T(8,128)(2,1)}, u32[]{:S(2)}, u32[]{:S(2)}) collective-permute-start(bf16[512,1536]{1,0:T(8,128)(2,1)} %refs_0_.1), channel_id=1, source_target_pairs={{0,1},{1,0},{2,3},{3,2},{4,5},{5,4},{6,7},{7,6},{8,9},{9,8},{10,11... | collective-permute-start | bytes 4718600 | tf_op jit(solution)/shard_map/ppermute | solution.py:54
  0.5 1.1 %constant_dynamic-slice_fusion.1 = bf16[128,1024]{1,0:T(8,128)(2,1)S(1)} fusion(bf16[512,1536]{1,0:T(8,128)(2,1)} %refs_0_.1, s32[]{:T(128)S(6)} %select_n.83), kind=kLoop, calls=%fused_computation.7 | loop fusion | bytes 524292 | tf_op jit(solution)/shard_map/dynamic_slice | solution.py:361
  1.6 2.6 %collective-permute-start.2 = (bf16[128,1024]{1,0:T(8,128)(2,1)S(1)}, bf16[128,1024]{1,0:T(8,128)(2,1)S(1)}, u32[]{:S(2)}, u32[]{:S(2)}) collective-permute-start(bf16[128,1024]{1,0:T(8,128)(2,1)S(1)} %constant_dynamic-slice_fusion.1), channel_id=1, source_target_pairs={{0,2},{1,3},{2,0},{3,1},{4,6},{5,7},{6,4},{7,5},{8,10},{9,11},{10,... | collective-permute-start | bytes 786440 | tf_op jit(solution)/shard_map/ppermute | solution.py:54
  4.2 1.6 %constant_dynamic-slice_fusion = bf16[64,1024]{1,0:T(8,128)(2,1)} fusion(bf16[512,1536]{1,0:T(8,128)(2,1)} %refs_0_.1, s32[]{:T(128)S(6)} %select_n.84), kind=kLoop, calls=%fused_computation.6 | loop fusion | bytes 262148 | tf_op jit(solution)/shard_map/dynamic_slice | solution.py:361
  5.8 1.7 %slice.6 = bf16[128,1024]{1,0:T(8,128)(2,1)} slice(bf16[512,1536]{1,0:T(8,128)(2,1)} %refs_0_.1), slice={[384:512], [512:1536]} | slice | bytes 524288 | tf_op jit(solution)/shard_map/slice | solution.py:375
  7.5 2.0 %collective-permute-start.6 = (bf16[128,1024]{1,0:T(8,128)(2,1)}, bf16[128,1024]{1,0:T(8,128)(2,1)S(1)}, u32[]{:S(2)}, u32[]{:S(2)}) collective-permute-start(bf16[128,1024]{1,0:T(8,128)(2,1)} %slice.6), channel_id=1, source_target_pairs={{0,2},{1,3},{2,0},{3,1},{4,6},{5,7},{6,4},{7,5},{8,10},{9,11},{10,... | collective-permute-start | bytes 786440 | tf_op jit(solution)/shard_map/ppermute | solution.py:54
  9.5 1.9 %slice.7 = bf16[512,512]{1,0:T(8,128)(2,1)} slice(bf16[512,1536]{1,0:T(8,128)(2,1)} %refs_0_.1), slice={[0:512], [0:512]} | slice | bytes 1048576 | tf_op jit(solution)/shard_map/slice | solution.py:382
  11.4 2.0 %collective-permute-start.3 = (bf16[128,1024]{1,0:T(8,128)(2,1)S(1)}, bf16[128,1024]{1,0:T(8,128)(2,1)S(1)}, u32[]{:S(2)}, u32[]{:S(2)}) collective-permute-start(bf16[128,1024]{1,0:T(8,128)(2,1)S(1)} %collective-permute-done.2.refs_0_), channel_id=1, source_target_pairs={{0,4},{4,0},{8,12},{12,8},{16,20},{20,16},{24,28},{28,24},{1,5},{5... | collective-permute-start | bytes 786440 | tf_op jit(solution)/shard_map/ppermute | solution.py:54
  13.5 0.6 %collective-permute-done.4.refs_2_ = bf16[64,1024]{1,0:T(8,128)(2,1)S(1)} collective-permute-done((bf16[64,1024]{1,0:T(8,128)(2,1)}, bf16[64,1024]{1,0:T(8,128)(2,1)S(1)}, u32[]{:S(2)}, u32[]{:S(2)}) %collective-permute-start.4) | collective-permute-done | bytes 131104 | tf_op jit(solution)/shard_map/ppermute | solution.py:54
  14.1 2.1 %collective-permute-start.5 = (bf16[64,1024]{1,0:T(8,128)(2,1)S(1)}, bf16[64,1024]{1,0:T(8,128)(2,1)}, u32[]{:S(2)}, u32[]{:S(2)}) collective-permute-start(bf16[64,1024]{1,0:T(8,128)(2,1)S(1)} %collective-permute-done.4.refs_2_), channel_id=1, source_target_pairs={{0,8},{4,12},{8,0},{12,4},{16,24},{20,28},{24,16},{28,20},{1,9},{5... | collective-permute-start | bytes 393224 | tf_op jit(solution)/shard_map/ppermute | solution.py:54
  16.5 1.4 %copy-done.1 = bf16[512,1536]{1,0:T(8,128)(2,1)S(1)} copy-done((bf16[512,1536]{1,0:T(8,128)(2,1)S(1)}, bf16[512,1536]{1,0:T(8,128)(2,1)}, u32[]{:S(2)}) %copy-start.1) | copy-done | bytes 1572888
  17.9 3.2 %project_own.1.partial = f32[512,1536]{1,0:T(8,128)S(1)} custom-call(s32[30]{0:T(128)S(1)} %concatenate.3.meta, bf16[512,2048]{1,0:T(8,128)(2,1)S(1)} %bitcast.19, bf16[512,1536]{1,0:T(8,128)(2,1)S(1)} %copy-done.1, bf16[512,1536]{1,0:T(8,128)(2,1)} %collective-permute-done.refs_1_), custom_call_target="tpu_custom_call" | custom-call | flops 3680000 | bytes 1000 | tf_op jit(solution)/shard_map/project_own/pallas_call | solution.py:331
  21.1 0.6 %collective-permute-start.7 = (bf16[128,1024]{1,0:T(8,128)(2,1)S(1)}, bf16[128,1024]{1,0:T(8,128)(2,1)S(1)}, u32[]{:S(2)}, u32[]{:S(2)}) collective-permute-start(bf16[128,1024]{1,0:T(8,128)(2,1)S(1)} %collective-permute-done.2.refs_0_), channel_id=1, source_target_pairs={{0,1},{1,0},{2,3},{3,2},{4,5},{5,4},{6,7},{7,6},{8,9},{9,8},{10,11... | collective-permute-start | bytes 786440 | tf_op jit(solution)/shard_map/ppermute | solution.py:54
  22.3 0.9 %collective-permute-done.11.refs_9_ = bf16[128,1024]{1,0:T(8,128)(2,1)S(1)} collective-permute-done((bf16[128,1024]{1,0:T(8,128)(2,1)S(1)}, bf16[128,1024]{1,0:T(8,128)(2,1)S(1)}, u32[]{:S(2)}, u32[]{:S(2)}) %collective-permute-start.11) | collective-permute-done | bytes 262176 | tf_op jit(solution)/shard_map/ppermute | solution.py:54
  23.2 0.8 %collective-permute-done.10.refs_8_ = bf16[64,1024]{1,0:T(8,128)(2,1)S(1)} collective-permute-done((bf16[64,1024]{1,0:T(8,128)(2,1)}, bf16[64,1024]{1,0:T(8,128)(2,1)S(1)}, u32[]{:S(2)}, u32[]{:S(2)}) %collective-permute-start.10) | collective-permute-done | bytes 131104 | tf_op jit(solution)/shard_map/ppermute | solution.py:54
  24.0 1.5 %project_pack.1 = (bf16[128,1024]{1,0:T(8,128)(2,1)S(1)}, bf16[1024,1024]{1,0:T(8,128)(2,1)S(1)}) custom-call(s32[30]{0:T(128)S(1)} %concatenate.3.meta, bf16[512,2048]{1,0:T(8,128)(2,1)S(1)} %bitcast.20, f32[512,1536]{1,0:T(8,128)S(1)} %project_own.1.partial, bf16[128,1024]{1,0:T(8,128)(2,1)S(1)} %collective-permute-done.2.refs_0_, ...), custom_call_target="tpu_custom_call" | custom-call | flops 689999 | bytes 1000 | tf_op jit(solution)/shard_map/project_pack/pallas_call | solution.py:331
  25.5 1.6 %collective-permute-start.12 = (bf16[128,1024]{1,0:T(8,128)(2,1)S(1)}, bf16[128,1024]{1,0:T(8,128)(2,1)S(1)}, u32[]{:S(2)}, u32[]{:S(2)}) collective-permute-start(bf16[128,1024]{1,0:T(8,128)(2,1)S(1)} %get-tuple-element.24), channel_id=1, source_target_pairs={{0,12},{4,8},{8,4},{12,0},{16,28},{20,24},{24,20},{28,16},{1,13},{... | collective-permute-start | bytes 786440 | tf_op jit(solution)/shard_map/ppermute | solution.py:412
  27.1 1.5 %collective-permute-start.13 = (bf16[128,1024]{1,0:T(8,128)(2,1)S(1)}, bf16[128,1024]{1,0:T(8,128)(2,1)S(1)}, u32[]{:S(2)}, u32[]{:S(2)}) collective-permute-start(bf16[128,1024]{1,0:T(8,128)(2,1)S(1)} %get-tuple-element.24), channel_id=1, source_target_pairs={{0,8},{4,12},{8,0},{12,4},{16,24},{20,28},{24,16},{28,20},{1,9},{5... | collective-permute-start | bytes 786440 | tf_op jit(solution)/shard_map/ppermute | solution.py:412
  29.0 1.8 %project_kv.1.refs_2_ = bf16[512,1024]{1,0:T(8,128)(2,1)S(1)} custom-call(s32[30]{0:T(128)S(1)} %concatenate.3.meta, bf16[512,2048]{1,0:T(8,128)(2,1)S(1)} %bitcast.21, f32[512,1536]{1,0:T(8,128)S(1)} %project_own.1.partial, bf16[1024,1024]{1,0:T(8,128)(2,1)S(1)} %get-tuple-element.26.joined), custom_call_target="tpu_custom_call" | custom-call | flops 2990000 | bytes 1000 | tf_op jit(solution)/shard_map/project_kv/pallas_call | solution.py:331
  30.9 0.6 %slot_queries.1 = bf16[2,512,512]{2,1,0:T(8,128)(2,1)S(1)} custom-call(s32[30]{0:T(128)S(1)} %concatenate.3.meta, bf16[512,512]{1,0:T(8,128)(2,1)S(1)} %collective-permute-done.1.source.refs_0_), custom_call_target="tpu_custom_call" | custom-call | flops 575000 | bytes 1000 | tf_op jit(solution)/shard_map/slot_queries/pallas_call | solution.py:331
  31.4 4.6 %all_to_all.5.refs_1_ = bf16[2,512,512]{2,1,0:T(8,128)(2,1)S(1)} all-to-all(bf16[2,512,512]{2,1,0:T(8,128)(2,1)S(1)} %slot_queries.1), channel_id=1, replica_groups={{0,1},{2,3},{4,5},{6,7},{8,9},{10,11},{12,13},{14,15},{16,17},{18,19},{..., dimensions={0} | all-to-all | bytes 2097152 | tf_op jit(solution)/shard_map/all_to_all | solution.py:422
  36.0 3.4 %attend_local.1 = (bf16[512,512]{1,0:T(8,128)(2,1)}, bf16[128,512]{1,0:T(8,128)(2,1)S(1)}, f32[128,512]{1,0:T(8,128)S(1)}, f32[128,512]{1,0:T(8,128)S(1)}, f32[128,512]{1,0:T(8,128)S(1)}) custom-call(s32[30]{0:T(128)S(1)} %concatenate.3.meta, bf16[512,2048]{1,0:T(8,128)(2,1)S(1)} %bitcast.22, f32[512,1536]{1,0:T(8,128)S(1)} %project_own.1.partial, ...), custom_call_target="tpu_custom_call" | custom-call | flops 6325000 | bytes 1000 | tf_op jit(solution)/shard_map/attend_local/pallas_call | solution.py:331
  39.4 1.2 %collective-permute-done.13.refs_5_ = bf16[128,1024]{1,0:T(8,128)(2,1)S(1)} collective-permute-done((bf16[128,1024]{1,0:T(8,128)(2,1)S(1)}, bf16[128,1024]{1,0:T(8,128)(2,1)S(1)}, u32[]{:S(2)}, u32[]{:S(2)}) %collective-permute-start.13) | collective-permute-done | bytes 262176 | tf_op jit(solution)/shard_map/ppermute | solution.py:412
  40.6 0.6 %merge_near.1 = bf16[512,512]{1,0:T(8,128)(2,1)} custom-call(s32[30]{0:T(128)S(1)} %concatenate.3.meta, bf16[128,512]{1,0:T(8,128)(2,1)S(1)} %get-tuple-element.28.refs_0_, f32[128,512]{1,0:T(8,128)S(1)} %get-tuple-element.29.refs_1_, f32[128,512]{1,0:T(8,128)S(1)} %get-tuple-element.30.refs_2_, ...), custom_call_target="tpu_custom_call", output_to_operand_aliasing={{}: (8, {})} | custom-call | flops 2990000 | bytes 1000 | tf_op jit(solution)/shard_map/merge_near/pallas_call | solution.py:436
  (28 shorter events, 1.4 us)
Async XLA Ops:
  0.0 13.4 %copy-start.3 = (s32[4]{0:T(128)S(1)}, s32[4]{0:T(128)}, u32[]{:S(2)}) copy-start(s32[4]{0:T(128)} %param.7) | copy-start | bytes 52
  0.0 16.3 %copy-start.2 = (s32[4]{0:T(128)S(1)}, s32[4]{0:T(128)}, u32[]{:S(2)}) copy-start(s32[4]{0:T(128)} %param.6) | copy-start | bytes 52
  0.0 16.5 %copy-start = (bf16[1,512,2048]{2,1,0:T(8,128)(2,1)S(1)}, bf16[1,512,2048]{2,1,0:T(8,128)(2,1)}, u32[]{:S(2)}) copy-start(bf16[1,512,2048]{2,1,0:T(8,128)(2,1)} %param.4) | copy-start | bytes 6291460
  0.0 16.4 %collective-permute-start = (bf16[512,1536]{1,0:T(8,128)(2,1)}, bf16[512,1536]{1,0:T(8,128)(2,1)}, u32[]{:S(2)}, u32[]{:S(2)}) collective-permute-start(bf16[512,1536]{1,0:T(8,128)(2,1)} %refs_0_.1), channel_id=1, source_target_pairs={{0,1},{1,0},{2,3},{3,2},{4,5},{5,4},{6,7},{7,6},{8,9},{9,8},{10,11... | collective-permute-start | bytes 4718600 | tf_op jit(solution)/shard_map/ppermute | solution.py:54
  1.6 9.8 %collective-permute-start.2 = (bf16[128,1024]{1,0:T(8,128)(2,1)S(1)}, bf16[128,1024]{1,0:T(8,128)(2,1)S(1)}, u32[]{:S(2)}, u32[]{:S(2)}) collective-permute-start(bf16[128,1024]{1,0:T(8,128)(2,1)S(1)} %constant_dynamic-slice_fusion.1), channel_id=1, source_target_pairs={{0,2},{1,3},{2,0},{3,1},{4,6},{5,7},{6,4},{7,5},{8,10},{9,11},{10,... | collective-permute-start | bytes 786440 | tf_op jit(solution)/shard_map/ppermute | solution.py:54
  5.8 8.3 %collective-permute-start.4 = (bf16[64,1024]{1,0:T(8,128)(2,1)}, bf16[64,1024]{1,0:T(8,128)(2,1)S(1)}, u32[]{:S(2)}, u32[]{:S(2)}) collective-permute-start(bf16[64,1024]{1,0:T(8,128)(2,1)} %constant_dynamic-slice_fusion), channel_id=1, source_target_pairs={{0,2},{1,3},{2,0},{3,1},{4,6},{5,7},{6,4},{7,5},{8,10},{9,11},{10,... | collective-permute-start | bytes 393224 | tf_op jit(solution)/shard_map/ppermute | solution.py:54
  7.5 13.6 %collective-permute-start.6 = (bf16[128,1024]{1,0:T(8,128)(2,1)}, bf16[128,1024]{1,0:T(8,128)(2,1)S(1)}, u32[]{:S(2)}, u32[]{:S(2)}) collective-permute-start(bf16[128,1024]{1,0:T(8,128)(2,1)} %slice.6), channel_id=1, source_target_pairs={{0,2},{1,3},{2,0},{3,1},{4,6},{5,7},{6,4},{7,5},{8,10},{9,11},{10,... | collective-permute-start | bytes 786440 | tf_op jit(solution)/shard_map/ppermute | solution.py:54
  11.4 19.5 %collective-permute-start.1 = (bf16[512,512]{1,0:T(8,128)(2,1)}, bf16[512,512]{1,0:T(8,128)(2,1)S(1)}, u32[]{:S(2)}, u32[]{:S(2)}) collective-permute-start(bf16[512,512]{1,0:T(8,128)(2,1)} %slice.7), channel_id=1, source_target_pairs={{0,2},{1,3},{2,0},{3,1},{4,6},{5,7},{6,4},{7,5},{8,10},{9,11},{10,... | collective-permute-start | bytes 1572872 | tf_op jit(solution)/shard_map/ppermute | solution.py:54
  11.4 10.3 %collective-permute-start.3 = (bf16[128,1024]{1,0:T(8,128)(2,1)S(1)}, bf16[128,1024]{1,0:T(8,128)(2,1)S(1)}, u32[]{:S(2)}, u32[]{:S(2)}) collective-permute-start(bf16[128,1024]{1,0:T(8,128)(2,1)S(1)} %collective-permute-done.2.refs_0_), channel_id=1, source_target_pairs={{0,4},{4,0},{8,12},{12,8},{16,20},{20,16},{24,28},{28,24},{1,5},{5... | collective-permute-start | bytes 786440 | tf_op jit(solution)/shard_map/ppermute | solution.py:54
  14.1 7.7 %collective-permute-start.5 = (bf16[64,1024]{1,0:T(8,128)(2,1)S(1)}, bf16[64,1024]{1,0:T(8,128)(2,1)}, u32[]{:S(2)}, u32[]{:S(2)}) collective-permute-start(bf16[64,1024]{1,0:T(8,128)(2,1)S(1)} %collective-permute-done.4.refs_2_), channel_id=1, source_target_pairs={{0,8},{4,12},{8,0},{12,4},{16,24},{20,28},{24,16},{28,20},{1,9},{5... | collective-permute-start | bytes 393224 | tf_op jit(solution)/shard_map/ppermute | solution.py:54
  16.4 5.8 %collective-permute-start.9 = (bf16[64,1024]{1,0:T(8,128)(2,1)S(1)}, bf16[64,1024]{1,0:T(8,128)(2,1)S(1)}, u32[]{:S(2)}, u32[]{:S(2)}) collective-permute-start(bf16[64,1024]{1,0:T(8,128)(2,1)S(1)} %collective-permute-done.4.refs_2_), channel_id=1, source_target_pairs={{0,1},{1,0},{2,3},{3,2},{4,5},{5,4},{6,7},{7,6},{8,9},{9,8},{10,11... | collective-permute-start | bytes 393224 | tf_op jit(solution)/shard_map/ppermute | solution.py:54
  16.5 1.4 %copy-start.1 = (bf16[512,1536]{1,0:T(8,128)(2,1)S(1)}, bf16[512,1536]{1,0:T(8,128)(2,1)}, u32[]{:S(2)}) copy-start(bf16[512,1536]{1,0:T(8,128)(2,1)} %refs_0_.1) | copy-start | bytes 4718596
  21.1 2.1 %collective-permute-start.7 = (bf16[128,1024]{1,0:T(8,128)(2,1)S(1)}, bf16[128,1024]{1,0:T(8,128)(2,1)S(1)}, u32[]{:S(2)}, u32[]{:S(2)}) collective-permute-start(bf16[128,1024]{1,0:T(8,128)(2,1)S(1)} %collective-permute-done.2.refs_0_), channel_id=1, source_target_pairs={{0,1},{1,0},{2,3},{3,2},{4,5},{5,4},{6,7},{7,6},{8,9},{9,8},{10,11... | collective-permute-start | bytes 786440 | tf_op jit(solution)/shard_map/ppermute | solution.py:54
  21.7 1.5 %collective-permute-start.11 = (bf16[128,1024]{1,0:T(8,128)(2,1)S(1)}, bf16[128,1024]{1,0:T(8,128)(2,1)S(1)}, u32[]{:S(2)}, u32[]{:S(2)}) collective-permute-start(bf16[128,1024]{1,0:T(8,128)(2,1)S(1)} %collective-permute-done.6.refs_4_), channel_id=1, source_target_pairs={{0,1},{1,0},{2,3},{3,2},{4,5},{5,4},{6,7},{7,6},{8,9},{9,8},{10,11... | collective-permute-start | bytes 786440 | tf_op jit(solution)/shard_map/ppermute | solution.py:54
  21.8 2.2 %collective-permute-start.8 = (bf16[128,1024]{1,0:T(8,128)(2,1)S(1)}, bf16[128,1024]{1,0:T(8,128)(2,1)S(1)}, u32[]{:S(2)}, u32[]{:S(2)}) collective-permute-start(bf16[128,1024]{1,0:T(8,128)(2,1)S(1)} %collective-permute-done.3.refs_1_), channel_id=1, source_target_pairs={{0,1},{1,0},{2,3},{3,2},{4,5},{5,4},{6,7},{7,6},{8,9},{9,8},{10,11... | collective-permute-start | bytes 786440 | tf_op jit(solution)/shard_map/ppermute | solution.py:54
  22.2 1.8 %collective-permute-start.10 = (bf16[64,1024]{1,0:T(8,128)(2,1)}, bf16[64,1024]{1,0:T(8,128)(2,1)S(1)}, u32[]{:S(2)}, u32[]{:S(2)}) collective-permute-start(bf16[64,1024]{1,0:T(8,128)(2,1)} %collective-permute-done.5.refs_3_), channel_id=1, source_target_pairs={{0,1},{1,0},{2,3},{3,2},{4,5},{5,4},{6,7},{7,6},{8,9},{9,8},{10,11... | collective-permute-start | bytes 393224 | tf_op jit(solution)/shard_map/ppermute | solution.py:54
  25.5 13.9 %collective-permute-start.12 = (bf16[128,1024]{1,0:T(8,128)(2,1)S(1)}, bf16[128,1024]{1,0:T(8,128)(2,1)S(1)}, u32[]{:S(2)}, u32[]{:S(2)}) collective-permute-start(bf16[128,1024]{1,0:T(8,128)(2,1)S(1)} %get-tuple-element.24), channel_id=1, source_target_pairs={{0,12},{4,8},{8,4},{12,0},{16,28},{20,24},{24,20},{28,16},{1,13},{... | collective-permute-start | bytes 786440 | tf_op jit(solution)/shard_map/ppermute | solution.py:412
  27.1 13.5 %collective-permute-start.13 = (bf16[128,1024]{1,0:T(8,128)(2,1)S(1)}, bf16[128,1024]{1,0:T(8,128)(2,1)S(1)}, u32[]{:S(2)}, u32[]{:S(2)}) collective-permute-start(bf16[128,1024]{1,0:T(8,128)(2,1)S(1)} %get-tuple-element.24), channel_id=1, source_target_pairs={{0,8},{4,12},{8,0},{12,4},{16,24},{20,28},{24,16},{28,20},{1,9},{5... | collective-permute-start | bytes 786440 | tf_op jit(solution)/shard_map/ppermute | solution.py:412
  28.5 12.0 %collective-permute-start.14 = (bf16[128,1024]{1,0:T(8,128)(2,1)S(1)}, bf16[128,1024]{1,0:T(8,128)(2,1)S(1)}, u32[]{:S(2)}, u32[]{:S(2)}) collective-permute-start(bf16[128,1024]{1,0:T(8,128)(2,1)S(1)} %get-tuple-element.24), channel_id=1, source_target_pairs={{0,4},{4,0},{8,12},{12,8},{16,20},{20,16},{24,28},{28,24},{1,5},{5... | collective-permute-start | bytes 786440 | tf_op jit(solution)/shard_map/ppermute | solution.py:412
where the time goes:
time: 41.5 us; the launch traced here: 41.2 us
  starting transfers between devices  14.1 us (34%)
  Pallas kernels  11.1 us (27%)
  local copies, waits for them, and re-layouts  7.72 us (19%)
  blocking collectives  4.58 us (11%)
  waiting for transfers between devices  3.46 us (8%)
    ppermute x12, starting transfers between devices, swap(): return lax.ppermute(value, axis, [(i, i ^ bit) for i in range(count)])  10.6 us
    pallas_call x5, Pallas kernels, call(): pl.pallas_call(kernel, in_specs=[scalar_spec] + [whole] * len(args), out_...  10.5 us
    all_to_all x1, blocking collectives, body(): lax.all_to_all(slots_out, 'fsdp', 0, 0, axis_index_groups=[[i, i + 1] for...  4.58 us
    ppermute x3, starting transfers between devices, body(): lax.ppermute(pack, 'seq', partners(seq_size, place, step))  3.55 us
    dynamic_slice x2, local copies, waits for them, and re-layouts, body(): lax.dynamic_slice(ordered('c' + tag, qkv_weight, known), (start + side *...  2.67 us
    ppermute x12, waiting for transfers between devices, swap(): return lax.ppermute(value, axis, [(i, i ^ bit) for i in range(count)])  2.3 us
    slice x1, local copies, waits for them, and re-layouts, body(): cut = ordered('cQ', qkv_weight, known)[:, :WIDTH]  1.87 us
    slice x1, local copies, waits for them, and re-layouts, body(): cut = ordered('cD', qkv_weight, known)[direct_from:, WIDTH:]  1.67 us
  transfers between devices with their start and end apart: 15, of which 4 were waited for; matrix products, arithmetic and copies ran while one was open for 15% of the time, Pallas kernels for 25%

commit v1 on v0

--- a/solution.py
+++ b/solution.py
@@ -18,7 +18,7 @@
 SCALE2 = HEAD_DIM ** (-0.5) * math.log2(math.e)
 VMEM_LIMIT = 24 * 1024 * 1024
 
-MODEL_FLOPS = {"slot_queries": 575000, "project_pack": 689999, "project_own": 3680000, "project_mid": 1610000, "project_kv": 2990000, "attend_local": 6325000, "merge_near": 2990000}
+MODEL_FLOPS = {"project_first": 689999, "slot_queries": 575000, "project_pack": 689999, "project_own": 3680000, "project_mid": 1610000, "project_kv": 2990000, "attend_local": 6325000, "merge_near": 2990000}
 ORDER = {
     'c1': ('c0',),
     'cD': ('c1',),
@@ -92,12 +92,14 @@
         out[:, lanes] = add_up(tokens, [meta[at] for at in range(count)], [weight.at[:, lanes] for weight in weights])
 
 
-def pack_kernel(layout, base_at, slots, slot_at, meta, tokens, partial, *refs):
-    arrived, packs, joined = refs[: len(layout)], refs[len(layout) : -1], refs[-1]
+def near_rows_kernel(layout, place_at, first, slots, slot_at, meta, tokens, before, *refs):
+    arrived, refs = refs[: len(layout)], refs[len(layout) :]
+    sums, joined = refs[:slots], refs[slots]
     for at, array in zip(layout, arrived):
         rows = array.shape[0]
         joined[pl.ds(pl.multiple_of(meta[at], rows), rows), :] = array[...]
-    columns = pl.ds(pl.multiple_of(meta[base_at], joined.shape[0]), joined.shape[0])
+    depth = joined.shape[0]
+    columns = pl.ds(pl.multiple_of(meta[place_at], depth), depth)
     for slot in range(slots):
         for head in range(HEADS):
             rows = rows_of(meta[slot_at + HEADS * slot + head])
@@ -105,20 +107,32 @@
             weight = jnp.concatenate([joined[:, part] for part in lanes], axis=1)
             product = jnp.dot(tokens[rows, columns], weight, preferred_element_type=F32)
             for field, part in enumerate(lanes):
-                own = partial[rows, WIDTH + part.start : WIDTH + part.stop]
-                total = own + product[:, field * HEAD_DIM : (field + 1) * HEAD_DIM]
-                packs[slot][:, part] = total.astype(BF16)
+                if first:
+                    total = before[0][rows, WIDTH + part.start : WIDTH + part.stop]
+                else:
+                    total = before[slot][:, part]
+                total = total + product[:, field * HEAD_DIM : (field + 1) * HEAD_DIM]
+                sums[slot][:, part] = total.astype(sums[slot].dtype)
+
+
+def first_rows_kernel(layout, place_at, slots, slot_at, meta, tokens, partial, *refs):
+    near_rows_kernel(layout, place_at, True, slots, slot_at, meta, tokens, [partial], *refs)
+
+
+def last_rows_kernel(layout, place_at, slots, slot_at, meta, tokens, *refs):
+    near_rows_kernel(layout, place_at, False, slots, slot_at, meta, tokens, refs[:slots], *refs[slots:])
 
 
 def slot_kernel(core_at, meta, source, out):
     out[1 - meta[core_at]] = source[...]
 
 
-def kv_kernel(base_at, meta, tokens, partial, joined, kv):
-    columns = pl.ds(pl.multiple_of(meta[base_at], joined.shape[0]), joined.shape[0])
+def kv_kernel(places_at, meta, tokens, partial, *refs):
+    parts, kv = refs[:-1], refs[-1]
+    places = [meta[at] for at in places_at]
     for j in range(2 * WIDTH // PAIR):
         lanes = slice(j * PAIR, (j + 1) * PAIR)
-        product = jnp.dot(tokens[:, columns], joined[:, lanes], preferred_element_type=F32)
+        product = add_up(tokens, places, [part.at[:, lanes] for part in parts])
         kv[:, lanes] = (partial[:, WIDTH + j * PAIR : WIDTH + (j + 1) * PAIR] + product).astype(BF16)
 
 
@@ -312,12 +326,10 @@
     match_at = slot_at + 2 * HEADS
     offsets_at = match_at + HEADS
     offsets = []
-    for core in range(2):
-        first = (mine % 2 ^ core) * share
-        for number, (start, rows) in enumerate(spans):
-            side = seq_index // (1 << number) % 2
-            offsets += [first + start + side * rows, first + start + (1 - side) * rows]
-        offsets.append(first + direct_from)
+    for number, (start, rows) in enumerate(spans):
+        side = seq_index // (1 << number) % 2
+        offsets += [start + side * rows, start + (1 - side) * rows]
+    offsets.append(direct_from)
     as_array = lambda values: jnp.stack([jnp.asarray(value, jnp.int32) for value in values])
     meta = jnp.concatenate(
         [as_array(scalars), near_offset, far_offset % block_rate, far_match, as_array(offsets)]
@@ -384,17 +396,25 @@
         queries.append(swap(cut, "fsdp", bit))
     assert len(bits) <= 1
     if bits:
-        layout = [offsets_at + i for i in range(len(direct_rows[0]))]
-        *packs, joined = call(
-            functools.partial(pack_kernel, layout, base_at, slots, slot_at),
-            [sequence, partial, *direct_rows[0]],
-            [shape((BLOCK, 2 * WIDTH), BF16)] * slots + [shape((2 * share, 2 * WIDTH), BF16)],
+        bit = bits[0]
+        count = len(direct_rows[0]) // 2
+        layout = [offsets_at + i for i in range(count)]
+        *sums, joined = call(
+            functools.partial(first_rows_kernel, layout, bit, slots, slot_at),
+            [sequence, ordered("a", partial, known), *direct_rows[0][:count]],
+            [shape((BLOCK, 2 * WIDTH), F32)] * slots + [shape((share, 2 * WIDTH), BF16)],
+            "project_first",
+        )
+        *packs, joined_other = call(
+            functools.partial(last_rows_kernel, layout, bit ^ 1, slots, slot_at),
+            [sequence, *sums, *direct_rows[0][count:]],
+            [shape((BLOCK, 2 * WIDTH), BF16)] * slots + [shape((share, 2 * WIDTH), BF16)],
             "project_pack",
         )
         known["pack"] = packs[0]
         (kv,) = call(
-            functools.partial(kv_kernel, base_at),
-            [sequence, ordered("kv", partial, known), joined],
+            functools.partial(kv_kernel, [bit, bit ^ 1]),
+            [sequence, ordered("kv", partial, known), joined, joined_other],
             [shape((row_count, 2 * WIDTH), BF16)],
             "project_kv",
         )

time: 41.5 us -> 40.9 us (0.986)
  waiting for transfers between devices: 3.46 us -> 2.1 us
  Pallas kernels: 11.1 us -> 11.8 us
    ppermute x12, waiting for transfers between devices: 2.3 us -> 1.38 us  [swap(): return lax.ppermute(value, axis, [(i, i ^ bit) for i in range(count)])]
    pallas_call x5 -> x6, Pallas kernels: 10.5 us -> 11.3 us  [call(): pl.pallas_call(kernel, in_specs=[scalar_spec] + [whole] * len(args), out_...]
    ppermute x3, waiting for transfers between devices: 1.16 us -> 0.72 us  [body(): lax.ppermute(pack, 'seq', partners(seq_size, place, step))]
  transfers between devices with their start and end apart: 15 -> 15, of which waited for: 4 -> 4; matrix products, arithmetic and copies ran while one was open for 15% -> 16% of each run, Pallas kernels for 25% -> 28%
where the time goes in v1:
time: 40.9 us; the launch traced here: 40.6 us
  starting transfers between devices  14.1 us (34%)
  Pallas kernels  11.8 us (29%)
  local copies, waits for them, and re-layouts  7.7 us (19%)
  blocking collectives  4.58 us (11%)
  waiting for transfers between devices  2.1 us (5%)
    pallas_call x6, Pallas kernels, call(): pl.pallas_call(kernel, in_specs=[scalar_spec] + [whole] * len(args), out_...  11.3 us
    ppermute x12, starting transfers between devices, swap(): return lax.ppermute(value, axis, [(i, i ^ bit) for i in range(count)])  10.6 us
    all_to_all x1, blocking collectives, body(): lax.all_to_all(slots_out, 'fsdp', 0, 0, axis_index_groups=[[i, i + 1] for...  4.58 us
    ppermute x3, starting transfers between devices, body(): lax.ppermute(pack, 'seq', partners(seq_size, place, step))  3.55 us
    dynamic_slice x2, local copies, waits for them, and re-layouts, body(): lax.dynamic_slice(ordered('c' + tag, qkv_weight, known), (start + side *...  2.67 us
    slice x1, local copies, waits for them, and re-layouts, body(): cut = ordered('cQ', qkv_weight, known)[:, :WIDTH]  1.87 us
    slice x1, local copies, waits for them, and re-layouts, body(): cut = ordered('cD', qkv_weight, known)[direct_from:, WIDTH:]  1.66 us
    unnamed x8, local copies, waits for them, and re-layouts  1.41 us
  transfers between devices with their start and end apart: 15, of which 4 were waited for; matrix products, arithmetic and copies ran while one was open for 16% of the time, Pallas kernels for 28%

profile of v1, /device:TPU:0, one launch (start us, length us, event | category | flops | bytes accessed | tf_op | source)
XLA Modules:
  0.0 40.6 jit_solution(5351071145790159533)
XLA Ops:
  0.0 0.5 %collective-permute-start = (bf16[512,1536]{1,0:T(8,128)(2,1)}, bf16[512,1536]{1,0:T(8,128)(2,1)}, u32[]{:S(2)}, u32[]{:S(2)}) collective-permute-start(bf16[512,1536]{1,0:T(8,128)(2,1)} %refs_0_.1), channel_id=1, source_target_pairs={{0,1},{1,0},{2,3},{3,2},{4,5},{5,4},{6,7},{7,6},{8,9},{9,8},{10,11... | collective-permute-start | bytes 4718600 | tf_op jit(solution)/shard_map/ppermute | solution.py:54
  0.5 1.1 %constant_dynamic-slice_fusion.1 = bf16[128,1024]{1,0:T(8,128)(2,1)S(1)} fusion(bf16[512,1536]{1,0:T(8,128)(2,1)} %refs_0_.1, s32[]{:T(128)S(6)} %select_n.73), kind=kLoop, calls=%fused_computation.7 | loop fusion | bytes 524292 | tf_op jit(solution)/shard_map/dynamic_slice | solution.py:373
  1.6 2.6 %collective-permute-start.2 = (bf16[128,1024]{1,0:T(8,128)(2,1)S(1)}, bf16[128,1024]{1,0:T(8,128)(2,1)S(1)}, u32[]{:S(2)}, u32[]{:S(2)}) collective-permute-start(bf16[128,1024]{1,0:T(8,128)(2,1)S(1)} %constant_dynamic-slice_fusion.1), channel_id=1, source_target_pairs={{0,2},{1,3},{2,0},{3,1},{4,6},{5,7},{6,4},{7,5},{8,10},{9,11},{10,... | collective-permute-start | bytes 786440 | tf_op jit(solution)/shard_map/ppermute | solution.py:54
  4.2 1.6 %constant_dynamic-slice_fusion = bf16[64,1024]{1,0:T(8,128)(2,1)} fusion(bf16[512,1536]{1,0:T(8,128)(2,1)} %refs_0_.1, s32[]{:T(128)S(6)} %select_n.74), kind=kLoop, calls=%fused_computation.6 | loop fusion | bytes 262148 | tf_op jit(solution)/shard_map/dynamic_slice | solution.py:373
  5.8 1.7 %slice.6 = bf16[128,1024]{1,0:T(8,128)(2,1)} slice(bf16[512,1536]{1,0:T(8,128)(2,1)} %refs_0_.1), slice={[384:512], [512:1536]} | slice | bytes 524288 | tf_op jit(solution)/shard_map/slice | solution.py:387
  7.5 2.0 %collective-permute-start.6 = (bf16[128,1024]{1,0:T(8,128)(2,1)}, bf16[128,1024]{1,0:T(8,128)(2,1)S(1)}, u32[]{:S(2)}, u32[]{:S(2)}) collective-permute-start(bf16[128,1024]{1,0:T(8,128)(2,1)} %slice.6), channel_id=1, source_target_pairs={{0,2},{1,3},{2,0},{3,1},{4,6},{5,7},{6,4},{7,5},{8,10},{9,11},{10,... | collective-permute-start | bytes 786440 | tf_op jit(solution)/shard_map/ppermute | solution.py:54
  9.5 1.9 %slice.7 = bf16[512,512]{1,0:T(8,128)(2,1)} slice(bf16[512,1536]{1,0:T(8,128)(2,1)} %refs_0_.1), slice={[0:512], [0:512]} | slice | bytes 1048576 | tf_op jit(solution)/shard_map/slice | solution.py:394
  11.4 2.0 %collective-permute-start.3 = (bf16[128,1024]{1,0:T(8,128)(2,1)S(1)}, bf16[128,1024]{1,0:T(8,128)(2,1)S(1)}, u32[]{:S(2)}, u32[]{:S(2)}) collective-permute-start(bf16[128,1024]{1,0:T(8,128)(2,1)S(1)} %collective-permute-done.2.refs_0_), channel_id=1, source_target_pairs={{0,4},{4,0},{8,12},{12,8},{16,20},{20,16},{24,28},{28,24},{1,5},{5... | collective-permute-start | bytes 786440 | tf_op jit(solution)/shard_map/ppermute | solution.py:54
  13.5 0.6 %collective-permute-done.4.refs_2_ = bf16[64,1024]{1,0:T(8,128)(2,1)S(1)} collective-permute-done((bf16[64,1024]{1,0:T(8,128)(2,1)}, bf16[64,1024]{1,0:T(8,128)(2,1)S(1)}, u32[]{:S(2)}, u32[]{:S(2)}) %collective-permute-start.4) | collective-permute-done | bytes 131104 | tf_op jit(solution)/shard_map/ppermute | solution.py:54
  14.1 2.1 %collective-permute-start.5 = (bf16[64,1024]{1,0:T(8,128)(2,1)S(1)}, bf16[64,1024]{1,0:T(8,128)(2,1)}, u32[]{:S(2)}, u32[]{:S(2)}) collective-permute-start(bf16[64,1024]{1,0:T(8,128)(2,1)S(1)} %collective-permute-done.4.refs_2_), channel_id=1, source_target_pairs={{0,8},{4,12},{8,0},{12,4},{16,24},{20,28},{24,16},{28,20},{1,9},{5... | collective-permute-start | bytes 393224 | tf_op jit(solution)/shard_map/ppermute | solution.py:54
  16.5 1.4 %copy-done.1 = bf16[512,1536]{1,0:T(8,128)(2,1)S(1)} copy-done((bf16[512,1536]{1,0:T(8,128)(2,1)S(1)}, bf16[512,1536]{1,0:T(8,128)(2,1)}, u32[]{:S(2)}) %copy-start.1) | copy-done | bytes 1572888
  17.9 3.2 %project_own.1.partial = f32[512,1536]{1,0:T(8,128)S(1)} custom-call(s32[25]{0:T(128)S(1)} %concatenate.3.meta, bf16[512,2048]{1,0:T(8,128)(2,1)S(1)} %bitcast.13, bf16[512,1536]{1,0:T(8,128)(2,1)S(1)} %copy-done.1, bf16[512,1536]{1,0:T(8,128)(2,1)} %collective-permute-done.refs_1_), custom_call_target="tpu_custom_call" | custom-call | flops 3680000 | bytes 1000 | tf_op jit(solution)/shard_map/project_own/pallas_call | solution.py:343
  21.1 0.6 %collective-permute-start.7 = (bf16[128,1024]{1,0:T(8,128)(2,1)S(1)}, bf16[128,1024]{1,0:T(8,128)(2,1)S(1)}, u32[]{:S(2)}, u32[]{:S(2)}) collective-permute-start(bf16[128,1024]{1,0:T(8,128)(2,1)S(1)} %collective-permute-done.2.refs_0_), channel_id=1, source_target_pairs={{0,1},{1,0},{2,3},{3,2},{4,5},{5,4},{6,7},{7,6},{8,9},{9,8},{10,11... | collective-permute-start | bytes 786440 | tf_op jit(solution)/shard_map/ppermute | solution.py:54
  22.3 1.3 %project_first.1 = (f32[128,1024]{1,0:T(8,128)S(1)}, bf16[512,1024]{1,0:T(8,128)(2,1)S(1)}) custom-call(s32[25]{0:T(128)S(1)} %concatenate.3.meta, bf16[512,2048]{1,0:T(8,128)(2,1)S(1)} %bitcast.14, f32[512,1536]{1,0:T(8,128)S(1)} %project_own.1.partial, bf16[128,1024]{1,0:T(8,128)(2,1)S(1)} %collective-permute-done.2.refs_0_, ...), custom_call_target="tpu_custom_call" | custom-call | flops 689999 | bytes 1000 | tf_op jit(solution)/shard_map/project_first/pallas_call | solution.py:343
  24.0 0.9 %project_pack.1 = (bf16[128,1024]{1,0:T(8,128)(2,1)S(1)}, bf16[512,1024]{1,0:T(8,128)(2,1)S(1)}) custom-call(s32[25]{0:T(128)S(1)} %concatenate.3.meta, bf16[512,2048]{1,0:T(8,128)(2,1)S(1)} %bitcast.15, f32[128,1024]{1,0:T(8,128)S(1)} %get-tuple-element.26.refs_0_, bf16[128,1024]{1,0:T(8,128)(2,1)S(1)} %collective-permute-done.7.refs_1_, ...), custom_call_target="tpu_custom_call" | custom-call | flops 689999 | bytes 1000 | tf_op jit(solution)/shard_map/project_pack/pallas_call | solution.py:343
  24.9 1.6 %collective-permute-start.12 = (bf16[128,1024]{1,0:T(8,128)(2,1)S(1)}, bf16[128,1024]{1,0:T(8,128)(2,1)S(1)}, u32[]{:S(2)}, u32[]{:S(2)}) collective-permute-start(bf16[128,1024]{1,0:T(8,128)(2,1)S(1)} %get-tuple-element.27), channel_id=1, source_target_pairs={{0,12},{4,8},{8,4},{12,0},{16,28},{20,24},{24,20},{28,16},{1,13},{... | collective-permute-start | bytes 786440 | tf_op jit(solution)/shard_map/ppermute | solution.py:432
  26.5 1.5 %collective-permute-start.13 = (bf16[128,1024]{1,0:T(8,128)(2,1)S(1)}, bf16[128,1024]{1,0:T(8,128)(2,1)S(1)}, u32[]{:S(2)}, u32[]{:S(2)}) collective-permute-start(bf16[128,1024]{1,0:T(8,128)(2,1)S(1)} %get-tuple-element.27), channel_id=1, source_target_pairs={{0,8},{4,12},{8,0},{12,4},{16,24},{20,28},{24,16},{28,20},{1,9},{5... | collective-permute-start | bytes 786440 | tf_op jit(solution)/shard_map/ppermute | solution.py:432
  28.0 0.5 %collective-permute-start.14 = (bf16[128,1024]{1,0:T(8,128)(2,1)S(1)}, bf16[128,1024]{1,0:T(8,128)(2,1)S(1)}, u32[]{:S(2)}, u32[]{:S(2)}) collective-permute-start(bf16[128,1024]{1,0:T(8,128)(2,1)S(1)} %get-tuple-element.27), channel_id=1, source_target_pairs={{0,4},{4,0},{8,12},{12,8},{16,20},{20,16},{24,28},{28,24},{1,5},{5... | collective-permute-start | bytes 786440 | tf_op jit(solution)/shard_map/ppermute | solution.py:432
  28.5 1.8 %project_kv.1.refs_2_ = bf16[512,1024]{1,0:T(8,128)(2,1)S(1)} custom-call(s32[25]{0:T(128)S(1)} %concatenate.3.meta, bf16[512,2048]{1,0:T(8,128)(2,1)S(1)} %bitcast.16, f32[512,1536]{1,0:T(8,128)S(1)} %project_own.1.partial, bf16[512,1024]{1,0:T(8,128)(2,1)S(1)} %get-tuple-element.29.refs_0_, bf16[512,1024]{1,0:T(8,128)(2,1)S(1)} %get-tuple-element.30.refs_1_), custom_call_target="tpu_custom_call" | custom-call | flops 2990000 | bytes 1000 | tf_op jit(solution)/shard_map/project_kv/pallas_call | solution.py:343
  30.7 0.6 %slot_queries.1 = bf16[2,512,512]{2,1,0:T(8,128)(2,1)S(1)} custom-call(s32[25]{0:T(128)S(1)} %concatenate.3.meta, bf16[512,512]{1,0:T(8,128)(2,1)S(1)} %collective-permute-done.1.source.refs_0_), custom_call_target="tpu_custom_call" | custom-call | flops 575000 | bytes 1000 | tf_op jit(solution)/shard_map/slot_queries/pallas_call | solution.py:343
  31.3 4.6 %all_to_all.5.refs_1_ = bf16[2,512,512]{2,1,0:T(8,128)(2,1)S(1)} all-to-all(bf16[2,512,512]{2,1,0:T(8,128)(2,1)S(1)} %slot_queries.1), channel_id=1, replica_groups={{0,1},{2,3},{4,5},{6,7},{8,9},{10,11},{12,13},{14,15},{16,17},{18,19},{..., dimensions={0} | all-to-all | bytes 2097152 | tf_op jit(solution)/shard_map/all_to_all | solution.py:442
  35.9 3.4 %attend_local.1 = (bf16[512,512]{1,0:T(8,128)(2,1)}, bf16[128,512]{1,0:T(8,128)(2,1)S(1)}, f32[128,512]{1,0:T(8,128)S(1)}, f32[128,512]{1,0:T(8,128)S(1)}, f32[128,512]{1,0:T(8,128)S(1)}) custom-call(s32[25]{0:T(128)S(1)} %concatenate.3.meta, bf16[512,2048]{1,0:T(8,128)(2,1)S(1)} %bitcast.17, f32[512,1536]{1,0:T(8,128)S(1)} %project_own.1.partial, ...), custom_call_target="tpu_custom_call" | custom-call | flops 6325000 | bytes 1000 | tf_op jit(solution)/shard_map/attend_local/pallas_call | solution.py:343
  39.3 0.7 %collective-permute-done.13.refs_5_ = bf16[128,1024]{1,0:T(8,128)(2,1)S(1)} collective-permute-done((bf16[128,1024]{1,0:T(8,128)(2,1)S(1)}, bf16[128,1024]{1,0:T(8,128)(2,1)S(1)}, u32[]{:S(2)}, u32[]{:S(2)}) %collective-permute-start.13) | collective-permute-done | bytes 262176 | tf_op jit(solution)/shard_map/ppermute | solution.py:432
  40.0 0.6 %merge_near.1 = bf16[512,512]{1,0:T(8,128)(2,1)} custom-call(s32[25]{0:T(128)S(1)} %concatenate.3.meta, bf16[128,512]{1,0:T(8,128)(2,1)S(1)} %get-tuple-element.32.refs_0_, f32[128,512]{1,0:T(8,128)S(1)} %get-tuple-element.33.refs_1_, f32[128,512]{1,0:T(8,128)S(1)} %get-tuple-element.34.refs_2_, ...), custom_call_target="tpu_custom_call", output_to_operand_aliasing={{}: (8, {})} | custom-call | flops 2990000 | bytes 1000 | tf_op jit(solution)/shard_map/merge_near/pallas_call | solution.py:456
  (29 shorter events, 1.7 us)
Async XLA Ops:
  0.0 13.4 %copy-start.3 = (s32[4]{0:T(128)S(1)}, s32[4]{0:T(128)}, u32[]{:S(2)}) copy-start(s32[4]{0:T(128)} %param.7) | copy-start | bytes 52
  0.0 16.3 %copy-start.2 = (s32[4]{0:T(128)S(1)}, s32[4]{0:T(128)}, u32[]{:S(2)}) copy-start(s32[4]{0:T(128)} %param.6) | copy-start | bytes 52
  0.0 16.5 %copy-start = (bf16[1,512,2048]{2,1,0:T(8,128)(2,1)S(1)}, bf16[1,512,2048]{2,1,0:T(8,128)(2,1)}, u32[]{:S(2)}) copy-start(bf16[1,512,2048]{2,1,0:T(8,128)(2,1)} %param.4) | copy-start | bytes 6291460
  0.0 16.4 %collective-permute-start = (bf16[512,1536]{1,0:T(8,128)(2,1)}, bf16[512,1536]{1,0:T(8,128)(2,1)}, u32[]{:S(2)}, u32[]{:S(2)}) collective-permute-start(bf16[512,1536]{1,0:T(8,128)(2,1)} %refs_0_.1), channel_id=1, source_target_pairs={{0,1},{1,0},{2,3},{3,2},{4,5},{5,4},{6,7},{7,6},{8,9},{9,8},{10,11... | collective-permute-start | bytes 4718600 | tf_op jit(solution)/shard_map/ppermute | solution.py:54
  1.6 9.8 %collective-permute-start.2 = (bf16[128,1024]{1,0:T(8,128)(2,1)S(1)}, bf16[128,1024]{1,0:T(8,128)(2,1)S(1)}, u32[]{:S(2)}, u32[]{:S(2)}) collective-permute-start(bf16[128,1024]{1,0:T(8,128)(2,1)S(1)} %constant_dynamic-slice_fusion.1), channel_id=1, source_target_pairs={{0,2},{1,3},{2,0},{3,1},{4,6},{5,7},{6,4},{7,5},{8,10},{9,11},{10,... | collective-permute-start | bytes 786440 | tf_op jit(solution)/shard_map/ppermute | solution.py:54
  5.8 8.3 %collective-permute-start.4 = (bf16[64,1024]{1,0:T(8,128)(2,1)}, bf16[64,1024]{1,0:T(8,128)(2,1)S(1)}, u32[]{:S(2)}, u32[]{:S(2)}) collective-permute-start(bf16[64,1024]{1,0:T(8,128)(2,1)} %constant_dynamic-slice_fusion), channel_id=1, source_target_pairs={{0,2},{1,3},{2,0},{3,1},{4,6},{5,7},{6,4},{7,5},{8,10},{9,11},{10,... | collective-permute-start | bytes 393224 | tf_op jit(solution)/shard_map/ppermute | solution.py:54
  7.5 13.6 %collective-permute-start.6 = (bf16[128,1024]{1,0:T(8,128)(2,1)}, bf16[128,1024]{1,0:T(8,128)(2,1)S(1)}, u32[]{:S(2)}, u32[]{:S(2)}) collective-permute-start(bf16[128,1024]{1,0:T(8,128)(2,1)} %slice.6), channel_id=1, source_target_pairs={{0,2},{1,3},{2,0},{3,1},{4,6},{5,7},{6,4},{7,5},{8,10},{9,11},{10,... | collective-permute-start | bytes 786440 | tf_op jit(solution)/shard_map/ppermute | solution.py:54
  11.3 19.3 %collective-permute-start.1 = (bf16[512,512]{1,0:T(8,128)(2,1)}, bf16[512,512]{1,0:T(8,128)(2,1)S(1)}, u32[]{:S(2)}, u32[]{:S(2)}) collective-permute-start(bf16[512,512]{1,0:T(8,128)(2,1)} %slice.7), channel_id=1, source_target_pairs={{0,2},{1,3},{2,0},{3,1},{4,6},{5,7},{6,4},{7,5},{8,10},{9,11},{10,... | collective-permute-start | bytes 1572872 | tf_op jit(solution)/shard_map/ppermute | solution.py:54
  11.4 10.3 %collective-permute-start.3 = (bf16[128,1024]{1,0:T(8,128)(2,1)S(1)}, bf16[128,1024]{1,0:T(8,128)(2,1)S(1)}, u32[]{:S(2)}, u32[]{:S(2)}) collective-permute-start(bf16[128,1024]{1,0:T(8,128)(2,1)S(1)} %collective-permute-done.2.refs_0_), channel_id=1, source_target_pairs={{0,4},{4,0},{8,12},{12,8},{16,20},{20,16},{24,28},{28,24},{1,5},{5... | collective-permute-start | bytes 786440 | tf_op jit(solution)/shard_map/ppermute | solution.py:54
  14.1 7.6 %collective-permute-start.5 = (bf16[64,1024]{1,0:T(8,128)(2,1)S(1)}, bf16[64,1024]{1,0:T(8,128)(2,1)}, u32[]{:S(2)}, u32[]{:S(2)}) collective-permute-start(bf16[64,1024]{1,0:T(8,128)(2,1)S(1)} %collective-permute-done.4.refs_2_), channel_id=1, source_target_pairs={{0,8},{4,12},{8,0},{12,4},{16,24},{20,28},{24,16},{28,20},{1,9},{5... | collective-permute-start | bytes 393224 | tf_op jit(solution)/shard_map/ppermute | solution.py:54
  16.4 5.8 %collective-permute-start.9 = (bf16[64,1024]{1,0:T(8,128)(2,1)S(1)}, bf16[64,1024]{1,0:T(8,128)(2,1)S(1)}, u32[]{:S(2)}, u32[]{:S(2)}) collective-permute-start(bf16[64,1024]{1,0:T(8,128)(2,1)S(1)} %collective-permute-done.4.refs_2_), channel_id=1, source_target_pairs={{0,1},{1,0},{2,3},{3,2},{4,5},{5,4},{6,7},{7,6},{8,9},{9,8},{10,11... | collective-permute-start | bytes 393224 | tf_op jit(solution)/shard_map/ppermute | solution.py:54
  16.5 1.4 %copy-start.1 = (bf16[512,1536]{1,0:T(8,128)(2,1)S(1)}, bf16[512,1536]{1,0:T(8,128)(2,1)}, u32[]{:S(2)}) copy-start(bf16[512,1536]{1,0:T(8,128)(2,1)} %refs_0_.1) | copy-start | bytes 4718596
  21.1 2.5 %collective-permute-start.7 = (bf16[128,1024]{1,0:T(8,128)(2,1)S(1)}, bf16[128,1024]{1,0:T(8,128)(2,1)S(1)}, u32[]{:S(2)}, u32[]{:S(2)}) collective-permute-start(bf16[128,1024]{1,0:T(8,128)(2,1)S(1)} %collective-permute-done.2.refs_0_), channel_id=1, source_target_pairs={{0,1},{1,0},{2,3},{3,2},{4,5},{5,4},{6,7},{7,6},{8,9},{9,8},{10,11... | collective-permute-start | bytes 786440 | tf_op jit(solution)/shard_map/ppermute | solution.py:54
  21.7 1.9 %collective-permute-start.11 = (bf16[128,1024]{1,0:T(8,128)(2,1)S(1)}, bf16[128,1024]{1,0:T(8,128)(2,1)S(1)}, u32[]{:S(2)}, u32[]{:S(2)}) collective-permute-start(bf16[128,1024]{1,0:T(8,128)(2,1)S(1)} %collective-permute-done.6.refs_4_), channel_id=1, source_target_pairs={{0,1},{1,0},{2,3},{3,2},{4,5},{5,4},{6,7},{7,6},{8,9},{9,8},{10,11... | collective-permute-start | bytes 786440 | tf_op jit(solution)/shard_map/ppermute | solution.py:54
  21.7 2.2 %collective-permute-start.8 = (bf16[128,1024]{1,0:T(8,128)(2,1)S(1)}, bf16[128,1024]{1,0:T(8,128)(2,1)S(1)}, u32[]{:S(2)}, u32[]{:S(2)}) collective-permute-start(bf16[128,1024]{1,0:T(8,128)(2,1)S(1)} %collective-permute-done.3.refs_1_), channel_id=1, source_target_pairs={{0,1},{1,0},{2,3},{3,2},{4,5},{5,4},{6,7},{7,6},{8,9},{9,8},{10,11... | collective-permute-start | bytes 786440 | tf_op jit(solution)/shard_map/ppermute | solution.py:54
  22.2 1.8 %collective-permute-start.10 = (bf16[64,1024]{1,0:T(8,128)(2,1)}, bf16[64,1024]{1,0:T(8,128)(2,1)S(1)}, u32[]{:S(2)}, u32[]{:S(2)}) collective-permute-start(bf16[64,1024]{1,0:T(8,128)(2,1)} %collective-permute-done.5.refs_3_), channel_id=1, source_target_pairs={{0,1},{1,0},{2,3},{3,2},{4,5},{5,4},{6,7},{7,6},{8,9},{9,8},{10,11... | collective-permute-start | bytes 393224 | tf_op jit(solution)/shard_map/ppermute | solution.py:54
  24.9 14.3 %collective-permute-start.12 = (bf16[128,1024]{1,0:T(8,128)(2,1)S(1)}, bf16[128,1024]{1,0:T(8,128)(2,1)S(1)}, u32[]{:S(2)}, u32[]{:S(2)}) collective-permute-start(bf16[128,1024]{1,0:T(8,128)(2,1)S(1)} %get-tuple-element.27), channel_id=1, source_target_pairs={{0,12},{4,8},{8,4},{12,0},{16,28},{20,24},{24,20},{28,16},{1,13},{... | collective-permute-start | bytes 786440 | tf_op jit(solution)/shard_map/ppermute | solution.py:432
  26.5 13.5 %collective-permute-start.13 = (bf16[128,1024]{1,0:T(8,128)(2,1)S(1)}, bf16[128,1024]{1,0:T(8,128)(2,1)S(1)}, u32[]{:S(2)}, u32[]{:S(2)}) collective-permute-start(bf16[128,1024]{1,0:T(8,128)(2,1)S(1)} %get-tuple-element.27), channel_id=1, source_target_pairs={{0,8},{4,12},{8,0},{12,4},{16,24},{20,28},{24,16},{28,20},{1,9},{5... | collective-permute-start | bytes 786440 | tf_op jit(solution)/shard_map/ppermute | solution.py:432
  28.0 12.0 %collective-permute-start.14 = (bf16[128,1024]{1,0:T(8,128)(2,1)S(1)}, bf16[128,1024]{1,0:T(8,128)(2,1)S(1)}, u32[]{:S(2)}, u32[]{:S(2)}) collective-permute-start(bf16[128,1024]{1,0:T(8,128)(2,1)S(1)} %get-tuple-element.27), channel_id=1, source_target_pairs={{0,4},{4,0},{8,12},{12,8},{16,20},{20,16},{24,28},{28,24},{1,5},{5... | collective-permute-start | bytes 786440 | tf_op jit(solution)/shard_map/ppermute | solution.py:432

commit v2 on v1

--- a/solution.py
+++ b/solution.py
@@ -123,8 +123,13 @@
     near_rows_kernel(layout, place_at, False, slots, slot_at, meta, tokens, refs[:slots], *refs[slots:])
 
 
-def slot_kernel(core_at, meta, source, out):
-    out[1 - meta[core_at]] = source[...]
+def slot_kernel(core_at, meta, source, *outs):
+    done = 0
+    for out in outs[:-1]:
+        rows = out.shape[0]
+        out[...] = source[done : done + rows, :]
+        done += rows
+    outs[-1][1 - meta[core_at]] = source[done:, :]
 
 
 def kv_kernel(places_at, meta, tokens, partial, *refs):
@@ -140,10 +145,10 @@
     return jnp.concatenate([value, jnp.ones(value.shape, BF16)], axis=1)
 
 
-def attend_kernel(bases_at, core_at, slots, slot_at, match_at, meta, tokens, partial, *refs):
-    weights, refs = refs[: len(bases_at)], refs[len(bases_at) :]
+def attend_kernel(count, bases_at, core_at, slots, slot_at, match_at, meta, tokens, partial, *refs):
+    weights, refs = refs[:count], refs[count:]
     kv, out, refs = refs[0], refs[1], refs[2:]
-    state, scratch = refs[: 4 * slots], refs[4 * slots :]
+    state, scratch, joined = refs[: 4 * slots], refs[4 * slots : -1], refs[-1]
     query, acc_all, top_all, sum_all = scratch
     blocks = query.shape[0] // BLOCK
     GROUP = 2 if blocks % 2 == 0 else 1
@@ -151,13 +156,17 @@
     column = lax.broadcasted_iota(jnp.int32, (BLOCK, BLOCK), 1)
     causal = column <= row
     places = [meta[at] for at in bases_at]
-    other = 1 - meta[core_at]
+    if weights:
+        done = 0
+        for weight in weights[2:]:
+            joined[done : done + weight.shape[0], :] = weight[...]
+            done += weight.shape[0]
+        joined[done:, :] = weights[1][1 - meta[core_at]]
     for pair in range(HEADS // 2):
         lanes = slice(pair * PAIR, (pair + 1) * PAIR)
         total = partial[:, lanes]
         if weights:
-            parts = [weights[0].at[:, lanes], weights[1].at[other, :, lanes]]
-            total = total + add_up(tokens, places, parts)
+            total = total + add_up(tokens, places, [weights[0].at[:, lanes], joined.at[:, lanes]])
         query[:, lanes] = total.astype(BF16)
 
     def lanes_of(head):
@@ -436,21 +445,27 @@
     crossed_q, q_places = [], []
     for bit, direct in zip(bits, queries):
         direct = ordered("q", direct, known)
-        (slots_out,) = call(
-            functools.partial(slot_kernel, core_at), [direct], [shape((2,) + direct.shape, BF16)], "slot_queries"
+        passing = [share * 15 // 32 // 16 * 16] * 2
+        left = share - sum(passing)
+        *parts, slots_out = call(
+            functools.partial(slot_kernel, core_at),
+            [direct],
+            [shape((rows, WIDTH), BF16) for rows in passing] + [shape((2, left, WIDTH), BF16)],
+            "slot_queries",
         )
         both = lax.all_to_all(
             slots_out, "fsdp", 0, 0, axis_index_groups=[[i, i + 1] for i in range(0, pieces, 2)]
         )
-        crossed_q += [direct, both]
+        crossed_q += [direct, both] + [swap(part, "fsdp", 1) for part in parts]
         q_places += [bit, bit ^ 1]
     state_types = [BF16, F32, F32, F32]
     partial_out, *state = call(
-        functools.partial(attend_kernel, q_places, core_at, slots, slot_at, match_at),
+        functools.partial(attend_kernel, len(crossed_q), q_places, core_at, slots, slot_at, match_at),
         [sequence, partial, *crossed_q, kv],
         [shape((row_count, WIDTH), BF16)] + [shape((BLOCK, WIDTH), kind) for kind in state_types] * slots,
         "attend_local",
-        [pltpu.VMEM((row_count, WIDTH), kind) for kind in state_types],
+        [pltpu.VMEM((row_count, WIDTH), kind) for kind in state_types]
+        + [pltpu.VMEM((share, WIDTH), BF16)],
     )
     count = 4 * slots + sum(shifts)
     merged = pl.pallas_call(

time: 40.9 us -> 40.9 us (level)
  blocking collectives: 4.58 us -> 3.78 us
  starting transfers between devices: 14.1 us -> 14.7 us
    all_to_all x1, blocking collectives: 4.58 us -> 3.78 us  [body(): lax.all_to_all(slots_out, 'fsdp', 0, 0, axis_index_groups=[[i, i + 1] for...]
    ppermute x12 -> x14, starting transfers between devices: 10.6 us -> 11.1 us  [swap(): return lax.ppermute(value, axis, [(i, i ^ bit) for i in range(count)])]
    ppermute x12 -> x14, waiting for transfers between devices: 1.38 us -> 1.37 us  [swap(): return lax.ppermute(value, axis, [(i, i ^ bit) for i in range(count)])]
  transfers between devices with their start and end apart: 15 -> 17, of which waited for: 4 -> 4; matrix products, arithmetic and copies ran while one was open for 16% -> 16% of each run, Pallas kernels for 28% -> 28%
where the time goes in v2:
time: 40.9 us; the launch traced here: 40.6 us
  starting transfers between devices  14.7 us (36%)
  Pallas kernels  11.8 us (29%)
  local copies, waits for them, and re-layouts  7.72 us (19%)
  blocking collectives  3.78 us (9%)
  waiting for transfers between devices  2.3 us (6%)
    pallas_call x6, Pallas kernels, call(): pl.pallas_call(kernel, in_specs=[scalar_spec] + [whole] * len(args), out_...  11.3 us
    ppermute x14, starting transfers between devices, swap(): return lax.ppermute(value, axis, [(i, i ^ bit) for i in range(count)])  11.1 us
    all_to_all x1, blocking collectives, body(): lax.all_to_all(slots_out, 'fsdp', 0, 0, axis_index_groups=[[i, i + 1] for...  3.78 us
    ppermute x3, starting transfers between devices, body(): lax.ppermute(pack, 'seq', partners(seq_size, place, step))  3.55 us
    dynamic_slice x2, local copies, waits for them, and re-layouts, body(): lax.dynamic_slice(ordered('c' + tag, qkv_weight, known), (start + side *...  2.66 us
    slice x1, local copies, waits for them, and re-layouts, body(): cut = ordered('cQ', qkv_weight, known)[:, :WIDTH]  1.87 us
    slice x1, local copies, waits for them, and re-layouts, body(): cut = ordered('cD', qkv_weight, known)[direct_from:, WIDTH:]  1.68 us
    unnamed x8, local copies, waits for them, and re-layouts  1.41 us
  transfers between devices with their start and end apart: 17, of which 4 were waited for; matrix products, arithmetic and copies ran while one was open for 16% of the time, Pallas kernels for 28%

profile of v2, /device:TPU:0, one launch (start us, length us, event | category | flops | bytes accessed | tf_op | source)
XLA Modules:
  0.0 40.6 jit_solution(3629112924221545490)
XLA Ops:
  0.0 0.5 %collective-permute-start = (bf16[512,1536]{1,0:T(8,128)(2,1)}, bf16[512,1536]{1,0:T(8,128)(2,1)}, u32[]{:S(2)}, u32[]{:S(2)}) collective-permute-start(bf16[512,1536]{1,0:T(8,128)(2,1)} %refs_0_.1), channel_id=1, source_target_pairs={{0,1},{1,0},{2,3},{3,2},{4,5},{5,4},{6,7},{7,6},{8,9},{9,8},{10,11... | collective-permute-start | bytes 4718600 | tf_op jit(solution)/shard_map/ppermute | solution.py:54
  0.5 1.1 %constant_dynamic-slice_fusion.1 = bf16[128,1024]{1,0:T(8,128)(2,1)S(1)} fusion(bf16[512,1536]{1,0:T(8,128)(2,1)} %refs_0_.1, s32[]{:T(128)S(6)} %select_n.73), kind=kLoop, calls=%fused_computation.7 | loop fusion | bytes 524292 | tf_op jit(solution)/shard_map/dynamic_slice | solution.py:382
  1.6 2.6 %collective-permute-start.2 = (bf16[128,1024]{1,0:T(8,128)(2,1)S(1)}, bf16[128,1024]{1,0:T(8,128)(2,1)S(1)}, u32[]{:S(2)}, u32[]{:S(2)}) collective-permute-start(bf16[128,1024]{1,0:T(8,128)(2,1)S(1)} %constant_dynamic-slice_fusion.1), channel_id=1, source_target_pairs={{0,2},{1,3},{2,0},{3,1},{4,6},{5,7},{6,4},{7,5},{8,10},{9,11},{10,... | collective-permute-start | bytes 786440 | tf_op jit(solution)/shard_map/ppermute | solution.py:54
  4.2 1.6 %constant_dynamic-slice_fusion = bf16[64,1024]{1,0:T(8,128)(2,1)} fusion(bf16[512,1536]{1,0:T(8,128)(2,1)} %refs_0_.1, s32[]{:T(128)S(6)} %select_n.74), kind=kLoop, calls=%fused_computation.6 | loop fusion | bytes 262148 | tf_op jit(solution)/shard_map/dynamic_slice | solution.py:382
  5.8 1.7 %slice.6 = bf16[128,1024]{1,0:T(8,128)(2,1)} slice(bf16[512,1536]{1,0:T(8,128)(2,1)} %refs_0_.1), slice={[384:512], [512:1536]} | slice | bytes 524288 | tf_op jit(solution)/shard_map/slice | solution.py:396
  7.5 2.0 %collective-permute-start.6 = (bf16[128,1024]{1,0:T(8,128)(2,1)}, bf16[128,1024]{1,0:T(8,128)(2,1)S(1)}, u32[]{:S(2)}, u32[]{:S(2)}) collective-permute-start(bf16[128,1024]{1,0:T(8,128)(2,1)} %slice.6), channel_id=1, source_target_pairs={{0,2},{1,3},{2,0},{3,1},{4,6},{5,7},{6,4},{7,5},{8,10},{9,11},{10,... | collective-permute-start | bytes 786440 | tf_op jit(solution)/shard_map/ppermute | solution.py:54
  9.5 1.9 %slice.7 = bf16[512,512]{1,0:T(8,128)(2,1)} slice(bf16[512,1536]{1,0:T(8,128)(2,1)} %refs_0_.1), slice={[0:512], [0:512]} | slice | bytes 1048576 | tf_op jit(solution)/shard_map/slice | solution.py:403
  11.4 2.0 %collective-permute-start.3 = (bf16[128,1024]{1,0:T(8,128)(2,1)S(1)}, bf16[128,1024]{1,0:T(8,128)(2,1)S(1)}, u32[]{:S(2)}, u32[]{:S(2)}) collective-permute-start(bf16[128,1024]{1,0:T(8,128)(2,1)S(1)} %collective-permute-done.2.refs_0_), channel_id=1, source_target_pairs={{0,4},{4,0},{8,12},{12,8},{16,20},{20,16},{24,28},{28,24},{1,5},{5... | collective-permute-start | bytes 786440 | tf_op jit(solution)/shard_map/ppermute | solution.py:54
  13.5 0.6 %collective-permute-done.4.refs_2_ = bf16[64,1024]{1,0:T(8,128)(2,1)S(1)} collective-permute-done((bf16[64,1024]{1,0:T(8,128)(2,1)}, bf16[64,1024]{1,0:T(8,128)(2,1)S(1)}, u32[]{:S(2)}, u32[]{:S(2)}) %collective-permute-start.4) | collective-permute-done | bytes 131104 | tf_op jit(solution)/shard_map/ppermute | solution.py:54
  14.1 2.1 %collective-permute-start.5 = (bf16[64,1024]{1,0:T(8,128)(2,1)S(1)}, bf16[64,1024]{1,0:T(8,128)(2,1)}, u32[]{:S(2)}, u32[]{:S(2)}) collective-permute-start(bf16[64,1024]{1,0:T(8,128)(2,1)S(1)} %collective-permute-done.4.refs_2_), channel_id=1, source_target_pairs={{0,8},{4,12},{8,0},{12,4},{16,24},{20,28},{24,16},{28,20},{1,9},{5... | collective-permute-start | bytes 393224 | tf_op jit(solution)/shard_map/ppermute | solution.py:54
  16.5 1.4 %copy-done.1 = bf16[512,1536]{1,0:T(8,128)(2,1)S(1)} copy-done((bf16[512,1536]{1,0:T(8,128)(2,1)S(1)}, bf16[512,1536]{1,0:T(8,128)(2,1)}, u32[]{:S(2)}) %copy-start.1) | copy-done | bytes 1572888
  17.9 3.2 %project_own.1.partial = f32[512,1536]{1,0:T(8,128)S(1)} custom-call(s32[25]{0:T(128)S(1)} %concatenate.3.meta, bf16[512,2048]{1,0:T(8,128)(2,1)S(1)} %bitcast.13, bf16[512,1536]{1,0:T(8,128)(2,1)S(1)} %copy-done.1, bf16[512,1536]{1,0:T(8,128)(2,1)} %collective-permute-done.refs_1_), custom_call_target="tpu_custom_call" | custom-call | flops 3680000 | bytes 1000 | tf_op jit(solution)/shard_map/project_own/pallas_call | solution.py:352
  21.1 0.6 %collective-permute-start.7 = (bf16[128,1024]{1,0:T(8,128)(2,1)S(1)}, bf16[128,1024]{1,0:T(8,128)(2,1)S(1)}, u32[]{:S(2)}, u32[]{:S(2)}) collective-permute-start(bf16[128,1024]{1,0:T(8,128)(2,1)S(1)} %collective-permute-done.2.refs_0_), channel_id=1, source_target_pairs={{0,1},{1,0},{2,3},{3,2},{4,5},{5,4},{6,7},{7,6},{8,9},{9,8},{10,11... | collective-permute-start | bytes 786440 | tf_op jit(solution)/shard_map/ppermute | solution.py:54
  22.3 1.3 %project_first.1 = (f32[128,1024]{1,0:T(8,128)S(1)}, bf16[512,1024]{1,0:T(8,128)(2,1)S(1)}) custom-call(s32[25]{0:T(128)S(1)} %concatenate.3.meta, bf16[512,2048]{1,0:T(8,128)(2,1)S(1)} %bitcast.14, f32[512,1536]{1,0:T(8,128)S(1)} %project_own.1.partial, bf16[128,1024]{1,0:T(8,128)(2,1)S(1)} %collective-permute-done.2.refs_0_, ...), custom_call_target="tpu_custom_call" | custom-call | flops 689999 | bytes 1000 | tf_op jit(solution)/shard_map/project_first/pallas_call | solution.py:352
  24.0 0.9 %project_pack.1 = (bf16[128,1024]{1,0:T(8,128)(2,1)S(1)}, bf16[512,1024]{1,0:T(8,128)(2,1)S(1)}) custom-call(s32[25]{0:T(128)S(1)} %concatenate.3.meta, bf16[512,2048]{1,0:T(8,128)(2,1)S(1)} %bitcast.15, f32[128,1024]{1,0:T(8,128)S(1)} %get-tuple-element.29.refs_0_, bf16[128,1024]{1,0:T(8,128)(2,1)S(1)} %collective-permute-done.7.refs_1_, ...), custom_call_target="tpu_custom_call" | custom-call | flops 689999 | bytes 1000 | tf_op jit(solution)/shard_map/project_pack/pallas_call | solution.py:352
  24.9 1.6 %collective-permute-start.14 = (bf16[128,1024]{1,0:T(8,128)(2,1)S(1)}, bf16[128,1024]{1,0:T(8,128)(2,1)S(1)}, u32[]{:S(2)}, u32[]{:S(2)}) collective-permute-start(bf16[128,1024]{1,0:T(8,128)(2,1)S(1)} %get-tuple-element.30), channel_id=1, source_target_pairs={{0,12},{4,8},{8,4},{12,0},{16,28},{20,24},{24,20},{28,16},{1,13},{... | collective-permute-start | bytes 786440 | tf_op jit(solution)/shard_map/ppermute | solution.py:441
  26.5 1.5 %collective-permute-start.15 = (bf16[128,1024]{1,0:T(8,128)(2,1)S(1)}, bf16[128,1024]{1,0:T(8,128)(2,1)S(1)}, u32[]{:S(2)}, u32[]{:S(2)}) collective-permute-start(bf16[128,1024]{1,0:T(8,128)(2,1)S(1)} %get-tuple-element.30), channel_id=1, source_target_pairs={{0,8},{4,12},{8,0},{12,4},{16,24},{20,28},{24,16},{28,20},{1,9},{5... | collective-permute-start | bytes 786440 | tf_op jit(solution)/shard_map/ppermute | solution.py:441
  28.5 1.8 %project_kv.1.refs_4_ = bf16[512,1024]{1,0:T(8,128)(2,1)S(1)} custom-call(s32[25]{0:T(128)S(1)} %concatenate.3.meta, bf16[512,2048]{1,0:T(8,128)(2,1)S(1)} %bitcast.16, f32[512,1536]{1,0:T(8,128)S(1)} %project_own.1.partial, bf16[512,1024]{1,0:T(8,128)(2,1)S(1)} %get-tuple-element.32.refs_0_, bf16[512,1024]{1,0:T(8,128)(2,1)S(1)} %get-tuple-element.33.refs_1_), custom_call_target="tpu_custom_call" | custom-call | flops 2990000 | bytes 1000 | tf_op jit(solution)/shard_map/project_kv/pallas_call | solution.py:352
  30.7 0.6 %slot_queries.1 = (bf16[240,512]{1,0:T(8,128)(2,1)S(1)}, bf16[240,512]{1,0:T(8,128)(2,1)S(1)}, bf16[2,32,512]{2,1,0:T(8,128)(2,1)S(1)}) custom-call(s32[25]{0:T(128)S(1)} %concatenate.3.meta, bf16[512,512]{1,0:T(8,128)(2,1)S(1)} %collective-permute-done.1.source.refs_0_), custom_call_target="tpu_custom_call" | custom-call | flops 575000 | bytes 1000 | tf_op jit(solution)/shard_map/slot_queries/pallas_call | solution.py:352
  31.4 0.5 %collective-permute-start.13 = (bf16[240,512]{1,0:T(8,128)(2,1)S(1)}, bf16[240,512]{1,0:T(8,128)(2,1)S(1)}, u32[]{:S(2)}, u32[]{:S(2)}) collective-permute-start(bf16[240,512]{1,0:T(8,128)(2,1)S(1)} %get-tuple-element.37), channel_id=1, source_target_pairs={{0,1},{1,0},{2,3},{3,2},{4,5},{5,4},{6,7},{7,6},{8,9},{9,8},{10,11... | collective-permute-start | bytes 737288 | tf_op jit(solution)/shard_map/ppermute | solution.py:54
  31.9 3.8 %all_to_all.5.refs_1_ = bf16[2,32,512]{2,1,0:T(8,128)(2,1)S(1)} all-to-all(bf16[2,32,512]{2,1,0:T(8,128)(2,1)S(1)} %get-tuple-element.35), channel_id=1, replica_groups={{0,1},{2,3},{4,5},{6,7},{8,9},{10,11},{12,13},{14,15},{16,17},{18,19},{..., dimensions={0} | all-to-all | bytes 131072 | tf_op jit(solution)/shard_map/all_to_all | solution.py:456
  35.6 3.4 %attend_local.1 = (bf16[512,512]{1,0:T(8,128)(2,1)}, bf16[128,512]{1,0:T(8,128)(2,1)S(1)}, f32[128,512]{1,0:T(8,128)S(1)}, f32[128,512]{1,0:T(8,128)S(1)}, f32[128,512]{1,0:T(8,128)S(1)}) custom-call(s32[25]{0:T(128)S(1)} %concatenate.3.meta, bf16[512,2048]{1,0:T(8,128)(2,1)S(1)} %bitcast.17, f32[512,1536]{1,0:T(8,128)S(1)} %project_own.1.partial, ...), custom_call_target="tpu_custom_call" | custom-call | flops 6325000 | bytes 1000 | tf_op jit(solution)/shard_map/attend_local/pallas_call | solution.py:352
  39.0 0.9 %collective-permute-done.15.refs_5_ = bf16[128,1024]{1,0:T(8,128)(2,1)S(1)} collective-permute-done((bf16[128,1024]{1,0:T(8,128)(2,1)S(1)}, bf16[128,1024]{1,0:T(8,128)(2,1)S(1)}, u32[]{:S(2)}, u32[]{:S(2)}) %collective-permute-start.15) | collective-permute-done | bytes 262176 | tf_op jit(solution)/shard_map/ppermute | solution.py:441
  40.0 0.6 %merge_near.1 = bf16[512,512]{1,0:T(8,128)(2,1)} custom-call(s32[25]{0:T(128)S(1)} %concatenate.3.meta, bf16[128,512]{1,0:T(8,128)(2,1)S(1)} %get-tuple-element.38.refs_0_, f32[128,512]{1,0:T(8,128)S(1)} %get-tuple-element.39.refs_1_, f32[128,512]{1,0:T(8,128)S(1)} %get-tuple-element.40.refs_2_, ...), custom_call_target="tpu_custom_call", output_to_operand_aliasing={{}: (8, {})} | custom-call | flops 2990000 | bytes 1000 | tf_op jit(solution)/shard_map/merge_near/pallas_call | solution.py:471
  (33 shorter events, 2.3 us)
Async XLA Ops:
  0.0 13.4 %copy-start.3 = (s32[4]{0:T(128)S(1)}, s32[4]{0:T(128)}, u32[]{:S(2)}) copy-start(s32[4]{0:T(128)} %param.7) | copy-start | bytes 52
  0.0 16.3 %copy-start.2 = (s32[4]{0:T(128)S(1)}, s32[4]{0:T(128)}, u32[]{:S(2)}) copy-start(s32[4]{0:T(128)} %param.6) | copy-start | bytes 52
  0.0 16.5 %copy-start = (bf16[1,512,2048]{2,1,0:T(8,128)(2,1)S(1)}, bf16[1,512,2048]{2,1,0:T(8,128)(2,1)}, u32[]{:S(2)}) copy-start(bf16[1,512,2048]{2,1,0:T(8,128)(2,1)} %param.4) | copy-start | bytes 6291460
  0.0 16.4 %collective-permute-start = (bf16[512,1536]{1,0:T(8,128)(2,1)}, bf16[512,1536]{1,0:T(8,128)(2,1)}, u32[]{:S(2)}, u32[]{:S(2)}) collective-permute-start(bf16[512,1536]{1,0:T(8,128)(2,1)} %refs_0_.1), channel_id=1, source_target_pairs={{0,1},{1,0},{2,3},{3,2},{4,5},{5,4},{6,7},{7,6},{8,9},{9,8},{10,11... | collective-permute-start | bytes 4718600 | tf_op jit(solution)/shard_map/ppermute | solution.py:54
  1.6 9.8 %collective-permute-start.2 = (bf16[128,1024]{1,0:T(8,128)(2,1)S(1)}, bf16[128,1024]{1,0:T(8,128)(2,1)S(1)}, u32[]{:S(2)}, u32[]{:S(2)}) collective-permute-start(bf16[128,1024]{1,0:T(8,128)(2,1)S(1)} %constant_dynamic-slice_fusion.1), channel_id=1, source_target_pairs={{0,2},{1,3},{2,0},{3,1},{4,6},{5,7},{6,4},{7,5},{8,10},{9,11},{10,... | collective-permute-start | bytes 786440 | tf_op jit(solution)/shard_map/ppermute | solution.py:54
  5.8 8.3 %collective-permute-start.4 = (bf16[64,1024]{1,0:T(8,128)(2,1)}, bf16[64,1024]{1,0:T(8,128)(2,1)S(1)}, u32[]{:S(2)}, u32[]{:S(2)}) collective-permute-start(bf16[64,1024]{1,0:T(8,128)(2,1)} %constant_dynamic-slice_fusion), channel_id=1, source_target_pairs={{0,2},{1,3},{2,0},{3,1},{4,6},{5,7},{6,4},{7,5},{8,10},{9,11},{10,... | collective-permute-start | bytes 393224 | tf_op jit(solution)/shard_map/ppermute | solution.py:54
  7.5 13.6 %collective-permute-start.6 = (bf16[128,1024]{1,0:T(8,128)(2,1)}, bf16[128,1024]{1,0:T(8,128)(2,1)S(1)}, u32[]{:S(2)}, u32[]{:S(2)}) collective-permute-start(bf16[128,1024]{1,0:T(8,128)(2,1)} %slice.6), channel_id=1, source_target_pairs={{0,2},{1,3},{2,0},{3,1},{4,6},{5,7},{6,4},{7,5},{8,10},{9,11},{10,... | collective-permute-start | bytes 786440 | tf_op jit(solution)/shard_map/ppermute | solution.py:54
  11.4 19.3 %collective-permute-start.1 = (bf16[512,512]{1,0:T(8,128)(2,1)}, bf16[512,512]{1,0:T(8,128)(2,1)S(1)}, u32[]{:S(2)}, u32[]{:S(2)}) collective-permute-start(bf16[512,512]{1,0:T(8,128)(2,1)} %slice.7), channel_id=1, source_target_pairs={{0,2},{1,3},{2,0},{3,1},{4,6},{5,7},{6,4},{7,5},{8,10},{9,11},{10,... | collective-permute-start | bytes 1572872 | tf_op jit(solution)/shard_map/ppermute | solution.py:54
  11.4 10.2 %collective-permute-start.3 = (bf16[128,1024]{1,0:T(8,128)(2,1)S(1)}, bf16[128,1024]{1,0:T(8,128)(2,1)S(1)}, u32[]{:S(2)}, u32[]{:S(2)}) collective-permute-start(bf16[128,1024]{1,0:T(8,128)(2,1)S(1)} %collective-permute-done.2.refs_0_), channel_id=1, source_target_pairs={{0,4},{4,0},{8,12},{12,8},{16,20},{20,16},{24,28},{28,24},{1,5},{5... | collective-permute-start | bytes 786440 | tf_op jit(solution)/shard_map/ppermute | solution.py:54
  14.1 7.6 %collective-permute-start.5 = (bf16[64,1024]{1,0:T(8,128)(2,1)S(1)}, bf16[64,1024]{1,0:T(8,128)(2,1)}, u32[]{:S(2)}, u32[]{:S(2)}) collective-permute-start(bf16[64,1024]{1,0:T(8,128)(2,1)S(1)} %collective-permute-done.4.refs_2_), channel_id=1, source_target_pairs={{0,8},{4,12},{8,0},{12,4},{16,24},{20,28},{24,16},{28,20},{1,9},{5... | collective-permute-start | bytes 393224 | tf_op jit(solution)/shard_map/ppermute | solution.py:54
  16.4 5.8 %collective-permute-start.9 = (bf16[64,1024]{1,0:T(8,128)(2,1)S(1)}, bf16[64,1024]{1,0:T(8,128)(2,1)S(1)}, u32[]{:S(2)}, u32[]{:S(2)}) collective-permute-start(bf16[64,1024]{1,0:T(8,128)(2,1)S(1)} %collective-permute-done.4.refs_2_), channel_id=1, source_target_pairs={{0,1},{1,0},{2,3},{3,2},{4,5},{5,4},{6,7},{7,6},{8,9},{9,8},{10,11... | collective-permute-start | bytes 393224 | tf_op jit(solution)/shard_map/ppermute | solution.py:54
  16.5 1.4 %copy-start.1 = (bf16[512,1536]{1,0:T(8,128)(2,1)S(1)}, bf16[512,1536]{1,0:T(8,128)(2,1)}, u32[]{:S(2)}) copy-start(bf16[512,1536]{1,0:T(8,128)(2,1)} %refs_0_.1) | copy-start | bytes 4718596
  21.1 2.5 %collective-permute-start.7 = (bf16[128,1024]{1,0:T(8,128)(2,1)S(1)}, bf16[128,1024]{1,0:T(8,128)(2,1)S(1)}, u32[]{:S(2)}, u32[]{:S(2)}) collective-permute-start(bf16[128,1024]{1,0:T(8,128)(2,1)S(1)} %collective-permute-done.2.refs_0_), channel_id=1, source_target_pairs={{0,1},{1,0},{2,3},{3,2},{4,5},{5,4},{6,7},{7,6},{8,9},{9,8},{10,11... | collective-permute-start | bytes 786440 | tf_op jit(solution)/shard_map/ppermute | solution.py:54
  21.7 1.9 %collective-permute-start.11 = (bf16[128,1024]{1,0:T(8,128)(2,1)S(1)}, bf16[128,1024]{1,0:T(8,128)(2,1)S(1)}, u32[]{:S(2)}, u32[]{:S(2)}) collective-permute-start(bf16[128,1024]{1,0:T(8,128)(2,1)S(1)} %collective-permute-done.6.refs_4_), channel_id=1, source_target_pairs={{0,1},{1,0},{2,3},{3,2},{4,5},{5,4},{6,7},{7,6},{8,9},{9,8},{10,11... | collective-permute-start | bytes 786440 | tf_op jit(solution)/shard_map/ppermute | solution.py:54
  21.7 2.2 %collective-permute-start.8 = (bf16[128,1024]{1,0:T(8,128)(2,1)S(1)}, bf16[128,1024]{1,0:T(8,128)(2,1)S(1)}, u32[]{:S(2)}, u32[]{:S(2)}) collective-permute-start(bf16[128,1024]{1,0:T(8,128)(2,1)S(1)} %collective-permute-done.3.refs_1_), channel_id=1, source_target_pairs={{0,1},{1,0},{2,3},{3,2},{4,5},{5,4},{6,7},{7,6},{8,9},{9,8},{10,11... | collective-permute-start | bytes 786440 | tf_op jit(solution)/shard_map/ppermute | solution.py:54
  22.2 1.8 %collective-permute-start.10 = (bf16[64,1024]{1,0:T(8,128)(2,1)}, bf16[64,1024]{1,0:T(8,128)(2,1)S(1)}, u32[]{:S(2)}, u32[]{:S(2)}) collective-permute-start(bf16[64,1024]{1,0:T(8,128)(2,1)} %collective-permute-done.5.refs_3_), channel_id=1, source_target_pairs={{0,1},{1,0},{2,3},{3,2},{4,5},{5,4},{6,7},{7,6},{8,9},{9,8},{10,11... | collective-permute-start | bytes 393224 | tf_op jit(solution)/shard_map/ppermute | solution.py:54
  24.9 14.1 %collective-permute-start.14 = (bf16[128,1024]{1,0:T(8,128)(2,1)S(1)}, bf16[128,1024]{1,0:T(8,128)(2,1)S(1)}, u32[]{:S(2)}, u32[]{:S(2)}) collective-permute-start(bf16[128,1024]{1,0:T(8,128)(2,1)S(1)} %get-tuple-element.30), channel_id=1, source_target_pairs={{0,12},{4,8},{8,4},{12,0},{16,28},{20,24},{24,20},{28,16},{1,13},{... | collective-permute-start | bytes 786440 | tf_op jit(solution)/shard_map/ppermute | solution.py:441
  26.5 13.5 %collective-permute-start.15 = (bf16[128,1024]{1,0:T(8,128)(2,1)S(1)}, bf16[128,1024]{1,0:T(8,128)(2,1)S(1)}, u32[]{:S(2)}, u32[]{:S(2)}) collective-permute-start(bf16[128,1024]{1,0:T(8,128)(2,1)S(1)} %get-tuple-element.30), channel_id=1, source_target_pairs={{0,8},{4,12},{8,0},{12,4},{16,24},{20,28},{24,16},{28,20},{1,9},{5... | collective-permute-start | bytes 786440 | tf_op jit(solution)/shard_map/ppermute | solution.py:441
  28.0 12.0 %collective-permute-start.16 = (bf16[128,1024]{1,0:T(8,128)(2,1)S(1)}, bf16[128,1024]{1,0:T(8,128)(2,1)S(1)}, u32[]{:S(2)}, u32[]{:S(2)}) collective-permute-start(bf16[128,1024]{1,0:T(8,128)(2,1)S(1)} %get-tuple-element.30), channel_id=1, source_target_pairs={{0,4},{4,0},{8,12},{12,8},{16,20},{20,16},{24,28},{28,24},{1,5},{5... | collective-permute-start | bytes 786440 | tf_op jit(solution)/shard_map/ppermute | solution.py:441
  31.3 4.4 %collective-permute-start.12 = (bf16[240,512]{1,0:T(8,128)(2,1)S(1)}, bf16[240,512]{1,0:T(8,128)(2,1)S(1)}, u32[]{:S(2)}, u32[]{:S(2)}) collective-permute-start(bf16[240,512]{1,0:T(8,128)(2,1)S(1)} %get-tuple-element.36), channel_id=1, source_target_pairs={{0,1},{1,0},{2,3},{3,2},{4,5},{5,4},{6,7},{7,6},{8,9},{9,8},{10,11... | collective-permute-start | bytes 737288 | tf_op jit(solution)/shard_map/ppermute | solution.py:54
  31.4 4.3 %collective-permute-start.13 = (bf16[240,512]{1,0:T(8,128)(2,1)S(1)}, bf16[240,512]{1,0:T(8,128)(2,1)S(1)}, u32[]{:S(2)}, u32[]{:S(2)}) collective-permute-start(bf16[240,512]{1,0:T(8,128)(2,1)S(1)} %get-tuple-element.37), channel_id=1, source_target_pairs={{0,1},{1,0},{2,3},{3,2},{4,5},{5,4},{6,7},{7,6},{8,9},{9,8},{10,11... | collective-permute-start | bytes 737288 | tf_op jit(solution)/shard_map/ppermute | solution.py:54

commit v3 on v2

--- a/solution.py
+++ b/solution.py
@@ -18,7 +18,7 @@
 SCALE2 = HEAD_DIM ** (-0.5) * math.log2(math.e)
 VMEM_LIMIT = 24 * 1024 * 1024
 
-MODEL_FLOPS = {"project_first": 689999, "slot_queries": 575000, "project_pack": 689999, "project_own": 3680000, "project_mid": 1610000, "project_kv": 2990000, "attend_local": 6325000, "merge_near": 2990000}
+MODEL_FLOPS = {"project_first": 689999, "split_queries": 575000, "project_pack": 689999, "project_own": 3680000, "project_mid": 1610000, "project_kv": 2990000, "attend_local": 6325000, "merge_near": 2990000}
 ORDER = {
     'c1': ('c0',),
     'cD': ('c1',),
@@ -28,7 +28,7 @@
     'q': ('kv',),
     'kv': ('pack',),
 }
-NEAR_ORDER = (3, 2, 1)
+NEAR_ORDER = (3, 1, 2)
 F32 = jnp.float32
 BF16 = jnp.bfloat16
 
@@ -44,7 +44,8 @@
     pairs = []
     for source in range(count):
         run, spot = place(source)
-        if (run, spot ^ bits) in where:
+        one_bit = bits & (bits - 1) == 0
+        if (run, spot ^ bits) in where and (one_bit or spot ^ bits > spot):
             pairs.append((source, where[run, spot ^ bits]))
     return pairs
 
@@ -123,13 +124,12 @@
     near_rows_kernel(layout, place_at, False, slots, slot_at, meta, tokens, refs[:slots], *refs[slots:])
 
 
-def slot_kernel(core_at, meta, source, *outs):
+def split_kernel(meta, source, *outs):
     done = 0
-    for out in outs[:-1]:
+    for out in outs:
         rows = out.shape[0]
         out[...] = source[done : done + rows, :]
         done += rows
-    outs[-1][1 - meta[core_at]] = source[done:, :]
 
 
 def kv_kernel(places_at, meta, tokens, partial, *refs):
@@ -145,7 +145,7 @@
     return jnp.concatenate([value, jnp.ones(value.shape, BF16)], axis=1)
 
 
-def attend_kernel(count, bases_at, core_at, slots, slot_at, match_at, meta, tokens, partial, *refs):
+def attend_kernel(count, bases_at, slots, slot_at, match_at, meta, tokens, partial, *refs):
     weights, refs = refs[:count], refs[count:]
     kv, out, refs = refs[0], refs[1], refs[2:]
     state, scratch, joined = refs[: 4 * slots], refs[4 * slots : -1], refs[-1]
@@ -158,15 +158,16 @@
     places = [meta[at] for at in bases_at]
     if weights:
         done = 0
-        for weight in weights[2:]:
+        for weight in weights[1:]:
             joined[done : done + weight.shape[0], :] = weight[...]
             done += weight.shape[0]
-        joined[done:, :] = weights[1][1 - meta[core_at]]
+        if done < joined.shape[0]:
+            joined[done:, :] = weights[0][joined.shape[0] :, :]
     for pair in range(HEADS // 2):
         lanes = slice(pair * PAIR, (pair + 1) * PAIR)
         total = partial[:, lanes]
         if weights:
-            total = total + add_up(tokens, places, [weights[0].at[:, lanes], joined.at[:, lanes]])
+            total = total + add_up(tokens, places, [weights[0].at[: joined.shape[0], lanes], joined.at[:, lanes]])
         query[:, lanes] = total.astype(BF16)
 
     def lanes_of(head):
@@ -360,6 +361,7 @@
             name=name,
         )(meta, *args)
 
+    passing = [share * 15 // 32 // 16 * 16] * 2
     local = [qkv_weight]
     bits = range(2, pieces, 2)
     known = {}
@@ -401,6 +403,9 @@
         known["fD"] = swap(rest, "fsdp", 1)
         direct_rows.append(mine_rows + [rest] + other_rows + [known["fD"]])
         cut = ordered("cQ", qkv_weight, known)[:, :WIDTH]
+        left = share - sum(passing)
+        if left:
+            cut = jnp.concatenate([cut, known["core"][share - left :, :WIDTH]], axis=0)
         known["cQ"] = cut
         queries.append(swap(cut, "fsdp", bit))
     assert len(bits) <= 1
@@ -445,22 +450,17 @@
     crossed_q, q_places = [], []
     for bit, direct in zip(bits, queries):
         direct = ordered("q", direct, known)
-        passing = [share * 15 // 32 // 16 * 16] * 2
-        left = share - sum(passing)
-        *parts, slots_out = call(
-            functools.partial(slot_kernel, core_at),
+        parts = call(
+            split_kernel,
             [direct],
-            [shape((rows, WIDTH), BF16) for rows in passing] + [shape((2, left, WIDTH), BF16)],
-            "slot_queries",
+            [shape((rows, WIDTH), BF16) for rows in passing],
+            "split_queries",
         )
-        both = lax.all_to_all(
-            slots_out, "fsdp", 0, 0, axis_index_groups=[[i, i + 1] for i in range(0, pieces, 2)]
-        )
-        crossed_q += [direct, both] + [swap(part, "fsdp", 1) for part in parts]
+        crossed_q += [direct] + [swap(part, "fsdp", 1) for part in parts]
         q_places += [bit, bit ^ 1]
     state_types = [BF16, F32, F32, F32]
     partial_out, *state = call(
-        functools.partial(attend_kernel, len(crossed_q), q_places, core_at, slots, slot_at, match_at),
+        functools.partial(attend_kernel, len(crossed_q), q_places, slots, slot_at, match_at),
         [sequence, partial, *crossed_q, kv],
         [shape((row_count, WIDTH), BF16)] + [shape((BLOCK, WIDTH), kind) for kind in state_types] * slots,
         "attend_local",

time: 40.9 us -> 41.8 us (1.022)
  the two profiles are of different devices: /device:TPU:0 before, /device:TPU:8 now
where the time goes in v3:
time: 41.8 us; the launch traced here: 41.4 us
  Pallas kernels  13.3 us (32%)
  starting transfers between devices  12.3 us (29%)
  local copies, waits for them, and re-layouts  7.71 us (18%)
  waiting for transfers between devices  6.97 us (17%)
  other arithmetic  0.86 us (2%)
    pallas_call x6, Pallas kernels, call(): pl.pallas_call(kernel, in_specs=[scalar_spec] + [whole] * len(args), out_...  11.3 us
    ppermute x14, starting transfers between devices, swap(): return lax.ppermute(value, axis, [(i, i ^ bit) for i in range(count)])  8.9 us
    ppermute x14, waiting for transfers between devices, swap(): return lax.ppermute(value, axis, [(i, i ^ bit) for i in range(count)])  3.6 us
    ppermute x3, starting transfers between devices, body(): lax.ppermute(pack, 'seq', partners(seq_size, place, step))  3.44 us
    ppermute x3, waiting for transfers between devices, body(): lax.ppermute(pack, 'seq', partners(seq_size, place, step))  3.37 us
    dynamic_slice x2, local copies, waits for them, and re-layouts, body(): lax.dynamic_slice(ordered('c' + tag, qkv_weight, known), (start + side *...  2.69 us
    pallas_call x1, Pallas kernels, body(): pl.pallas_call(functools.partial(merge_kernel, shifts, steps, slot_at, ma...  1.96 us
    slice x1, local copies, waits for them, and re-layouts, body(): cut = ordered('cD', qkv_weight, known)[direct_from:, WIDTH:]  1.67 us
  transfers between devices with their start and end apart: 17, of which 6 were waited for; matrix products, arithmetic and copies ran while one was open for 17% of the time, Pallas kernels for 27%

profile of v3, /device:TPU:8, one launch (start us, length us, event | category | flops | bytes accessed | tf_op | source)
XLA Modules:
  0.0 41.4 jit_solution(1559412580658252201)
XLA Ops:
  0.0 1.0 %constant_dynamic-slice_fusion.1 = bf16[128,1024]{1,0:T(8,128)(2,1)S(1)} fusion(bf16[512,1536]{1,0:T(8,128)(2,1)} %refs_0_.1, s32[]{:T(128)S(6)} %select_n.73), kind=kLoop, calls=%fused_computation.8 | loop fusion | bytes 524292 | tf_op jit(solution)/shard_map/dynamic_slice | solution.py:384
  1.0 1.6 %collective-permute-start.2 = (bf16[128,1024]{1,0:T(8,128)(2,1)S(1)}, bf16[128,1024]{1,0:T(8,128)(2,1)S(1)}, u32[]{:S(2)}, u32[]{:S(2)}) collective-permute-start(bf16[128,1024]{1,0:T(8,128)(2,1)S(1)} %constant_dynamic-slice_fusion.1), channel_id=1, source_target_pairs={{0,2},{1,3},{2,0},{3,1},{4,6},{5,7},{6,4},{7,5},{8,10},{9,11},{10,... | collective-permute-start | bytes 786440 | tf_op jit(solution)/shard_map/ppermute | solution.py:55
  2.5 1.7 %constant_dynamic-slice_fusion = bf16[64,1024]{1,0:T(8,128)(2,1)} fusion(bf16[512,1536]{1,0:T(8,128)(2,1)} %refs_0_.1, s32[]{:T(128)S(6)} %select_n.74), kind=kLoop, calls=%fused_computation.7 | loop fusion | bytes 262148 | tf_op jit(solution)/shard_map/dynamic_slice | solution.py:384
  4.8 1.7 %slice.9 = bf16[128,1024]{1,0:T(8,128)(2,1)} slice(bf16[512,1536]{1,0:T(8,128)(2,1)} %refs_0_.1), slice={[384:512], [512:1536]} | slice | bytes 524288 | tf_op jit(solution)/shard_map/slice | solution.py:398
  6.5 1.5 %collective-permute-start.6 = (bf16[128,1024]{1,0:T(8,128)(2,1)}, bf16[128,1024]{1,0:T(8,128)(2,1)S(1)}, u32[]{:S(2)}, u32[]{:S(2)}) collective-permute-start(bf16[128,1024]{1,0:T(8,128)(2,1)} %slice.9), channel_id=1, source_target_pairs={{0,2},{1,3},{2,0},{3,1},{4,6},{5,7},{6,4},{7,5},{8,10},{9,11},{10,... | collective-permute-start | bytes 786440 | tf_op jit(solution)/shard_map/ppermute | solution.py:55
  8.0 1.1 %slice.10 = bf16[512,512]{1,0:T(8,128)(2,1)S(1)} slice(bf16[512,1536]{1,0:T(8,128)(2,1)} %refs_0_.1), slice={[0:512], [0:512]} | slice | bytes 1048576 | tf_op jit(solution)/shard_map/slice | solution.py:405
  9.0 1.1 %collective-permute-done.2.refs_0_ = bf16[128,1024]{1,0:T(8,128)(2,1)S(1)} collective-permute-done((bf16[128,1024]{1,0:T(8,128)(2,1)S(1)}, bf16[128,1024]{1,0:T(8,128)(2,1)S(1)}, u32[]{:S(2)}, u32[]{:S(2)}) %collective-permute-start.2) | collective-permute-done | bytes 262176 | tf_op jit(solution)/shard_map/ppermute | solution.py:55
  10.2 1.5 %collective-permute-start.3 = (bf16[128,1024]{1,0:T(8,128)(2,1)S(1)}, bf16[128,1024]{1,0:T(8,128)(2,1)S(1)}, u32[]{:S(2)}, u32[]{:S(2)}) collective-permute-start(bf16[128,1024]{1,0:T(8,128)(2,1)S(1)} %collective-permute-done.2.refs_0_), channel_id=1, source_target_pairs={{0,4},{4,0},{8,12},{12,8},{16,20},{20,16},{24,28},{28,24},{1,5},{5... | collective-permute-start | bytes 786440 | tf_op jit(solution)/shard_map/ppermute | solution.py:55
  11.7 0.8 %slice.12 = bf16[32,512]{1,0:T(8,128)(2,1)S(1)} slice(bf16[512,1536]{1,0:T(8,128)(2,1)} %collective-permute-done.refs_1_), slice={[480:512], [0:512]} | slice | bytes 65536 | tf_op jit(solution)/shard_map/slice | solution.py:408
  12.4 0.8 %pad_maximum_fusion = bf16[544,512]{1,0:T(8,128)(2,1)} fusion(bf16[32,512]{1,0:T(8,128)(2,1)S(1)} %slice.12, bf16[512,512]{1,0:T(8,128)(2,1)S(1)} %slice.10), kind=kLoop, calls=%fused_computation | loop fusion | flops 1114112 | bytes 1114112 | tf_op jit(solution)/shard_map/concatenate | solution.py:408
  13.3 1.5 %collective-permute-start.1 = (bf16[544,512]{1,0:T(8,128)(2,1)}, bf16[544,512]{1,0:T(8,128)(2,1)S(1)}, u32[]{:S(2)}, u32[]{:S(2)}) collective-permute-start(bf16[544,512]{1,0:T(8,128)(2,1)} %pad_maximum_fusion), channel_id=1, source_target_pairs={{0,2},{1,3},{2,0},{3,1},{4,6},{5,7},{6,4},{7,5},{8,10},{9,11},{10,... | collective-permute-start | bytes 1671176 | tf_op jit(solution)/shard_map/ppermute | solution.py:55
  15.6 1.4 %copy-done.1 = bf16[512,1536]{1,0:T(8,128)(2,1)S(1)} copy-done((bf16[512,1536]{1,0:T(8,128)(2,1)S(1)}, bf16[512,1536]{1,0:T(8,128)(2,1)}, u32[]{:S(2)}) %copy-start.1) | copy-done | bytes 1572888
  17.0 3.2 %project_own.1.partial = f32[512,1536]{1,0:T(8,128)S(1)} custom-call(s32[25]{0:T(128)S(1)} %concatenate.6.meta, bf16[512,2048]{1,0:T(8,128)(2,1)S(1)} %bitcast.13, bf16[512,1536]{1,0:T(8,128)(2,1)S(1)} %copy-done.1, bf16[512,1536]{1,0:T(8,128)(2,1)} %collective-permute-done.refs_1_), custom_call_target="tpu_custom_call" | custom-call | flops 3680000 | bytes 1000 | tf_op jit(solution)/shard_map/project_own/pallas_call | solution.py:353
  21.4 1.4 %project_first.1 = (f32[128,1024]{1,0:T(8,128)S(1)}, bf16[512,1024]{1,0:T(8,128)(2,1)S(1)}) custom-call(s32[25]{0:T(128)S(1)} %concatenate.6.meta, bf16[512,2048]{1,0:T(8,128)(2,1)S(1)} %bitcast.14, f32[512,1536]{1,0:T(8,128)S(1)} %project_own.1.partial, bf16[128,1024]{1,0:T(8,128)(2,1)S(1)} %collective-permute-done.2.refs_0_, ...), custom_call_target="tpu_custom_call" | custom-call | flops 689999 | bytes 1000 | tf_op jit(solution)/shard_map/project_first/pallas_call | solution.py:353
  23.1 0.9 %project_pack.1 = (bf16[128,1024]{1,0:T(8,128)(2,1)S(1)}, bf16[512,1024]{1,0:T(8,128)(2,1)S(1)}) custom-call(s32[25]{0:T(128)S(1)} %concatenate.6.meta, bf16[512,2048]{1,0:T(8,128)(2,1)S(1)} %bitcast.15, f32[128,1024]{1,0:T(8,128)S(1)} %get-tuple-element.28.refs_0_, bf16[128,1024]{1,0:T(8,128)(2,1)S(1)} %collective-permute-done.7.refs_1_, ...), custom_call_target="tpu_custom_call" | custom-call | flops 689999 | bytes 1000 | tf_op jit(solution)/shard_map/project_pack/pallas_call | solution.py:353
  24.1 1.6 %collective-permute-start.16 = (bf16[128,1024]{1,0:T(8,128)(2,1)S(1)}, bf16[128,1024]{1,0:T(8,128)(2,1)S(1)}, u32[]{:S(2)}, u32[]{:S(2)}) collective-permute-start(bf16[128,1024]{1,0:T(8,128)(2,1)S(1)} %get-tuple-element.29), channel_id=1, source_target_pairs={{0,8},{4,12},{8,0},{12,4},{16,24},{20,28},{24,16},{28,20},{1,9},{5... | collective-permute-start | bytes 786440 | tf_op jit(solution)/shard_map/ppermute | solution.py:446
  26.2 1.3 %collective-permute-start.14 = (bf16[128,1024]{1,0:T(8,128)(2,1)S(1)}, bf16[128,1024]{1,0:T(8,128)(2,1)S(1)}, u32[]{:S(2)}, u32[]{:S(2)}) collective-permute-start(bf16[128,1024]{1,0:T(8,128)(2,1)S(1)} %get-tuple-element.29), channel_id=1, source_target_pairs={{0,12},{4,8},{16,28},{20,24},{1,13},{5,9},{17,29},{21,25},{2,14},{... | collective-permute-start | bytes 786440 | tf_op jit(solution)/shard_map/ppermute | solution.py:446
  27.5 1.8 %project_kv.1.refs_3_ = bf16[512,1024]{1,0:T(8,128)(2,1)S(1)} custom-call(s32[25]{0:T(128)S(1)} %concatenate.6.meta, bf16[512,2048]{1,0:T(8,128)(2,1)S(1)} %bitcast.16, f32[512,1536]{1,0:T(8,128)S(1)} %project_own.1.partial, bf16[512,1024]{1,0:T(8,128)(2,1)S(1)} %get-tuple-element.31.refs_0_, bf16[512,1024]{1,0:T(8,128)(2,1)S(1)} %get-tuple-element.32.refs_1_), custom_call_target="tpu_custom_call" | custom-call | flops 2990000 | bytes 1000 | tf_op jit(solution)/shard_map/project_kv/pallas_call | solution.py:353
  29.3 0.8 %collective-permute-done.1.source.refs_0_ = bf16[544,512]{1,0:T(8,128)(2,1)S(1)} collective-permute-done((bf16[544,512]{1,0:T(8,128)(2,1)}, bf16[544,512]{1,0:T(8,128)(2,1)S(1)}, u32[]{:S(2)}, u32[]{:S(2)}) %collective-permute-start.1) | collective-permute-done | bytes 557088 | tf_op jit(solution)/shard_map/ppermute | solution.py:55
  30.1 0.6 %split_queries.1 = (bf16[240,512]{1,0:T(8,128)(2,1)S(1)}, bf16[240,512]{1,0:T(8,128)(2,1)S(1)}) custom-call(s32[25]{0:T(128)S(1)} %concatenate.6.meta, bf16[544,512]{1,0:T(8,128)(2,1)S(1)} %collective-permute-done.1.source.refs_0_), custom_call_target="tpu_custom_call" | custom-call | flops 575000 | bytes 1000 | tf_op jit(solution)/shard_map/split_queries/pallas_call | solution.py:353
  31.3 1.0 %collective-permute-done.12.refs_1_ = bf16[240,512]{1,0:T(8,128)(2,1)S(1)} collective-permute-done((bf16[240,512]{1,0:T(8,128)(2,1)S(1)}, bf16[240,512]{1,0:T(8,128)(2,1)S(1)}, u32[]{:S(2)}, u32[]{:S(2)}) %collective-permute-start.12) | collective-permute-done | bytes 245792 | tf_op jit(solution)/shard_map/ppermute | solution.py:55
  32.6 3.4 %attend_local.1 = (bf16[512,512]{1,0:T(8,128)(2,1)}, bf16[128,512]{1,0:T(8,128)(2,1)S(1)}, f32[128,512]{1,0:T(8,128)S(1)}, f32[128,512]{1,0:T(8,128)S(1)}, f32[128,512]{1,0:T(8,128)S(1)}) custom-call(s32[25]{0:T(128)S(1)} %concatenate.6.meta, bf16[512,2048]{1,0:T(8,128)(2,1)S(1)} %bitcast.17, f32[512,1536]{1,0:T(8,128)S(1)} %project_own.1.partial, ...), custom_call_target="tpu_custom_call" | custom-call | flops 6325000 | bytes 1000 | tf_op jit(solution)/shard_map/attend_local/pallas_call | solution.py:353
  36.0 3.4 %collective-permute-done.15.refs_5_ = bf16[128,1024]{1,0:T(8,128)(2,1)S(1)} collective-permute-done((bf16[128,1024]{1,0:T(8,128)(2,1)S(1)}, bf16[128,1024]{1,0:T(8,128)(2,1)S(1)}, u32[]{:S(2)}, u32[]{:S(2)}) %collective-permute-start.15) | collective-permute-done | bytes 262176 | tf_op jit(solution)/shard_map/ppermute | solution.py:446
  39.4 2.0 %merge_near.1 = bf16[512,512]{1,0:T(8,128)(2,1)} custom-call(s32[25]{0:T(128)S(1)} %concatenate.6.meta, bf16[128,512]{1,0:T(8,128)(2,1)S(1)} %get-tuple-element.36.refs_0_, f32[128,512]{1,0:T(8,128)S(1)} %get-tuple-element.37.refs_1_, f32[128,512]{1,0:T(8,128)S(1)} %get-tuple-element.38.refs_2_, ...), custom_call_target="tpu_custom_call", output_to_operand_aliasing={{}: (8, {})} | custom-call | flops 2990000 | bytes 1000 | tf_op jit(solution)/shard_map/merge_near/pallas_call | solution.py:471
  (34 shorter events, 4.2 us)
Async XLA Ops:
  0.0 11.7 %collective-permute-start = (bf16[512,1536]{1,0:T(8,128)(2,1)}, bf16[512,1536]{1,0:T(8,128)(2,1)}, u32[]{:S(2)}, u32[]{:S(2)}) collective-permute-start(bf16[512,1536]{1,0:T(8,128)(2,1)} %refs_0_.1), channel_id=1, source_target_pairs={{0,1},{1,0},{2,3},{3,2},{4,5},{5,4},{6,7},{7,6},{8,9},{9,8},{10,11... | collective-permute-start | bytes 4718600 | tf_op jit(solution)/shard_map/ppermute | solution.py:55
  1.0 13.8 %copy-start.3 = (s32[4]{0:T(128)S(1)}, s32[4]{0:T(128)}, u32[]{:S(2)}) copy-start(s32[4]{0:T(128)} %param.7) | copy-start | bytes 52
  1.0 9.2 %collective-permute-start.2 = (bf16[128,1024]{1,0:T(8,128)(2,1)S(1)}, bf16[128,1024]{1,0:T(8,128)(2,1)S(1)}, u32[]{:S(2)}, u32[]{:S(2)}) collective-permute-start(bf16[128,1024]{1,0:T(8,128)(2,1)S(1)} %constant_dynamic-slice_fusion.1), channel_id=1, source_target_pairs={{0,2},{1,3},{2,0},{3,1},{4,6},{5,7},{6,4},{7,5},{8,10},{9,11},{10,... | collective-permute-start | bytes 786440 | tf_op jit(solution)/shard_map/ppermute | solution.py:55
  2.5 12.9 %copy-start.2 = (s32[4]{0:T(128)S(1)}, s32[4]{0:T(128)}, u32[]{:S(2)}) copy-start(s32[4]{0:T(128)} %param.6) | copy-start | bytes 52
  2.5 13.1 %copy-start = (bf16[1,512,2048]{2,1,0:T(8,128)(2,1)S(1)}, bf16[1,512,2048]{2,1,0:T(8,128)(2,1)}, u32[]{:S(2)}) copy-start(bf16[1,512,2048]{2,1,0:T(8,128)(2,1)} %param.4) | copy-start | bytes 6291460
  4.3 10.6 %collective-permute-start.4 = (bf16[64,1024]{1,0:T(8,128)(2,1)}, bf16[64,1024]{1,0:T(8,128)(2,1)}, u32[]{:S(2)}, u32[]{:S(2)}) collective-permute-start(bf16[64,1024]{1,0:T(8,128)(2,1)} %constant_dynamic-slice_fusion), channel_id=1, source_target_pairs={{0,2},{1,3},{2,0},{3,1},{4,6},{5,7},{6,4},{7,5},{8,10},{9,11},{10,... | collective-permute-start | bytes 393224 | tf_op jit(solution)/shard_map/ppermute | solution.py:55
  6.5 13.8 %collective-permute-start.6 = (bf16[128,1024]{1,0:T(8,128)(2,1)}, bf16[128,1024]{1,0:T(8,128)(2,1)S(1)}, u32[]{:S(2)}, u32[]{:S(2)}) collective-permute-start(bf16[128,1024]{1,0:T(8,128)(2,1)} %slice.9), channel_id=1, source_target_pairs={{0,2},{1,3},{2,0},{3,1},{4,6},{5,7},{6,4},{7,5},{8,10},{9,11},{10,... | collective-permute-start | bytes 786440 | tf_op jit(solution)/shard_map/ppermute | solution.py:55
  10.2 10.6 %collective-permute-start.3 = (bf16[128,1024]{1,0:T(8,128)(2,1)S(1)}, bf16[128,1024]{1,0:T(8,128)(2,1)S(1)}, u32[]{:S(2)}, u32[]{:S(2)}) collective-permute-start(bf16[128,1024]{1,0:T(8,128)(2,1)S(1)} %collective-permute-done.2.refs_0_), channel_id=1, source_target_pairs={{0,4},{4,0},{8,12},{12,8},{16,20},{20,16},{24,28},{28,24},{1,5},{5... | collective-permute-start | bytes 786440 | tf_op jit(solution)/shard_map/ppermute | solution.py:55
  13.3 16.9 %collective-permute-start.1 = (bf16[544,512]{1,0:T(8,128)(2,1)}, bf16[544,512]{1,0:T(8,128)(2,1)S(1)}, u32[]{:S(2)}, u32[]{:S(2)}) collective-permute-start(bf16[544,512]{1,0:T(8,128)(2,1)} %pad_maximum_fusion), channel_id=1, source_target_pairs={{0,2},{1,3},{2,0},{3,1},{4,6},{5,7},{6,4},{7,5},{8,10},{9,11},{10,... | collective-permute-start | bytes 1671176 | tf_op jit(solution)/shard_map/ppermute | solution.py:55
  14.9 6.0 %collective-permute-start.5 = (bf16[64,1024]{1,0:T(8,128)(2,1)}, bf16[64,1024]{1,0:T(8,128)(2,1)}, u32[]{:S(2)}, u32[]{:S(2)}) collective-permute-start(bf16[64,1024]{1,0:T(8,128)(2,1)} %collective-permute-done.4.refs_2_), channel_id=1, source_target_pairs={{0,8},{4,12},{8,0},{12,4},{16,24},{20,28},{24,16},{28,20},{1,9},{5... | collective-permute-start | bytes 393224 | tf_op jit(solution)/shard_map/ppermute | solution.py:55
  15.5 5.8 %collective-permute-start.9 = (bf16[64,1024]{1,0:T(8,128)(2,1)}, bf16[64,1024]{1,0:T(8,128)(2,1)S(1)}, u32[]{:S(2)}, u32[]{:S(2)}) collective-permute-start(bf16[64,1024]{1,0:T(8,128)(2,1)} %collective-permute-done.4.refs_2_), channel_id=1, source_target_pairs={{0,1},{1,0},{2,3},{3,2},{4,5},{5,4},{6,7},{7,6},{8,9},{9,8},{10,11... | collective-permute-start | bytes 393224 | tf_op jit(solution)/shard_map/ppermute | solution.py:55
  15.6 1.4 %copy-start.1 = (bf16[512,1536]{1,0:T(8,128)(2,1)S(1)}, bf16[512,1536]{1,0:T(8,128)(2,1)}, u32[]{:S(2)}) copy-start(bf16[512,1536]{1,0:T(8,128)(2,1)} %refs_0_.1) | copy-start | bytes 4718596
  20.2 2.5 %collective-permute-start.7 = (bf16[128,1024]{1,0:T(8,128)(2,1)S(1)}, bf16[128,1024]{1,0:T(8,128)(2,1)S(1)}, u32[]{:S(2)}, u32[]{:S(2)}) collective-permute-start(bf16[128,1024]{1,0:T(8,128)(2,1)S(1)} %collective-permute-done.2.refs_0_), channel_id=1, source_target_pairs={{0,1},{1,0},{2,3},{3,2},{4,5},{5,4},{6,7},{7,6},{8,9},{9,8},{10,11... | collective-permute-start | bytes 786440 | tf_op jit(solution)/shard_map/ppermute | solution.py:55
  20.8 2.0 %collective-permute-start.11 = (bf16[128,1024]{1,0:T(8,128)(2,1)S(1)}, bf16[128,1024]{1,0:T(8,128)(2,1)S(1)}, u32[]{:S(2)}, u32[]{:S(2)}) collective-permute-start(bf16[128,1024]{1,0:T(8,128)(2,1)S(1)} %collective-permute-done.6.refs_4_), channel_id=1, source_target_pairs={{0,1},{1,0},{2,3},{3,2},{4,5},{5,4},{6,7},{7,6},{8,9},{9,8},{10,11... | collective-permute-start | bytes 786440 | tf_op jit(solution)/shard_map/ppermute | solution.py:55
  20.9 2.2 %collective-permute-start.8 = (bf16[128,1024]{1,0:T(8,128)(2,1)S(1)}, bf16[128,1024]{1,0:T(8,128)(2,1)S(1)}, u32[]{:S(2)}, u32[]{:S(2)}) collective-permute-start(bf16[128,1024]{1,0:T(8,128)(2,1)S(1)} %collective-permute-done.3.refs_1_), channel_id=1, source_target_pairs={{0,1},{1,0},{2,3},{3,2},{4,5},{5,4},{6,7},{7,6},{8,9},{9,8},{10,11... | collective-permute-start | bytes 786440 | tf_op jit(solution)/shard_map/ppermute | solution.py:55
  21.3 1.8 %collective-permute-start.10 = (bf16[64,1024]{1,0:T(8,128)(2,1)}, bf16[64,1024]{1,0:T(8,128)(2,1)S(1)}, u32[]{:S(2)}, u32[]{:S(2)}) collective-permute-start(bf16[64,1024]{1,0:T(8,128)(2,1)} %collective-permute-done.5.refs_3_), channel_id=1, source_target_pairs={{0,1},{1,0},{2,3},{3,2},{4,5},{5,4},{6,7},{7,6},{8,9},{9,8},{10,11... | collective-permute-start | bytes 393224 | tf_op jit(solution)/shard_map/ppermute | solution.py:55
  24.1 12.0 %collective-permute-start.16 = (bf16[128,1024]{1,0:T(8,128)(2,1)S(1)}, bf16[128,1024]{1,0:T(8,128)(2,1)S(1)}, u32[]{:S(2)}, u32[]{:S(2)}) collective-permute-start(bf16[128,1024]{1,0:T(8,128)(2,1)S(1)} %get-tuple-element.29), channel_id=1, source_target_pairs={{0,8},{4,12},{8,0},{12,4},{16,24},{20,28},{24,16},{28,20},{1,9},{5... | collective-permute-start | bytes 786440 | tf_op jit(solution)/shard_map/ppermute | solution.py:446
  25.7 13.7 %collective-permute-start.15 = (bf16[128,1024]{1,0:T(8,128)(2,1)S(1)}, bf16[128,1024]{1,0:T(8,128)(2,1)S(1)}, u32[]{:S(2)}, u32[]{:S(2)}) collective-permute-start(bf16[128,1024]{1,0:T(8,128)(2,1)S(1)} %get-tuple-element.29), channel_id=1, source_target_pairs={{0,4},{4,0},{8,12},{12,8},{16,20},{20,16},{24,28},{28,24},{1,5},{5... | collective-permute-start | bytes 786440 | tf_op jit(solution)/shard_map/ppermute | solution.py:446
  26.2 13.2 %collective-permute-start.14 = (bf16[128,1024]{1,0:T(8,128)(2,1)S(1)}, bf16[128,1024]{1,0:T(8,128)(2,1)S(1)}, u32[]{:S(2)}, u32[]{:S(2)}) collective-permute-start(bf16[128,1024]{1,0:T(8,128)(2,1)S(1)} %get-tuple-element.29), channel_id=1, source_target_pairs={{0,12},{4,8},{16,28},{20,24},{1,13},{5,9},{17,29},{21,25},{2,14},{... | collective-permute-start | bytes 786440 | tf_op jit(solution)/shard_map/ppermute | solution.py:446
  30.7 1.6 %collective-permute-start.12 = (bf16[240,512]{1,0:T(8,128)(2,1)S(1)}, bf16[240,512]{1,0:T(8,128)(2,1)S(1)}, u32[]{:S(2)}, u32[]{:S(2)}) collective-permute-start(bf16[240,512]{1,0:T(8,128)(2,1)S(1)} %get-tuple-element.34), channel_id=1, source_target_pairs={{0,1},{1,0},{2,3},{3,2},{4,5},{5,4},{6,7},{7,6},{8,9},{9,8},{10,11... | collective-permute-start | bytes 737288 | tf_op jit(solution)/shard_map/ppermute | solution.py:55
  30.8 1.9 %collective-permute-start.13 = (bf16[240,512]{1,0:T(8,128)(2,1)S(1)}, bf16[240,512]{1,0:T(8,128)(2,1)S(1)}, u32[]{:S(2)}, u32[]{:S(2)}) collective-permute-start(bf16[240,512]{1,0:T(8,128)(2,1)S(1)} %get-tuple-element.35), channel_id=1, source_target_pairs={{0,1},{1,0},{2,3},{3,2},{4,5},{5,4},{6,7},{7,6},{8,9},{9,8},{10,11... | collective-permute-start | bytes 737288 | tf_op jit(solution)/shard_map/ppermute | solution.py:55

commit v4 on v3

--- a/solution.py
+++ b/solution.py
@@ -20,9 +20,6 @@
 
 MODEL_FLOPS = {"project_first": 689999, "split_queries": 575000, "project_pack": 689999, "project_own": 3680000, "project_mid": 1610000, "project_kv": 2990000, "attend_local": 6325000, "merge_near": 2990000}
 ORDER = {
-    'c1': ('c0',),
-    'cD': ('c1',),
-    'cQ': ('cD',),
     'p0': ('partial', 'xD'),
     'p1': ('partial',),
     'q': ('kv',),

time: 41.8 us -> 42.5 us (1.017)
  waiting for transfers between devices: 6.97 us -> 8.8 us
  local copies, waits for them, and re-layouts: 7.71 us -> 6.68 us
    ppermute x14, waiting for transfers between devices: 3.6 us -> 5.44 us  [swap(): return lax.ppermute(value, axis, [(i, i ^ bit) for i in range(count)])]
    dynamic_slice x2 -> x1, local copies, waits for them, and re-layouts: 2.69 us -> 1.55 us  [body(): lax.dynamic_slice(ordered('c' + tag, qkv_weight, known), (start + side *...]
  transfers between devices with their start and end apart: 17 -> 17, of which waited for: 6 -> 6; matrix products, arithmetic and copies ran while one was open for 17% -> 15% of each run, Pallas kernels for 27% -> 27%
where the time goes in v4:
time: 42.5 us; the launch traced here: 42.1 us
  Pallas kernels  13.3 us (31%)
  starting transfers between devices  12.3 us (29%)
  waiting for transfers between devices  8.8 us (21%)
  local copies, waits for them, and re-layouts  6.68 us (16%)
  other arithmetic  0.85 us (2%)
    pallas_call x6, Pallas kernels, call(): pl.pallas_call(kernel, in_specs=[scalar_spec] + [whole] * len(args), out_...  11.3 us
    ppermute x14, starting transfers between devices, swap(): return lax.ppermute(value, axis, [(i, i ^ bit) for i in range(count)])  8.83 us
    ppermute x14, waiting for transfers between devices, swap(): return lax.ppermute(value, axis, [(i, i ^ bit) for i in range(count)])  5.44 us
    ppermute x3, starting transfers between devices, body(): lax.ppermute(pack, 'seq', partners(seq_size, place, step))  3.42 us
    ppermute x3, waiting for transfers between devices, body(): lax.ppermute(pack, 'seq', partners(seq_size, place, step))  3.36 us
    pallas_call x1, Pallas kernels, body(): pl.pallas_call(functools.partial(merge_kernel, shifts, steps, slot_at, ma...  1.96 us
    slice x1, local copies, waits for them, and re-layouts, body(): cut = ordered('cD', qkv_weight, known)[direct_from:, WIDTH:]  1.78 us
    dynamic_slice x1, local copies, waits for them, and re-layouts, body(): lax.dynamic_slice(ordered('c' + tag, qkv_weight, known), (start + side *...  1.55 us
  transfers between devices with their start and end apart: 17, of which 6 were waited for; matrix products, arithmetic and copies ran while one was open for 15% of the time, Pallas kernels for 27%

profile of v4, /device:TPU:8, one launch (start us, length us, event | category | flops | bytes accessed | tf_op | source)
XLA Modules:
  0.0 42.1 jit_solution(12399823055731949016)
XLA Ops:
  0.0 1.8 %fusion = (bf16[128,1024]{1,0:T(8,128)(2,1)}, bf16[128,1024]{1,0:T(8,128)(2,1)S(1)}) fusion(bf16[512,1536]{1,0:T(8,128)(2,1)} %refs_0_.1, s32[]{:T(128)S(6)} %select_n.73), kind=kLoop, calls=%fused_computation.9 | loop fusion | bytes 1048580 | tf_op jit(solution)/shard_map/slice | solution.py:395
  1.8 1.5 %collective-permute-start.2 = (bf16[128,1024]{1,0:T(8,128)(2,1)S(1)}, bf16[128,1024]{1,0:T(8,128)(2,1)S(1)}, u32[]{:S(2)}, u32[]{:S(2)}) collective-permute-start(bf16[128,1024]{1,0:T(8,128)(2,1)S(1)} %get-tuple-element.36), channel_id=1, source_target_pairs={{0,2},{1,3},{2,0},{3,1},{4,6},{5,7},{6,4},{7,5},{8,10},{9,11},{10,... | collective-permute-start | bytes 786440 | tf_op jit(solution)/shard_map/ppermute | solution.py:52
  3.3 1.6 %constant_dynamic-slice_fusion = bf16[64,1024]{1,0:T(8,128)(2,1)} fusion(bf16[512,1536]{1,0:T(8,128)(2,1)} %refs_0_.1, s32[]{:T(128)S(6)} %select_n.74), kind=kLoop, calls=%fused_computation.7 | loop fusion | bytes 262148 | tf_op jit(solution)/shard_map/dynamic_slice | solution.py:381
  4.8 0.6 %collective-permute-start.4 = (bf16[64,1024]{1,0:T(8,128)(2,1)}, bf16[64,1024]{1,0:T(8,128)(2,1)}, u32[]{:S(2)}, u32[]{:S(2)}) collective-permute-start(bf16[64,1024]{1,0:T(8,128)(2,1)} %constant_dynamic-slice_fusion), channel_id=1, source_target_pairs={{0,2},{1,3},{2,0},{3,1},{4,6},{5,7},{6,4},{7,5},{8,10},{9,11},{10,... | collective-permute-start | bytes 393224 | tf_op jit(solution)/shard_map/ppermute | solution.py:52
  5.5 1.4 %collective-permute-start.6 = (bf16[128,1024]{1,0:T(8,128)(2,1)}, bf16[128,1024]{1,0:T(8,128)(2,1)S(1)}, u32[]{:S(2)}, u32[]{:S(2)}) collective-permute-start(bf16[128,1024]{1,0:T(8,128)(2,1)} %get-tuple-element.35), channel_id=1, source_target_pairs={{0,2},{1,3},{2,0},{3,1},{4,6},{5,7},{6,4},{7,5},{8,10},{9,11},{10,... | collective-permute-start | bytes 786440 | tf_op jit(solution)/shard_map/ppermute | solution.py:52
  6.9 1.1 %slice.9 = bf16[512,512]{1,0:T(8,128)(2,1)S(1)} slice(bf16[512,1536]{1,0:T(8,128)(2,1)} %refs_0_.1), slice={[0:512], [0:512]} | slice | bytes 1048576 | tf_op jit(solution)/shard_map/slice | solution.py:402
  7.9 3.0 %collective-permute-done.2.refs_0_ = bf16[128,1024]{1,0:T(8,128)(2,1)S(1)} collective-permute-done((bf16[128,1024]{1,0:T(8,128)(2,1)S(1)}, bf16[128,1024]{1,0:T(8,128)(2,1)S(1)}, u32[]{:S(2)}, u32[]{:S(2)}) %collective-permute-start.2) | collective-permute-done | bytes 262176 | tf_op jit(solution)/shard_map/ppermute | solution.py:52
  10.9 1.5 %collective-permute-start.3 = (bf16[128,1024]{1,0:T(8,128)(2,1)S(1)}, bf16[128,1024]{1,0:T(8,128)(2,1)S(1)}, u32[]{:S(2)}, u32[]{:S(2)}) collective-permute-start(bf16[128,1024]{1,0:T(8,128)(2,1)S(1)} %collective-permute-done.2.refs_0_), channel_id=1, source_target_pairs={{0,4},{4,0},{8,12},{12,8},{16,20},{20,16},{24,28},{28,24},{1,5},{5... | collective-permute-start | bytes 786440 | tf_op jit(solution)/shard_map/ppermute | solution.py:52
  12.4 0.8 %slice.12 = bf16[32,512]{1,0:T(8,128)(2,1)S(1)} slice(bf16[512,1536]{1,0:T(8,128)(2,1)} %collective-permute-done.refs_1_), slice={[480:512], [0:512]} | slice | bytes 65536 | tf_op jit(solution)/shard_map/slice | solution.py:405
  13.2 0.8 %pad_maximum_fusion = bf16[544,512]{1,0:T(8,128)(2,1)} fusion(bf16[32,512]{1,0:T(8,128)(2,1)S(1)} %slice.12, bf16[512,512]{1,0:T(8,128)(2,1)S(1)} %slice.9), kind=kLoop, calls=%fused_computation | loop fusion | flops 1114112 | bytes 1114112 | tf_op jit(solution)/shard_map/concatenate | solution.py:405
  14.0 1.5 %collective-permute-start.1 = (bf16[544,512]{1,0:T(8,128)(2,1)}, bf16[544,512]{1,0:T(8,128)(2,1)S(1)}, u32[]{:S(2)}, u32[]{:S(2)}) collective-permute-start(bf16[544,512]{1,0:T(8,128)(2,1)} %pad_maximum_fusion), channel_id=1, source_target_pairs={{0,2},{1,3},{2,0},{3,1},{4,6},{5,7},{6,4},{7,5},{8,10},{9,11},{10,... | collective-permute-start | bytes 1671176 | tf_op jit(solution)/shard_map/ppermute | solution.py:52
  16.3 1.4 %copy-done.1 = bf16[512,1536]{1,0:T(8,128)(2,1)S(1)} copy-done((bf16[512,1536]{1,0:T(8,128)(2,1)S(1)}, bf16[512,1536]{1,0:T(8,128)(2,1)}, u32[]{:S(2)}) %copy-start.1) | copy-done | bytes 1572888
  17.7 3.2 %project_own.1.partial = f32[512,1536]{1,0:T(8,128)S(1)} custom-call(s32[25]{0:T(128)S(1)} %concatenate.6.meta, bf16[512,2048]{1,0:T(8,128)(2,1)S(1)} %bitcast.13, bf16[512,1536]{1,0:T(8,128)(2,1)S(1)} %copy-done.1, bf16[512,1536]{1,0:T(8,128)(2,1)} %collective-permute-done.refs_1_), custom_call_target="tpu_custom_call" | custom-call | flops 3680000 | bytes 1000 | tf_op jit(solution)/shard_map/project_own/pallas_call | solution.py:350
  22.1 1.4 %project_first.1 = (f32[128,1024]{1,0:T(8,128)S(1)}, bf16[512,1024]{1,0:T(8,128)(2,1)S(1)}) custom-call(s32[25]{0:T(128)S(1)} %concatenate.6.meta, bf16[512,2048]{1,0:T(8,128)(2,1)S(1)} %bitcast.14, f32[512,1536]{1,0:T(8,128)S(1)} %project_own.1.partial, bf16[128,1024]{1,0:T(8,128)(2,1)S(1)} %collective-permute-done.2.refs_0_, ...), custom_call_target="tpu_custom_call" | custom-call | flops 689999 | bytes 1000 | tf_op jit(solution)/shard_map/project_first/pallas_call | solution.py:350
  23.8 1.0 %project_pack.1 = (bf16[128,1024]{1,0:T(8,128)(2,1)S(1)}, bf16[512,1024]{1,0:T(8,128)(2,1)S(1)}) custom-call(s32[25]{0:T(128)S(1)} %concatenate.6.meta, bf16[512,2048]{1,0:T(8,128)(2,1)S(1)} %bitcast.15, f32[128,1024]{1,0:T(8,128)S(1)} %get-tuple-element.22.refs_0_, bf16[128,1024]{1,0:T(8,128)(2,1)S(1)} %collective-permute-done.7.refs_1_, ...), custom_call_target="tpu_custom_call" | custom-call | flops 689999 | bytes 1000 | tf_op jit(solution)/shard_map/project_pack/pallas_call | solution.py:350
  24.8 1.6 %collective-permute-start.16 = (bf16[128,1024]{1,0:T(8,128)(2,1)S(1)}, bf16[128,1024]{1,0:T(8,128)(2,1)S(1)}, u32[]{:S(2)}, u32[]{:S(2)}) collective-permute-start(bf16[128,1024]{1,0:T(8,128)(2,1)S(1)} %get-tuple-element.23), channel_id=1, source_target_pairs={{0,8},{4,12},{8,0},{12,4},{16,24},{20,28},{24,16},{28,20},{1,9},{5... | collective-permute-start | bytes 786440 | tf_op jit(solution)/shard_map/ppermute | solution.py:443
  26.9 1.3 %collective-permute-start.14 = (bf16[128,1024]{1,0:T(8,128)(2,1)S(1)}, bf16[128,1024]{1,0:T(8,128)(2,1)S(1)}, u32[]{:S(2)}, u32[]{:S(2)}) collective-permute-start(bf16[128,1024]{1,0:T(8,128)(2,1)S(1)} %get-tuple-element.23), channel_id=1, source_target_pairs={{0,12},{4,8},{16,28},{20,24},{1,13},{5,9},{17,29},{21,25},{2,14},{... | collective-permute-start | bytes 786440 | tf_op jit(solution)/shard_map/ppermute | solution.py:443
  28.2 1.8 %project_kv.1.refs_3_ = bf16[512,1024]{1,0:T(8,128)(2,1)S(1)} custom-call(s32[25]{0:T(128)S(1)} %concatenate.6.meta, bf16[512,2048]{1,0:T(8,128)(2,1)S(1)} %bitcast.16, f32[512,1536]{1,0:T(8,128)S(1)} %project_own.1.partial, bf16[512,1024]{1,0:T(8,128)(2,1)S(1)} %get-tuple-element.25.refs_0_, bf16[512,1024]{1,0:T(8,128)(2,1)S(1)} %get-tuple-element.26.refs_1_), custom_call_target="tpu_custom_call" | custom-call | flops 2990000 | bytes 1000 | tf_op jit(solution)/shard_map/project_kv/pallas_call | solution.py:350
  30.1 0.8 %collective-permute-done.1.source.refs_0_ = bf16[544,512]{1,0:T(8,128)(2,1)S(1)} collective-permute-done((bf16[544,512]{1,0:T(8,128)(2,1)}, bf16[544,512]{1,0:T(8,128)(2,1)S(1)}, u32[]{:S(2)}, u32[]{:S(2)}) %collective-permute-start.1) | collective-permute-done | bytes 557088 | tf_op jit(solution)/shard_map/ppermute | solution.py:52
  30.9 0.6 %split_queries.1 = (bf16[240,512]{1,0:T(8,128)(2,1)S(1)}, bf16[240,512]{1,0:T(8,128)(2,1)S(1)}) custom-call(s32[25]{0:T(128)S(1)} %concatenate.6.meta, bf16[544,512]{1,0:T(8,128)(2,1)S(1)} %collective-permute-done.1.source.refs_0_), custom_call_target="tpu_custom_call" | custom-call | flops 575000 | bytes 1000 | tf_op jit(solution)/shard_map/split_queries/pallas_call | solution.py:350
  32.0 1.0 %collective-permute-done.12.refs_1_ = bf16[240,512]{1,0:T(8,128)(2,1)S(1)} collective-permute-done((bf16[240,512]{1,0:T(8,128)(2,1)S(1)}, bf16[240,512]{1,0:T(8,128)(2,1)S(1)}, u32[]{:S(2)}, u32[]{:S(2)}) %collective-permute-start.12) | collective-permute-done | bytes 245792 | tf_op jit(solution)/shard_map/ppermute | solution.py:52
  33.4 3.4 %attend_local.1 = (bf16[512,512]{1,0:T(8,128)(2,1)}, bf16[128,512]{1,0:T(8,128)(2,1)S(1)}, f32[128,512]{1,0:T(8,128)S(1)}, f32[128,512]{1,0:T(8,128)S(1)}, f32[128,512]{1,0:T(8,128)S(1)}) custom-call(s32[25]{0:T(128)S(1)} %concatenate.6.meta, bf16[512,2048]{1,0:T(8,128)(2,1)S(1)} %bitcast.17, f32[512,1536]{1,0:T(8,128)S(1)} %project_own.1.partial, ...), custom_call_target="tpu_custom_call" | custom-call | flops 6325000 | bytes 1000 | tf_op jit(solution)/shard_map/attend_local/pallas_call | solution.py:350
  36.8 3.4 %collective-permute-done.15.refs_5_ = bf16[128,1024]{1,0:T(8,128)(2,1)S(1)} collective-permute-done((bf16[128,1024]{1,0:T(8,128)(2,1)S(1)}, bf16[128,1024]{1,0:T(8,128)(2,1)S(1)}, u32[]{:S(2)}, u32[]{:S(2)}) %collective-permute-start.15) | collective-permute-done | bytes 262176 | tf_op jit(solution)/shard_map/ppermute | solution.py:443
  40.1 2.0 %merge_near.1 = bf16[512,512]{1,0:T(8,128)(2,1)} custom-call(s32[25]{0:T(128)S(1)} %concatenate.6.meta, bf16[128,512]{1,0:T(8,128)(2,1)S(1)} %get-tuple-element.30.refs_0_, f32[128,512]{1,0:T(8,128)S(1)} %get-tuple-element.31.refs_1_, f32[128,512]{1,0:T(8,128)S(1)} %get-tuple-element.32.refs_2_, ...), custom_call_target="tpu_custom_call", output_to_operand_aliasing={{}: (8, {})} | custom-call | flops 2990000 | bytes 1000 | tf_op jit(solution)/shard_map/merge_near/pallas_call | solution.py:468
  (33 shorter events, 3.6 us)
Async XLA Ops:
  0.0 12.4 %collective-permute-start = (bf16[512,1536]{1,0:T(8,128)(2,1)}, bf16[512,1536]{1,0:T(8,128)(2,1)}, u32[]{:S(2)}, u32[]{:S(2)}) collective-permute-start(bf16[512,1536]{1,0:T(8,128)(2,1)} %refs_0_.1), channel_id=1, source_target_pairs={{0,1},{1,0},{2,3},{3,2},{4,5},{5,4},{6,7},{7,6},{8,9},{9,8},{10,11... | collective-permute-start | bytes 4718600 | tf_op jit(solution)/shard_map/ppermute | solution.py:52
  0.0 15.5 %copy-start.3 = (s32[4]{0:T(128)S(1)}, s32[4]{0:T(128)}, u32[]{:S(2)}) copy-start(s32[4]{0:T(128)} %param.7) | copy-start | bytes 52
  1.8 14.4 %copy-start.2 = (s32[4]{0:T(128)S(1)}, s32[4]{0:T(128)}, u32[]{:S(2)}) copy-start(s32[4]{0:T(128)} %param.6) | copy-start | bytes 52
  1.8 14.5 %copy-start = (bf16[1,512,2048]{2,1,0:T(8,128)(2,1)S(1)}, bf16[1,512,2048]{2,1,0:T(8,128)(2,1)}, u32[]{:S(2)}) copy-start(bf16[1,512,2048]{2,1,0:T(8,128)(2,1)} %param.4) | copy-start | bytes 6291460
  1.8 9.1 %collective-permute-start.2 = (bf16[128,1024]{1,0:T(8,128)(2,1)S(1)}, bf16[128,1024]{1,0:T(8,128)(2,1)S(1)}, u32[]{:S(2)}, u32[]{:S(2)}) collective-permute-start(bf16[128,1024]{1,0:T(8,128)(2,1)S(1)} %get-tuple-element.36), channel_id=1, source_target_pairs={{0,2},{1,3},{2,0},{3,1},{4,6},{5,7},{6,4},{7,5},{8,10},{9,11},{10,... | collective-permute-start | bytes 786440 | tf_op jit(solution)/shard_map/ppermute | solution.py:52
  4.8 10.8 %collective-permute-start.4 = (bf16[64,1024]{1,0:T(8,128)(2,1)}, bf16[64,1024]{1,0:T(8,128)(2,1)}, u32[]{:S(2)}, u32[]{:S(2)}) collective-permute-start(bf16[64,1024]{1,0:T(8,128)(2,1)} %constant_dynamic-slice_fusion), channel_id=1, source_target_pairs={{0,2},{1,3},{2,0},{3,1},{4,6},{5,7},{6,4},{7,5},{8,10},{9,11},{10,... | collective-permute-start | bytes 393224 | tf_op jit(solution)/shard_map/ppermute | solution.py:52
  5.5 15.5 %collective-permute-start.6 = (bf16[128,1024]{1,0:T(8,128)(2,1)}, bf16[128,1024]{1,0:T(8,128)(2,1)S(1)}, u32[]{:S(2)}, u32[]{:S(2)}) collective-permute-start(bf16[128,1024]{1,0:T(8,128)(2,1)} %get-tuple-element.35), channel_id=1, source_target_pairs={{0,2},{1,3},{2,0},{3,1},{4,6},{5,7},{6,4},{7,5},{8,10},{9,11},{10,... | collective-permute-start | bytes 786440 | tf_op jit(solution)/shard_map/ppermute | solution.py:52
  10.9 10.6 %collective-permute-start.3 = (bf16[128,1024]{1,0:T(8,128)(2,1)S(1)}, bf16[128,1024]{1,0:T(8,128)(2,1)S(1)}, u32[]{:S(2)}, u32[]{:S(2)}) collective-permute-start(bf16[128,1024]{1,0:T(8,128)(2,1)S(1)} %collective-permute-done.2.refs_0_), channel_id=1, source_target_pairs={{0,4},{4,0},{8,12},{12,8},{16,20},{20,16},{24,28},{28,24},{1,5},{5... | collective-permute-start | bytes 786440 | tf_op jit(solution)/shard_map/ppermute | solution.py:52
  14.0 16.9 %collective-permute-start.1 = (bf16[544,512]{1,0:T(8,128)(2,1)}, bf16[544,512]{1,0:T(8,128)(2,1)S(1)}, u32[]{:S(2)}, u32[]{:S(2)}) collective-permute-start(bf16[544,512]{1,0:T(8,128)(2,1)} %pad_maximum_fusion), channel_id=1, source_target_pairs={{0,2},{1,3},{2,0},{3,1},{4,6},{5,7},{6,4},{7,5},{8,10},{9,11},{10,... | collective-permute-start | bytes 1671176 | tf_op jit(solution)/shard_map/ppermute | solution.py:52
  15.6 6.0 %collective-permute-start.5 = (bf16[64,1024]{1,0:T(8,128)(2,1)}, bf16[64,1024]{1,0:T(8,128)(2,1)}, u32[]{:S(2)}, u32[]{:S(2)}) collective-permute-start(bf16[64,1024]{1,0:T(8,128)(2,1)} %collective-permute-done.4.refs_2_), channel_id=1, source_target_pairs={{0,8},{4,12},{8,0},{12,4},{16,24},{20,28},{24,16},{28,20},{1,9},{5... | collective-permute-start | bytes 393224 | tf_op jit(solution)/shard_map/ppermute | solution.py:52
  16.2 5.8 %collective-permute-start.9 = (bf16[64,1024]{1,0:T(8,128)(2,1)}, bf16[64,1024]{1,0:T(8,128)(2,1)S(1)}, u32[]{:S(2)}, u32[]{:S(2)}) collective-permute-start(bf16[64,1024]{1,0:T(8,128)(2,1)} %collective-permute-done.4.refs_2_), channel_id=1, source_target_pairs={{0,1},{1,0},{2,3},{3,2},{4,5},{5,4},{6,7},{7,6},{8,9},{9,8},{10,11... | collective-permute-start | bytes 393224 | tf_op jit(solution)/shard_map/ppermute | solution.py:52
  16.3 1.4 %copy-start.1 = (bf16[512,1536]{1,0:T(8,128)(2,1)S(1)}, bf16[512,1536]{1,0:T(8,128)(2,1)}, u32[]{:S(2)}) copy-start(bf16[512,1536]{1,0:T(8,128)(2,1)} %refs_0_.1) | copy-start | bytes 4718596
  21.0 2.5 %collective-permute-start.7 = (bf16[128,1024]{1,0:T(8,128)(2,1)S(1)}, bf16[128,1024]{1,0:T(8,128)(2,1)S(1)}, u32[]{:S(2)}, u32[]{:S(2)}) collective-permute-start(bf16[128,1024]{1,0:T(8,128)(2,1)S(1)} %collective-permute-done.2.refs_0_), channel_id=1, source_target_pairs={{0,1},{1,0},{2,3},{3,2},{4,5},{5,4},{6,7},{7,6},{8,9},{9,8},{10,11... | collective-permute-start | bytes 786440 | tf_op jit(solution)/shard_map/ppermute | solution.py:52
  21.5 2.0 %collective-permute-start.11 = (bf16[128,1024]{1,0:T(8,128)(2,1)S(1)}, bf16[128,1024]{1,0:T(8,128)(2,1)S(1)}, u32[]{:S(2)}, u32[]{:S(2)}) collective-permute-start(bf16[128,1024]{1,0:T(8,128)(2,1)S(1)} %collective-permute-done.6.refs_4_), channel_id=1, source_target_pairs={{0,1},{1,0},{2,3},{3,2},{4,5},{5,4},{6,7},{7,6},{8,9},{9,8},{10,11... | collective-permute-start | bytes 786440 | tf_op jit(solution)/shard_map/ppermute | solution.py:52
  21.6 2.2 %collective-permute-start.8 = (bf16[128,1024]{1,0:T(8,128)(2,1)S(1)}, bf16[128,1024]{1,0:T(8,128)(2,1)S(1)}, u32[]{:S(2)}, u32[]{:S(2)}) collective-permute-start(bf16[128,1024]{1,0:T(8,128)(2,1)S(1)} %collective-permute-done.3.refs_1_), channel_id=1, source_target_pairs={{0,1},{1,0},{2,3},{3,2},{4,5},{5,4},{6,7},{7,6},{8,9},{9,8},{10,11... | collective-permute-start | bytes 786440 | tf_op jit(solution)/shard_map/ppermute | solution.py:52
  22.0 1.8 %collective-permute-start.10 = (bf16[64,1024]{1,0:T(8,128)(2,1)}, bf16[64,1024]{1,0:T(8,128)(2,1)S(1)}, u32[]{:S(2)}, u32[]{:S(2)}) collective-permute-start(bf16[64,1024]{1,0:T(8,128)(2,1)} %collective-permute-done.5.refs_3_), channel_id=1, source_target_pairs={{0,1},{1,0},{2,3},{3,2},{4,5},{5,4},{6,7},{7,6},{8,9},{9,8},{10,11... | collective-permute-start | bytes 393224 | tf_op jit(solution)/shard_map/ppermute | solution.py:52
  24.8 12.0 %collective-permute-start.16 = (bf16[128,1024]{1,0:T(8,128)(2,1)S(1)}, bf16[128,1024]{1,0:T(8,128)(2,1)S(1)}, u32[]{:S(2)}, u32[]{:S(2)}) collective-permute-start(bf16[128,1024]{1,0:T(8,128)(2,1)S(1)} %get-tuple-element.23), channel_id=1, source_target_pairs={{0,8},{4,12},{8,0},{12,4},{16,24},{20,28},{24,16},{28,20},{1,9},{5... | collective-permute-start | bytes 786440 | tf_op jit(solution)/shard_map/ppermute | solution.py:443
  26.4 13.7 %collective-permute-start.15 = (bf16[128,1024]{1,0:T(8,128)(2,1)S(1)}, bf16[128,1024]{1,0:T(8,128)(2,1)S(1)}, u32[]{:S(2)}, u32[]{:S(2)}) collective-permute-start(bf16[128,1024]{1,0:T(8,128)(2,1)S(1)} %get-tuple-element.23), channel_id=1, source_target_pairs={{0,4},{4,0},{8,12},{12,8},{16,20},{20,16},{24,28},{28,24},{1,5},{5... | collective-permute-start | bytes 786440 | tf_op jit(solution)/shard_map/ppermute | solution.py:443
  26.9 13.2 %collective-permute-start.14 = (bf16[128,1024]{1,0:T(8,128)(2,1)S(1)}, bf16[128,1024]{1,0:T(8,128)(2,1)S(1)}, u32[]{:S(2)}, u32[]{:S(2)}) collective-permute-start(bf16[128,1024]{1,0:T(8,128)(2,1)S(1)} %get-tuple-element.23), channel_id=1, source_target_pairs={{0,12},{4,8},{16,28},{20,24},{1,13},{5,9},{17,29},{21,25},{2,14},{... | collective-permute-start | bytes 786440 | tf_op jit(solution)/shard_map/ppermute | solution.py:443
  31.5 1.6 %collective-permute-start.12 = (bf16[240,512]{1,0:T(8,128)(2,1)S(1)}, bf16[240,512]{1,0:T(8,128)(2,1)S(1)}, u32[]{:S(2)}, u32[]{:S(2)}) collective-permute-start(bf16[240,512]{1,0:T(8,128)(2,1)S(1)} %get-tuple-element.28), channel_id=1, source_target_pairs={{0,1},{1,0},{2,3},{3,2},{4,5},{5,4},{6,7},{7,6},{8,9},{9,8},{10,11... | collective-permute-start | bytes 737288 | tf_op jit(solution)/shard_map/ppermute | solution.py:52
  31.5 1.9 %collective-permute-start.13 = (bf16[240,512]{1,0:T(8,128)(2,1)S(1)}, bf16[240,512]{1,0:T(8,128)(2,1)S(1)}, u32[]{:S(2)}, u32[]{:S(2)}) collective-permute-start(bf16[240,512]{1,0:T(8,128)(2,1)S(1)} %get-tuple-element.29), channel_id=1, source_target_pairs={{0,1},{1,0},{2,3},{3,2},{4,5},{5,4},{6,7},{7,6},{8,9},{9,8},{10,11... | collective-permute-start | bytes 737288 | tf_op jit(solution)/shard_map/ppermute | solution.py:52

commit v5 on v1

--- a/solution.py
+++ b/solution.py
@@ -16,9 +16,9 @@
 PAIR = 2 * HEAD_DIM
 NEG = -1e30
 SCALE2 = HEAD_DIM ** (-0.5) * math.log2(math.e)
-VMEM_LIMIT = 24 * 1024 * 1024
-
-MODEL_FLOPS = {"project_first": 689999, "slot_queries": 575000, "project_pack": 689999, "project_own": 3680000, "project_mid": 1610000, "project_kv": 2990000, "attend_local": 6325000, "merge_near": 2990000}
+VMEM_LIMIT = 12 * 1024 * 1024
+
+MODEL_FLOPS = {"slot_queries": 575000, "project_first": 689999, "project_pack": 689999, "project_own": 3680000, "project_mid": 1610000, "project_kv": 2990000, "attend_local": 6325000, "merge_near": 2990000}
 ORDER = {
     'c1': ('c0',),
     'cD': ('c1',),

time: 40.9 us -> 40.9 us (level)
  no operation moved by 1% of the time
where the time goes in v5:
time: 40.9 us; the launch traced here: 40.6 us
  starting transfers between devices  14.1 us (34%)
  Pallas kernels  11.8 us (29%)
  local copies, waits for them, and re-layouts  7.7 us (19%)
  blocking collectives  4.58 us (11%)
  waiting for transfers between devices  2.1 us (5%)
    pallas_call x6, Pallas kernels, call(): pl.pallas_call(kernel, in_specs=[scalar_spec] + [whole] * len(args), out_...  11.3 us
    ppermute x12, starting transfers between devices, swap(): return lax.ppermute(value, axis, [(i, i ^ bit) for i in range(count)])  10.6 us
    all_to_all x1, blocking collectives, body(): lax.all_to_all(slots_out, 'fsdp', 0, 0, axis_index_groups=[[i, i + 1] for...  4.58 us
    ppermute x3, starting transfers between devices, body(): lax.ppermute(pack, 'seq', partners(seq_size, place, step))  3.55 us
    dynamic_slice x2, local copies, waits for them, and re-layouts, body(): lax.dynamic_slice(ordered('c' + tag, qkv_weight, known), (start + side *...  2.67 us
    slice x1, local copies, waits for them, and re-layouts, body(): cut = ordered('cQ', qkv_weight, known)[:, :WIDTH]  1.87 us
    slice x1, local copies, waits for them, and re-layouts, body(): cut = ordered('cD', qkv_weight, known)[direct_from:, WIDTH:]  1.66 us
    unnamed x8, local copies, waits for them, and re-layouts  1.41 us
  transfers between devices with their start and end apart: 15, of which 4 were waited for; matrix products, arithmetic and copies ran while one was open for 16% of the time, Pallas kernels for 28%

profile of v5, /device:TPU:0, one launch (start us, length us, event | category | flops | bytes accessed | tf_op | source)
XLA Modules:
  0.0 40.6 jit_solution(5792130905668485195)
XLA Ops:
  0.0 0.5 %collective-permute-start = (bf16[512,1536]{1,0:T(8,128)(2,1)}, bf16[512,1536]{1,0:T(8,128)(2,1)}, u32[]{:S(2)}, u32[]{:S(2)}) collective-permute-start(bf16[512,1536]{1,0:T(8,128)(2,1)} %refs_0_.1), channel_id=1, source_target_pairs={{0,1},{1,0},{2,3},{3,2},{4,5},{5,4},{6,7},{7,6},{8,9},{9,8},{10,11... | collective-permute-start | bytes 4718600 | tf_op jit(solution)/shard_map/ppermute | solution.py:54
  0.5 1.1 %constant_dynamic-slice_fusion.1 = bf16[128,1024]{1,0:T(8,128)(2,1)S(1)} fusion(bf16[512,1536]{1,0:T(8,128)(2,1)} %refs_0_.1, s32[]{:T(128)S(6)} %select_n.73), kind=kLoop, calls=%fused_computation.7 | loop fusion | bytes 524292 | tf_op jit(solution)/shard_map/dynamic_slice | solution.py:373
  1.6 2.6 %collective-permute-start.2 = (bf16[128,1024]{1,0:T(8,128)(2,1)S(1)}, bf16[128,1024]{1,0:T(8,128)(2,1)S(1)}, u32[]{:S(2)}, u32[]{:S(2)}) collective-permute-start(bf16[128,1024]{1,0:T(8,128)(2,1)S(1)} %constant_dynamic-slice_fusion.1), channel_id=1, source_target_pairs={{0,2},{1,3},{2,0},{3,1},{4,6},{5,7},{6,4},{7,5},{8,10},{9,11},{10,... | collective-permute-start | bytes 786440 | tf_op jit(solution)/shard_map/ppermute | solution.py:54
  4.2 1.6 %constant_dynamic-slice_fusion = bf16[64,1024]{1,0:T(8,128)(2,1)} fusion(bf16[512,1536]{1,0:T(8,128)(2,1)} %refs_0_.1, s32[]{:T(128)S(6)} %select_n.74), kind=kLoop, calls=%fused_computation.6 | loop fusion | bytes 262148 | tf_op jit(solution)/shard_map/dynamic_slice | solution.py:373
  5.8 1.7 %slice.6 = bf16[128,1024]{1,0:T(8,128)(2,1)} slice(bf16[512,1536]{1,0:T(8,128)(2,1)} %refs_0_.1), slice={[384:512], [512:1536]} | slice | bytes 524288 | tf_op jit(solution)/shard_map/slice | solution.py:387
  7.5 2.0 %collective-permute-start.6 = (bf16[128,1024]{1,0:T(8,128)(2,1)}, bf16[128,1024]{1,0:T(8,128)(2,1)S(1)}, u32[]{:S(2)}, u32[]{:S(2)}) collective-permute-start(bf16[128,1024]{1,0:T(8,128)(2,1)} %slice.6), channel_id=1, source_target_pairs={{0,2},{1,3},{2,0},{3,1},{4,6},{5,7},{6,4},{7,5},{8,10},{9,11},{10,... | collective-permute-start | bytes 786440 | tf_op jit(solution)/shard_map/ppermute | solution.py:54
  9.5 1.9 %slice.7 = bf16[512,512]{1,0:T(8,128)(2,1)} slice(bf16[512,1536]{1,0:T(8,128)(2,1)} %refs_0_.1), slice={[0:512], [0:512]} | slice | bytes 1048576 | tf_op jit(solution)/shard_map/slice | solution.py:394
  11.4 2.0 %collective-permute-start.3 = (bf16[128,1024]{1,0:T(8,128)(2,1)S(1)}, bf16[128,1024]{1,0:T(8,128)(2,1)S(1)}, u32[]{:S(2)}, u32[]{:S(2)}) collective-permute-start(bf16[128,1024]{1,0:T(8,128)(2,1)S(1)} %collective-permute-done.2.refs_0_), channel_id=1, source_target_pairs={{0,4},{4,0},{8,12},{12,8},{16,20},{20,16},{24,28},{28,24},{1,5},{5... | collective-permute-start | bytes 786440 | tf_op jit(solution)/shard_map/ppermute | solution.py:54
  13.5 0.6 %collective-permute-done.4.refs_2_ = bf16[64,1024]{1,0:T(8,128)(2,1)S(1)} collective-permute-done((bf16[64,1024]{1,0:T(8,128)(2,1)}, bf16[64,1024]{1,0:T(8,128)(2,1)S(1)}, u32[]{:S(2)}, u32[]{:S(2)}) %collective-permute-start.4) | collective-permute-done | bytes 131104 | tf_op jit(solution)/shard_map/ppermute | solution.py:54
  14.1 2.1 %collective-permute-start.5 = (bf16[64,1024]{1,0:T(8,128)(2,1)S(1)}, bf16[64,1024]{1,0:T(8,128)(2,1)}, u32[]{:S(2)}, u32[]{:S(2)}) collective-permute-start(bf16[64,1024]{1,0:T(8,128)(2,1)S(1)} %collective-permute-done.4.refs_2_), channel_id=1, source_target_pairs={{0,8},{4,12},{8,0},{12,4},{16,24},{20,28},{24,16},{28,20},{1,9},{5... | collective-permute-start | bytes 393224 | tf_op jit(solution)/shard_map/ppermute | solution.py:54
  16.5 1.4 %copy-done.1 = bf16[512,1536]{1,0:T(8,128)(2,1)S(1)} copy-done((bf16[512,1536]{1,0:T(8,128)(2,1)S(1)}, bf16[512,1536]{1,0:T(8,128)(2,1)}, u32[]{:S(2)}) %copy-start.1) | copy-done | bytes 1572888
  17.9 3.2 %project_own.1.partial = f32[512,1536]{1,0:T(8,128)S(1)} custom-call(s32[25]{0:T(128)S(1)} %concatenate.3.meta, bf16[512,2048]{1,0:T(8,128)(2,1)S(1)} %bitcast.13, bf16[512,1536]{1,0:T(8,128)(2,1)S(1)} %copy-done.1, bf16[512,1536]{1,0:T(8,128)(2,1)} %collective-permute-done.refs_1_), custom_call_target="tpu_custom_call" | custom-call | flops 3680000 | bytes 1000 | tf_op jit(solution)/shard_map/project_own/pallas_call | solution.py:343
  21.1 0.6 %collective-permute-start.7 = (bf16[128,1024]{1,0:T(8,128)(2,1)S(1)}, bf16[128,1024]{1,0:T(8,128)(2,1)S(1)}, u32[]{:S(2)}, u32[]{:S(2)}) collective-permute-start(bf16[128,1024]{1,0:T(8,128)(2,1)S(1)} %collective-permute-done.2.refs_0_), channel_id=1, source_target_pairs={{0,1},{1,0},{2,3},{3,2},{4,5},{5,4},{6,7},{7,6},{8,9},{9,8},{10,11... | collective-permute-start | bytes 786440 | tf_op jit(solution)/shard_map/ppermute | solution.py:54
  22.3 1.3 %project_first.1 = (f32[128,1024]{1,0:T(8,128)S(1)}, bf16[512,1024]{1,0:T(8,128)(2,1)S(1)}) custom-call(s32[25]{0:T(128)S(1)} %concatenate.3.meta, bf16[512,2048]{1,0:T(8,128)(2,1)S(1)} %bitcast.14, f32[512,1536]{1,0:T(8,128)S(1)} %project_own.1.partial, bf16[128,1024]{1,0:T(8,128)(2,1)S(1)} %collective-permute-done.2.refs_0_, ...), custom_call_target="tpu_custom_call" | custom-call | flops 689999 | bytes 1000 | tf_op jit(solution)/shard_map/project_first/pallas_call | solution.py:343
  24.0 0.9 %project_pack.1 = (bf16[128,1024]{1,0:T(8,128)(2,1)S(1)}, bf16[512,1024]{1,0:T(8,128)(2,1)S(1)}) custom-call(s32[25]{0:T(128)S(1)} %concatenate.3.meta, bf16[512,2048]{1,0:T(8,128)(2,1)S(1)} %bitcast.15, f32[128,1024]{1,0:T(8,128)S(1)} %get-tuple-element.26.refs_0_, bf16[128,1024]{1,0:T(8,128)(2,1)S(1)} %collective-permute-done.7.refs_1_, ...), custom_call_target="tpu_custom_call" | custom-call | flops 689999 | bytes 1000 | tf_op jit(solution)/shard_map/project_pack/pallas_call | solution.py:343
  24.9 1.6 %collective-permute-start.12 = (bf16[128,1024]{1,0:T(8,128)(2,1)S(1)}, bf16[128,1024]{1,0:T(8,128)(2,1)S(1)}, u32[]{:S(2)}, u32[]{:S(2)}) collective-permute-start(bf16[128,1024]{1,0:T(8,128)(2,1)S(1)} %get-tuple-element.27), channel_id=1, source_target_pairs={{0,12},{4,8},{8,4},{12,0},{16,28},{20,24},{24,20},{28,16},{1,13},{... | collective-permute-start | bytes 786440 | tf_op jit(solution)/shard_map/ppermute | solution.py:432
  26.5 1.5 %collective-permute-start.13 = (bf16[128,1024]{1,0:T(8,128)(2,1)S(1)}, bf16[128,1024]{1,0:T(8,128)(2,1)S(1)}, u32[]{:S(2)}, u32[]{:S(2)}) collective-permute-start(bf16[128,1024]{1,0:T(8,128)(2,1)S(1)} %get-tuple-element.27), channel_id=1, source_target_pairs={{0,8},{4,12},{8,0},{12,4},{16,24},{20,28},{24,16},{28,20},{1,9},{5... | collective-permute-start | bytes 786440 | tf_op jit(solution)/shard_map/ppermute | solution.py:432
  28.0 0.5 %collective-permute-start.14 = (bf16[128,1024]{1,0:T(8,128)(2,1)S(1)}, bf16[128,1024]{1,0:T(8,128)(2,1)S(1)}, u32[]{:S(2)}, u32[]{:S(2)}) collective-permute-start(bf16[128,1024]{1,0:T(8,128)(2,1)S(1)} %get-tuple-element.27), channel_id=1, source_target_pairs={{0,4},{4,0},{8,12},{12,8},{16,20},{20,16},{24,28},{28,24},{1,5},{5... | collective-permute-start | bytes 786440 | tf_op jit(solution)/shard_map/ppermute | solution.py:432
  28.5 1.8 %project_kv.1.refs_2_ = bf16[512,1024]{1,0:T(8,128)(2,1)S(1)} custom-call(s32[25]{0:T(128)S(1)} %concatenate.3.meta, bf16[512,2048]{1,0:T(8,128)(2,1)S(1)} %bitcast.16, f32[512,1536]{1,0:T(8,128)S(1)} %project_own.1.partial, bf16[512,1024]{1,0:T(8,128)(2,1)S(1)} %get-tuple-element.29.refs_0_, bf16[512,1024]{1,0:T(8,128)(2,1)S(1)} %get-tuple-element.30.refs_1_), custom_call_target="tpu_custom_call" | custom-call | flops 2990000 | bytes 1000 | tf_op jit(solution)/shard_map/project_kv/pallas_call | solution.py:343
  30.7 0.6 %slot_queries.1 = bf16[2,512,512]{2,1,0:T(8,128)(2,1)S(1)} custom-call(s32[25]{0:T(128)S(1)} %concatenate.3.meta, bf16[512,512]{1,0:T(8,128)(2,1)S(1)} %collective-permute-done.1.source.refs_0_), custom_call_target="tpu_custom_call" | custom-call | flops 575000 | bytes 1000 | tf_op jit(solution)/shard_map/slot_queries/pallas_call | solution.py:343
  31.3 4.6 %all_to_all.5.refs_1_ = bf16[2,512,512]{2,1,0:T(8,128)(2,1)S(1)} all-to-all(bf16[2,512,512]{2,1,0:T(8,128)(2,1)S(1)} %slot_queries.1), channel_id=1, replica_groups={{0,1},{2,3},{4,5},{6,7},{8,9},{10,11},{12,13},{14,15},{16,17},{18,19},{..., dimensions={0} | all-to-all | bytes 2097152 | tf_op jit(solution)/shard_map/all_to_all | solution.py:442
  35.9 3.4 %attend_local.1 = (bf16[512,512]{1,0:T(8,128)(2,1)}, bf16[128,512]{1,0:T(8,128)(2,1)S(1)}, f32[128,512]{1,0:T(8,128)S(1)}, f32[128,512]{1,0:T(8,128)S(1)}, f32[128,512]{1,0:T(8,128)S(1)}) custom-call(s32[25]{0:T(128)S(1)} %concatenate.3.meta, bf16[512,2048]{1,0:T(8,128)(2,1)S(1)} %bitcast.17, f32[512,1536]{1,0:T(8,128)S(1)} %project_own.1.partial, ...), custom_call_target="tpu_custom_call" | custom-call | flops 6325000 | bytes 1000 | tf_op jit(solution)/shard_map/attend_local/pallas_call | solution.py:343
  39.3 0.7 %collective-permute-done.13.refs_5_ = bf16[128,1024]{1,0:T(8,128)(2,1)S(1)} collective-permute-done((bf16[128,1024]{1,0:T(8,128)(2,1)S(1)}, bf16[128,1024]{1,0:T(8,128)(2,1)S(1)}, u32[]{:S(2)}, u32[]{:S(2)}) %collective-permute-start.13) | collective-permute-done | bytes 262176 | tf_op jit(solution)/shard_map/ppermute | solution.py:432
  40.0 0.6 %merge_near.1 = bf16[512,512]{1,0:T(8,128)(2,1)} custom-call(s32[25]{0:T(128)S(1)} %concatenate.3.meta, bf16[128,512]{1,0:T(8,128)(2,1)S(1)} %get-tuple-element.32.refs_0_, f32[128,512]{1,0:T(8,128)S(1)} %get-tuple-element.33.refs_1_, f32[128,512]{1,0:T(8,128)S(1)} %get-tuple-element.34.refs_2_, ...), custom_call_target="tpu_custom_call", output_to_operand_aliasing={{}: (8, {})} | custom-call | flops 2990000 | bytes 1000 | tf_op jit(solution)/shard_map/merge_near/pallas_call | solution.py:456
  (29 shorter events, 1.7 us)
Async XLA Ops:
  0.0 13.4 %copy-start.3 = (s32[4]{0:T(128)S(1)}, s32[4]{0:T(128)}, u32[]{:S(2)}) copy-start(s32[4]{0:T(128)} %param.7) | copy-start | bytes 52
  0.0 16.3 %copy-start.2 = (s32[4]{0:T(128)S(1)}, s32[4]{0:T(128)}, u32[]{:S(2)}) copy-start(s32[4]{0:T(128)} %param.6) | copy-start | bytes 52
  0.0 16.5 %copy-start = (bf16[1,512,2048]{2,1,0:T(8,128)(2,1)S(1)}, bf16[1,512,2048]{2,1,0:T(8,128)(2,1)}, u32[]{:S(2)}) copy-start(bf16[1,512,2048]{2,1,0:T(8,128)(2,1)} %param.4) | copy-start | bytes 6291460
  0.0 16.4 %collective-permute-start = (bf16[512,1536]{1,0:T(8,128)(2,1)}, bf16[512,1536]{1,0:T(8,128)(2,1)}, u32[]{:S(2)}, u32[]{:S(2)}) collective-permute-start(bf16[512,1536]{1,0:T(8,128)(2,1)} %refs_0_.1), channel_id=1, source_target_pairs={{0,1},{1,0},{2,3},{3,2},{4,5},{5,4},{6,7},{7,6},{8,9},{9,8},{10,11... | collective-permute-start | bytes 4718600 | tf_op jit(solution)/shard_map/ppermute | solution.py:54
  1.6 9.8 %collective-permute-start.2 = (bf16[128,1024]{1,0:T(8,128)(2,1)S(1)}, bf16[128,1024]{1,0:T(8,128)(2,1)S(1)}, u32[]{:S(2)}, u32[]{:S(2)}) collective-permute-start(bf16[128,1024]{1,0:T(8,128)(2,1)S(1)} %constant_dynamic-slice_fusion.1), channel_id=1, source_target_pairs={{0,2},{1,3},{2,0},{3,1},{4,6},{5,7},{6,4},{7,5},{8,10},{9,11},{10,... | collective-permute-start | bytes 786440 | tf_op jit(solution)/shard_map/ppermute | solution.py:54
  5.8 8.3 %collective-permute-start.4 = (bf16[64,1024]{1,0:T(8,128)(2,1)}, bf16[64,1024]{1,0:T(8,128)(2,1)S(1)}, u32[]{:S(2)}, u32[]{:S(2)}) collective-permute-start(bf16[64,1024]{1,0:T(8,128)(2,1)} %constant_dynamic-slice_fusion), channel_id=1, source_target_pairs={{0,2},{1,3},{2,0},{3,1},{4,6},{5,7},{6,4},{7,5},{8,10},{9,11},{10,... | collective-permute-start | bytes 393224 | tf_op jit(solution)/shard_map/ppermute | solution.py:54
  7.5 13.6 %collective-permute-start.6 = (bf16[128,1024]{1,0:T(8,128)(2,1)}, bf16[128,1024]{1,0:T(8,128)(2,1)S(1)}, u32[]{:S(2)}, u32[]{:S(2)}) collective-permute-start(bf16[128,1024]{1,0:T(8,128)(2,1)} %slice.6), channel_id=1, source_target_pairs={{0,2},{1,3},{2,0},{3,1},{4,6},{5,7},{6,4},{7,5},{8,10},{9,11},{10,... | collective-permute-start | bytes 786440 | tf_op jit(solution)/shard_map/ppermute | solution.py:54
  11.3 19.3 %collective-permute-start.1 = (bf16[512,512]{1,0:T(8,128)(2,1)}, bf16[512,512]{1,0:T(8,128)(2,1)S(1)}, u32[]{:S(2)}, u32[]{:S(2)}) collective-permute-start(bf16[512,512]{1,0:T(8,128)(2,1)} %slice.7), channel_id=1, source_target_pairs={{0,2},{1,3},{2,0},{3,1},{4,6},{5,7},{6,4},{7,5},{8,10},{9,11},{10,... | collective-permute-start | bytes 1572872 | tf_op jit(solution)/shard_map/ppermute | solution.py:54
  11.4 10.3 %collective-permute-start.3 = (bf16[128,1024]{1,0:T(8,128)(2,1)S(1)}, bf16[128,1024]{1,0:T(8,128)(2,1)S(1)}, u32[]{:S(2)}, u32[]{:S(2)}) collective-permute-start(bf16[128,1024]{1,0:T(8,128)(2,1)S(1)} %collective-permute-done.2.refs_0_), channel_id=1, source_target_pairs={{0,4},{4,0},{8,12},{12,8},{16,20},{20,16},{24,28},{28,24},{1,5},{5... | collective-permute-start | bytes 786440 | tf_op jit(solution)/shard_map/ppermute | solution.py:54
  14.1 7.6 %collective-permute-start.5 = (bf16[64,1024]{1,0:T(8,128)(2,1)S(1)}, bf16[64,1024]{1,0:T(8,128)(2,1)}, u32[]{:S(2)}, u32[]{:S(2)}) collective-permute-start(bf16[64,1024]{1,0:T(8,128)(2,1)S(1)} %collective-permute-done.4.refs_2_), channel_id=1, source_target_pairs={{0,8},{4,12},{8,0},{12,4},{16,24},{20,28},{24,16},{28,20},{1,9},{5... | collective-permute-start | bytes 393224 | tf_op jit(solution)/shard_map/ppermute | solution.py:54
  16.4 5.8 %collective-permute-start.9 = (bf16[64,1024]{1,0:T(8,128)(2,1)S(1)}, bf16[64,1024]{1,0:T(8,128)(2,1)S(1)}, u32[]{:S(2)}, u32[]{:S(2)}) collective-permute-start(bf16[64,1024]{1,0:T(8,128)(2,1)S(1)} %collective-permute-done.4.refs_2_), channel_id=1, source_target_pairs={{0,1},{1,0},{2,3},{3,2},{4,5},{5,4},{6,7},{7,6},{8,9},{9,8},{10,11... | collective-permute-start | bytes 393224 | tf_op jit(solution)/shard_map/ppermute | solution.py:54
  16.5 1.4 %copy-start.1 = (bf16[512,1536]{1,0:T(8,128)(2,1)S(1)}, bf16[512,1536]{1,0:T(8,128)(2,1)}, u32[]{:S(2)}) copy-start(bf16[512,1536]{1,0:T(8,128)(2,1)} %refs_0_.1) | copy-start | bytes 4718596
  21.1 2.5 %collective-permute-start.7 = (bf16[128,1024]{1,0:T(8,128)(2,1)S(1)}, bf16[128,1024]{1,0:T(8,128)(2,1)S(1)}, u32[]{:S(2)}, u32[]{:S(2)}) collective-permute-start(bf16[128,1024]{1,0:T(8,128)(2,1)S(1)} %collective-permute-done.2.refs_0_), channel_id=1, source_target_pairs={{0,1},{1,0},{2,3},{3,2},{4,5},{5,4},{6,7},{7,6},{8,9},{9,8},{10,11... | collective-permute-start | bytes 786440 | tf_op jit(solution)/shard_map/ppermute | solution.py:54
  21.7 1.9 %collective-permute-start.11 = (bf16[128,1024]{1,0:T(8,128)(2,1)S(1)}, bf16[128,1024]{1,0:T(8,128)(2,1)S(1)}, u32[]{:S(2)}, u32[]{:S(2)}) collective-permute-start(bf16[128,1024]{1,0:T(8,128)(2,1)S(1)} %collective-permute-done.6.refs_4_), channel_id=1, source_target_pairs={{0,1},{1,0},{2,3},{3,2},{4,5},{5,4},{6,7},{7,6},{8,9},{9,8},{10,11... | collective-permute-start | bytes 786440 | tf_op jit(solution)/shard_map/ppermute | solution.py:54
  21.7 2.2 %collective-permute-start.8 = (bf16[128,1024]{1,0:T(8,128)(2,1)S(1)}, bf16[128,1024]{1,0:T(8,128)(2,1)S(1)}, u32[]{:S(2)}, u32[]{:S(2)}) collective-permute-start(bf16[128,1024]{1,0:T(8,128)(2,1)S(1)} %collective-permute-done.3.refs_1_), channel_id=1, source_target_pairs={{0,1},{1,0},{2,3},{3,2},{4,5},{5,4},{6,7},{7,6},{8,9},{9,8},{10,11... | collective-permute-start | bytes 786440 | tf_op jit(solution)/shard_map/ppermute | solution.py:54
  22.2 1.8 %collective-permute-start.10 = (bf16[64,1024]{1,0:T(8,128)(2,1)}, bf16[64,1024]{1,0:T(8,128)(2,1)S(1)}, u32[]{:S(2)}, u32[]{:S(2)}) collective-permute-start(bf16[64,1024]{1,0:T(8,128)(2,1)} %collective-permute-done.5.refs_3_), channel_id=1, source_target_pairs={{0,1},{1,0},{2,3},{3,2},{4,5},{5,4},{6,7},{7,6},{8,9},{9,8},{10,11... | collective-permute-start | bytes 393224 | tf_op jit(solution)/shard_map/ppermute | solution.py:54
  24.9 14.3 %collective-permute-start.12 = (bf16[128,1024]{1,0:T(8,128)(2,1)S(1)}, bf16[128,1024]{1,0:T(8,128)(2,1)S(1)}, u32[]{:S(2)}, u32[]{:S(2)}) collective-permute-start(bf16[128,1024]{1,0:T(8,128)(2,1)S(1)} %get-tuple-element.27), channel_id=1, source_target_pairs={{0,12},{4,8},{8,4},{12,0},{16,28},{20,24},{24,20},{28,16},{1,13},{... | collective-permute-start | bytes 786440 | tf_op jit(solution)/shard_map/ppermute | solution.py:432
  26.5 13.5 %collective-permute-start.13 = (bf16[128,1024]{1,0:T(8,128)(2,1)S(1)}, bf16[128,1024]{1,0:T(8,128)(2,1)S(1)}, u32[]{:S(2)}, u32[]{:S(2)}) collective-permute-start(bf16[128,1024]{1,0:T(8,128)(2,1)S(1)} %get-tuple-element.27), channel_id=1, source_target_pairs={{0,8},{4,12},{8,0},{12,4},{16,24},{20,28},{24,16},{28,20},{1,9},{5... | collective-permute-start | bytes 786440 | tf_op jit(solution)/shard_map/ppermute | solution.py:432
  28.0 12.0 %collective-permute-start.14 = (bf16[128,1024]{1,0:T(8,128)(2,1)S(1)}, bf16[128,1024]{1,0:T(8,128)(2,1)S(1)}, u32[]{:S(2)}, u32[]{:S(2)}) collective-permute-start(bf16[128,1024]{1,0:T(8,128)(2,1)S(1)} %get-tuple-element.27), channel_id=1, source_target_pairs={{0,4},{4,0},{8,12},{12,8},{16,20},{20,16},{24,28},{28,24},{1,5},{5... | collective-permute-start | bytes 786440 | tf_op jit(solution)/shard_map/ppermute | solution.py:432

commit v6 on v4

--- a/solution.py
+++ b/solution.py
@@ -18,14 +18,15 @@
 SCALE2 = HEAD_DIM ** (-0.5) * math.log2(math.e)
 VMEM_LIMIT = 24 * 1024 * 1024
 
-MODEL_FLOPS = {"project_first": 689999, "split_queries": 575000, "project_pack": 689999, "project_own": 3680000, "project_mid": 1610000, "project_kv": 2990000, "attend_local": 6325000, "merge_near": 2990000}
+MODEL_FLOPS = {"project_first": 689999, "split_queries": 575000, "sides": 11500000000, "cut_rest": 1150000, "project_pack": 689999, "project_own": 3680000, "project_mid": 1610000, "project_kv": 2990000, "attend_local": 6325000, "merge_near": 2990000}
 ORDER = {
+    'cut': ('c0',),
     'p0': ('partial', 'xD'),
     'p1': ('partial',),
     'q': ('kv',),
     'kv': ('pack',),
 }
-NEAR_ORDER = (3, 1, 2)
+NEAR_ORDER = (1, 2, 3)
 F32 = jnp.float32
 BF16 = jnp.bfloat16
 
@@ -41,8 +42,7 @@
     pairs = []
     for source in range(count):
         run, spot = place(source)
-        one_bit = bits & (bits - 1) == 0
-        if (run, spot ^ bits) in where and (one_bit or spot ^ bits > spot):
+        if (run, spot ^ bits) in where:
             pairs.append((source, where[run, spot ^ bits]))
     return pairs
 
@@ -88,6 +88,14 @@
     for j in range(out.shape[1] // PAIR):
         lanes = slice(j * PAIR, (j + 1) * PAIR)
         out[:, lanes] = add_up(tokens, [meta[at] for at in range(count)], [weight.at[:, lanes] for weight in weights])
+
+
+def cut_kernel(spans, direct_from, sides, weight, *outs):
+    for (number, start, rows), out in zip(spans, outs):
+        first = pl.multiple_of(start + sides[number] * rows, rows)
+        out[...] = weight[pl.ds(first, rows), WIDTH:]
+    outs[-2][...] = weight[direct_from:, WIDTH:]
+    outs[-1][: weight.shape[0], :] = weight[:, :WIDTH]
 
 
 def near_rows_kernel(layout, place_at, first, slots, slot_at, meta, tokens, before, *refs):
@@ -346,7 +354,7 @@
     whole = pl.BlockSpec(memory_space=pltpu.VMEM)
     shape = jax.ShapeDtypeStruct
 
-    def call(kernel, args, results, name, scratch=()):
+    def call(kernel, args, results, name, scratch=(), scalars=None):
         return pl.pallas_call(
             kernel,
             in_specs=[scalar_spec] + [whole] * len(args),
@@ -356,7 +364,7 @@
             compiler_params=pltpu.CompilerParams(vmem_limit_bytes=VMEM_LIMIT),
             cost_estimate=pl.CostEstimate(flops=MODEL_FLOPS[name], bytes_accessed=1000, transcendentals=0),
             name=name,
-        )(meta, *args)
+        )(meta if scalars is None else scalars, *args)
 
     passing = [share * 15 // 32 // 16 * 16] * 2
     local = [qkv_weight]
@@ -375,12 +383,25 @@
     direct_rows, queries = [], []
     for bit in bits:
         mine_rows, other_rows = [], []
+        first_cut = [
+            lax.dynamic_slice(qkv_weight, (start + seq_index % 2 * rows, WIDTH), (rows, 2 * WIDTH))
+            for start, rows in spans[:1]
+        ]
+        known |= {"c0": value for value in first_cut}
+        rest_spans = [(number, *span) for number, span in enumerate(spans)][1:]
+        left = share - sum(passing)
+        *rest_cuts, direct_cut, query_cut = call(
+            functools.partial(cut_kernel, rest_spans, direct_from),
+            [ordered("cut", qkv_weight, known)],
+            [shape((rows, 2 * WIDTH), BF16) for _, _, rows in rest_spans]
+            + [shape((share - direct_from, 2 * WIDTH), BF16), shape((share + left, WIDTH), BF16)],
+            "cut_rest",
+            scalars=as_array([seq_index % 2, seq_index // 2 % 2]),
+        )
+        span_cuts = first_cut + rest_cuts
         for number, (start, rows) in enumerate(spans):
             tag = str(number)
-            side = seq_index // (1 << number) % 2
-            cut = lax.dynamic_slice(
-                ordered("c" + tag, qkv_weight, known), (start + side * rows, WIDTH), (rows, 2 * WIDTH)
-            )
+            cut = span_cuts[number]
             known["c" + tag] = cut
             direct = swap(cut, "fsdp", bit)
             known["x" + tag] = direct
@@ -391,18 +412,16 @@
             mine_rows += [direct, passed]
             other_rows += [across, swap(passed, "fsdp", 1)]
             known["q" + tag] = other_rows[-1]
-        known["meta"] = meta
-        cut = ordered("cD", qkv_weight, known)[direct_from:, WIDTH:]
+        cut = direct_cut
         known["cD"] = cut
         rest = swap(cut, "fsdp", bit)
         known["xD"] = rest
         rest = ordered("pD", rest, known)
         known["fD"] = swap(rest, "fsdp", 1)
         direct_rows.append(mine_rows + [rest] + other_rows + [known["fD"]])
-        cut = ordered("cQ", qkv_weight, known)[:, :WIDTH]
-        left = share - sum(passing)
+        cut = query_cut
         if left:
-            cut = jnp.concatenate([cut, known["core"][share - left :, :WIDTH]], axis=0)
+            cut = lax.dynamic_update_slice(cut, known["core"][share - left :, :WIDTH], (share, 0))
         known["cQ"] = cut
         queries.append(swap(cut, "fsdp", bit))
     assert len(bits) <= 1

time: 42.5 us -> 42.4 us (level)
  the two profiles are of different devices: /device:TPU:8 before, /device:TPU:0 now
where the time goes in v6:
time: 42.4 us; the launch traced here: 42.1 us
  starting transfers between devices  15.5 us (37%)
  Pallas kernels  13.4 us (32%)
  waiting for transfers between devices  7.43 us (18%)
  local copies, waits for them, and re-layouts  5.44 us (13%)
    pallas_call x7, Pallas kernels, call(): pl.pallas_call(kernel, in_specs=[scalar_spec] + [whole] * len(args), out_...  12.8 us
    ppermute x14, starting transfers between devices, swap(): return lax.ppermute(value, axis, [(i, i ^ bit) for i in range(count)])  12 us
    ppermute x14, waiting for transfers between devices, swap(): return lax.ppermute(value, axis, [(i, i ^ bit) for i in range(count)])  3.8 us
    ppermute x3, waiting for transfers between devices, body(): lax.ppermute(pack, 'seq', partners(seq_size, place, step))  3.64 us
    ppermute x3, starting transfers between devices, body(): lax.ppermute(pack, 'seq', partners(seq_size, place, step))  3.55 us
    unnamed x10, local copies, waits for them, and re-layouts  2.82 us
    dynamic_update_slice x1, local copies, waits for them, and re-layouts, body(): lax.dynamic_update_slice(cut, known['core'][share - left:, :WIDTH], (shar...  1.38 us
    dynamic_slice x1, local copies, waits for them, and re-layouts, body(): lax.dynamic_slice(qkv_weight, (start + seq_index % 2 * rows, WIDTH), (row...  1.14 us
  transfers between devices with their start and end apart: 17, of which 6 were waited for; matrix products, arithmetic and copies ran while one was open for 6% of the time, Pallas kernels for 31%

profile of v6, /device:TPU:0, one launch (start us, length us, event | category | flops | bytes accessed | tf_op | source)
XLA Modules:
  0.0 42.1 jit_solution(9500734358767101887)
XLA Ops:
  0.5 1.1 %constant_dynamic-slice_fusion = bf16[128,1024]{1,0:T(8,128)(2,1)S(1)} fusion(bf16[512,1536]{1,0:T(8,128)(2,1)} %weight, s32[]{:T(128)S(6)} %select_n.71), kind=kLoop, calls=%fused_computation.8 | loop fusion | bytes 524292 | tf_op jit(solution)/shard_map/dynamic_slice | solution.py:387
  1.6 2.5 %collective-permute-start.2 = (bf16[128,1024]{1,0:T(8,128)(2,1)S(1)}, bf16[128,1024]{1,0:T(8,128)(2,1)S(1)}, u32[]{:S(2)}, u32[]{:S(2)}) collective-permute-start(bf16[128,1024]{1,0:T(8,128)(2,1)S(1)} %constant_dynamic-slice_fusion), channel_id=1, source_target_pairs={{0,2},{1,3},{2,0},{3,1},{4,6},{5,7},{6,4},{7,5},{8,10},{9,11},{10,... | collective-permute-start | bytes 786440 | tf_op jit(solution)/shard_map/ppermute | solution.py:52
  4.2 1.4 %copy-done.1 = bf16[512,1536]{1,0:T(8,128)(2,1)S(1)} copy-done((bf16[512,1536]{1,0:T(8,128)(2,1)S(1)}, bf16[512,1536]{1,0:T(8,128)(2,1)}, u32[]{:S(2)}) %copy-start.1) | copy-done | bytes 1572888
  5.6 1.5 %cut_rest.1 = (bf16[64,1024]{1,0:T(8,128)(2,1)}, bf16[128,1024]{1,0:T(8,128)(2,1)}, bf16[544,512]{1,0:T(8,128)(2,1)}) custom-call(s32[2]{0:T(128)S(1)} %pad_add_fusion.sides, bf16[512,1536]{1,0:T(8,128)(2,1)S(1)} %copy-done.1), custom_call_target="tpu_custom_call" | custom-call | flops 1150000 | bytes 1000 | tf_op jit(solution)/shard_map/cut_rest/pallas_call | solution.py:358
  7.2 2.0 %collective-permute-start.6 = (bf16[128,1024]{1,0:T(8,128)(2,1)}, bf16[128,1024]{1,0:T(8,128)(2,1)S(1)}, u32[]{:S(2)}, u32[]{:S(2)}) collective-permute-start(bf16[128,1024]{1,0:T(8,128)(2,1)} %get-tuple-element.29), channel_id=1, source_target_pairs={{0,2},{1,3},{2,0},{3,1},{4,6},{5,7},{6,4},{7,5},{8,10},{9,11},{10,... | collective-permute-start | bytes 786440 | tf_op jit(solution)/shard_map/ppermute | solution.py:52
  9.2 2.1 %collective-permute-done.2.refs_0_ = bf16[128,1024]{1,0:T(8,128)(2,1)S(1)} collective-permute-done((bf16[128,1024]{1,0:T(8,128)(2,1)S(1)}, bf16[128,1024]{1,0:T(8,128)(2,1)S(1)}, u32[]{:S(2)}, u32[]{:S(2)}) %collective-permute-start.2) | collective-permute-done | bytes 262176 | tf_op jit(solution)/shard_map/ppermute | solution.py:52
  11.3 2.0 %collective-permute-start.3 = (bf16[128,1024]{1,0:T(8,128)(2,1)S(1)}, bf16[128,1024]{1,0:T(8,128)(2,1)S(1)}, u32[]{:S(2)}, u32[]{:S(2)}) collective-permute-start(bf16[128,1024]{1,0:T(8,128)(2,1)S(1)} %collective-permute-done.2.refs_0_), channel_id=1, source_target_pairs={{0,4},{4,0},{8,12},{12,8},{16,20},{20,16},{24,28},{28,24},{1,5},{5... | collective-permute-start | bytes 786440 | tf_op jit(solution)/shard_map/ppermute | solution.py:52
  13.3 1.4 %slice_dynamic-update-slice_fusion = bf16[544,512]{1,0:T(8,128)(2,1)} fusion(bf16[544,512]{1,0:T(8,128)(2,1)} %get-tuple-element.25, bf16[512,1536]{1,0:T(8,128)(2,1)} %collective-permute-done.refs_1_), kind=kLoop, calls=%fused_computation | loop fusion | bytes 65536 | tf_op jit(solution)/shard_map/dynamic_update_slice | solution.py:424
  14.7 1.5 %collective-permute-start.1 = (bf16[544,512]{1,0:T(8,128)(2,1)}, bf16[544,512]{1,0:T(8,128)(2,1)S(1)}, u32[]{:S(2)}, u32[]{:S(2)}) collective-permute-start(bf16[544,512]{1,0:T(8,128)(2,1)} %slice_dynamic-update-slice_fusion), channel_id=1, source_target_pairs={{0,2},{1,3},{2,0},{3,1},{4,6},{5,7},{6,4},{7,5},{8,10},{9,11},{10,... | collective-permute-start | bytes 1671176 | tf_op jit(solution)/shard_map/ppermute | solution.py:52
  16.3 1.6 %collective-permute-start.5 = (bf16[64,1024]{1,0:T(8,128)(2,1)}, bf16[64,1024]{1,0:T(8,128)(2,1)}, u32[]{:S(2)}, u32[]{:S(2)}) collective-permute-start(bf16[64,1024]{1,0:T(8,128)(2,1)} %collective-permute-done.4.refs_2_), channel_id=1, source_target_pairs={{0,8},{4,12},{8,0},{12,4},{16,24},{20,28},{24,16},{28,20},{1,9},{5... | collective-permute-start | bytes 393224 | tf_op jit(solution)/shard_map/ppermute | solution.py:52
  18.1 1.4 %copy-done.2 = bf16[512,1536]{1,0:T(8,128)(2,1)S(1)} copy-done((bf16[512,1536]{1,0:T(8,128)(2,1)S(1)}, bf16[512,1536]{1,0:T(8,128)(2,1)}, u32[]{:S(2)}) %copy-start.2) | copy-done | bytes 1572888
  19.5 3.2 %project_own.1.partial = f32[512,1536]{1,0:T(8,128)S(1)} custom-call(s32[25]{0:T(128)S(1)} %concatenate.3.meta, bf16[512,2048]{1,0:T(8,128)(2,1)S(1)} %bitcast.15, bf16[512,1536]{1,0:T(8,128)(2,1)S(1)} %copy-done.2, bf16[512,1536]{1,0:T(8,128)(2,1)} %collective-permute-done.refs_1_), custom_call_target="tpu_custom_call" | custom-call | flops 3680000 | bytes 1000 | tf_op jit(solution)/shard_map/project_own/pallas_call | solution.py:358
  22.8 0.6 %collective-permute-start.7 = (bf16[128,1024]{1,0:T(8,128)(2,1)S(1)}, bf16[128,1024]{1,0:T(8,128)(2,1)S(1)}, u32[]{:S(2)}, u32[]{:S(2)}) collective-permute-start(bf16[128,1024]{1,0:T(8,128)(2,1)S(1)} %collective-permute-done.2.refs_0_), channel_id=1, source_target_pairs={{0,1},{1,0},{2,3},{3,2},{4,5},{5,4},{6,7},{7,6},{8,9},{9,8},{10,11... | collective-permute-start | bytes 786440 | tf_op jit(solution)/shard_map/ppermute | solution.py:52
  23.9 1.4 %project_first.1 = (f32[128,1024]{1,0:T(8,128)S(1)}, bf16[512,1024]{1,0:T(8,128)(2,1)S(1)}) custom-call(s32[25]{0:T(128)S(1)} %concatenate.3.meta, bf16[512,2048]{1,0:T(8,128)(2,1)S(1)} %bitcast.16, f32[512,1536]{1,0:T(8,128)S(1)} %project_own.1.partial, bf16[128,1024]{1,0:T(8,128)(2,1)S(1)} %collective-permute-done.2.refs_0_, ...), custom_call_target="tpu_custom_call" | custom-call | flops 689999 | bytes 1000 | tf_op jit(solution)/shard_map/project_first/pallas_call | solution.py:358
  25.6 0.9 %project_pack.1 = (bf16[128,1024]{1,0:T(8,128)(2,1)S(1)}, bf16[512,1024]{1,0:T(8,128)(2,1)S(1)}) custom-call(s32[25]{0:T(128)S(1)} %concatenate.3.meta, bf16[512,2048]{1,0:T(8,128)(2,1)S(1)} %bitcast.17, f32[128,1024]{1,0:T(8,128)S(1)} %get-tuple-element.30.refs_0_, bf16[128,1024]{1,0:T(8,128)(2,1)S(1)} %collective-permute-done.7.refs_1_, ...), custom_call_target="tpu_custom_call" | custom-call | flops 689999 | bytes 1000 | tf_op jit(solution)/shard_map/project_pack/pallas_call | solution.py:358
  27.0 1.6 %collective-permute-start.15 = (bf16[128,1024]{1,0:T(8,128)(2,1)S(1)}, bf16[128,1024]{1,0:T(8,128)(2,1)S(1)}, u32[]{:S(2)}, u32[]{:S(2)}) collective-permute-start(bf16[128,1024]{1,0:T(8,128)(2,1)S(1)} %get-tuple-element.31), channel_id=1, source_target_pairs={{0,8},{4,12},{8,0},{12,4},{16,24},{20,28},{24,16},{28,20},{1,9},{5... | collective-permute-start | bytes 786440 | tf_op jit(solution)/shard_map/ppermute | solution.py:462
  28.6 1.5 %collective-permute-start.14 = (bf16[128,1024]{1,0:T(8,128)(2,1)S(1)}, bf16[128,1024]{1,0:T(8,128)(2,1)S(1)}, u32[]{:S(2)}, u32[]{:S(2)}) collective-permute-start(bf16[128,1024]{1,0:T(8,128)(2,1)S(1)} %get-tuple-element.31), channel_id=1, source_target_pairs={{0,4},{4,0},{8,12},{12,8},{16,20},{20,16},{24,28},{28,24},{1,5},{5... | collective-permute-start | bytes 786440 | tf_op jit(solution)/shard_map/ppermute | solution.py:462
  30.1 1.8 %project_kv.1.refs_3_ = bf16[512,1024]{1,0:T(8,128)(2,1)S(1)} custom-call(s32[25]{0:T(128)S(1)} %concatenate.3.meta, bf16[512,2048]{1,0:T(8,128)(2,1)S(1)} %bitcast.18, f32[512,1536]{1,0:T(8,128)S(1)} %project_own.1.partial, bf16[512,1024]{1,0:T(8,128)(2,1)S(1)} %get-tuple-element.33.refs_0_, bf16[512,1024]{1,0:T(8,128)(2,1)S(1)} %get-tuple-element.34.refs_1_), custom_call_target="tpu_custom_call" | custom-call | flops 2990000 | bytes 1000 | tf_op jit(solution)/shard_map/project_kv/pallas_call | solution.py:358
  32.0 0.6 %split_queries.1 = (bf16[240,512]{1,0:T(8,128)(2,1)S(1)}, bf16[240,512]{1,0:T(8,128)(2,1)S(1)}) custom-call(s32[25]{0:T(128)S(1)} %concatenate.3.meta, bf16[544,512]{1,0:T(8,128)(2,1)S(1)} %collective-permute-done.1.source.refs_0_), custom_call_target="tpu_custom_call" | custom-call | flops 575000 | bytes 1000 | tf_op jit(solution)/shard_map/split_queries/pallas_call | solution.py:358
  33.1 1.0 %collective-permute-done.12.refs_1_ = bf16[240,512]{1,0:T(8,128)(2,1)S(1)} collective-permute-done((bf16[240,512]{1,0:T(8,128)(2,1)S(1)}, bf16[240,512]{1,0:T(8,128)(2,1)S(1)}, u32[]{:S(2)}, u32[]{:S(2)}) %collective-permute-start.12) | collective-permute-done | bytes 245792 | tf_op jit(solution)/shard_map/ppermute | solution.py:52
  34.5 3.4 %attend_local.1 = (bf16[512,512]{1,0:T(8,128)(2,1)}, bf16[128,512]{1,0:T(8,128)(2,1)S(1)}, f32[128,512]{1,0:T(8,128)S(1)}, f32[128,512]{1,0:T(8,128)S(1)}, f32[128,512]{1,0:T(8,128)S(1)}) custom-call(s32[25]{0:T(128)S(1)} %concatenate.3.meta, bf16[512,2048]{1,0:T(8,128)(2,1)S(1)} %bitcast.19, f32[512,1536]{1,0:T(8,128)S(1)} %project_own.1.partial, ...), custom_call_target="tpu_custom_call" | custom-call | flops 6325000 | bytes 1000 | tf_op jit(solution)/shard_map/attend_local/pallas_call | solution.py:358
  37.9 2.7 %collective-permute-done.15.refs_5_ = bf16[128,1024]{1,0:T(8,128)(2,1)S(1)} collective-permute-done((bf16[128,1024]{1,0:T(8,128)(2,1)S(1)}, bf16[128,1024]{1,0:T(8,128)(2,1)S(1)}, u32[]{:S(2)}, u32[]{:S(2)}) %collective-permute-start.15) | collective-permute-done | bytes 262176 | tf_op jit(solution)/shard_map/ppermute | solution.py:462
  40.6 0.9 %collective-permute-done.14.refs_4_ = bf16[128,1024]{1,0:T(8,128)(2,1)S(1)} collective-permute-done((bf16[128,1024]{1,0:T(8,128)(2,1)S(1)}, bf16[128,1024]{1,0:T(8,128)(2,1)S(1)}, u32[]{:S(2)}, u32[]{:S(2)}) %collective-permute-start.14) | collective-permute-done | bytes 262176 | tf_op jit(solution)/shard_map/ppermute | solution.py:462
  41.5 0.6 %merge_near.1 = bf16[512,512]{1,0:T(8,128)(2,1)} custom-call(s32[25]{0:T(128)S(1)} %concatenate.3.meta, bf16[128,512]{1,0:T(8,128)(2,1)S(1)} %get-tuple-element.38.refs_0_, f32[128,512]{1,0:T(8,128)S(1)} %get-tuple-element.39.refs_1_, f32[128,512]{1,0:T(8,128)S(1)} %get-tuple-element.40.refs_2_, ...), custom_call_target="tpu_custom_call", output_to_operand_aliasing={{}: (8, {})} | custom-call | flops 2990000 | bytes 1000 | tf_op jit(solution)/shard_map/merge_near/pallas_call | solution.py:487
  (34 shorter events, 3.1 us)
Async XLA Ops:
  0.0 18.1 %copy-start = (bf16[1,512,2048]{2,1,0:T(8,128)(2,1)S(1)}, bf16[1,512,2048]{2,1,0:T(8,128)(2,1)}, u32[]{:S(2)}) copy-start(bf16[1,512,2048]{2,1,0:T(8,128)(2,1)} %param.4) | copy-start | bytes 6291460
  0.0 13.3 %collective-permute-start = (bf16[512,1536]{1,0:T(8,128)(2,1)}, bf16[512,1536]{1,0:T(8,128)(2,1)}, u32[]{:S(2)}, u32[]{:S(2)}) collective-permute-start(bf16[512,1536]{1,0:T(8,128)(2,1)} %weight), channel_id=1, source_target_pairs={{0,1},{1,0},{2,3},{3,2},{4,5},{5,4},{6,7},{7,6},{8,9},{9,8},{10,11... | collective-permute-start | bytes 4718600 | tf_op jit(solution)/shard_map/ppermute | solution.py:52
  1.6 9.7 %collective-permute-start.2 = (bf16[128,1024]{1,0:T(8,128)(2,1)S(1)}, bf16[128,1024]{1,0:T(8,128)(2,1)S(1)}, u32[]{:S(2)}, u32[]{:S(2)}) collective-permute-start(bf16[128,1024]{1,0:T(8,128)(2,1)S(1)} %constant_dynamic-slice_fusion), channel_id=1, source_target_pairs={{0,2},{1,3},{2,0},{3,1},{4,6},{5,7},{6,4},{7,5},{8,10},{9,11},{10,... | collective-permute-start | bytes 786440 | tf_op jit(solution)/shard_map/ppermute | solution.py:52
  4.2 1.4 %copy-start.1 = (bf16[512,1536]{1,0:T(8,128)(2,1)S(1)}, bf16[512,1536]{1,0:T(8,128)(2,1)}, u32[]{:S(2)}) copy-start(bf16[512,1536]{1,0:T(8,128)(2,1)} %weight) | copy-start | bytes 4718596
  5.6 10.5 %copy-start.4 = (s32[4]{0:T(128)S(1)}, s32[4]{0:T(128)}, u32[]{:S(2)}) copy-start(s32[4]{0:T(128)} %param.7) | copy-start | bytes 52
  5.6 12.3 %copy-start.3 = (s32[4]{0:T(128)S(1)}, s32[4]{0:T(128)}, u32[]{:S(2)}) copy-start(s32[4]{0:T(128)} %param.6) | copy-start | bytes 52
  7.2 9.1 %collective-permute-start.4 = (bf16[64,1024]{1,0:T(8,128)(2,1)}, bf16[64,1024]{1,0:T(8,128)(2,1)}, u32[]{:S(2)}, u32[]{:S(2)}) collective-permute-start(bf16[64,1024]{1,0:T(8,128)(2,1)} %get-tuple-element.27), channel_id=1, source_target_pairs={{0,2},{1,3},{2,0},{3,1},{4,6},{5,7},{6,4},{7,5},{8,10},{9,11},{10,... | collective-permute-start | bytes 393224 | tf_op jit(solution)/shard_map/ppermute | solution.py:52
  7.2 15.6 %collective-permute-start.6 = (bf16[128,1024]{1,0:T(8,128)(2,1)}, bf16[128,1024]{1,0:T(8,128)(2,1)S(1)}, u32[]{:S(2)}, u32[]{:S(2)}) collective-permute-start(bf16[128,1024]{1,0:T(8,128)(2,1)} %get-tuple-element.29), channel_id=1, source_target_pairs={{0,2},{1,3},{2,0},{3,1},{4,6},{5,7},{6,4},{7,5},{8,10},{9,11},{10,... | collective-permute-start | bytes 786440 | tf_op jit(solution)/shard_map/ppermute | solution.py:52
  11.3 12.0 %collective-permute-start.3 = (bf16[128,1024]{1,0:T(8,128)(2,1)S(1)}, bf16[128,1024]{1,0:T(8,128)(2,1)S(1)}, u32[]{:S(2)}, u32[]{:S(2)}) collective-permute-start(bf16[128,1024]{1,0:T(8,128)(2,1)S(1)} %collective-permute-done.2.refs_0_), channel_id=1, source_target_pairs={{0,4},{4,0},{8,12},{12,8},{16,20},{20,16},{24,28},{28,24},{1,5},{5... | collective-permute-start | bytes 786440 | tf_op jit(solution)/shard_map/ppermute | solution.py:52
  14.7 17.3 %collective-permute-start.1 = (bf16[544,512]{1,0:T(8,128)(2,1)}, bf16[544,512]{1,0:T(8,128)(2,1)S(1)}, u32[]{:S(2)}, u32[]{:S(2)}) collective-permute-start(bf16[544,512]{1,0:T(8,128)(2,1)} %slice_dynamic-update-slice_fusion), channel_id=1, source_target_pairs={{0,2},{1,3},{2,0},{3,1},{4,6},{5,7},{6,4},{7,5},{8,10},{9,11},{10,... | collective-permute-start | bytes 1671176 | tf_op jit(solution)/shard_map/ppermute | solution.py:52
  16.3 7.1 %collective-permute-start.5 = (bf16[64,1024]{1,0:T(8,128)(2,1)}, bf16[64,1024]{1,0:T(8,128)(2,1)}, u32[]{:S(2)}, u32[]{:S(2)}) collective-permute-start(bf16[64,1024]{1,0:T(8,128)(2,1)} %collective-permute-done.4.refs_2_), channel_id=1, source_target_pairs={{0,8},{4,12},{8,0},{12,4},{16,24},{20,28},{24,16},{28,20},{1,9},{5... | collective-permute-start | bytes 393224 | tf_op jit(solution)/shard_map/ppermute | solution.py:52
  18.0 5.8 %collective-permute-start.9 = (bf16[64,1024]{1,0:T(8,128)(2,1)}, bf16[64,1024]{1,0:T(8,128)(2,1)S(1)}, u32[]{:S(2)}, u32[]{:S(2)}) collective-permute-start(bf16[64,1024]{1,0:T(8,128)(2,1)} %collective-permute-done.4.refs_2_), channel_id=1, source_target_pairs={{0,1},{1,0},{2,3},{3,2},{4,5},{5,4},{6,7},{7,6},{8,9},{9,8},{10,11... | collective-permute-start | bytes 393224 | tf_op jit(solution)/shard_map/ppermute | solution.py:52
  18.1 1.4 %copy-start.2 = (bf16[512,1536]{1,0:T(8,128)(2,1)S(1)}, bf16[512,1536]{1,0:T(8,128)(2,1)}, u32[]{:S(2)}) copy-start(bf16[512,1536]{1,0:T(8,128)(2,1)} %weight) | copy-start | bytes 4718596
  22.8 2.5 %collective-permute-start.7 = (bf16[128,1024]{1,0:T(8,128)(2,1)S(1)}, bf16[128,1024]{1,0:T(8,128)(2,1)S(1)}, u32[]{:S(2)}, u32[]{:S(2)}) collective-permute-start(bf16[128,1024]{1,0:T(8,128)(2,1)S(1)} %collective-permute-done.2.refs_0_), channel_id=1, source_target_pairs={{0,1},{1,0},{2,3},{3,2},{4,5},{5,4},{6,7},{7,6},{8,9},{9,8},{10,11... | collective-permute-start | bytes 786440 | tf_op jit(solution)/shard_map/ppermute | solution.py:52
  23.3 2.0 %collective-permute-start.11 = (bf16[128,1024]{1,0:T(8,128)(2,1)S(1)}, bf16[128,1024]{1,0:T(8,128)(2,1)S(1)}, u32[]{:S(2)}, u32[]{:S(2)}) collective-permute-start(bf16[128,1024]{1,0:T(8,128)(2,1)S(1)} %collective-permute-done.6.refs_4_), channel_id=1, source_target_pairs={{0,1},{1,0},{2,3},{3,2},{4,5},{5,4},{6,7},{7,6},{8,9},{9,8},{10,11... | collective-permute-start | bytes 786440 | tf_op jit(solution)/shard_map/ppermute | solution.py:52
  23.4 2.2 %collective-permute-start.8 = (bf16[128,1024]{1,0:T(8,128)(2,1)S(1)}, bf16[128,1024]{1,0:T(8,128)(2,1)S(1)}, u32[]{:S(2)}, u32[]{:S(2)}) collective-permute-start(bf16[128,1024]{1,0:T(8,128)(2,1)S(1)} %collective-permute-done.3.refs_1_), channel_id=1, source_target_pairs={{0,1},{1,0},{2,3},{3,2},{4,5},{5,4},{6,7},{7,6},{8,9},{9,8},{10,11... | collective-permute-start | bytes 786440 | tf_op jit(solution)/shard_map/ppermute | solution.py:52
  23.8 1.8 %collective-permute-start.10 = (bf16[64,1024]{1,0:T(8,128)(2,1)}, bf16[64,1024]{1,0:T(8,128)(2,1)S(1)}, u32[]{:S(2)}, u32[]{:S(2)}) collective-permute-start(bf16[64,1024]{1,0:T(8,128)(2,1)} %collective-permute-done.5.refs_3_), channel_id=1, source_target_pairs={{0,1},{1,0},{2,3},{3,2},{4,5},{5,4},{6,7},{7,6},{8,9},{9,8},{10,11... | collective-permute-start | bytes 393224 | tf_op jit(solution)/shard_map/ppermute | solution.py:52
  26.6 11.3 %collective-permute-start.16 = (bf16[128,1024]{1,0:T(8,128)(2,1)S(1)}, bf16[128,1024]{1,0:T(8,128)(2,1)S(1)}, u32[]{:S(2)}, u32[]{:S(2)}) collective-permute-start(bf16[128,1024]{1,0:T(8,128)(2,1)S(1)} %get-tuple-element.31), channel_id=1, source_target_pairs={{0,12},{4,8},{8,4},{12,0},{16,28},{20,24},{24,20},{28,16},{1,13},{... | collective-permute-start | bytes 786440 | tf_op jit(solution)/shard_map/ppermute | solution.py:462
  27.0 13.6 %collective-permute-start.15 = (bf16[128,1024]{1,0:T(8,128)(2,1)S(1)}, bf16[128,1024]{1,0:T(8,128)(2,1)S(1)}, u32[]{:S(2)}, u32[]{:S(2)}) collective-permute-start(bf16[128,1024]{1,0:T(8,128)(2,1)S(1)} %get-tuple-element.31), channel_id=1, source_target_pairs={{0,8},{4,12},{8,0},{12,4},{16,24},{20,28},{24,16},{28,20},{1,9},{5... | collective-permute-start | bytes 786440 | tf_op jit(solution)/shard_map/ppermute | solution.py:462
  28.6 12.9 %collective-permute-start.14 = (bf16[128,1024]{1,0:T(8,128)(2,1)S(1)}, bf16[128,1024]{1,0:T(8,128)(2,1)S(1)}, u32[]{:S(2)}, u32[]{:S(2)}) collective-permute-start(bf16[128,1024]{1,0:T(8,128)(2,1)S(1)} %get-tuple-element.31), channel_id=1, source_target_pairs={{0,4},{4,0},{8,12},{12,8},{16,20},{20,16},{24,28},{28,24},{1,5},{5... | collective-permute-start | bytes 786440 | tf_op jit(solution)/shard_map/ppermute | solution.py:462
  32.6 1.6 %collective-permute-start.12 = (bf16[240,512]{1,0:T(8,128)(2,1)S(1)}, bf16[240,512]{1,0:T(8,128)(2,1)S(1)}, u32[]{:S(2)}, u32[]{:S(2)}) collective-permute-start(bf16[240,512]{1,0:T(8,128)(2,1)S(1)} %get-tuple-element.36), channel_id=1, source_target_pairs={{0,1},{1,0},{2,3},{3,2},{4,5},{5,4},{6,7},{7,6},{8,9},{9,8},{10,11... | collective-permute-start | bytes 737288 | tf_op jit(solution)/shard_map/ppermute | solution.py:52
  32.6 1.9 %collective-permute-start.13 = (bf16[240,512]{1,0:T(8,128)(2,1)S(1)}, bf16[240,512]{1,0:T(8,128)(2,1)S(1)}, u32[]{:S(2)}, u32[]{:S(2)}) collective-permute-start(bf16[240,512]{1,0:T(8,128)(2,1)S(1)} %get-tuple-element.37), channel_id=1, source_target_pairs={{0,1},{1,0},{2,3},{3,2},{4,5},{5,4},{6,7},{7,6},{8,9},{9,8},{10,11... | collective-permute-start | bytes 737288 | tf_op jit(solution)/shard_map/ppermute | solution.py:52

commit v7 on v5

--- a/solution.py
+++ b/solution.py
@@ -16,10 +16,11 @@
 PAIR = 2 * HEAD_DIM
 NEG = -1e30
 SCALE2 = HEAD_DIM ** (-0.5) * math.log2(math.e)
-VMEM_LIMIT = 12 * 1024 * 1024
+VMEM_LIMIT = 24 * 1024 * 1024
 
 MODEL_FLOPS = {"slot_queries": 575000, "project_first": 689999, "project_pack": 689999, "project_own": 3680000, "project_mid": 1610000, "project_kv": 2990000, "attend_local": 6325000, "merge_near": 2990000}
 ORDER = {
+    'core': ('c0',),
     'c1': ('c0',),
     'cD': ('c1',),
     'cQ': ('cD',),
@@ -354,8 +355,11 @@
     local = [qkv_weight]
     bits = range(2, pieces, 2)
     known = {}
+    if pieces > 2 and spans:
+        start, rows = spans[0]
+        known["c0"] = lax.dynamic_slice(qkv_weight, (start + seq_index % 2 * rows, WIDTH), (rows, 2 * WIDTH))
     if pieces > 1:
-        local.append(swap(qkv_weight, "fsdp", 1))
+        local.append(swap(ordered("core", qkv_weight, known), "fsdp", 1))
         known["core"] = local[-1]
     (partial,) = call(
         functools.partial(own_kernel, len(local)),
@@ -370,10 +374,11 @@
         for number, (start, rows) in enumerate(spans):
             tag = str(number)
             side = seq_index // (1 << number) % 2
-            cut = lax.dynamic_slice(
-                ordered("c" + tag, qkv_weight, known), (start + side * rows, WIDTH), (rows, 2 * WIDTH)
-            )
-            known["c" + tag] = cut
+            if number:
+                known["c" + tag] = lax.dynamic_slice(
+                    ordered("c" + tag, qkv_weight, known), (start + side * rows, WIDTH), (rows, 2 * WIDTH)
+                )
+            cut = known["c" + tag]
             direct = swap(cut, "fsdp", bit)
             known["x" + tag] = direct
             across = swap(ordered("f" + tag, direct, known), "fsdp", 1)

time: 40.9 us -> 40.9 us (level)
    dynamic_slice x0 -> x1, local copies, waits for them, and re-layouts: none -> 1.12 us  [body(): lax.dynamic_slice(qkv_weight, (start + seq_index % 2 * rows, WIDTH), (row...]
    dynamic_slice x2 -> x1, local copies, waits for them, and re-layouts: 2.67 us -> 1.56 us  [body(): lax.dynamic_slice(ordered('c' + tag, qkv_weight, known), (start + side *...]
  transfers between devices with their start and end apart: 15 -> 15, of which waited for: 4 -> 4; matrix products, arithmetic and copies ran while one was open for 16% -> 13% of each run, Pallas kernels for 28% -> 28%
where the time goes in v7:
time: 40.9 us; the launch traced here: 40.6 us
  starting transfers between devices  14 us (34%)
  Pallas kernels  11.9 us (29%)
  local copies, waits for them, and re-layouts  7.72 us (19%)
  blocking collectives  4.58 us (11%)
  waiting for transfers between devices  2.19 us (5%)
    pallas_call x6, Pallas kernels, call(): pl.pallas_call(kernel, in_specs=[scalar_spec] + [whole] * len(args), out_...  11.3 us
    ppermute x12, starting transfers between devices, swap(): return lax.ppermute(value, axis, [(i, i ^ bit) for i in range(count)])  10.5 us
    all_to_all x1, blocking collectives, body(): lax.all_to_all(slots_out, 'fsdp', 0, 0, axis_index_groups=[[i, i + 1] for...  4.58 us
    ppermute x3, starting transfers between devices, body(): lax.ppermute(pack, 'seq', partners(seq_size, place, step))  3.55 us
    slice x1, local copies, waits for them, and re-layouts, body(): cut = ordered('cQ', qkv_weight, known)[:, :WIDTH]  1.87 us
    slice x1, local copies, waits for them, and re-layouts, body(): cut = ordered('cD', qkv_weight, known)[direct_from:, WIDTH:]  1.66 us
    ppermute x12, waiting for transfers between devices, swap(): return lax.ppermute(value, axis, [(i, i ^ bit) for i in range(count)])  1.56 us
    dynamic_slice x1, local copies, waits for them, and re-layouts, body(): lax.dynamic_slice(ordered('c' + tag, qkv_weight, known), (start + side *...  1.56 us
  transfers between devices with their start and end apart: 15, of which 4 were waited for; matrix products, arithmetic and copies ran while one was open for 13% of the time, Pallas kernels for 28%

profile of v7, /device:TPU:0, one launch (start us, length us, event | category | flops | bytes accessed | tf_op | source)
XLA Modules:
  0.0 40.6 jit_solution(2030983236721867505)
XLA Ops:
  0.0 1.1 %constant_dynamic-slice_fusion.1 = bf16[128,1024]{1,0:T(8,128)(2,1)S(1)} fusion(bf16[512,1536]{1,0:T(8,128)(2,1)} %refs_0_.1, s32[]{:T(128)S(6)} %select_n.72), kind=kLoop, calls=%fused_computation.7 | loop fusion | bytes 524292 | tf_op jit(solution)/shard_map/dynamic_slice | solution.py:360
  1.1 0.5 %collective-permute-start = (bf16[512,1536]{1,0:T(8,128)(2,1)}, bf16[512,1536]{1,0:T(8,128)(2,1)}, u32[]{:S(2)}, u32[]{:S(2)}) collective-permute-start(bf16[512,1536]{1,0:T(8,128)(2,1)} %refs_0_.1), channel_id=1, source_target_pairs={{0,1},{1,0},{2,3},{3,2},{4,5},{5,4},{6,7},{7,6},{8,9},{9,8},{10,11... | collective-permute-start | bytes 4718600 | tf_op jit(solution)/shard_map/ppermute | solution.py:55
  1.7 2.6 %collective-permute-start.2 = (bf16[128,1024]{1,0:T(8,128)(2,1)S(1)}, bf16[128,1024]{1,0:T(8,128)(2,1)S(1)}, u32[]{:S(2)}, u32[]{:S(2)}) collective-permute-start(bf16[128,1024]{1,0:T(8,128)(2,1)S(1)} %constant_dynamic-slice_fusion.1), channel_id=1, source_target_pairs={{0,2},{1,3},{2,0},{3,1},{4,6},{5,7},{6,4},{7,5},{8,10},{9,11},{10,... | collective-permute-start | bytes 786440 | tf_op jit(solution)/shard_map/ppermute | solution.py:55
  4.2 1.6 %constant_dynamic-slice_fusion = bf16[64,1024]{1,0:T(8,128)(2,1)} fusion(bf16[512,1536]{1,0:T(8,128)(2,1)} %refs_0_.1, s32[]{:T(128)S(6)} %select_n.73), kind=kLoop, calls=%fused_computation.6 | loop fusion | bytes 262148 | tf_op jit(solution)/shard_map/dynamic_slice | solution.py:378
  5.9 1.7 %slice.6 = bf16[128,1024]{1,0:T(8,128)(2,1)} slice(bf16[512,1536]{1,0:T(8,128)(2,1)} %refs_0_.1), slice={[384:512], [512:1536]} | slice | bytes 524288 | tf_op jit(solution)/shard_map/slice | solution.py:392
  7.5 2.0 %collective-permute-start.6 = (bf16[128,1024]{1,0:T(8,128)(2,1)}, bf16[128,1024]{1,0:T(8,128)(2,1)S(1)}, u32[]{:S(2)}, u32[]{:S(2)}) collective-permute-start(bf16[128,1024]{1,0:T(8,128)(2,1)} %slice.6), channel_id=1, source_target_pairs={{0,2},{1,3},{2,0},{3,1},{4,6},{5,7},{6,4},{7,5},{8,10},{9,11},{10,... | collective-permute-start | bytes 786440 | tf_op jit(solution)/shard_map/ppermute | solution.py:55
  9.5 1.9 %slice.7 = bf16[512,512]{1,0:T(8,128)(2,1)} slice(bf16[512,1536]{1,0:T(8,128)(2,1)} %refs_0_.1), slice={[0:512], [0:512]} | slice | bytes 1048576 | tf_op jit(solution)/shard_map/slice | solution.py:399
  11.4 2.0 %collective-permute-start.3 = (bf16[128,1024]{1,0:T(8,128)(2,1)S(1)}, bf16[128,1024]{1,0:T(8,128)(2,1)S(1)}, u32[]{:S(2)}, u32[]{:S(2)}) collective-permute-start(bf16[128,1024]{1,0:T(8,128)(2,1)S(1)} %collective-permute-done.2.refs_0_), channel_id=1, source_target_pairs={{0,4},{4,0},{8,12},{12,8},{16,20},{20,16},{24,28},{28,24},{1,5},{5... | collective-permute-start | bytes 786440 | tf_op jit(solution)/shard_map/ppermute | solution.py:55
  13.5 0.7 %collective-permute-done.4.refs_2_ = bf16[64,1024]{1,0:T(8,128)(2,1)S(1)} collective-permute-done((bf16[64,1024]{1,0:T(8,128)(2,1)}, bf16[64,1024]{1,0:T(8,128)(2,1)S(1)}, u32[]{:S(2)}, u32[]{:S(2)}) %collective-permute-start.4) | collective-permute-done | bytes 131104 | tf_op jit(solution)/shard_map/ppermute | solution.py:55
  14.2 2.0 %collective-permute-start.5 = (bf16[64,1024]{1,0:T(8,128)(2,1)S(1)}, bf16[64,1024]{1,0:T(8,128)(2,1)}, u32[]{:S(2)}, u32[]{:S(2)}) collective-permute-start(bf16[64,1024]{1,0:T(8,128)(2,1)S(1)} %collective-permute-done.4.refs_2_), channel_id=1, source_target_pairs={{0,8},{4,12},{8,0},{12,4},{16,24},{20,28},{24,16},{28,20},{1,9},{5... | collective-permute-start | bytes 393224 | tf_op jit(solution)/shard_map/ppermute | solution.py:55
  16.5 1.4 %copy-done.1 = bf16[512,1536]{1,0:T(8,128)(2,1)S(1)} copy-done((bf16[512,1536]{1,0:T(8,128)(2,1)S(1)}, bf16[512,1536]{1,0:T(8,128)(2,1)}, u32[]{:S(2)}) %copy-start.1) | copy-done | bytes 1572888
  17.9 3.2 %project_own.1.partial = f32[512,1536]{1,0:T(8,128)S(1)} custom-call(s32[25]{0:T(128)S(1)} %concatenate.3.meta, bf16[512,2048]{1,0:T(8,128)(2,1)S(1)} %bitcast.13, bf16[512,1536]{1,0:T(8,128)(2,1)S(1)} %copy-done.1, bf16[512,1536]{1,0:T(8,128)(2,1)} %collective-permute-done.refs_1_), custom_call_target="tpu_custom_call" | custom-call | flops 3680000 | bytes 1000 | tf_op jit(solution)/shard_map/project_own/pallas_call | solution.py:344
  21.1 0.6 %collective-permute-start.7 = (bf16[128,1024]{1,0:T(8,128)(2,1)S(1)}, bf16[128,1024]{1,0:T(8,128)(2,1)S(1)}, u32[]{:S(2)}, u32[]{:S(2)}) collective-permute-start(bf16[128,1024]{1,0:T(8,128)(2,1)S(1)} %collective-permute-done.2.refs_0_), channel_id=1, source_target_pairs={{0,1},{1,0},{2,3},{3,2},{4,5},{5,4},{6,7},{7,6},{8,9},{9,8},{10,11... | collective-permute-start | bytes 786440 | tf_op jit(solution)/shard_map/ppermute | solution.py:55
  22.3 1.3 %project_first.1 = (f32[128,1024]{1,0:T(8,128)S(1)}, bf16[512,1024]{1,0:T(8,128)(2,1)S(1)}) custom-call(s32[25]{0:T(128)S(1)} %concatenate.3.meta, bf16[512,2048]{1,0:T(8,128)(2,1)S(1)} %bitcast.14, f32[512,1536]{1,0:T(8,128)S(1)} %project_own.1.partial, bf16[128,1024]{1,0:T(8,128)(2,1)S(1)} %collective-permute-done.2.refs_0_, ...), custom_call_target="tpu_custom_call" | custom-call | flops 689999 | bytes 1000 | tf_op jit(solution)/shard_map/project_first/pallas_call | solution.py:344
  24.0 1.0 %project_pack.1 = (bf16[128,1024]{1,0:T(8,128)(2,1)S(1)}, bf16[512,1024]{1,0:T(8,128)(2,1)S(1)}) custom-call(s32[25]{0:T(128)S(1)} %concatenate.3.meta, bf16[512,2048]{1,0:T(8,128)(2,1)S(1)} %bitcast.15, f32[128,1024]{1,0:T(8,128)S(1)} %get-tuple-element.26.refs_0_, bf16[128,1024]{1,0:T(8,128)(2,1)S(1)} %collective-permute-done.7.refs_1_, ...), custom_call_target="tpu_custom_call" | custom-call | flops 689999 | bytes 1000 | tf_op jit(solution)/shard_map/project_pack/pallas_call | solution.py:344
  24.9 1.6 %collective-permute-start.12 = (bf16[128,1024]{1,0:T(8,128)(2,1)S(1)}, bf16[128,1024]{1,0:T(8,128)(2,1)S(1)}, u32[]{:S(2)}, u32[]{:S(2)}) collective-permute-start(bf16[128,1024]{1,0:T(8,128)(2,1)S(1)} %get-tuple-element.27), channel_id=1, source_target_pairs={{0,12},{4,8},{8,4},{12,0},{16,28},{20,24},{24,20},{28,16},{1,13},{... | collective-permute-start | bytes 786440 | tf_op jit(solution)/shard_map/ppermute | solution.py:437
  26.5 1.5 %collective-permute-start.13 = (bf16[128,1024]{1,0:T(8,128)(2,1)S(1)}, bf16[128,1024]{1,0:T(8,128)(2,1)S(1)}, u32[]{:S(2)}, u32[]{:S(2)}) collective-permute-start(bf16[128,1024]{1,0:T(8,128)(2,1)S(1)} %get-tuple-element.27), channel_id=1, source_target_pairs={{0,8},{4,12},{8,0},{12,4},{16,24},{20,28},{24,16},{28,20},{1,9},{5... | collective-permute-start | bytes 786440 | tf_op jit(solution)/shard_map/ppermute | solution.py:437
  28.0 0.5 %collective-permute-start.14 = (bf16[128,1024]{1,0:T(8,128)(2,1)S(1)}, bf16[128,1024]{1,0:T(8,128)(2,1)S(1)}, u32[]{:S(2)}, u32[]{:S(2)}) collective-permute-start(bf16[128,1024]{1,0:T(8,128)(2,1)S(1)} %get-tuple-element.27), channel_id=1, source_target_pairs={{0,4},{4,0},{8,12},{12,8},{16,20},{20,16},{24,28},{28,24},{1,5},{5... | collective-permute-start | bytes 786440 | tf_op jit(solution)/shard_map/ppermute | solution.py:437
  28.5 1.8 %project_kv.1.refs_2_ = bf16[512,1024]{1,0:T(8,128)(2,1)S(1)} custom-call(s32[25]{0:T(128)S(1)} %concatenate.3.meta, bf16[512,2048]{1,0:T(8,128)(2,1)S(1)} %bitcast.16, f32[512,1536]{1,0:T(8,128)S(1)} %project_own.1.partial, bf16[512,1024]{1,0:T(8,128)(2,1)S(1)} %get-tuple-element.29.refs_0_, bf16[512,1024]{1,0:T(8,128)(2,1)S(1)} %get-tuple-element.30.refs_1_), custom_call_target="tpu_custom_call" | custom-call | flops 2990000 | bytes 1000 | tf_op jit(solution)/shard_map/project_kv/pallas_call | solution.py:344
  30.8 0.6 %slot_queries.1 = bf16[2,512,512]{2,1,0:T(8,128)(2,1)S(1)} custom-call(s32[25]{0:T(128)S(1)} %concatenate.3.meta, bf16[512,512]{1,0:T(8,128)(2,1)S(1)} %collective-permute-done.1.source.refs_0_), custom_call_target="tpu_custom_call" | custom-call | flops 575000 | bytes 1000 | tf_op jit(solution)/shard_map/slot_queries/pallas_call | solution.py:344
  31.4 4.6 %all_to_all.5.refs_1_ = bf16[2,512,512]{2,1,0:T(8,128)(2,1)S(1)} all-to-all(bf16[2,512,512]{2,1,0:T(8,128)(2,1)S(1)} %slot_queries.1), channel_id=1, replica_groups={{0,1},{2,3},{4,5},{6,7},{8,9},{10,11},{12,13},{14,15},{16,17},{18,19},{..., dimensions={0} | all-to-all | bytes 2097152 | tf_op jit(solution)/shard_map/all_to_all | solution.py:447
  36.0 3.4 %attend_local.1 = (bf16[512,512]{1,0:T(8,128)(2,1)}, bf16[128,512]{1,0:T(8,128)(2,1)S(1)}, f32[128,512]{1,0:T(8,128)S(1)}, f32[128,512]{1,0:T(8,128)S(1)}, f32[128,512]{1,0:T(8,128)S(1)}) custom-call(s32[25]{0:T(128)S(1)} %concatenate.3.meta, bf16[512,2048]{1,0:T(8,128)(2,1)S(1)} %bitcast.17, f32[512,1536]{1,0:T(8,128)S(1)} %project_own.1.partial, ...), custom_call_target="tpu_custom_call" | custom-call | flops 6325000 | bytes 1000 | tf_op jit(solution)/shard_map/attend_local/pallas_call | solution.py:344
  39.4 0.6 %collective-permute-done.13.refs_5_ = bf16[128,1024]{1,0:T(8,128)(2,1)S(1)} collective-permute-done((bf16[128,1024]{1,0:T(8,128)(2,1)S(1)}, bf16[128,1024]{1,0:T(8,128)(2,1)S(1)}, u32[]{:S(2)}, u32[]{:S(2)}) %collective-permute-start.13) | collective-permute-done | bytes 262176 | tf_op jit(solution)/shard_map/ppermute | solution.py:437
  40.0 0.6 %merge_near.1 = bf16[512,512]{1,0:T(8,128)(2,1)} custom-call(s32[25]{0:T(128)S(1)} %concatenate.3.meta, bf16[128,512]{1,0:T(8,128)(2,1)S(1)} %get-tuple-element.32.refs_0_, f32[128,512]{1,0:T(8,128)S(1)} %get-tuple-element.33.refs_1_, f32[128,512]{1,0:T(8,128)S(1)} %get-tuple-element.34.refs_2_, ...), custom_call_target="tpu_custom_call", output_to_operand_aliasing={{}: (8, {})} | custom-call | flops 2990000 | bytes 1000 | tf_op jit(solution)/shard_map/merge_near/pallas_call | solution.py:461
  (29 shorter events, 1.8 us)
Async XLA Ops:
  0.0 13.4 %copy-start.3 = (s32[4]{0:T(128)S(1)}, s32[4]{0:T(128)}, u32[]{:S(2)}) copy-start(s32[4]{0:T(128)} %param.7) | copy-start | bytes 52
  0.0 16.3 %copy-start.2 = (s32[4]{0:T(128)S(1)}, s32[4]{0:T(128)}, u32[]{:S(2)}) copy-start(s32[4]{0:T(128)} %param.6) | copy-start | bytes 52
  0.0 16.5 %copy-start = (bf16[1,512,2048]{2,1,0:T(8,128)(2,1)S(1)}, bf16[1,512,2048]{2,1,0:T(8,128)(2,1)}, u32[]{:S(2)}) copy-start(bf16[1,512,2048]{2,1,0:T(8,128)(2,1)} %param.4) | copy-start | bytes 6291460
  1.1 15.2 %collective-permute-start = (bf16[512,1536]{1,0:T(8,128)(2,1)}, bf16[512,1536]{1,0:T(8,128)(2,1)}, u32[]{:S(2)}, u32[]{:S(2)}) collective-permute-start(bf16[512,1536]{1,0:T(8,128)(2,1)} %refs_0_.1), channel_id=1, source_target_pairs={{0,1},{1,0},{2,3},{3,2},{4,5},{5,4},{6,7},{7,6},{8,9},{9,8},{10,11... | collective-permute-start | bytes 4718600 | tf_op jit(solution)/shard_map/ppermute | solution.py:55
  1.7 9.8 %collective-permute-start.2 = (bf16[128,1024]{1,0:T(8,128)(2,1)S(1)}, bf16[128,1024]{1,0:T(8,128)(2,1)S(1)}, u32[]{:S(2)}, u32[]{:S(2)}) collective-permute-start(bf16[128,1024]{1,0:T(8,128)(2,1)S(1)} %constant_dynamic-slice_fusion.1), channel_id=1, source_target_pairs={{0,2},{1,3},{2,0},{3,1},{4,6},{5,7},{6,4},{7,5},{8,10},{9,11},{10,... | collective-permute-start | bytes 786440 | tf_op jit(solution)/shard_map/ppermute | solution.py:55
  5.8 8.4 %collective-permute-start.4 = (bf16[64,1024]{1,0:T(8,128)(2,1)}, bf16[64,1024]{1,0:T(8,128)(2,1)S(1)}, u32[]{:S(2)}, u32[]{:S(2)}) collective-permute-start(bf16[64,1024]{1,0:T(8,128)(2,1)} %constant_dynamic-slice_fusion), channel_id=1, source_target_pairs={{0,2},{1,3},{2,0},{3,1},{4,6},{5,7},{6,4},{7,5},{8,10},{9,11},{10,... | collective-permute-start | bytes 393224 | tf_op jit(solution)/shard_map/ppermute | solution.py:55
  7.5 13.6 %collective-permute-start.6 = (bf16[128,1024]{1,0:T(8,128)(2,1)}, bf16[128,1024]{1,0:T(8,128)(2,1)S(1)}, u32[]{:S(2)}, u32[]{:S(2)}) collective-permute-start(bf16[128,1024]{1,0:T(8,128)(2,1)} %slice.6), channel_id=1, source_target_pairs={{0,2},{1,3},{2,0},{3,1},{4,6},{5,7},{6,4},{7,5},{8,10},{9,11},{10,... | collective-permute-start | bytes 786440 | tf_op jit(solution)/shard_map/ppermute | solution.py:55
  11.4 19.4 %collective-permute-start.1 = (bf16[512,512]{1,0:T(8,128)(2,1)}, bf16[512,512]{1,0:T(8,128)(2,1)S(1)}, u32[]{:S(2)}, u32[]{:S(2)}) collective-permute-start(bf16[512,512]{1,0:T(8,128)(2,1)} %slice.7), channel_id=1, source_target_pairs={{0,2},{1,3},{2,0},{3,1},{4,6},{5,7},{6,4},{7,5},{8,10},{9,11},{10,... | collective-permute-start | bytes 1572872 | tf_op jit(solution)/shard_map/ppermute | solution.py:55
  11.4 10.2 %collective-permute-start.3 = (bf16[128,1024]{1,0:T(8,128)(2,1)S(1)}, bf16[128,1024]{1,0:T(8,128)(2,1)S(1)}, u32[]{:S(2)}, u32[]{:S(2)}) collective-permute-start(bf16[128,1024]{1,0:T(8,128)(2,1)S(1)} %collective-permute-done.2.refs_0_), channel_id=1, source_target_pairs={{0,4},{4,0},{8,12},{12,8},{16,20},{20,16},{24,28},{28,24},{1,5},{5... | collective-permute-start | bytes 786440 | tf_op jit(solution)/shard_map/ppermute | solution.py:55
  14.2 7.5 %collective-permute-start.5 = (bf16[64,1024]{1,0:T(8,128)(2,1)S(1)}, bf16[64,1024]{1,0:T(8,128)(2,1)}, u32[]{:S(2)}, u32[]{:S(2)}) collective-permute-start(bf16[64,1024]{1,0:T(8,128)(2,1)S(1)} %collective-permute-done.4.refs_2_), channel_id=1, source_target_pairs={{0,8},{4,12},{8,0},{12,4},{16,24},{20,28},{24,16},{28,20},{1,9},{5... | collective-permute-start | bytes 393224 | tf_op jit(solution)/shard_map/ppermute | solution.py:55
  16.4 5.8 %collective-permute-start.9 = (bf16[64,1024]{1,0:T(8,128)(2,1)S(1)}, bf16[64,1024]{1,0:T(8,128)(2,1)S(1)}, u32[]{:S(2)}, u32[]{:S(2)}) collective-permute-start(bf16[64,1024]{1,0:T(8,128)(2,1)S(1)} %collective-permute-done.4.refs_2_), channel_id=1, source_target_pairs={{0,1},{1,0},{2,3},{3,2},{4,5},{5,4},{6,7},{7,6},{8,9},{9,8},{10,11... | collective-permute-start | bytes 393224 | tf_op jit(solution)/shard_map/ppermute | solution.py:55
  16.5 1.4 %copy-start.1 = (bf16[512,1536]{1,0:T(8,128)(2,1)S(1)}, bf16[512,1536]{1,0:T(8,128)(2,1)}, u32[]{:S(2)}) copy-start(bf16[512,1536]{1,0:T(8,128)(2,1)} %refs_0_.1) | copy-start | bytes 4718596
  21.1 2.5 %collective-permute-start.7 = (bf16[128,1024]{1,0:T(8,128)(2,1)S(1)}, bf16[128,1024]{1,0:T(8,128)(2,1)S(1)}, u32[]{:S(2)}, u32[]{:S(2)}) collective-permute-start(bf16[128,1024]{1,0:T(8,128)(2,1)S(1)} %collective-permute-done.2.refs_0_), channel_id=1, source_target_pairs={{0,1},{1,0},{2,3},{3,2},{4,5},{5,4},{6,7},{7,6},{8,9},{9,8},{10,11... | collective-permute-start | bytes 786440 | tf_op jit(solution)/shard_map/ppermute | solution.py:55
  21.7 1.9 %collective-permute-start.11 = (bf16[128,1024]{1,0:T(8,128)(2,1)S(1)}, bf16[128,1024]{1,0:T(8,128)(2,1)S(1)}, u32[]{:S(2)}, u32[]{:S(2)}) collective-permute-start(bf16[128,1024]{1,0:T(8,128)(2,1)S(1)} %collective-permute-done.6.refs_4_), channel_id=1, source_target_pairs={{0,1},{1,0},{2,3},{3,2},{4,5},{5,4},{6,7},{7,6},{8,9},{9,8},{10,11... | collective-permute-start | bytes 786440 | tf_op jit(solution)/shard_map/ppermute | solution.py:55
  21.8 2.2 %collective-permute-start.8 = (bf16[128,1024]{1,0:T(8,128)(2,1)S(1)}, bf16[128,1024]{1,0:T(8,128)(2,1)S(1)}, u32[]{:S(2)}, u32[]{:S(2)}) collective-permute-start(bf16[128,1024]{1,0:T(8,128)(2,1)S(1)} %collective-permute-done.3.refs_1_), channel_id=1, source_target_pairs={{0,1},{1,0},{2,3},{3,2},{4,5},{5,4},{6,7},{7,6},{8,9},{9,8},{10,11... | collective-permute-start | bytes 786440 | tf_op jit(solution)/shard_map/ppermute | solution.py:55
  22.2 1.8 %collective-permute-start.10 = (bf16[64,1024]{1,0:T(8,128)(2,1)}, bf16[64,1024]{1,0:T(8,128)(2,1)S(1)}, u32[]{:S(2)}, u32[]{:S(2)}) collective-permute-start(bf16[64,1024]{1,0:T(8,128)(2,1)} %collective-permute-done.5.refs_3_), channel_id=1, source_target_pairs={{0,1},{1,0},{2,3},{3,2},{4,5},{5,4},{6,7},{7,6},{8,9},{9,8},{10,11... | collective-permute-start | bytes 393224 | tf_op jit(solution)/shard_map/ppermute | solution.py:55
  24.9 14.4 %collective-permute-start.12 = (bf16[128,1024]{1,0:T(8,128)(2,1)S(1)}, bf16[128,1024]{1,0:T(8,128)(2,1)S(1)}, u32[]{:S(2)}, u32[]{:S(2)}) collective-permute-start(bf16[128,1024]{1,0:T(8,128)(2,1)S(1)} %get-tuple-element.27), channel_id=1, source_target_pairs={{0,12},{4,8},{8,4},{12,0},{16,28},{20,24},{24,20},{28,16},{1,13},{... | collective-permute-start | bytes 786440 | tf_op jit(solution)/shard_map/ppermute | solution.py:437
  26.5 13.5 %collective-permute-start.13 = (bf16[128,1024]{1,0:T(8,128)(2,1)S(1)}, bf16[128,1024]{1,0:T(8,128)(2,1)S(1)}, u32[]{:S(2)}, u32[]{:S(2)}) collective-permute-start(bf16[128,1024]{1,0:T(8,128)(2,1)S(1)} %get-tuple-element.27), channel_id=1, source_target_pairs={{0,8},{4,12},{8,0},{12,4},{16,24},{20,28},{24,16},{28,20},{1,9},{5... | collective-permute-start | bytes 786440 | tf_op jit(solution)/shard_map/ppermute | solution.py:437
  28.0 12.0 %collective-permute-start.14 = (bf16[128,1024]{1,0:T(8,128)(2,1)S(1)}, bf16[128,1024]{1,0:T(8,128)(2,1)S(1)}, u32[]{:S(2)}, u32[]{:S(2)}) collective-permute-start(bf16[128,1024]{1,0:T(8,128)(2,1)S(1)} %get-tuple-element.27), channel_id=1, source_target_pairs={{0,4},{4,0},{8,12},{12,8},{16,20},{20,16},{24,28},{28,24},{1,5},{5... | collective-permute-start | bytes 786440 | tf_op jit(solution)/shard_map/ppermute | solution.py:437

commit v8 on v1

--- a/solution.py
+++ b/solution.py
@@ -18,17 +18,25 @@
 SCALE2 = HEAD_DIM ** (-0.5) * math.log2(math.e)
 VMEM_LIMIT = 24 * 1024 * 1024
 
-MODEL_FLOPS = {"project_first": 689999, "slot_queries": 575000, "project_pack": 689999, "project_own": 3680000, "project_mid": 1610000, "project_kv": 2990000, "attend_local": 6325000, "merge_near": 2990000}
+MODEL_FLOPS = {
+    "slot_queries": 575000,
+    "project_first": 689999,
+    "project_pack": 689999,
+    "project_own": 3680000,
+    "project_kv": 2990000,
+    "attend_local": 6325000,
+    "merge_near": 2990000,
+}
 ORDER = {
-    'c1': ('c0',),
-    'cD': ('c1',),
-    'cQ': ('cD',),
-    'p0': ('partial', 'xD'),
-    'p1': ('partial',),
-    'q': ('kv',),
-    'kv': ('pack',),
+    "c1": ("c0",),
+    "cD": ("c1",),
+    "cQ": ("cD",),
+    "p0": ("partial", "xD"),
+    "p1": ("partial",),
+    "q": ("kv",),
+    "kv": ("pack",),
 }
-NEAR_ORDER = (3, 2, 1)
+NEAR_ORDER = (2, 3, 1)
 F32 = jnp.float32
 BF16 = jnp.bfloat16
 
@@ -69,10 +77,6 @@
 
 def qk(query, key):
     return lax.dot_general(query, key, (((1,), (1,)), ((), ())), preferred_element_type=F32)
-
-
-def pv(weights, value):
-    return jnp.dot(weights.astype(BF16), value, preferred_element_type=F32)
 
 
 def add_up(tokens, places, weights):
@@ -318,8 +322,6 @@
     scalars = list(full_places)
     place_at = len(scalars)
     scalars += [near_position, far_position]
-    base_at = len(scalars)
-    scalars += [(mine ^ bit) // 2 * 2 * share for bit in range(2, pieces, 2)]
     core_at = len(scalars)
     scalars.append(mine % 2)
     slot_at = len(scalars)
@@ -383,7 +385,6 @@
             mine_rows += [direct, passed]
             other_rows += [across, swap(passed, "fsdp", 1)]
             known["q" + tag] = other_rows[-1]
-        known["meta"] = meta
         cut = ordered("cD", qkv_weight, known)[direct_from:, WIDTH:]
         known["cD"] = cut
         rest = swap(cut, "fsdp", bit)

time: 40.9 us -> 42.3 us (1.034)
  waiting for transfers between devices: 2.1 us -> 3.55 us
    ppermute x3, waiting for transfers between devices: 0.72 us -> 2.14 us  [body(): lax.ppermute(pack, 'seq', partners(seq_size, place, step))]
  transfers between devices with their start and end apart: 15 -> 15, of which waited for: 4 -> 5; matrix products, arithmetic and copies ran while one was open for 16% -> 15% of each run, Pallas kernels for 28% -> 27%
where the time goes in v8:
time: 42.3 us; the launch traced here: 42 us
  starting transfers between devices  14.1 us (33%)
  Pallas kernels  11.8 us (28%)
  local copies, waits for them, and re-layouts  7.7 us (18%)
  blocking collectives  4.58 us (11%)
  waiting for transfers between devices  3.55 us (8%)
    pallas_call x6, Pallas kernels, call(): pl.pallas_call(kernel, in_specs=[scalar_spec] + [whole] * len(args), out_...  11.3 us
    ppermute x12, starting transfers between devices, swap(): return lax.ppermute(value, axis, [(i, i ^ bit) for i in range(count)])  10.6 us
    all_to_all x1, blocking collectives, body(): lax.all_to_all(slots_out, 'fsdp', 0, 0, axis_index_groups=[[i, i + 1] for...  4.58 us
    ppermute x3, starting transfers between devices, body(): lax.ppermute(pack, 'seq', partners(seq_size, place, step))  3.55 us
    dynamic_slice x2, local copies, waits for them, and re-layouts, body(): lax.dynamic_slice(ordered('c' + tag, qkv_weight, known), (start + side *...  2.67 us
    ppermute x3, waiting for transfers between devices, body(): lax.ppermute(pack, 'seq', partners(seq_size, place, step))  2.14 us
    slice x1, local copies, waits for them, and re-layouts, body(): cut = ordered('cQ', qkv_weight, known)[:, :WIDTH]  1.87 us
    slice x1, local copies, waits for them, and re-layouts, body(): cut = ordered('cD', qkv_weight, known)[direct_from:, WIDTH:]  1.66 us
  transfers between devices with their start and end apart: 15, of which 5 were waited for; matrix products, arithmetic and copies ran while one was open for 15% of the time, Pallas kernels for 27%

profile of v8, /device:TPU:0, one launch (start us, length us, event | category | flops | bytes accessed | tf_op | source)
XLA Modules:
  0.0 42.0 jit_solution(2687276187952337945)
XLA Ops:
  0.0 0.5 %collective-permute-start = (bf16[512,1536]{1,0:T(8,128)(2,1)}, bf16[512,1536]{1,0:T(8,128)(2,1)}, u32[]{:S(2)}, u32[]{:S(2)}) collective-permute-start(bf16[512,1536]{1,0:T(8,128)(2,1)} %refs_0_.1), channel_id=1, source_target_pairs={{0,1},{1,0},{2,3},{3,2},{4,5},{5,4},{6,7},{7,6},{8,9},{9,8},{10,11... | collective-permute-start | bytes 4718600 | tf_op jit(solution)/shard_map/ppermute | solution.py:62
  0.5 1.1 %constant_dynamic-slice_fusion.1 = bf16[128,1024]{1,0:T(8,128)(2,1)S(1)} fusion(bf16[512,1536]{1,0:T(8,128)(2,1)} %refs_0_.1, s32[]{:T(128)S(6)} %select_n.69), kind=kLoop, calls=%fused_computation.7 | loop fusion | bytes 524292 | tf_op jit(solution)/shard_map/dynamic_slice | solution.py:375
  1.6 2.6 %collective-permute-start.2 = (bf16[128,1024]{1,0:T(8,128)(2,1)S(1)}, bf16[128,1024]{1,0:T(8,128)(2,1)S(1)}, u32[]{:S(2)}, u32[]{:S(2)}) collective-permute-start(bf16[128,1024]{1,0:T(8,128)(2,1)S(1)} %constant_dynamic-slice_fusion.1), channel_id=1, source_target_pairs={{0,2},{1,3},{2,0},{3,1},{4,6},{5,7},{6,4},{7,5},{8,10},{9,11},{10,... | collective-permute-start | bytes 786440 | tf_op jit(solution)/shard_map/ppermute | solution.py:62
  4.2 1.6 %constant_dynamic-slice_fusion = bf16[64,1024]{1,0:T(8,128)(2,1)} fusion(bf16[512,1536]{1,0:T(8,128)(2,1)} %refs_0_.1, s32[]{:T(128)S(6)} %select_n.70), kind=kLoop, calls=%fused_computation.6 | loop fusion | bytes 262148 | tf_op jit(solution)/shard_map/dynamic_slice | solution.py:375
  5.8 1.7 %slice.6 = bf16[128,1024]{1,0:T(8,128)(2,1)} slice(bf16[512,1536]{1,0:T(8,128)(2,1)} %refs_0_.1), slice={[384:512], [512:1536]} | slice | bytes 524288 | tf_op jit(solution)/shard_map/slice | solution.py:388
  7.5 2.0 %collective-permute-start.6 = (bf16[128,1024]{1,0:T(8,128)(2,1)}, bf16[128,1024]{1,0:T(8,128)(2,1)S(1)}, u32[]{:S(2)}, u32[]{:S(2)}) collective-permute-start(bf16[128,1024]{1,0:T(8,128)(2,1)} %slice.6), channel_id=1, source_target_pairs={{0,2},{1,3},{2,0},{3,1},{4,6},{5,7},{6,4},{7,5},{8,10},{9,11},{10,... | collective-permute-start | bytes 786440 | tf_op jit(solution)/shard_map/ppermute | solution.py:62
  9.5 1.9 %slice.7 = bf16[512,512]{1,0:T(8,128)(2,1)} slice(bf16[512,1536]{1,0:T(8,128)(2,1)} %refs_0_.1), slice={[0:512], [0:512]} | slice | bytes 1048576 | tf_op jit(solution)/shard_map/slice | solution.py:395
  11.4 2.0 %collective-permute-start.3 = (bf16[128,1024]{1,0:T(8,128)(2,1)S(1)}, bf16[128,1024]{1,0:T(8,128)(2,1)S(1)}, u32[]{:S(2)}, u32[]{:S(2)}) collective-permute-start(bf16[128,1024]{1,0:T(8,128)(2,1)S(1)} %collective-permute-done.2.refs_0_), channel_id=1, source_target_pairs={{0,4},{4,0},{8,12},{12,8},{16,20},{20,16},{24,28},{28,24},{1,5},{5... | collective-permute-start | bytes 786440 | tf_op jit(solution)/shard_map/ppermute | solution.py:62
  13.5 0.6 %collective-permute-done.4.refs_2_ = bf16[64,1024]{1,0:T(8,128)(2,1)S(1)} collective-permute-done((bf16[64,1024]{1,0:T(8,128)(2,1)}, bf16[64,1024]{1,0:T(8,128)(2,1)S(1)}, u32[]{:S(2)}, u32[]{:S(2)}) %collective-permute-start.4) | collective-permute-done | bytes 131104 | tf_op jit(solution)/shard_map/ppermute | solution.py:62
  14.1 2.1 %collective-permute-start.5 = (bf16[64,1024]{1,0:T(8,128)(2,1)S(1)}, bf16[64,1024]{1,0:T(8,128)(2,1)}, u32[]{:S(2)}, u32[]{:S(2)}) collective-permute-start(bf16[64,1024]{1,0:T(8,128)(2,1)S(1)} %collective-permute-done.4.refs_2_), channel_id=1, source_target_pairs={{0,8},{4,12},{8,0},{12,4},{16,24},{20,28},{24,16},{28,20},{1,9},{5... | collective-permute-start | bytes 393224 | tf_op jit(solution)/shard_map/ppermute | solution.py:62
  16.5 1.4 %copy-done.1 = bf16[512,1536]{1,0:T(8,128)(2,1)S(1)} copy-done((bf16[512,1536]{1,0:T(8,128)(2,1)S(1)}, bf16[512,1536]{1,0:T(8,128)(2,1)}, u32[]{:S(2)}) %copy-start.1) | copy-done | bytes 1572888
  17.9 3.2 %project_own.1.partial = f32[512,1536]{1,0:T(8,128)S(1)} custom-call(s32[24]{0:T(128)S(1)} %concatenate.3.meta, bf16[512,2048]{1,0:T(8,128)(2,1)S(1)} %bitcast.12, bf16[512,1536]{1,0:T(8,128)(2,1)S(1)} %copy-done.1, bf16[512,1536]{1,0:T(8,128)(2,1)} %collective-permute-done.refs_1_), custom_call_target="tpu_custom_call" | custom-call | flops 3680000 | bytes 1000 | tf_op jit(solution)/shard_map/project_own/pallas_call | solution.py:345
  21.1 0.6 %collective-permute-start.7 = (bf16[128,1024]{1,0:T(8,128)(2,1)S(1)}, bf16[128,1024]{1,0:T(8,128)(2,1)S(1)}, u32[]{:S(2)}, u32[]{:S(2)}) collective-permute-start(bf16[128,1024]{1,0:T(8,128)(2,1)S(1)} %collective-permute-done.2.refs_0_), channel_id=1, source_target_pairs={{0,1},{1,0},{2,3},{3,2},{4,5},{5,4},{6,7},{7,6},{8,9},{9,8},{10,11... | collective-permute-start | bytes 786440 | tf_op jit(solution)/shard_map/ppermute | solution.py:62
  22.3 1.3 %project_first.1 = (f32[128,1024]{1,0:T(8,128)S(1)}, bf16[512,1024]{1,0:T(8,128)(2,1)S(1)}) custom-call(s32[24]{0:T(128)S(1)} %concatenate.3.meta, bf16[512,2048]{1,0:T(8,128)(2,1)S(1)} %bitcast.13, f32[512,1536]{1,0:T(8,128)S(1)} %project_own.1.partial, bf16[128,1024]{1,0:T(8,128)(2,1)S(1)} %collective-permute-done.2.refs_0_, ...), custom_call_target="tpu_custom_call" | custom-call | flops 689999 | bytes 1000 | tf_op jit(solution)/shard_map/project_first/pallas_call | solution.py:345
  24.0 0.9 %project_pack.1 = (bf16[128,1024]{1,0:T(8,128)(2,1)S(1)}, bf16[512,1024]{1,0:T(8,128)(2,1)S(1)}) custom-call(s32[24]{0:T(128)S(1)} %concatenate.3.meta, bf16[512,2048]{1,0:T(8,128)(2,1)S(1)} %bitcast.14, f32[128,1024]{1,0:T(8,128)S(1)} %get-tuple-element.26.refs_0_, bf16[128,1024]{1,0:T(8,128)(2,1)S(1)} %collective-permute-done.7.refs_1_, ...), custom_call_target="tpu_custom_call" | custom-call | flops 689999 | bytes 1000 | tf_op jit(solution)/shard_map/project_pack/pallas_call | solution.py:345
  25.4 2.6 %collective-permute-start.13 = (bf16[128,1024]{1,0:T(8,128)(2,1)S(1)}, bf16[128,1024]{1,0:T(8,128)(2,1)S(1)}, u32[]{:S(2)}, u32[]{:S(2)}) collective-permute-start(bf16[128,1024]{1,0:T(8,128)(2,1)S(1)} %get-tuple-element.27), channel_id=1, source_target_pairs={{0,12},{4,8},{8,4},{12,0},{16,28},{20,24},{24,20},{28,16},{1,13},{... | collective-permute-start | bytes 786440 | tf_op jit(solution)/shard_map/ppermute | solution.py:433
  28.0 0.5 %collective-permute-start.14 = (bf16[128,1024]{1,0:T(8,128)(2,1)S(1)}, bf16[128,1024]{1,0:T(8,128)(2,1)S(1)}, u32[]{:S(2)}, u32[]{:S(2)}) collective-permute-start(bf16[128,1024]{1,0:T(8,128)(2,1)S(1)} %get-tuple-element.27), channel_id=1, source_target_pairs={{0,4},{4,0},{8,12},{12,8},{16,20},{20,16},{24,28},{28,24},{1,5},{5... | collective-permute-start | bytes 786440 | tf_op jit(solution)/shard_map/ppermute | solution.py:433
  28.5 1.8 %project_kv.1.refs_2_ = bf16[512,1024]{1,0:T(8,128)(2,1)S(1)} custom-call(s32[24]{0:T(128)S(1)} %concatenate.3.meta, bf16[512,2048]{1,0:T(8,128)(2,1)S(1)} %bitcast.15, f32[512,1536]{1,0:T(8,128)S(1)} %project_own.1.partial, bf16[512,1024]{1,0:T(8,128)(2,1)S(1)} %get-tuple-element.29.refs_0_, bf16[512,1024]{1,0:T(8,128)(2,1)S(1)} %get-tuple-element.30.refs_1_), custom_call_target="tpu_custom_call" | custom-call | flops 2990000 | bytes 1000 | tf_op jit(solution)/shard_map/project_kv/pallas_call | solution.py:345
  30.7 0.6 %slot_queries.1 = bf16[2,512,512]{2,1,0:T(8,128)(2,1)S(1)} custom-call(s32[24]{0:T(128)S(1)} %concatenate.3.meta, bf16[512,512]{1,0:T(8,128)(2,1)S(1)} %collective-permute-done.1.source.refs_0_), custom_call_target="tpu_custom_call" | custom-call | flops 575000 | bytes 1000 | tf_op jit(solution)/shard_map/slot_queries/pallas_call | solution.py:345
  31.3 4.6 %all_to_all.5.refs_1_ = bf16[2,512,512]{2,1,0:T(8,128)(2,1)S(1)} all-to-all(bf16[2,512,512]{2,1,0:T(8,128)(2,1)S(1)} %slot_queries.1), channel_id=1, replica_groups={{0,1},{2,3},{4,5},{6,7},{8,9},{10,11},{12,13},{14,15},{16,17},{18,19},{..., dimensions={0} | all-to-all | bytes 2097152 | tf_op jit(solution)/shard_map/all_to_all | solution.py:443
  35.9 3.4 %attend_local.1 = (bf16[512,512]{1,0:T(8,128)(2,1)}, bf16[128,512]{1,0:T(8,128)(2,1)S(1)}, f32[128,512]{1,0:T(8,128)S(1)}, f32[128,512]{1,0:T(8,128)S(1)}, f32[128,512]{1,0:T(8,128)S(1)}) custom-call(s32[24]{0:T(128)S(1)} %concatenate.3.meta, bf16[512,2048]{1,0:T(8,128)(2,1)S(1)} %bitcast.16, f32[512,1536]{1,0:T(8,128)S(1)} %project_own.1.partial, ...), custom_call_target="tpu_custom_call" | custom-call | flops 6325000 | bytes 1000 | tf_op jit(solution)/shard_map/attend_local/pallas_call | solution.py:345
  39.3 0.8 %collective-permute-done.13.refs_5_ = bf16[128,1024]{1,0:T(8,128)(2,1)S(1)} collective-permute-done((bf16[128,1024]{1,0:T(8,128)(2,1)S(1)}, bf16[128,1024]{1,0:T(8,128)(2,1)S(1)}, u32[]{:S(2)}, u32[]{:S(2)}) %collective-permute-start.13) | collective-permute-done | bytes 262176 | tf_op jit(solution)/shard_map/ppermute | solution.py:433
  40.0 1.4 %collective-permute-done.14.refs_6_ = bf16[128,1024]{1,0:T(8,128)(2,1)S(1)} collective-permute-done((bf16[128,1024]{1,0:T(8,128)(2,1)S(1)}, bf16[128,1024]{1,0:T(8,128)(2,1)S(1)}, u32[]{:S(2)}, u32[]{:S(2)}) %collective-permute-start.14) | collective-permute-done | bytes 262176 | tf_op jit(solution)/shard_map/ppermute | solution.py:433
  41.4 0.6 %merge_near.1 = bf16[512,512]{1,0:T(8,128)(2,1)} custom-call(s32[24]{0:T(128)S(1)} %concatenate.3.meta, bf16[128,512]{1,0:T(8,128)(2,1)S(1)} %get-tuple-element.32.refs_0_, f32[128,512]{1,0:T(8,128)S(1)} %get-tuple-element.33.refs_1_, f32[128,512]{1,0:T(8,128)S(1)} %get-tuple-element.34.refs_2_, ...), custom_call_target="tpu_custom_call", output_to_operand_aliasing={{}: (8, {})} | custom-call | flops 2990000 | bytes 1000 | tf_op jit(solution)/shard_map/merge_near/pallas_call | solution.py:457
  (29 shorter events, 2.2 us)
Async XLA Ops:
  0.0 13.4 %copy-start.3 = (s32[4]{0:T(128)S(1)}, s32[4]{0:T(128)}, u32[]{:S(2)}) copy-start(s32[4]{0:T(128)} %param.7) | copy-start | bytes 52
  0.0 16.3 %copy-start.2 = (s32[4]{0:T(128)S(1)}, s32[4]{0:T(128)}, u32[]{:S(2)}) copy-start(s32[4]{0:T(128)} %param.6) | copy-start | bytes 52
  0.0 16.4 %copy-start = (bf16[1,512,2048]{2,1,0:T(8,128)(2,1)S(1)}, bf16[1,512,2048]{2,1,0:T(8,128)(2,1)}, u32[]{:S(2)}) copy-start(bf16[1,512,2048]{2,1,0:T(8,128)(2,1)} %param.4) | copy-start | bytes 6291460
  0.0 16.4 %collective-permute-start = (bf16[512,1536]{1,0:T(8,128)(2,1)}, bf16[512,1536]{1,0:T(8,128)(2,1)}, u32[]{:S(2)}, u32[]{:S(2)}) collective-permute-start(bf16[512,1536]{1,0:T(8,128)(2,1)} %refs_0_.1), channel_id=1, source_target_pairs={{0,1},{1,0},{2,3},{3,2},{4,5},{5,4},{6,7},{7,6},{8,9},{9,8},{10,11... | collective-permute-start | bytes 4718600 | tf_op jit(solution)/shard_map/ppermute | solution.py:62
  1.6 9.8 %collective-permute-start.2 = (bf16[128,1024]{1,0:T(8,128)(2,1)S(1)}, bf16[128,1024]{1,0:T(8,128)(2,1)S(1)}, u32[]{:S(2)}, u32[]{:S(2)}) collective-permute-start(bf16[128,1024]{1,0:T(8,128)(2,1)S(1)} %constant_dynamic-slice_fusion.1), channel_id=1, source_target_pairs={{0,2},{1,3},{2,0},{3,1},{4,6},{5,7},{6,4},{7,5},{8,10},{9,11},{10,... | collective-permute-start | bytes 786440 | tf_op jit(solution)/shard_map/ppermute | solution.py:62
  5.8 8.3 %collective-permute-start.4 = (bf16[64,1024]{1,0:T(8,128)(2,1)}, bf16[64,1024]{1,0:T(8,128)(2,1)S(1)}, u32[]{:S(2)}, u32[]{:S(2)}) collective-permute-start(bf16[64,1024]{1,0:T(8,128)(2,1)} %constant_dynamic-slice_fusion), channel_id=1, source_target_pairs={{0,2},{1,3},{2,0},{3,1},{4,6},{5,7},{6,4},{7,5},{8,10},{9,11},{10,... | collective-permute-start | bytes 393224 | tf_op jit(solution)/shard_map/ppermute | solution.py:62
  7.5 13.6 %collective-permute-start.6 = (bf16[128,1024]{1,0:T(8,128)(2,1)}, bf16[128,1024]{1,0:T(8,128)(2,1)S(1)}, u32[]{:S(2)}, u32[]{:S(2)}) collective-permute-start(bf16[128,1024]{1,0:T(8,128)(2,1)} %slice.6), channel_id=1, source_target_pairs={{0,2},{1,3},{2,0},{3,1},{4,6},{5,7},{6,4},{7,5},{8,10},{9,11},{10,... | collective-permute-start | bytes 786440 | tf_op jit(solution)/shard_map/ppermute | solution.py:62
  11.3 19.3 %collective-permute-start.1 = (bf16[512,512]{1,0:T(8,128)(2,1)}, bf16[512,512]{1,0:T(8,128)(2,1)S(1)}, u32[]{:S(2)}, u32[]{:S(2)}) collective-permute-start(bf16[512,512]{1,0:T(8,128)(2,1)} %slice.7), channel_id=1, source_target_pairs={{0,2},{1,3},{2,0},{3,1},{4,6},{5,7},{6,4},{7,5},{8,10},{9,11},{10,... | collective-permute-start | bytes 1572872 | tf_op jit(solution)/shard_map/ppermute | solution.py:62
  11.4 10.3 %collective-permute-start.3 = (bf16[128,1024]{1,0:T(8,128)(2,1)S(1)}, bf16[128,1024]{1,0:T(8,128)(2,1)S(1)}, u32[]{:S(2)}, u32[]{:S(2)}) collective-permute-start(bf16[128,1024]{1,0:T(8,128)(2,1)S(1)} %collective-permute-done.2.refs_0_), channel_id=1, source_target_pairs={{0,4},{4,0},{8,12},{12,8},{16,20},{20,16},{24,28},{28,24},{1,5},{5... | collective-permute-start | bytes 786440 | tf_op jit(solution)/shard_map/ppermute | solution.py:62
  14.1 7.6 %collective-permute-start.5 = (bf16[64,1024]{1,0:T(8,128)(2,1)S(1)}, bf16[64,1024]{1,0:T(8,128)(2,1)}, u32[]{:S(2)}, u32[]{:S(2)}) collective-permute-start(bf16[64,1024]{1,0:T(8,128)(2,1)S(1)} %collective-permute-done.4.refs_2_), channel_id=1, source_target_pairs={{0,8},{4,12},{8,0},{12,4},{16,24},{20,28},{24,16},{28,20},{1,9},{5... | collective-permute-start | bytes 393224 | tf_op jit(solution)/shard_map/ppermute | solution.py:62
  16.4 5.8 %collective-permute-start.9 = (bf16[64,1024]{1,0:T(8,128)(2,1)S(1)}, bf16[64,1024]{1,0:T(8,128)(2,1)S(1)}, u32[]{:S(2)}, u32[]{:S(2)}) collective-permute-start(bf16[64,1024]{1,0:T(8,128)(2,1)S(1)} %collective-permute-done.4.refs_2_), channel_id=1, source_target_pairs={{0,1},{1,0},{2,3},{3,2},{4,5},{5,4},{6,7},{7,6},{8,9},{9,8},{10,11... | collective-permute-start | bytes 393224 | tf_op jit(solution)/shard_map/ppermute | solution.py:62
  16.5 1.4 %copy-start.1 = (bf16[512,1536]{1,0:T(8,128)(2,1)S(1)}, bf16[512,1536]{1,0:T(8,128)(2,1)}, u32[]{:S(2)}) copy-start(bf16[512,1536]{1,0:T(8,128)(2,1)} %refs_0_.1) | copy-start | bytes 4718596
  21.1 2.5 %collective-permute-start.7 = (bf16[128,1024]{1,0:T(8,128)(2,1)S(1)}, bf16[128,1024]{1,0:T(8,128)(2,1)S(1)}, u32[]{:S(2)}, u32[]{:S(2)}) collective-permute-start(bf16[128,1024]{1,0:T(8,128)(2,1)S(1)} %collective-permute-done.2.refs_0_), channel_id=1, source_target_pairs={{0,1},{1,0},{2,3},{3,2},{4,5},{5,4},{6,7},{7,6},{8,9},{9,8},{10,11... | collective-permute-start | bytes 786440 | tf_op jit(solution)/shard_map/ppermute | solution.py:62
  21.7 1.9 %collective-permute-start.11 = (bf16[128,1024]{1,0:T(8,128)(2,1)S(1)}, bf16[128,1024]{1,0:T(8,128)(2,1)S(1)}, u32[]{:S(2)}, u32[]{:S(2)}) collective-permute-start(bf16[128,1024]{1,0:T(8,128)(2,1)S(1)} %collective-permute-done.6.refs_4_), channel_id=1, source_target_pairs={{0,1},{1,0},{2,3},{3,2},{4,5},{5,4},{6,7},{7,6},{8,9},{9,8},{10,11... | collective-permute-start | bytes 786440 | tf_op jit(solution)/shard_map/ppermute | solution.py:62
  21.7 2.2 %collective-permute-start.8 = (bf16[128,1024]{1,0:T(8,128)(2,1)S(1)}, bf16[128,1024]{1,0:T(8,128)(2,1)S(1)}, u32[]{:S(2)}, u32[]{:S(2)}) collective-permute-start(bf16[128,1024]{1,0:T(8,128)(2,1)S(1)} %collective-permute-done.3.refs_1_), channel_id=1, source_target_pairs={{0,1},{1,0},{2,3},{3,2},{4,5},{5,4},{6,7},{7,6},{8,9},{9,8},{10,11... | collective-permute-start | bytes 786440 | tf_op jit(solution)/shard_map/ppermute | solution.py:62
  22.2 1.8 %collective-permute-start.10 = (bf16[64,1024]{1,0:T(8,128)(2,1)}, bf16[64,1024]{1,0:T(8,128)(2,1)S(1)}, u32[]{:S(2)}, u32[]{:S(2)}) collective-permute-start(bf16[64,1024]{1,0:T(8,128)(2,1)} %collective-permute-done.5.refs_3_), channel_id=1, source_target_pairs={{0,1},{1,0},{2,3},{3,2},{4,5},{5,4},{6,7},{7,6},{8,9},{9,8},{10,11... | collective-permute-start | bytes 393224 | tf_op jit(solution)/shard_map/ppermute | solution.py:62
  24.9 14.4 %collective-permute-start.12 = (bf16[128,1024]{1,0:T(8,128)(2,1)S(1)}, bf16[128,1024]{1,0:T(8,128)(2,1)S(1)}, u32[]{:S(2)}, u32[]{:S(2)}) collective-permute-start(bf16[128,1024]{1,0:T(8,128)(2,1)S(1)} %get-tuple-element.27), channel_id=1, source_target_pairs={{0,8},{4,12},{8,0},{12,4},{16,24},{20,28},{24,16},{28,20},{1,9},{5... | collective-permute-start | bytes 786440 | tf_op jit(solution)/shard_map/ppermute | solution.py:433
  25.4 14.7 %collective-permute-start.13 = (bf16[128,1024]{1,0:T(8,128)(2,1)S(1)}, bf16[128,1024]{1,0:T(8,128)(2,1)S(1)}, u32[]{:S(2)}, u32[]{:S(2)}) collective-permute-start(bf16[128,1024]{1,0:T(8,128)(2,1)S(1)} %get-tuple-element.27), channel_id=1, source_target_pairs={{0,12},{4,8},{8,4},{12,0},{16,28},{20,24},{24,20},{28,16},{1,13},{... | collective-permute-start | bytes 786440 | tf_op jit(solution)/shard_map/ppermute | solution.py:433
  28.0 13.4 %collective-permute-start.14 = (bf16[128,1024]{1,0:T(8,128)(2,1)S(1)}, bf16[128,1024]{1,0:T(8,128)(2,1)S(1)}, u32[]{:S(2)}, u32[]{:S(2)}) collective-permute-start(bf16[128,1024]{1,0:T(8,128)(2,1)S(1)} %get-tuple-element.27), channel_id=1, source_target_pairs={{0,4},{4,0},{8,12},{12,8},{16,20},{20,16},{24,28},{28,24},{1,5},{5... | collective-permute-start | bytes 786440 | tf_op jit(solution)/shard_map/ppermute | solution.py:433

commit v9 on v8

--- a/solution.py
+++ b/solution.py
@@ -36,7 +36,7 @@
     "q": ("kv",),
     "kv": ("pack",),
 }
-NEAR_ORDER = (2, 3, 1)
+NEAR_ORDER = (3, 2, 1)
 F32 = jnp.float32
 BF16 = jnp.bfloat16
 

time: 42.3 us -> 40.9 us (0.967)
  waiting for transfers between devices: 3.55 us -> 2.13 us
    ppermute x3, waiting for transfers between devices: 2.14 us -> 0.72 us  [body(): lax.ppermute(pack, 'seq', partners(seq_size, place, step))]
  transfers between devices with their start and end apart: 15 -> 15, of which waited for: 5 -> 4; matrix products, arithmetic and copies ran while one was open for 15% -> 16% of each run, Pallas kernels for 27% -> 28%
where the time goes in v9:
time: 40.9 us; the launch traced here: 40.6 us
  starting transfers between devices  14.1 us (34%)
  Pallas kernels  11.8 us (29%)
  local copies, waits for them, and re-layouts  7.7 us (19%)
  blocking collectives  4.58 us (11%)
  waiting for transfers between devices  2.13 us (5%)
    pallas_call x6, Pallas kernels, call(): pl.pallas_call(kernel, in_specs=[scalar_spec] + [whole] * len(args), out_...  11.3 us
    ppermute x12, starting transfers between devices, swap(): return lax.ppermute(value, axis, [(i, i ^ bit) for i in range(count)])  10.6 us
    all_to_all x1, blocking collectives, body(): lax.all_to_all(slots_out, 'fsdp', 0, 0, axis_index_groups=[[i, i + 1] for...  4.58 us
    ppermute x3, starting transfers between devices, body(): lax.ppermute(pack, 'seq', partners(seq_size, place, step))  3.55 us
    dynamic_slice x2, local copies, waits for them, and re-layouts, body(): lax.dynamic_slice(ordered('c' + tag, qkv_weight, known), (start + side *...  2.67 us
    slice x1, local copies, waits for them, and re-layouts, body(): cut = ordered('cQ', qkv_weight, known)[:, :WIDTH]  1.87 us
    slice x1, local copies, waits for them, and re-layouts, body(): cut = ordered('cD', qkv_weight, known)[direct_from:, WIDTH:]  1.66 us
    unnamed x8, local copies, waits for them, and re-layouts  1.41 us
  transfers between devices with their start and end apart: 15, of which 4 were waited for; matrix products, arithmetic and copies ran while one was open for 16% of the time, Pallas kernels for 28%

profile of v9, /device:TPU:0, one launch (start us, length us, event | category | flops | bytes accessed | tf_op | source)
XLA Modules:
  0.0 40.6 jit_solution(16985187677834871896)
XLA Ops:
  0.0 0.5 %collective-permute-start = (bf16[512,1536]{1,0:T(8,128)(2,1)}, bf16[512,1536]{1,0:T(8,128)(2,1)}, u32[]{:S(2)}, u32[]{:S(2)}) collective-permute-start(bf16[512,1536]{1,0:T(8,128)(2,1)} %refs_0_.1), channel_id=1, source_target_pairs={{0,1},{1,0},{2,3},{3,2},{4,5},{5,4},{6,7},{7,6},{8,9},{9,8},{10,11... | collective-permute-start | bytes 4718600 | tf_op jit(solution)/shard_map/ppermute | solution.py:62
  0.5 1.1 %constant_dynamic-slice_fusion.1 = bf16[128,1024]{1,0:T(8,128)(2,1)S(1)} fusion(bf16[512,1536]{1,0:T(8,128)(2,1)} %refs_0_.1, s32[]{:T(128)S(6)} %select_n.69), kind=kLoop, calls=%fused_computation.7 | loop fusion | bytes 524292 | tf_op jit(solution)/shard_map/dynamic_slice | solution.py:375
  1.6 2.6 %collective-permute-start.2 = (bf16[128,1024]{1,0:T(8,128)(2,1)S(1)}, bf16[128,1024]{1,0:T(8,128)(2,1)S(1)}, u32[]{:S(2)}, u32[]{:S(2)}) collective-permute-start(bf16[128,1024]{1,0:T(8,128)(2,1)S(1)} %constant_dynamic-slice_fusion.1), channel_id=1, source_target_pairs={{0,2},{1,3},{2,0},{3,1},{4,6},{5,7},{6,4},{7,5},{8,10},{9,11},{10,... | collective-permute-start | bytes 786440 | tf_op jit(solution)/shard_map/ppermute | solution.py:62
  4.2 1.6 %constant_dynamic-slice_fusion = bf16[64,1024]{1,0:T(8,128)(2,1)} fusion(bf16[512,1536]{1,0:T(8,128)(2,1)} %refs_0_.1, s32[]{:T(128)S(6)} %select_n.70), kind=kLoop, calls=%fused_computation.6 | loop fusion | bytes 262148 | tf_op jit(solution)/shard_map/dynamic_slice | solution.py:375
  5.8 1.7 %slice.6 = bf16[128,1024]{1,0:T(8,128)(2,1)} slice(bf16[512,1536]{1,0:T(8,128)(2,1)} %refs_0_.1), slice={[384:512], [512:1536]} | slice | bytes 524288 | tf_op jit(solution)/shard_map/slice | solution.py:388
  7.5 2.0 %collective-permute-start.6 = (bf16[128,1024]{1,0:T(8,128)(2,1)}, bf16[128,1024]{1,0:T(8,128)(2,1)S(1)}, u32[]{:S(2)}, u32[]{:S(2)}) collective-permute-start(bf16[128,1024]{1,0:T(8,128)(2,1)} %slice.6), channel_id=1, source_target_pairs={{0,2},{1,3},{2,0},{3,1},{4,6},{5,7},{6,4},{7,5},{8,10},{9,11},{10,... | collective-permute-start | bytes 786440 | tf_op jit(solution)/shard_map/ppermute | solution.py:62
  9.5 1.9 %slice.7 = bf16[512,512]{1,0:T(8,128)(2,1)} slice(bf16[512,1536]{1,0:T(8,128)(2,1)} %refs_0_.1), slice={[0:512], [0:512]} | slice | bytes 1048576 | tf_op jit(solution)/shard_map/slice | solution.py:395
  11.4 2.0 %collective-permute-start.3 = (bf16[128,1024]{1,0:T(8,128)(2,1)S(1)}, bf16[128,1024]{1,0:T(8,128)(2,1)S(1)}, u32[]{:S(2)}, u32[]{:S(2)}) collective-permute-start(bf16[128,1024]{1,0:T(8,128)(2,1)S(1)} %collective-permute-done.2.refs_0_), channel_id=1, source_target_pairs={{0,4},{4,0},{8,12},{12,8},{16,20},{20,16},{24,28},{28,24},{1,5},{5... | collective-permute-start | bytes 786440 | tf_op jit(solution)/shard_map/ppermute | solution.py:62
  13.5 0.6 %collective-permute-done.4.refs_2_ = bf16[64,1024]{1,0:T(8,128)(2,1)S(1)} collective-permute-done((bf16[64,1024]{1,0:T(8,128)(2,1)}, bf16[64,1024]{1,0:T(8,128)(2,1)S(1)}, u32[]{:S(2)}, u32[]{:S(2)}) %collective-permute-start.4) | collective-permute-done | bytes 131104 | tf_op jit(solution)/shard_map/ppermute | solution.py:62
  14.1 2.1 %collective-permute-start.5 = (bf16[64,1024]{1,0:T(8,128)(2,1)S(1)}, bf16[64,1024]{1,0:T(8,128)(2,1)}, u32[]{:S(2)}, u32[]{:S(2)}) collective-permute-start(bf16[64,1024]{1,0:T(8,128)(2,1)S(1)} %collective-permute-done.4.refs_2_), channel_id=1, source_target_pairs={{0,8},{4,12},{8,0},{12,4},{16,24},{20,28},{24,16},{28,20},{1,9},{5... | collective-permute-start | bytes 393224 | tf_op jit(solution)/shard_map/ppermute | solution.py:62
  16.5 1.4 %copy-done.1 = bf16[512,1536]{1,0:T(8,128)(2,1)S(1)} copy-done((bf16[512,1536]{1,0:T(8,128)(2,1)S(1)}, bf16[512,1536]{1,0:T(8,128)(2,1)}, u32[]{:S(2)}) %copy-start.1) | copy-done | bytes 1572888
  17.9 3.2 %project_own.1.partial = f32[512,1536]{1,0:T(8,128)S(1)} custom-call(s32[24]{0:T(128)S(1)} %concatenate.3.meta, bf16[512,2048]{1,0:T(8,128)(2,1)S(1)} %bitcast.12, bf16[512,1536]{1,0:T(8,128)(2,1)S(1)} %copy-done.1, bf16[512,1536]{1,0:T(8,128)(2,1)} %collective-permute-done.refs_1_), custom_call_target="tpu_custom_call" | custom-call | flops 3680000 | bytes 1000 | tf_op jit(solution)/shard_map/project_own/pallas_call | solution.py:345
  21.1 0.6 %collective-permute-start.7 = (bf16[128,1024]{1,0:T(8,128)(2,1)S(1)}, bf16[128,1024]{1,0:T(8,128)(2,1)S(1)}, u32[]{:S(2)}, u32[]{:S(2)}) collective-permute-start(bf16[128,1024]{1,0:T(8,128)(2,1)S(1)} %collective-permute-done.2.refs_0_), channel_id=1, source_target_pairs={{0,1},{1,0},{2,3},{3,2},{4,5},{5,4},{6,7},{7,6},{8,9},{9,8},{10,11... | collective-permute-start | bytes 786440 | tf_op jit(solution)/shard_map/ppermute | solution.py:62
  22.3 1.3 %project_first.1 = (f32[128,1024]{1,0:T(8,128)S(1)}, bf16[512,1024]{1,0:T(8,128)(2,1)S(1)}) custom-call(s32[24]{0:T(128)S(1)} %concatenate.3.meta, bf16[512,2048]{1,0:T(8,128)(2,1)S(1)} %bitcast.13, f32[512,1536]{1,0:T(8,128)S(1)} %project_own.1.partial, bf16[128,1024]{1,0:T(8,128)(2,1)S(1)} %collective-permute-done.2.refs_0_, ...), custom_call_target="tpu_custom_call" | custom-call | flops 689999 | bytes 1000 | tf_op jit(solution)/shard_map/project_first/pallas_call | solution.py:345
  24.0 0.9 %project_pack.1 = (bf16[128,1024]{1,0:T(8,128)(2,1)S(1)}, bf16[512,1024]{1,0:T(8,128)(2,1)S(1)}) custom-call(s32[24]{0:T(128)S(1)} %concatenate.3.meta, bf16[512,2048]{1,0:T(8,128)(2,1)S(1)} %bitcast.14, f32[128,1024]{1,0:T(8,128)S(1)} %get-tuple-element.26.refs_0_, bf16[128,1024]{1,0:T(8,128)(2,1)S(1)} %collective-permute-done.7.refs_1_, ...), custom_call_target="tpu_custom_call" | custom-call | flops 689999 | bytes 1000 | tf_op jit(solution)/shard_map/project_pack/pallas_call | solution.py:345
  24.9 1.6 %collective-permute-start.12 = (bf16[128,1024]{1,0:T(8,128)(2,1)S(1)}, bf16[128,1024]{1,0:T(8,128)(2,1)S(1)}, u32[]{:S(2)}, u32[]{:S(2)}) collective-permute-start(bf16[128,1024]{1,0:T(8,128)(2,1)S(1)} %get-tuple-element.27), channel_id=1, source_target_pairs={{0,12},{4,8},{8,4},{12,0},{16,28},{20,24},{24,20},{28,16},{1,13},{... | collective-permute-start | bytes 786440 | tf_op jit(solution)/shard_map/ppermute | solution.py:433
  26.5 1.4 %collective-permute-start.13 = (bf16[128,1024]{1,0:T(8,128)(2,1)S(1)}, bf16[128,1024]{1,0:T(8,128)(2,1)S(1)}, u32[]{:S(2)}, u32[]{:S(2)}) collective-permute-start(bf16[128,1024]{1,0:T(8,128)(2,1)S(1)} %get-tuple-element.27), channel_id=1, source_target_pairs={{0,8},{4,12},{8,0},{12,4},{16,24},{20,28},{24,16},{28,20},{1,9},{5... | collective-permute-start | bytes 786440 | tf_op jit(solution)/shard_map/ppermute | solution.py:433
  28.0 0.5 %collective-permute-start.14 = (bf16[128,1024]{1,0:T(8,128)(2,1)S(1)}, bf16[128,1024]{1,0:T(8,128)(2,1)S(1)}, u32[]{:S(2)}, u32[]{:S(2)}) collective-permute-start(bf16[128,1024]{1,0:T(8,128)(2,1)S(1)} %get-tuple-element.27), channel_id=1, source_target_pairs={{0,4},{4,0},{8,12},{12,8},{16,20},{20,16},{24,28},{28,24},{1,5},{5... | collective-permute-start | bytes 786440 | tf_op jit(solution)/shard_map/ppermute | solution.py:433
  28.5 1.8 %project_kv.1.refs_2_ = bf16[512,1024]{1,0:T(8,128)(2,1)S(1)} custom-call(s32[24]{0:T(128)S(1)} %concatenate.3.meta, bf16[512,2048]{1,0:T(8,128)(2,1)S(1)} %bitcast.15, f32[512,1536]{1,0:T(8,128)S(1)} %project_own.1.partial, bf16[512,1024]{1,0:T(8,128)(2,1)S(1)} %get-tuple-element.29.refs_0_, bf16[512,1024]{1,0:T(8,128)(2,1)S(1)} %get-tuple-element.30.refs_1_), custom_call_target="tpu_custom_call" | custom-call | flops 2990000 | bytes 1000 | tf_op jit(solution)/shard_map/project_kv/pallas_call | solution.py:345
  30.7 0.6 %slot_queries.1 = bf16[2,512,512]{2,1,0:T(8,128)(2,1)S(1)} custom-call(s32[24]{0:T(128)S(1)} %concatenate.3.meta, bf16[512,512]{1,0:T(8,128)(2,1)S(1)} %collective-permute-done.1.source.refs_0_), custom_call_target="tpu_custom_call" | custom-call | flops 575000 | bytes 1000 | tf_op jit(solution)/shard_map/slot_queries/pallas_call | solution.py:345
  31.3 4.6 %all_to_all.5.refs_1_ = bf16[2,512,512]{2,1,0:T(8,128)(2,1)S(1)} all-to-all(bf16[2,512,512]{2,1,0:T(8,128)(2,1)S(1)} %slot_queries.1), channel_id=1, replica_groups={{0,1},{2,3},{4,5},{6,7},{8,9},{10,11},{12,13},{14,15},{16,17},{18,19},{..., dimensions={0} | all-to-all | bytes 2097152 | tf_op jit(solution)/shard_map/all_to_all | solution.py:443
  35.9 3.4 %attend_local.1 = (bf16[512,512]{1,0:T(8,128)(2,1)}, bf16[128,512]{1,0:T(8,128)(2,1)S(1)}, f32[128,512]{1,0:T(8,128)S(1)}, f32[128,512]{1,0:T(8,128)S(1)}, f32[128,512]{1,0:T(8,128)S(1)}) custom-call(s32[24]{0:T(128)S(1)} %concatenate.3.meta, bf16[512,2048]{1,0:T(8,128)(2,1)S(1)} %bitcast.16, f32[512,1536]{1,0:T(8,128)S(1)} %project_own.1.partial, ...), custom_call_target="tpu_custom_call" | custom-call | flops 6325000 | bytes 1000 | tf_op jit(solution)/shard_map/attend_local/pallas_call | solution.py:345
  39.3 0.7 %collective-permute-done.13.refs_5_ = bf16[128,1024]{1,0:T(8,128)(2,1)S(1)} collective-permute-done((bf16[128,1024]{1,0:T(8,128)(2,1)S(1)}, bf16[128,1024]{1,0:T(8,128)(2,1)S(1)}, u32[]{:S(2)}, u32[]{:S(2)}) %collective-permute-start.13) | collective-permute-done | bytes 262176 | tf_op jit(solution)/shard_map/ppermute | solution.py:433
  40.0 0.6 %merge_near.1 = bf16[512,512]{1,0:T(8,128)(2,1)} custom-call(s32[24]{0:T(128)S(1)} %concatenate.3.meta, bf16[128,512]{1,0:T(8,128)(2,1)S(1)} %get-tuple-element.32.refs_0_, f32[128,512]{1,0:T(8,128)S(1)} %get-tuple-element.33.refs_1_, f32[128,512]{1,0:T(8,128)S(1)} %get-tuple-element.34.refs_2_, ...), custom_call_target="tpu_custom_call", output_to_operand_aliasing={{}: (8, {})} | custom-call | flops 2990000 | bytes 1000 | tf_op jit(solution)/shard_map/merge_near/pallas_call | solution.py:457
  (29 shorter events, 1.7 us)
Async XLA Ops:
  0.0 13.4 %copy-start.3 = (s32[4]{0:T(128)S(1)}, s32[4]{0:T(128)}, u32[]{:S(2)}) copy-start(s32[4]{0:T(128)} %param.7) | copy-start | bytes 52
  0.0 16.3 %copy-start.2 = (s32[4]{0:T(128)S(1)}, s32[4]{0:T(128)}, u32[]{:S(2)}) copy-start(s32[4]{0:T(128)} %param.6) | copy-start | bytes 52
  0.0 16.4 %copy-start = (bf16[1,512,2048]{2,1,0:T(8,128)(2,1)S(1)}, bf16[1,512,2048]{2,1,0:T(8,128)(2,1)}, u32[]{:S(2)}) copy-start(bf16[1,512,2048]{2,1,0:T(8,128)(2,1)} %param.4) | copy-start | bytes 6291460
  0.0 16.4 %collective-permute-start = (bf16[512,1536]{1,0:T(8,128)(2,1)}, bf16[512,1536]{1,0:T(8,128)(2,1)}, u32[]{:S(2)}, u32[]{:S(2)}) collective-permute-start(bf16[512,1536]{1,0:T(8,128)(2,1)} %refs_0_.1), channel_id=1, source_target_pairs={{0,1},{1,0},{2,3},{3,2},{4,5},{5,4},{6,7},{7,6},{8,9},{9,8},{10,11... | collective-permute-start | bytes 4718600 | tf_op jit(solution)/shard_map/ppermute | solution.py:62
  1.6 9.8 %collective-permute-start.2 = (bf16[128,1024]{1,0:T(8,128)(2,1)S(1)}, bf16[128,1024]{1,0:T(8,128)(2,1)S(1)}, u32[]{:S(2)}, u32[]{:S(2)}) collective-permute-start(bf16[128,1024]{1,0:T(8,128)(2,1)S(1)} %constant_dynamic-slice_fusion.1), channel_id=1, source_target_pairs={{0,2},{1,3},{2,0},{3,1},{4,6},{5,7},{6,4},{7,5},{8,10},{9,11},{10,... | collective-permute-start | bytes 786440 | tf_op jit(solution)/shard_map/ppermute | solution.py:62
  5.8 8.3 %collective-permute-start.4 = (bf16[64,1024]{1,0:T(8,128)(2,1)}, bf16[64,1024]{1,0:T(8,128)(2,1)S(1)}, u32[]{:S(2)}, u32[]{:S(2)}) collective-permute-start(bf16[64,1024]{1,0:T(8,128)(2,1)} %constant_dynamic-slice_fusion), channel_id=1, source_target_pairs={{0,2},{1,3},{2,0},{3,1},{4,6},{5,7},{6,4},{7,5},{8,10},{9,11},{10,... | collective-permute-start | bytes 393224 | tf_op jit(solution)/shard_map/ppermute | solution.py:62
  7.5 13.6 %collective-permute-start.6 = (bf16[128,1024]{1,0:T(8,128)(2,1)}, bf16[128,1024]{1,0:T(8,128)(2,1)S(1)}, u32[]{:S(2)}, u32[]{:S(2)}) collective-permute-start(bf16[128,1024]{1,0:T(8,128)(2,1)} %slice.6), channel_id=1, source_target_pairs={{0,2},{1,3},{2,0},{3,1},{4,6},{5,7},{6,4},{7,5},{8,10},{9,11},{10,... | collective-permute-start | bytes 786440 | tf_op jit(solution)/shard_map/ppermute | solution.py:62
  11.3 19.3 %collective-permute-start.1 = (bf16[512,512]{1,0:T(8,128)(2,1)}, bf16[512,512]{1,0:T(8,128)(2,1)S(1)}, u32[]{:S(2)}, u32[]{:S(2)}) collective-permute-start(bf16[512,512]{1,0:T(8,128)(2,1)} %slice.7), channel_id=1, source_target_pairs={{0,2},{1,3},{2,0},{3,1},{4,6},{5,7},{6,4},{7,5},{8,10},{9,11},{10,... | collective-permute-start | bytes 1572872 | tf_op jit(solution)/shard_map/ppermute | solution.py:62
  11.4 10.3 %collective-permute-start.3 = (bf16[128,1024]{1,0:T(8,128)(2,1)S(1)}, bf16[128,1024]{1,0:T(8,128)(2,1)S(1)}, u32[]{:S(2)}, u32[]{:S(2)}) collective-permute-start(bf16[128,1024]{1,0:T(8,128)(2,1)S(1)} %collective-permute-done.2.refs_0_), channel_id=1, source_target_pairs={{0,4},{4,0},{8,12},{12,8},{16,20},{20,16},{24,28},{28,24},{1,5},{5... | collective-permute-start | bytes 786440 | tf_op jit(solution)/shard_map/ppermute | solution.py:62
  14.1 7.6 %collective-permute-start.5 = (bf16[64,1024]{1,0:T(8,128)(2,1)S(1)}, bf16[64,1024]{1,0:T(8,128)(2,1)}, u32[]{:S(2)}, u32[]{:S(2)}) collective-permute-start(bf16[64,1024]{1,0:T(8,128)(2,1)S(1)} %collective-permute-done.4.refs_2_), channel_id=1, source_target_pairs={{0,8},{4,12},{8,0},{12,4},{16,24},{20,28},{24,16},{28,20},{1,9},{5... | collective-permute-start | bytes 393224 | tf_op jit(solution)/shard_map/ppermute | solution.py:62
  16.4 5.8 %collective-permute-start.9 = (bf16[64,1024]{1,0:T(8,128)(2,1)S(1)}, bf16[64,1024]{1,0:T(8,128)(2,1)S(1)}, u32[]{:S(2)}, u32[]{:S(2)}) collective-permute-start(bf16[64,1024]{1,0:T(8,128)(2,1)S(1)} %collective-permute-done.4.refs_2_), channel_id=1, source_target_pairs={{0,1},{1,0},{2,3},{3,2},{4,5},{5,4},{6,7},{7,6},{8,9},{9,8},{10,11... | collective-permute-start | bytes 393224 | tf_op jit(solution)/shard_map/ppermute | solution.py:62
  16.5 1.4 %copy-start.1 = (bf16[512,1536]{1,0:T(8,128)(2,1)S(1)}, bf16[512,1536]{1,0:T(8,128)(2,1)}, u32[]{:S(2)}) copy-start(bf16[512,1536]{1,0:T(8,128)(2,1)} %refs_0_.1) | copy-start | bytes 4718596
  21.1 2.5 %collective-permute-start.7 = (bf16[128,1024]{1,0:T(8,128)(2,1)S(1)}, bf16[128,1024]{1,0:T(8,128)(2,1)S(1)}, u32[]{:S(2)}, u32[]{:S(2)}) collective-permute-start(bf16[128,1024]{1,0:T(8,128)(2,1)S(1)} %collective-permute-done.2.refs_0_), channel_id=1, source_target_pairs={{0,1},{1,0},{2,3},{3,2},{4,5},{5,4},{6,7},{7,6},{8,9},{9,8},{10,11... | collective-permute-start | bytes 786440 | tf_op jit(solution)/shard_map/ppermute | solution.py:62
  21.7 1.9 %collective-permute-start.11 = (bf16[128,1024]{1,0:T(8,128)(2,1)S(1)}, bf16[128,1024]{1,0:T(8,128)(2,1)S(1)}, u32[]{:S(2)}, u32[]{:S(2)}) collective-permute-start(bf16[128,1024]{1,0:T(8,128)(2,1)S(1)} %collective-permute-done.6.refs_4_), channel_id=1, source_target_pairs={{0,1},{1,0},{2,3},{3,2},{4,5},{5,4},{6,7},{7,6},{8,9},{9,8},{10,11... | collective-permute-start | bytes 786440 | tf_op jit(solution)/shard_map/ppermute | solution.py:62
  21.7 2.2 %collective-permute-start.8 = (bf16[128,1024]{1,0:T(8,128)(2,1)S(1)}, bf16[128,1024]{1,0:T(8,128)(2,1)S(1)}, u32[]{:S(2)}, u32[]{:S(2)}) collective-permute-start(bf16[128,1024]{1,0:T(8,128)(2,1)S(1)} %collective-permute-done.3.refs_1_), channel_id=1, source_target_pairs={{0,1},{1,0},{2,3},{3,2},{4,5},{5,4},{6,7},{7,6},{8,9},{9,8},{10,11... | collective-permute-start | bytes 786440 | tf_op jit(solution)/shard_map/ppermute | solution.py:62
  22.2 1.8 %collective-permute-start.10 = (bf16[64,1024]{1,0:T(8,128)(2,1)}, bf16[64,1024]{1,0:T(8,128)(2,1)S(1)}, u32[]{:S(2)}, u32[]{:S(2)}) collective-permute-start(bf16[64,1024]{1,0:T(8,128)(2,1)} %collective-permute-done.5.refs_3_), channel_id=1, source_target_pairs={{0,1},{1,0},{2,3},{3,2},{4,5},{5,4},{6,7},{7,6},{8,9},{9,8},{10,11... | collective-permute-start | bytes 393224 | tf_op jit(solution)/shard_map/ppermute | solution.py:62
  24.9 14.4 %collective-permute-start.12 = (bf16[128,1024]{1,0:T(8,128)(2,1)S(1)}, bf16[128,1024]{1,0:T(8,128)(2,1)S(1)}, u32[]{:S(2)}, u32[]{:S(2)}) collective-permute-start(bf16[128,1024]{1,0:T(8,128)(2,1)S(1)} %get-tuple-element.27), channel_id=1, source_target_pairs={{0,12},{4,8},{8,4},{12,0},{16,28},{20,24},{24,20},{28,16},{1,13},{... | collective-permute-start | bytes 786440 | tf_op jit(solution)/shard_map/ppermute | solution.py:433
  26.5 13.5 %collective-permute-start.13 = (bf16[128,1024]{1,0:T(8,128)(2,1)S(1)}, bf16[128,1024]{1,0:T(8,128)(2,1)S(1)}, u32[]{:S(2)}, u32[]{:S(2)}) collective-permute-start(bf16[128,1024]{1,0:T(8,128)(2,1)S(1)} %get-tuple-element.27), channel_id=1, source_target_pairs={{0,8},{4,12},{8,0},{12,4},{16,24},{20,28},{24,16},{28,20},{1,9},{5... | collective-permute-start | bytes 786440 | tf_op jit(solution)/shard_map/ppermute | solution.py:433
  28.0 12.0 %collective-permute-start.14 = (bf16[128,1024]{1,0:T(8,128)(2,1)S(1)}, bf16[128,1024]{1,0:T(8,128)(2,1)S(1)}, u32[]{:S(2)}, u32[]{:S(2)}) collective-permute-start(bf16[128,1024]{1,0:T(8,128)(2,1)S(1)} %get-tuple-element.27), channel_id=1, source_target_pairs={{0,4},{4,0},{8,12},{12,8},{16,20},{20,16},{24,28},{28,24},{1,5},{5... | collective-permute-start | bytes 786440 | tf_op jit(solution)/shard_map/ppermute | solution.py:433

commit v10 on v1

--- a/solution.py
+++ b/solution.py
@@ -97,7 +97,7 @@
     sums, joined = refs[:slots], refs[slots]
     for at, array in zip(layout, arrived):
         rows = array.shape[0]
-        joined[pl.ds(pl.multiple_of(meta[at], rows), rows), :] = array[...]
+        joined[pl.ds(pl.multiple_of(meta[at], 16), rows), :] = array[...]
     depth = joined.shape[0]
     columns = pl.ds(pl.multiple_of(meta[place_at], depth), depth)
     for slot in range(slots):
@@ -312,7 +312,7 @@
     near_position = jnp.where(seq_index < half, seq_index, (seq_index - half) % near_size)
     far_position = seq_index // STRIDE % far_size
     far_match = (seq_index % STRIDE == far_offset // block_rate).astype(jnp.int32)
-    spans = [(0, share // 4), (share // 2, share // 8)] if seq_size % 4 == 0 else []
+    spans = [(0, share // 4), (share // 2, share * 5 // 512 * 16)] if seq_size % 4 == 0 else []
     direct_from = spans[-1][0] + 2 * spans[-1][1] if spans else 0
     full_places = [(mine ^ j) * share for j in range(pieces)]
     scalars = list(full_places)

time: 40.9 us -> 45.2 us (1.11)
  waiting for transfers between devices: 2.1 us -> 5.46 us
  starting transfers between devices: 14.1 us -> 15.6 us
  local copies, waits for them, and re-layouts: 7.7 us -> 6.39 us
  other arithmetic: 0.02 us -> 1.33 us
    ppermute x12, waiting for transfers between devices: 1.38 us -> 4.28 us  [swap(): return lax.ppermute(value, axis, [(i, i ^ bit) for i in range(count)])]
    ppermute x12, starting transfers between devices: 10.6 us -> 12 us  [swap(): return lax.ppermute(value, axis, [(i, i ^ bit) for i in range(count)])]
    slice x1, local copies, waits for them, and re-layouts: 1.66 us -> 0.94 us  [body(): cut = ordered('cD', qkv_weight, known)[direct_from:, WIDTH:]]
    convert_element_type x1, other arithmetic: 0.01 us -> 0.66 us  [body(): (seq_index % STRIDE == far_offset // block_rate).astype(jnp.int32)]
    select_n x1, other arithmetic: 0.01 us -> 0.66 us  [body(): far_offset % block_rate]
    dynamic_slice x2, local copies, waits for them, and re-layouts: 2.67 us -> 2.08 us  [body(): lax.dynamic_slice(ordered('c' + tag, qkv_weight, known), (start + side *...]
    ppermute x3, waiting for transfers between devices: 0.72 us -> 1.18 us  [body(): lax.ppermute(pack, 'seq', partners(seq_size, place, step))]
    unnamed x8 -> x6, local copies, waits for them, and re-layouts: 1.41 us -> 1.42 us
  transfers between devices with their start and end apart: 15 -> 15, of which waited for: 4 -> 5; matrix products, arithmetic and copies ran while one was open for 16% -> 14% of each run, Pallas kernels for 28% -> 24%
where the time goes in v10:
time: 45.2 us; the launch traced here: 44.9 us
  starting transfers between devices  15.6 us (35%)
  Pallas kernels  11.4 us (25%)
  local copies, waits for them, and re-layouts  6.39 us (14%)
  waiting for transfers between devices  5.46 us (12%)
  blocking collectives  4.58 us (10%)
  other arithmetic  1.33 us (3%)
    ppermute x12, starting transfers between devices, swap(): return lax.ppermute(value, axis, [(i, i ^ bit) for i in range(count)])  12 us
    pallas_call x6, Pallas kernels, call(): pl.pallas_call(kernel, in_specs=[scalar_spec] + [whole] * len(args), out_...  10.8 us
    all_to_all x1, blocking collectives, body(): lax.all_to_all(slots_out, 'fsdp', 0, 0, axis_index_groups=[[i, i + 1] for...  4.58 us
    ppermute x12, waiting for transfers between devices, swap(): return lax.ppermute(value, axis, [(i, i ^ bit) for i in range(count)])  4.28 us
    ppermute x3, starting transfers between devices, body(): lax.ppermute(pack, 'seq', partners(seq_size, place, step))  3.55 us
    dynamic_slice x2, local copies, waits for them, and re-layouts, body(): lax.dynamic_slice(ordered('c' + tag, qkv_weight, known), (start + side *...  2.08 us
    slice x1, local copies, waits for them, and re-layouts, body(): cut = ordered('cQ', qkv_weight, known)[:, :WIDTH]  1.87 us
    unnamed x6, local copies, waits for them, and re-layouts  1.42 us
  transfers between devices with their start and end apart: 15, of which 5 were waited for; matrix products, arithmetic and copies ran while one was open for 14% of the time, Pallas kernels for 24%

profile of v10, /device:TPU:0, one launch (start us, length us, event | category | flops | bytes accessed | tf_op | source)
XLA Modules:
  0.0 44.9 jit_solution(10744183696494488586)
XLA Ops:
  0.5 1.2 %constant_dynamic-slice_fusion.1 = bf16[128,1024]{1,0:T(8,128)(2,1)S(1)} fusion(bf16[512,1536]{1,0:T(8,128)(2,1)} %refs_0_.1, s32[]{:T(128)S(6)} %select_n.73), kind=kLoop, calls=%fused_computation.7 | loop fusion | bytes 524292 | tf_op jit(solution)/shard_map/dynamic_slice | solution.py:373
  1.6 2.5 %collective-permute-start.2 = (bf16[128,1024]{1,0:T(8,128)(2,1)S(1)}, bf16[128,1024]{1,0:T(8,128)(2,1)S(1)}, u32[]{:S(2)}, u32[]{:S(2)}) collective-permute-start(bf16[128,1024]{1,0:T(8,128)(2,1)S(1)} %constant_dynamic-slice_fusion.1), channel_id=1, source_target_pairs={{0,2},{1,3},{2,0},{3,1},{4,6},{5,7},{6,4},{7,5},{8,10},{9,11},{10,... | collective-permute-start | bytes 786440 | tf_op jit(solution)/shard_map/ppermute | solution.py:54
  4.2 0.9 %constant_dynamic-slice_fusion = bf16[80,1024]{1,0:T(8,128)(2,1)S(1)} fusion(bf16[512,1536]{1,0:T(8,128)(2,1)} %refs_0_.1, s32[]{:T(128)S(6)} %select_n.74), kind=kLoop, calls=%fused_computation.6 | loop fusion | bytes 327684 | tf_op jit(solution)/shard_map/dynamic_slice | solution.py:373
  5.2 0.9 %slice.6 = bf16[96,1024]{1,0:T(8,128)(2,1)S(1)} slice(bf16[512,1536]{1,0:T(8,128)(2,1)} %refs_0_.1), slice={[416:512], [512:1536]} | slice | bytes 393216 | tf_op jit(solution)/shard_map/slice | solution.py:387
  6.2 2.0 %collective-permute-start.6 = (bf16[96,1024]{1,0:T(8,128)(2,1)S(1)}, bf16[96,1024]{1,0:T(8,128)(2,1)S(1)}, u32[]{:S(2)}, u32[]{:S(2)}) collective-permute-start(bf16[96,1024]{1,0:T(8,128)(2,1)S(1)} %slice.6), channel_id=1, source_target_pairs={{0,2},{1,3},{2,0},{3,1},{4,6},{5,7},{6,4},{7,5},{8,10},{9,11},{10,... | collective-permute-start | bytes 589832 | tf_op jit(solution)/shard_map/ppermute | solution.py:54
  8.2 3.0 %collective-permute-done.2.refs_0_ = bf16[128,1024]{1,0:T(8,128)(2,1)S(1)} collective-permute-done((bf16[128,1024]{1,0:T(8,128)(2,1)S(1)}, bf16[128,1024]{1,0:T(8,128)(2,1)S(1)}, u32[]{:S(2)}, u32[]{:S(2)}) %collective-permute-start.2) | collective-permute-done | bytes 262176 | tf_op jit(solution)/shard_map/ppermute | solution.py:54
  11.2 2.1 %collective-permute-start.3 = (bf16[128,1024]{1,0:T(8,128)(2,1)S(1)}, bf16[128,1024]{1,0:T(8,128)(2,1)S(1)}, u32[]{:S(2)}, u32[]{:S(2)}) collective-permute-start(bf16[128,1024]{1,0:T(8,128)(2,1)S(1)} %collective-permute-done.2.refs_0_), channel_id=1, source_target_pairs={{0,4},{4,0},{8,12},{12,8},{16,20},{20,16},{24,28},{28,24},{1,5},{5... | collective-permute-start | bytes 786440 | tf_op jit(solution)/shard_map/ppermute | solution.py:54
  13.3 0.7 %and_select_fusion.1 = s32[4]{0:T(128)S(1)} fusion(s32[4]{0:T(128)} %param.7), kind=kLoop, calls=%fused_computation.2 | loop fusion | flops 44 | bytes 32 | tf_op jit(solution)/shard_map/jit(remainder)/select_n | solution.py:335
  14.0 0.8 %collective-permute-done.4.refs_2_ = bf16[80,1024]{1,0:T(8,128)(2,1)S(1)} collective-permute-done((bf16[80,1024]{1,0:T(8,128)(2,1)S(1)}, bf16[80,1024]{1,0:T(8,128)(2,1)S(1)}, u32[]{:S(2)}, u32[]{:S(2)}) %collective-permute-start.4) | collective-permute-done | bytes 163872 | tf_op jit(solution)/shard_map/ppermute | solution.py:54
  14.7 2.1 %collective-permute-start.5 = (bf16[80,1024]{1,0:T(8,128)(2,1)S(1)}, bf16[80,1024]{1,0:T(8,128)(2,1)S(1)}, u32[]{:S(2)}, u32[]{:S(2)}) collective-permute-start(bf16[80,1024]{1,0:T(8,128)(2,1)S(1)} %collective-permute-done.4.refs_2_), channel_id=1, source_target_pairs={{0,8},{4,12},{8,0},{12,4},{16,24},{20,28},{24,16},{28,20},{1,9},{5... | collective-permute-start | bytes 491528 | tf_op jit(solution)/shard_map/ppermute | solution.py:54
  16.9 0.7 %compare_convert_fusion = s32[4]{0:T(128)S(1)} fusion(s32[4]{0:T(128)} %param.7, s32[]{:T(128)S(6)} %select_n.67), kind=kLoop, calls=%fused_computation | loop fusion | flops 68 | bytes 36 | tf_op jit(solution)/shard_map/convert_element_type | solution.py:314
  17.6 1.9 %slice.7 = bf16[512,512]{1,0:T(8,128)(2,1)} slice(bf16[512,1536]{1,0:T(8,128)(2,1)} %refs_0_.1), slice={[0:512], [0:512]} | slice | bytes 1048576 | tf_op jit(solution)/shard_map/slice | solution.py:394
  19.5 1.6 %collective-permute-start.1 = (bf16[512,512]{1,0:T(8,128)(2,1)}, bf16[512,512]{1,0:T(8,128)(2,1)S(1)}, u32[]{:S(2)}, u32[]{:S(2)}) collective-permute-start(bf16[512,512]{1,0:T(8,128)(2,1)} %slice.7), channel_id=1, source_target_pairs={{0,2},{1,3},{2,0},{3,1},{4,6},{5,7},{6,4},{7,5},{8,10},{9,11},{10,... | collective-permute-start | bytes 1572872 | tf_op jit(solution)/shard_map/ppermute | solution.py:54
  21.1 1.4 %copy-done.1 = bf16[512,1536]{1,0:T(8,128)(2,1)S(1)} copy-done((bf16[512,1536]{1,0:T(8,128)(2,1)S(1)}, bf16[512,1536]{1,0:T(8,128)(2,1)}, u32[]{:S(2)}) %copy-start.1) | copy-done | bytes 1572888
  22.5 3.2 %project_own.1.partial = f32[512,1536]{1,0:T(8,128)S(1)} custom-call(s32[25]{0:T(128)S(1)} %concatenate.3.meta, bf16[512,2048]{1,0:T(8,128)(2,1)S(1)} %bitcast.13, bf16[512,1536]{1,0:T(8,128)(2,1)S(1)} %copy-done.1, bf16[512,1536]{1,0:T(8,128)(2,1)} %collective-permute-done.refs_1_), custom_call_target="tpu_custom_call" | custom-call | flops 3680000 | bytes 1000 | tf_op jit(solution)/shard_map/project_own/pallas_call | solution.py:343
  26.8 0.9 %project_first.1 = (f32[128,1024]{1,0:T(8,128)S(1)}, bf16[512,1024]{1,0:T(8,128)(2,1)S(1)}) custom-call(s32[25]{0:T(128)S(1)} %concatenate.3.meta, bf16[512,2048]{1,0:T(8,128)(2,1)S(1)} %bitcast.14, f32[512,1536]{1,0:T(8,128)S(1)} %project_own.1.partial, bf16[128,1024]{1,0:T(8,128)(2,1)S(1)} %collective-permute-done.2.refs_0_, ...), custom_call_target="tpu_custom_call" | custom-call | flops 689999 | bytes 1000 | tf_op jit(solution)/shard_map/project_first/pallas_call | solution.py:343
  28.2 1.0 %project_pack.1 = (bf16[128,1024]{1,0:T(8,128)(2,1)S(1)}, bf16[512,1024]{1,0:T(8,128)(2,1)S(1)}) custom-call(s32[25]{0:T(128)S(1)} %concatenate.3.meta, bf16[512,2048]{1,0:T(8,128)(2,1)S(1)} %bitcast.15, f32[128,1024]{1,0:T(8,128)S(1)} %get-tuple-element.26.refs_0_, bf16[128,1024]{1,0:T(8,128)(2,1)S(1)} %collective-permute-done.7.refs_1_, ...), custom_call_target="tpu_custom_call" | custom-call | flops 689999 | bytes 1000 | tf_op jit(solution)/shard_map/project_pack/pallas_call | solution.py:343
  29.2 1.5 %collective-permute-start.12 = (bf16[128,1024]{1,0:T(8,128)(2,1)S(1)}, bf16[128,1024]{1,0:T(8,128)(2,1)S(1)}, u32[]{:S(2)}, u32[]{:S(2)}) collective-permute-start(bf16[128,1024]{1,0:T(8,128)(2,1)S(1)} %get-tuple-element.27), channel_id=1, source_target_pairs={{0,12},{4,8},{8,4},{12,0},{16,28},{20,24},{24,20},{28,16},{1,13},{... | collective-permute-start | bytes 786440 | tf_op jit(solution)/shard_map/ppermute | solution.py:432
  30.6 1.6 %collective-permute-start.13 = (bf16[128,1024]{1,0:T(8,128)(2,1)S(1)}, bf16[128,1024]{1,0:T(8,128)(2,1)S(1)}, u32[]{:S(2)}, u32[]{:S(2)}) collective-permute-start(bf16[128,1024]{1,0:T(8,128)(2,1)S(1)} %get-tuple-element.27), channel_id=1, source_target_pairs={{0,8},{4,12},{8,0},{12,4},{16,24},{20,28},{24,16},{28,20},{1,9},{5... | collective-permute-start | bytes 786440 | tf_op jit(solution)/shard_map/ppermute | solution.py:432
  32.7 1.8 %project_kv.1.refs_2_ = bf16[512,1024]{1,0:T(8,128)(2,1)S(1)} custom-call(s32[25]{0:T(128)S(1)} %concatenate.3.meta, bf16[512,2048]{1,0:T(8,128)(2,1)S(1)} %bitcast.16, f32[512,1536]{1,0:T(8,128)S(1)} %project_own.1.partial, bf16[512,1024]{1,0:T(8,128)(2,1)S(1)} %get-tuple-element.29.refs_0_, bf16[512,1024]{1,0:T(8,128)(2,1)S(1)} %get-tuple-element.30.refs_1_), custom_call_target="tpu_custom_call" | custom-call | flops 2990000 | bytes 1000 | tf_op jit(solution)/shard_map/project_kv/pallas_call | solution.py:343
  35.2 4.6 %all_to_all.5.refs_1_ = bf16[2,512,512]{2,1,0:T(8,128)(2,1)S(1)} all-to-all(bf16[2,512,512]{2,1,0:T(8,128)(2,1)S(1)} %slot_queries.1), channel_id=1, replica_groups={{0,1},{2,3},{4,5},{6,7},{8,9},{10,11},{12,13},{14,15},{16,17},{18,19},{..., dimensions={0} | all-to-all | bytes 2097152 | tf_op jit(solution)/shard_map/all_to_all | solution.py:442
  39.7 3.4 %attend_local.1 = (bf16[512,512]{1,0:T(8,128)(2,1)}, bf16[128,512]{1,0:T(8,128)(2,1)S(1)}, f32[128,512]{1,0:T(8,128)S(1)}, f32[128,512]{1,0:T(8,128)S(1)}, f32[128,512]{1,0:T(8,128)S(1)}) custom-call(s32[25]{0:T(128)S(1)} %concatenate.3.meta, bf16[512,2048]{1,0:T(8,128)(2,1)S(1)} %bitcast.17, f32[512,1536]{1,0:T(8,128)S(1)} %project_own.1.partial, ...), custom_call_target="tpu_custom_call" | custom-call | flops 6325000 | bytes 1000 | tf_op jit(solution)/shard_map/attend_local/pallas_call | solution.py:343
  43.1 1.2 %collective-permute-done.13.refs_5_ = bf16[128,1024]{1,0:T(8,128)(2,1)S(1)} collective-permute-done((bf16[128,1024]{1,0:T(8,128)(2,1)S(1)}, bf16[128,1024]{1,0:T(8,128)(2,1)S(1)}, u32[]{:S(2)}, u32[]{:S(2)}) %collective-permute-start.13) | collective-permute-done | bytes 262176 | tf_op jit(solution)/shard_map/ppermute | solution.py:432
  44.3 0.6 %merge_near.1 = bf16[512,512]{1,0:T(8,128)(2,1)} custom-call(s32[25]{0:T(128)S(1)} %concatenate.3.meta, bf16[128,512]{1,0:T(8,128)(2,1)S(1)} %get-tuple-element.32.refs_0_, f32[128,512]{1,0:T(8,128)S(1)} %get-tuple-element.33.refs_1_, f32[128,512]{1,0:T(8,128)S(1)} %get-tuple-element.34.refs_2_, ...), custom_call_target="tpu_custom_call", output_to_operand_aliasing={{}: (8, {})} | custom-call | flops 2990000 | bytes 1000 | tf_op jit(solution)/shard_map/merge_near/pallas_call | solution.py:456
  (27 shorter events, 3.3 us)
Async XLA Ops:
  0.0 19.4 %copy-start.2 = (s32[4]{0:T(128)S(1)}, s32[4]{0:T(128)}, u32[]{:S(2)}) copy-start(s32[4]{0:T(128)} %param.6) | copy-start | bytes 52
  0.0 21.1 %copy-start = (bf16[1,512,2048]{2,1,0:T(8,128)(2,1)S(1)}, bf16[1,512,2048]{2,1,0:T(8,128)(2,1)}, u32[]{:S(2)}) copy-start(bf16[1,512,2048]{2,1,0:T(8,128)(2,1)} %param.4) | copy-start | bytes 6291460
  0.0 19.5 %collective-permute-start = (bf16[512,1536]{1,0:T(8,128)(2,1)}, bf16[512,1536]{1,0:T(8,128)(2,1)}, u32[]{:S(2)}, u32[]{:S(2)}) collective-permute-start(bf16[512,1536]{1,0:T(8,128)(2,1)} %refs_0_.1), channel_id=1, source_target_pairs={{0,1},{1,0},{2,3},{3,2},{4,5},{5,4},{6,7},{7,6},{8,9},{9,8},{10,11... | collective-permute-start | bytes 4718600 | tf_op jit(solution)/shard_map/ppermute | solution.py:54
  1.6 9.6 %collective-permute-start.2 = (bf16[128,1024]{1,0:T(8,128)(2,1)S(1)}, bf16[128,1024]{1,0:T(8,128)(2,1)S(1)}, u32[]{:S(2)}, u32[]{:S(2)}) collective-permute-start(bf16[128,1024]{1,0:T(8,128)(2,1)S(1)} %constant_dynamic-slice_fusion.1), channel_id=1, source_target_pairs={{0,2},{1,3},{2,0},{3,1},{4,6},{5,7},{6,4},{7,5},{8,10},{9,11},{10,... | collective-permute-start | bytes 786440 | tf_op jit(solution)/shard_map/ppermute | solution.py:54
  5.1 9.6 %collective-permute-start.4 = (bf16[80,1024]{1,0:T(8,128)(2,1)S(1)}, bf16[80,1024]{1,0:T(8,128)(2,1)S(1)}, u32[]{:S(2)}, u32[]{:S(2)}) collective-permute-start(bf16[80,1024]{1,0:T(8,128)(2,1)S(1)} %constant_dynamic-slice_fusion), channel_id=1, source_target_pairs={{0,2},{1,3},{2,0},{3,1},{4,6},{5,7},{6,4},{7,5},{8,10},{9,11},{10,... | collective-permute-start | bytes 491528 | tf_op jit(solution)/shard_map/ppermute | solution.py:54
  6.2 19.9 %collective-permute-start.6 = (bf16[96,1024]{1,0:T(8,128)(2,1)S(1)}, bf16[96,1024]{1,0:T(8,128)(2,1)S(1)}, u32[]{:S(2)}, u32[]{:S(2)}) collective-permute-start(bf16[96,1024]{1,0:T(8,128)(2,1)S(1)} %slice.6), channel_id=1, source_target_pairs={{0,2},{1,3},{2,0},{3,1},{4,6},{5,7},{6,4},{7,5},{8,10},{9,11},{10,... | collective-permute-start | bytes 589832 | tf_op jit(solution)/shard_map/ppermute | solution.py:54
  11.2 14.5 %collective-permute-start.3 = (bf16[128,1024]{1,0:T(8,128)(2,1)S(1)}, bf16[128,1024]{1,0:T(8,128)(2,1)S(1)}, u32[]{:S(2)}, u32[]{:S(2)}) collective-permute-start(bf16[128,1024]{1,0:T(8,128)(2,1)S(1)} %collective-permute-done.2.refs_0_), channel_id=1, source_target_pairs={{0,4},{4,0},{8,12},{12,8},{16,20},{20,16},{24,28},{28,24},{1,5},{5... | collective-permute-start | bytes 786440 | tf_op jit(solution)/shard_map/ppermute | solution.py:54
  14.7 11.6 %collective-permute-start.5 = (bf16[80,1024]{1,0:T(8,128)(2,1)S(1)}, bf16[80,1024]{1,0:T(8,128)(2,1)S(1)}, u32[]{:S(2)}, u32[]{:S(2)}) collective-permute-start(bf16[80,1024]{1,0:T(8,128)(2,1)S(1)} %collective-permute-done.4.refs_2_), channel_id=1, source_target_pairs={{0,8},{4,12},{8,0},{12,4},{16,24},{20,28},{24,16},{28,20},{1,9},{5... | collective-permute-start | bytes 491528 | tf_op jit(solution)/shard_map/ppermute | solution.py:54
  16.9 9.6 %collective-permute-start.9 = (bf16[80,1024]{1,0:T(8,128)(2,1)S(1)}, bf16[80,1024]{1,0:T(8,128)(2,1)S(1)}, u32[]{:S(2)}, u32[]{:S(2)}) collective-permute-start(bf16[80,1024]{1,0:T(8,128)(2,1)S(1)} %collective-permute-done.4.refs_2_), channel_id=1, source_target_pairs={{0,1},{1,0},{2,3},{3,2},{4,5},{5,4},{6,7},{7,6},{8,9},{9,8},{10,11... | collective-permute-start | bytes 491528 | tf_op jit(solution)/shard_map/ppermute | solution.py:54
  19.5 15.0 %collective-permute-start.1 = (bf16[512,512]{1,0:T(8,128)(2,1)}, bf16[512,512]{1,0:T(8,128)(2,1)S(1)}, u32[]{:S(2)}, u32[]{:S(2)}) collective-permute-start(bf16[512,512]{1,0:T(8,128)(2,1)} %slice.7), channel_id=1, source_target_pairs={{0,2},{1,3},{2,0},{3,1},{4,6},{5,7},{6,4},{7,5},{8,10},{9,11},{10,... | collective-permute-start | bytes 1572872 | tf_op jit(solution)/shard_map/ppermute | solution.py:54
  21.1 1.4 %copy-start.1 = (bf16[512,1536]{1,0:T(8,128)(2,1)S(1)}, bf16[512,1536]{1,0:T(8,128)(2,1)}, u32[]{:S(2)}) copy-start(bf16[512,1536]{1,0:T(8,128)(2,1)} %refs_0_.1) | copy-start | bytes 4718596
  25.7 2.3 %collective-permute-start.7 = (bf16[128,1024]{1,0:T(8,128)(2,1)S(1)}, bf16[128,1024]{1,0:T(8,128)(2,1)S(1)}, u32[]{:S(2)}, u32[]{:S(2)}) collective-permute-start(bf16[128,1024]{1,0:T(8,128)(2,1)S(1)} %collective-permute-done.2.refs_0_), channel_id=1, source_target_pairs={{0,1},{1,0},{2,3},{3,2},{4,5},{5,4},{6,7},{7,6},{8,9},{9,8},{10,11... | collective-permute-start | bytes 786440 | tf_op jit(solution)/shard_map/ppermute | solution.py:54
  26.0 2.2 %collective-permute-start.8 = (bf16[128,1024]{1,0:T(8,128)(2,1)S(1)}, bf16[128,1024]{1,0:T(8,128)(2,1)S(1)}, u32[]{:S(2)}, u32[]{:S(2)}) collective-permute-start(bf16[128,1024]{1,0:T(8,128)(2,1)S(1)} %collective-permute-done.3.refs_1_), channel_id=1, source_target_pairs={{0,1},{1,0},{2,3},{3,2},{4,5},{5,4},{6,7},{7,6},{8,9},{9,8},{10,11... | collective-permute-start | bytes 786440 | tf_op jit(solution)/shard_map/ppermute | solution.py:54
  26.3 1.7 %collective-permute-start.11 = (bf16[96,1024]{1,0:T(8,128)(2,1)S(1)}, bf16[96,1024]{1,0:T(8,128)(2,1)S(1)}, u32[]{:S(2)}, u32[]{:S(2)}) collective-permute-start(bf16[96,1024]{1,0:T(8,128)(2,1)S(1)} %collective-permute-done.6.refs_4_), channel_id=1, source_target_pairs={{0,1},{1,0},{2,3},{3,2},{4,5},{5,4},{6,7},{7,6},{8,9},{9,8},{10,11... | collective-permute-start | bytes 589832 | tf_op jit(solution)/shard_map/ppermute | solution.py:54
  26.5 1.7 %collective-permute-start.10 = (bf16[80,1024]{1,0:T(8,128)(2,1)S(1)}, bf16[80,1024]{1,0:T(8,128)(2,1)S(1)}, u32[]{:S(2)}, u32[]{:S(2)}) collective-permute-start(bf16[80,1024]{1,0:T(8,128)(2,1)S(1)} %collective-permute-done.5.refs_3_), channel_id=1, source_target_pairs={{0,1},{1,0},{2,3},{3,2},{4,5},{5,4},{6,7},{7,6},{8,9},{9,8},{10,11... | collective-permute-start | bytes 491528 | tf_op jit(solution)/shard_map/ppermute | solution.py:54
  29.2 13.9 %collective-permute-start.12 = (bf16[128,1024]{1,0:T(8,128)(2,1)S(1)}, bf16[128,1024]{1,0:T(8,128)(2,1)S(1)}, u32[]{:S(2)}, u32[]{:S(2)}) collective-permute-start(bf16[128,1024]{1,0:T(8,128)(2,1)S(1)} %get-tuple-element.27), channel_id=1, source_target_pairs={{0,12},{4,8},{8,4},{12,0},{16,28},{20,24},{24,20},{28,16},{1,13},{... | collective-permute-start | bytes 786440 | tf_op jit(solution)/shard_map/ppermute | solution.py:432
  30.6 13.6 %collective-permute-start.13 = (bf16[128,1024]{1,0:T(8,128)(2,1)S(1)}, bf16[128,1024]{1,0:T(8,128)(2,1)S(1)}, u32[]{:S(2)}, u32[]{:S(2)}) collective-permute-start(bf16[128,1024]{1,0:T(8,128)(2,1)S(1)} %get-tuple-element.27), channel_id=1, source_target_pairs={{0,8},{4,12},{8,0},{12,4},{16,24},{20,28},{24,16},{28,20},{1,9},{5... | collective-permute-start | bytes 786440 | tf_op jit(solution)/shard_map/ppermute | solution.py:432
  32.2 12.0 %collective-permute-start.14 = (bf16[128,1024]{1,0:T(8,128)(2,1)S(1)}, bf16[128,1024]{1,0:T(8,128)(2,1)S(1)}, u32[]{:S(2)}, u32[]{:S(2)}) collective-permute-start(bf16[128,1024]{1,0:T(8,128)(2,1)S(1)} %get-tuple-element.27), channel_id=1, source_target_pairs={{0,4},{4,0},{8,12},{12,8},{16,20},{20,16},{24,28},{28,24},{1,5},{5... | collective-permute-start | bytes 786440 | tf_op jit(solution)/shard_map/ppermute | solution.py:432

commit v11 on v1

--- a/solution.py
+++ b/solution.py
@@ -87,8 +87,8 @@
 
 def own_kernel(count, meta, tokens, *refs):
     weights, out = refs[:count], refs[count]
-    for j in range(out.shape[1] // PAIR):
-        lanes = slice(j * PAIR, (j + 1) * PAIR)
+    for j in range(out.shape[1] // WIDTH):
+        lanes = slice(j * WIDTH, (j + 1) * WIDTH)
         out[:, lanes] = add_up(tokens, [meta[at] for at in range(count)], [weight.at[:, lanes] for weight in weights])
 
 
@@ -130,10 +130,10 @@
 def kv_kernel(places_at, meta, tokens, partial, *refs):
     parts, kv = refs[:-1], refs[-1]
     places = [meta[at] for at in places_at]
-    for j in range(2 * WIDTH // PAIR):
-        lanes = slice(j * PAIR, (j + 1) * PAIR)
+    for j in range(2):
+        lanes = slice(j * WIDTH, (j + 1) * WIDTH)
         product = add_up(tokens, places, [part.at[:, lanes] for part in parts])
-        kv[:, lanes] = (partial[:, WIDTH + j * PAIR : WIDTH + (j + 1) * PAIR] + product).astype(BF16)
+        kv[:, lanes] = (partial[:, (j + 1) * WIDTH : (j + 2) * WIDTH] + product).astype(BF16)
 
 
 def with_ones(value):

time: 40.9 us -> 40.9 us (level)
  no operation moved by 1% of the time
where the time goes in v11:
time: 40.9 us; the launch traced here: 40.6 us
  starting transfers between devices  14.1 us (34%)
  Pallas kernels  11.9 us (29%)
  local copies, waits for them, and re-layouts  7.7 us (19%)
  blocking collectives  4.58 us (11%)
  waiting for transfers between devices  2.09 us (5%)
    pallas_call x6, Pallas kernels, call(): pl.pallas_call(kernel, in_specs=[scalar_spec] + [whole] * len(args), out_...  11.3 us
    ppermute x12, starting transfers between devices, swap(): return lax.ppermute(value, axis, [(i, i ^ bit) for i in range(count)])  10.6 us
    all_to_all x1, blocking collectives, body(): lax.all_to_all(slots_out, 'fsdp', 0, 0, axis_index_groups=[[i, i + 1] for...  4.58 us
    ppermute x3, starting transfers between devices, body(): lax.ppermute(pack, 'seq', partners(seq_size, place, step))  3.55 us
    dynamic_slice x2, local copies, waits for them, and re-layouts, body(): lax.dynamic_slice(ordered('c' + tag, qkv_weight, known), (start + side *...  2.67 us
    slice x1, local copies, waits for them, and re-layouts, body(): cut = ordered('cQ', qkv_weight, known)[:, :WIDTH]  1.87 us
    slice x1, local copies, waits for them, and re-layouts, body(): cut = ordered('cD', qkv_weight, known)[direct_from:, WIDTH:]  1.66 us
    unnamed x8, local copies, waits for them, and re-layouts  1.41 us
  transfers between devices with their start and end apart: 15, of which 4 were waited for; matrix products, arithmetic and copies ran while one was open for 16% of the time, Pallas kernels for 28%

profile of v11, /device:TPU:0, one launch (start us, length us, event | category | flops | bytes accessed | tf_op | source)
XLA Modules:
  0.0 40.6 jit_solution(16295569549742096581)
XLA Ops:
  0.0 0.5 %collective-permute-start = (bf16[512,1536]{1,0:T(8,128)(2,1)}, bf16[512,1536]{1,0:T(8,128)(2,1)}, u32[]{:S(2)}, u32[]{:S(2)}) collective-permute-start(bf16[512,1536]{1,0:T(8,128)(2,1)} %refs_0_.1), channel_id=1, source_target_pairs={{0,1},{1,0},{2,3},{3,2},{4,5},{5,4},{6,7},{7,6},{8,9},{9,8},{10,11... | collective-permute-start | bytes 4718600 | tf_op jit(solution)/shard_map/ppermute | solution.py:54
  0.5 1.1 %constant_dynamic-slice_fusion.1 = bf16[128,1024]{1,0:T(8,128)(2,1)S(1)} fusion(bf16[512,1536]{1,0:T(8,128)(2,1)} %refs_0_.1, s32[]{:T(128)S(6)} %select_n.73), kind=kLoop, calls=%fused_computation.7 | loop fusion | bytes 524292 | tf_op jit(solution)/shard_map/dynamic_slice | solution.py:373
  1.6 2.6 %collective-permute-start.2 = (bf16[128,1024]{1,0:T(8,128)(2,1)S(1)}, bf16[128,1024]{1,0:T(8,128)(2,1)S(1)}, u32[]{:S(2)}, u32[]{:S(2)}) collective-permute-start(bf16[128,1024]{1,0:T(8,128)(2,1)S(1)} %constant_dynamic-slice_fusion.1), channel_id=1, source_target_pairs={{0,2},{1,3},{2,0},{3,1},{4,6},{5,7},{6,4},{7,5},{8,10},{9,11},{10,... | collective-permute-start | bytes 786440 | tf_op jit(solution)/shard_map/ppermute | solution.py:54
  4.2 1.6 %constant_dynamic-slice_fusion = bf16[64,1024]{1,0:T(8,128)(2,1)} fusion(bf16[512,1536]{1,0:T(8,128)(2,1)} %refs_0_.1, s32[]{:T(128)S(6)} %select_n.74), kind=kLoop, calls=%fused_computation.6 | loop fusion | bytes 262148 | tf_op jit(solution)/shard_map/dynamic_slice | solution.py:373
  5.8 1.7 %slice.6 = bf16[128,1024]{1,0:T(8,128)(2,1)} slice(bf16[512,1536]{1,0:T(8,128)(2,1)} %refs_0_.1), slice={[384:512], [512:1536]} | slice | bytes 524288 | tf_op jit(solution)/shard_map/slice | solution.py:387
  7.5 2.0 %collective-permute-start.6 = (bf16[128,1024]{1,0:T(8,128)(2,1)}, bf16[128,1024]{1,0:T(8,128)(2,1)S(1)}, u32[]{:S(2)}, u32[]{:S(2)}) collective-permute-start(bf16[128,1024]{1,0:T(8,128)(2,1)} %slice.6), channel_id=1, source_target_pairs={{0,2},{1,3},{2,0},{3,1},{4,6},{5,7},{6,4},{7,5},{8,10},{9,11},{10,... | collective-permute-start | bytes 786440 | tf_op jit(solution)/shard_map/ppermute | solution.py:54
  9.5 1.9 %slice.7 = bf16[512,512]{1,0:T(8,128)(2,1)} slice(bf16[512,1536]{1,0:T(8,128)(2,1)} %refs_0_.1), slice={[0:512], [0:512]} | slice | bytes 1048576 | tf_op jit(solution)/shard_map/slice | solution.py:394
  11.4 2.0 %collective-permute-start.3 = (bf16[128,1024]{1,0:T(8,128)(2,1)S(1)}, bf16[128,1024]{1,0:T(8,128)(2,1)S(1)}, u32[]{:S(2)}, u32[]{:S(2)}) collective-permute-start(bf16[128,1024]{1,0:T(8,128)(2,1)S(1)} %collective-permute-done.2.refs_0_), channel_id=1, source_target_pairs={{0,4},{4,0},{8,12},{12,8},{16,20},{20,16},{24,28},{28,24},{1,5},{5... | collective-permute-start | bytes 786440 | tf_op jit(solution)/shard_map/ppermute | solution.py:54
  13.5 0.6 %collective-permute-done.4.refs_2_ = bf16[64,1024]{1,0:T(8,128)(2,1)S(1)} collective-permute-done((bf16[64,1024]{1,0:T(8,128)(2,1)}, bf16[64,1024]{1,0:T(8,128)(2,1)S(1)}, u32[]{:S(2)}, u32[]{:S(2)}) %collective-permute-start.4) | collective-permute-done | bytes 131104 | tf_op jit(solution)/shard_map/ppermute | solution.py:54
  14.1 2.1 %collective-permute-start.5 = (bf16[64,1024]{1,0:T(8,128)(2,1)S(1)}, bf16[64,1024]{1,0:T(8,128)(2,1)}, u32[]{:S(2)}, u32[]{:S(2)}) collective-permute-start(bf16[64,1024]{1,0:T(8,128)(2,1)S(1)} %collective-permute-done.4.refs_2_), channel_id=1, source_target_pairs={{0,8},{4,12},{8,0},{12,4},{16,24},{20,28},{24,16},{28,20},{1,9},{5... | collective-permute-start | bytes 393224 | tf_op jit(solution)/shard_map/ppermute | solution.py:54
  16.5 1.4 %copy-done.1 = bf16[512,1536]{1,0:T(8,128)(2,1)S(1)} copy-done((bf16[512,1536]{1,0:T(8,128)(2,1)S(1)}, bf16[512,1536]{1,0:T(8,128)(2,1)}, u32[]{:S(2)}) %copy-start.1) | copy-done | bytes 1572888
  17.9 3.2 %project_own.1.partial = f32[512,1536]{1,0:T(8,128)S(1)} custom-call(s32[25]{0:T(128)S(1)} %concatenate.3.meta, bf16[512,2048]{1,0:T(8,128)(2,1)S(1)} %bitcast.13, bf16[512,1536]{1,0:T(8,128)(2,1)S(1)} %copy-done.1, bf16[512,1536]{1,0:T(8,128)(2,1)} %collective-permute-done.refs_1_), custom_call_target="tpu_custom_call" | custom-call | flops 3680000 | bytes 1000 | tf_op jit(solution)/shard_map/project_own/pallas_call | solution.py:343
  21.1 0.6 %collective-permute-start.7 = (bf16[128,1024]{1,0:T(8,128)(2,1)S(1)}, bf16[128,1024]{1,0:T(8,128)(2,1)S(1)}, u32[]{:S(2)}, u32[]{:S(2)}) collective-permute-start(bf16[128,1024]{1,0:T(8,128)(2,1)S(1)} %collective-permute-done.2.refs_0_), channel_id=1, source_target_pairs={{0,1},{1,0},{2,3},{3,2},{4,5},{5,4},{6,7},{7,6},{8,9},{9,8},{10,11... | collective-permute-start | bytes 786440 | tf_op jit(solution)/shard_map/ppermute | solution.py:54
  22.3 1.3 %project_first.1 = (f32[128,1024]{1,0:T(8,128)S(1)}, bf16[512,1024]{1,0:T(8,128)(2,1)S(1)}) custom-call(s32[25]{0:T(128)S(1)} %concatenate.3.meta, bf16[512,2048]{1,0:T(8,128)(2,1)S(1)} %bitcast.14, f32[512,1536]{1,0:T(8,128)S(1)} %project_own.1.partial, bf16[128,1024]{1,0:T(8,128)(2,1)S(1)} %collective-permute-done.2.refs_0_, ...), custom_call_target="tpu_custom_call" | custom-call | flops 689999 | bytes 1000 | tf_op jit(solution)/shard_map/project_first/pallas_call | solution.py:343
  24.0 1.0 %project_pack.1 = (bf16[128,1024]{1,0:T(8,128)(2,1)S(1)}, bf16[512,1024]{1,0:T(8,128)(2,1)S(1)}) custom-call(s32[25]{0:T(128)S(1)} %concatenate.3.meta, bf16[512,2048]{1,0:T(8,128)(2,1)S(1)} %bitcast.15, f32[128,1024]{1,0:T(8,128)S(1)} %get-tuple-element.26.refs_0_, bf16[128,1024]{1,0:T(8,128)(2,1)S(1)} %collective-permute-done.7.refs_1_, ...), custom_call_target="tpu_custom_call" | custom-call | flops 689999 | bytes 1000 | tf_op jit(solution)/shard_map/project_pack/pallas_call | solution.py:343
  24.9 1.6 %collective-permute-start.12 = (bf16[128,1024]{1,0:T(8,128)(2,1)S(1)}, bf16[128,1024]{1,0:T(8,128)(2,1)S(1)}, u32[]{:S(2)}, u32[]{:S(2)}) collective-permute-start(bf16[128,1024]{1,0:T(8,128)(2,1)S(1)} %get-tuple-element.27), channel_id=1, source_target_pairs={{0,12},{4,8},{8,4},{12,0},{16,28},{20,24},{24,20},{28,16},{1,13},{... | collective-permute-start | bytes 786440 | tf_op jit(solution)/shard_map/ppermute | solution.py:432
  26.5 1.4 %collective-permute-start.13 = (bf16[128,1024]{1,0:T(8,128)(2,1)S(1)}, bf16[128,1024]{1,0:T(8,128)(2,1)S(1)}, u32[]{:S(2)}, u32[]{:S(2)}) collective-permute-start(bf16[128,1024]{1,0:T(8,128)(2,1)S(1)} %get-tuple-element.27), channel_id=1, source_target_pairs={{0,8},{4,12},{8,0},{12,4},{16,24},{20,28},{24,16},{28,20},{1,9},{5... | collective-permute-start | bytes 786440 | tf_op jit(solution)/shard_map/ppermute | solution.py:432
  28.0 0.5 %collective-permute-start.14 = (bf16[128,1024]{1,0:T(8,128)(2,1)S(1)}, bf16[128,1024]{1,0:T(8,128)(2,1)S(1)}, u32[]{:S(2)}, u32[]{:S(2)}) collective-permute-start(bf16[128,1024]{1,0:T(8,128)(2,1)S(1)} %get-tuple-element.27), channel_id=1, source_target_pairs={{0,4},{4,0},{8,12},{12,8},{16,20},{20,16},{24,28},{28,24},{1,5},{5... | collective-permute-start | bytes 786440 | tf_op jit(solution)/shard_map/ppermute | solution.py:432
  28.5 1.8 %project_kv.1.refs_2_ = bf16[512,1024]{1,0:T(8,128)(2,1)S(1)} custom-call(s32[25]{0:T(128)S(1)} %concatenate.3.meta, bf16[512,2048]{1,0:T(8,128)(2,1)S(1)} %bitcast.16, f32[512,1536]{1,0:T(8,128)S(1)} %project_own.1.partial, bf16[512,1024]{1,0:T(8,128)(2,1)S(1)} %get-tuple-element.29.refs_0_, bf16[512,1024]{1,0:T(8,128)(2,1)S(1)} %get-tuple-element.30.refs_1_), custom_call_target="tpu_custom_call" | custom-call | flops 2990000 | bytes 1000 | tf_op jit(solution)/shard_map/project_kv/pallas_call | solution.py:343
  30.7 0.6 %slot_queries.1 = bf16[2,512,512]{2,1,0:T(8,128)(2,1)S(1)} custom-call(s32[25]{0:T(128)S(1)} %concatenate.3.meta, bf16[512,512]{1,0:T(8,128)(2,1)S(1)} %collective-permute-done.1.source.refs_0_), custom_call_target="tpu_custom_call" | custom-call | flops 575000 | bytes 1000 | tf_op jit(solution)/shard_map/slot_queries/pallas_call | solution.py:343
  31.3 4.6 %all_to_all.5.refs_1_ = bf16[2,512,512]{2,1,0:T(8,128)(2,1)S(1)} all-to-all(bf16[2,512,512]{2,1,0:T(8,128)(2,1)S(1)} %slot_queries.1), channel_id=1, replica_groups={{0,1},{2,3},{4,5},{6,7},{8,9},{10,11},{12,13},{14,15},{16,17},{18,19},{..., dimensions={0} | all-to-all | bytes 2097152 | tf_op jit(solution)/shard_map/all_to_all | solution.py:442
  35.9 3.4 %attend_local.1 = (bf16[512,512]{1,0:T(8,128)(2,1)}, bf16[128,512]{1,0:T(8,128)(2,1)S(1)}, f32[128,512]{1,0:T(8,128)S(1)}, f32[128,512]{1,0:T(8,128)S(1)}, f32[128,512]{1,0:T(8,128)S(1)}) custom-call(s32[25]{0:T(128)S(1)} %concatenate.3.meta, bf16[512,2048]{1,0:T(8,128)(2,1)S(1)} %bitcast.17, f32[512,1536]{1,0:T(8,128)S(1)} %project_own.1.partial, ...), custom_call_target="tpu_custom_call" | custom-call | flops 6325000 | bytes 1000 | tf_op jit(solution)/shard_map/attend_local/pallas_call | solution.py:343
  39.3 0.7 %collective-permute-done.13.refs_5_ = bf16[128,1024]{1,0:T(8,128)(2,1)S(1)} collective-permute-done((bf16[128,1024]{1,0:T(8,128)(2,1)S(1)}, bf16[128,1024]{1,0:T(8,128)(2,1)S(1)}, u32[]{:S(2)}, u32[]{:S(2)}) %collective-permute-start.13) | collective-permute-done | bytes 262176 | tf_op jit(solution)/shard_map/ppermute | solution.py:432
  40.0 0.6 %merge_near.1 = bf16[512,512]{1,0:T(8,128)(2,1)} custom-call(s32[25]{0:T(128)S(1)} %concatenate.3.meta, bf16[128,512]{1,0:T(8,128)(2,1)S(1)} %get-tuple-element.32.refs_0_, f32[128,512]{1,0:T(8,128)S(1)} %get-tuple-element.33.refs_1_, f32[128,512]{1,0:T(8,128)S(1)} %get-tuple-element.34.refs_2_, ...), custom_call_target="tpu_custom_call", output_to_operand_aliasing={{}: (8, {})} | custom-call | flops 2990000 | bytes 1000 | tf_op jit(solution)/shard_map/merge_near/pallas_call | solution.py:456
  (29 shorter events, 1.7 us)
Async XLA Ops:
  0.0 13.4 %copy-start.3 = (s32[4]{0:T(128)S(1)}, s32[4]{0:T(128)}, u32[]{:S(2)}) copy-start(s32[4]{0:T(128)} %param.7) | copy-start | bytes 52
  0.0 16.3 %copy-start.2 = (s32[4]{0:T(128)S(1)}, s32[4]{0:T(128)}, u32[]{:S(2)}) copy-start(s32[4]{0:T(128)} %param.6) | copy-start | bytes 52
  0.0 16.5 %copy-start = (bf16[1,512,2048]{2,1,0:T(8,128)(2,1)S(1)}, bf16[1,512,2048]{2,1,0:T(8,128)(2,1)}, u32[]{:S(2)}) copy-start(bf16[1,512,2048]{2,1,0:T(8,128)(2,1)} %param.4) | copy-start | bytes 6291460
  0.0 16.4 %collective-permute-start = (bf16[512,1536]{1,0:T(8,128)(2,1)}, bf16[512,1536]{1,0:T(8,128)(2,1)}, u32[]{:S(2)}, u32[]{:S(2)}) collective-permute-start(bf16[512,1536]{1,0:T(8,128)(2,1)} %refs_0_.1), channel_id=1, source_target_pairs={{0,1},{1,0},{2,3},{3,2},{4,5},{5,4},{6,7},{7,6},{8,9},{9,8},{10,11... | collective-permute-start | bytes 4718600 | tf_op jit(solution)/shard_map/ppermute | solution.py:54
  1.6 9.8 %collective-permute-start.2 = (bf16[128,1024]{1,0:T(8,128)(2,1)S(1)}, bf16[128,1024]{1,0:T(8,128)(2,1)S(1)}, u32[]{:S(2)}, u32[]{:S(2)}) collective-permute-start(bf16[128,1024]{1,0:T(8,128)(2,1)S(1)} %constant_dynamic-slice_fusion.1), channel_id=1, source_target_pairs={{0,2},{1,3},{2,0},{3,1},{4,6},{5,7},{6,4},{7,5},{8,10},{9,11},{10,... | collective-permute-start | bytes 786440 | tf_op jit(solution)/shard_map/ppermute | solution.py:54
  5.8 8.3 %collective-permute-start.4 = (bf16[64,1024]{1,0:T(8,128)(2,1)}, bf16[64,1024]{1,0:T(8,128)(2,1)S(1)}, u32[]{:S(2)}, u32[]{:S(2)}) collective-permute-start(bf16[64,1024]{1,0:T(8,128)(2,1)} %constant_dynamic-slice_fusion), channel_id=1, source_target_pairs={{0,2},{1,3},{2,0},{3,1},{4,6},{5,7},{6,4},{7,5},{8,10},{9,11},{10,... | collective-permute-start | bytes 393224 | tf_op jit(solution)/shard_map/ppermute | solution.py:54
  7.5 13.6 %collective-permute-start.6 = (bf16[128,1024]{1,0:T(8,128)(2,1)}, bf16[128,1024]{1,0:T(8,128)(2,1)S(1)}, u32[]{:S(2)}, u32[]{:S(2)}) collective-permute-start(bf16[128,1024]{1,0:T(8,128)(2,1)} %slice.6), channel_id=1, source_target_pairs={{0,2},{1,3},{2,0},{3,1},{4,6},{5,7},{6,4},{7,5},{8,10},{9,11},{10,... | collective-permute-start | bytes 786440 | tf_op jit(solution)/shard_map/ppermute | solution.py:54
  11.3 19.3 %collective-permute-start.1 = (bf16[512,512]{1,0:T(8,128)(2,1)}, bf16[512,512]{1,0:T(8,128)(2,1)S(1)}, u32[]{:S(2)}, u32[]{:S(2)}) collective-permute-start(bf16[512,512]{1,0:T(8,128)(2,1)} %slice.7), channel_id=1, source_target_pairs={{0,2},{1,3},{2,0},{3,1},{4,6},{5,7},{6,4},{7,5},{8,10},{9,11},{10,... | collective-permute-start | bytes 1572872 | tf_op jit(solution)/shard_map/ppermute | solution.py:54
  11.4 10.2 %collective-permute-start.3 = (bf16[128,1024]{1,0:T(8,128)(2,1)S(1)}, bf16[128,1024]{1,0:T(8,128)(2,1)S(1)}, u32[]{:S(2)}, u32[]{:S(2)}) collective-permute-start(bf16[128,1024]{1,0:T(8,128)(2,1)S(1)} %collective-permute-done.2.refs_0_), channel_id=1, source_target_pairs={{0,4},{4,0},{8,12},{12,8},{16,20},{20,16},{24,28},{28,24},{1,5},{5... | collective-permute-start | bytes 786440 | tf_op jit(solution)/shard_map/ppermute | solution.py:54
  14.1 7.6 %collective-permute-start.5 = (bf16[64,1024]{1,0:T(8,128)(2,1)S(1)}, bf16[64,1024]{1,0:T(8,128)(2,1)}, u32[]{:S(2)}, u32[]{:S(2)}) collective-permute-start(bf16[64,1024]{1,0:T(8,128)(2,1)S(1)} %collective-permute-done.4.refs_2_), channel_id=1, source_target_pairs={{0,8},{4,12},{8,0},{12,4},{16,24},{20,28},{24,16},{28,20},{1,9},{5... | collective-permute-start | bytes 393224 | tf_op jit(solution)/shard_map/ppermute | solution.py:54
  16.4 5.8 %collective-permute-start.9 = (bf16[64,1024]{1,0:T(8,128)(2,1)S(1)}, bf16[64,1024]{1,0:T(8,128)(2,1)S(1)}, u32[]{:S(2)}, u32[]{:S(2)}) collective-permute-start(bf16[64,1024]{1,0:T(8,128)(2,1)S(1)} %collective-permute-done.4.refs_2_), channel_id=1, source_target_pairs={{0,1},{1,0},{2,3},{3,2},{4,5},{5,4},{6,7},{7,6},{8,9},{9,8},{10,11... | collective-permute-start | bytes 393224 | tf_op jit(solution)/shard_map/ppermute | solution.py:54
  16.5 1.4 %copy-start.1 = (bf16[512,1536]{1,0:T(8,128)(2,1)S(1)}, bf16[512,1536]{1,0:T(8,128)(2,1)}, u32[]{:S(2)}) copy-start(bf16[512,1536]{1,0:T(8,128)(2,1)} %refs_0_.1) | copy-start | bytes 4718596
  21.1 2.5 %collective-permute-start.7 = (bf16[128,1024]{1,0:T(8,128)(2,1)S(1)}, bf16[128,1024]{1,0:T(8,128)(2,1)S(1)}, u32[]{:S(2)}, u32[]{:S(2)}) collective-permute-start(bf16[128,1024]{1,0:T(8,128)(2,1)S(1)} %collective-permute-done.2.refs_0_), channel_id=1, source_target_pairs={{0,1},{1,0},{2,3},{3,2},{4,5},{5,4},{6,7},{7,6},{8,9},{9,8},{10,11... | collective-permute-start | bytes 786440 | tf_op jit(solution)/shard_map/ppermute | solution.py:54
  21.6 1.9 %collective-permute-start.11 = (bf16[128,1024]{1,0:T(8,128)(2,1)S(1)}, bf16[128,1024]{1,0:T(8,128)(2,1)S(1)}, u32[]{:S(2)}, u32[]{:S(2)}) collective-permute-start(bf16[128,1024]{1,0:T(8,128)(2,1)S(1)} %collective-permute-done.6.refs_4_), channel_id=1, source_target_pairs={{0,1},{1,0},{2,3},{3,2},{4,5},{5,4},{6,7},{7,6},{8,9},{9,8},{10,11... | collective-permute-start | bytes 786440 | tf_op jit(solution)/shard_map/ppermute | solution.py:54
  21.7 2.2 %collective-permute-start.8 = (bf16[128,1024]{1,0:T(8,128)(2,1)S(1)}, bf16[128,1024]{1,0:T(8,128)(2,1)S(1)}, u32[]{:S(2)}, u32[]{:S(2)}) collective-permute-start(bf16[128,1024]{1,0:T(8,128)(2,1)S(1)} %collective-permute-done.3.refs_1_), channel_id=1, source_target_pairs={{0,1},{1,0},{2,3},{3,2},{4,5},{5,4},{6,7},{7,6},{8,9},{9,8},{10,11... | collective-permute-start | bytes 786440 | tf_op jit(solution)/shard_map/ppermute | solution.py:54
  22.2 1.8 %collective-permute-start.10 = (bf16[64,1024]{1,0:T(8,128)(2,1)}, bf16[64,1024]{1,0:T(8,128)(2,1)S(1)}, u32[]{:S(2)}, u32[]{:S(2)}) collective-permute-start(bf16[64,1024]{1,0:T(8,128)(2,1)} %collective-permute-done.5.refs_3_), channel_id=1, source_target_pairs={{0,1},{1,0},{2,3},{3,2},{4,5},{5,4},{6,7},{7,6},{8,9},{9,8},{10,11... | collective-permute-start | bytes 393224 | tf_op jit(solution)/shard_map/ppermute | solution.py:54
  24.9 14.3 %collective-permute-start.12 = (bf16[128,1024]{1,0:T(8,128)(2,1)S(1)}, bf16[128,1024]{1,0:T(8,128)(2,1)S(1)}, u32[]{:S(2)}, u32[]{:S(2)}) collective-permute-start(bf16[128,1024]{1,0:T(8,128)(2,1)S(1)} %get-tuple-element.27), channel_id=1, source_target_pairs={{0,12},{4,8},{8,4},{12,0},{16,28},{20,24},{24,20},{28,16},{1,13},{... | collective-permute-start | bytes 786440 | tf_op jit(solution)/shard_map/ppermute | solution.py:432
  26.5 13.4 %collective-permute-start.13 = (bf16[128,1024]{1,0:T(8,128)(2,1)S(1)}, bf16[128,1024]{1,0:T(8,128)(2,1)S(1)}, u32[]{:S(2)}, u32[]{:S(2)}) collective-permute-start(bf16[128,1024]{1,0:T(8,128)(2,1)S(1)} %get-tuple-element.27), channel_id=1, source_target_pairs={{0,8},{4,12},{8,0},{12,4},{16,24},{20,28},{24,16},{28,20},{1,9},{5... | collective-permute-start | bytes 786440 | tf_op jit(solution)/shard_map/ppermute | solution.py:432
  28.0 12.0 %collective-permute-start.14 = (bf16[128,1024]{1,0:T(8,128)(2,1)S(1)}, bf16[128,1024]{1,0:T(8,128)(2,1)S(1)}, u32[]{:S(2)}, u32[]{:S(2)}) collective-permute-start(bf16[128,1024]{1,0:T(8,128)(2,1)S(1)} %get-tuple-element.27), channel_id=1, source_target_pairs={{0,4},{4,0},{8,12},{12,8},{16,20},{20,16},{24,28},{28,24},{1,5},{5... | collective-permute-start | bytes 786440 | tf_op jit(solution)/shard_map/ppermute | solution.py:432

commit v12 on v11

--- a/solution.py
+++ b/solution.py
@@ -152,8 +152,7 @@
     causal = column <= row
     places = [meta[at] for at in bases_at]
     other = 1 - meta[core_at]
-    for pair in range(HEADS // 2):
-        lanes = slice(pair * PAIR, (pair + 1) * PAIR)
+    for lanes in (slice(0, WIDTH),):
         total = partial[:, lanes]
         if weights:
             parts = [weights[0].at[:, lanes], weights[1].at[other, :, lanes]]

time: 40.9 us -> 40.9 us (level)
  no operation moved by 1% of the time
where the time goes in v12:
time: 40.9 us; the launch traced here: 40.6 us
  starting transfers between devices  14.1 us (34%)
  Pallas kernels  11.9 us (29%)
  local copies, waits for them, and re-layouts  7.7 us (19%)
  blocking collectives  4.58 us (11%)
  waiting for transfers between devices  2.09 us (5%)
    pallas_call x6, Pallas kernels, call(): pl.pallas_call(kernel, in_specs=[scalar_spec] + [whole] * len(args), out_...  11.3 us
    ppermute x12, starting transfers between devices, swap(): return lax.ppermute(value, axis, [(i, i ^ bit) for i in range(count)])  10.6 us
    all_to_all x1, blocking collectives, body(): lax.all_to_all(slots_out, 'fsdp', 0, 0, axis_index_groups=[[i, i + 1] for...  4.58 us
    ppermute x3, starting transfers between devices, body(): lax.ppermute(pack, 'seq', partners(seq_size, place, step))  3.55 us
    dynamic_slice x2, local copies, waits for them, and re-layouts, body(): lax.dynamic_slice(ordered('c' + tag, qkv_weight, known), (start + side *...  2.67 us
    slice x1, local copies, waits for them, and re-layouts, body(): cut = ordered('cQ', qkv_weight, known)[:, :WIDTH]  1.87 us
    slice x1, local copies, waits for them, and re-layouts, body(): cut = ordered('cD', qkv_weight, known)[direct_from:, WIDTH:]  1.66 us
    unnamed x8, local copies, waits for them, and re-layouts  1.41 us
  transfers between devices with their start and end apart: 15, of which 4 were waited for; matrix products, arithmetic and copies ran while one was open for 16% of the time, Pallas kernels for 28%

profile of v12, /device:TPU:0, one launch (start us, length us, event | category | flops | bytes accessed | tf_op | source)
XLA Modules:
  0.0 40.6 jit_solution(7625070424090314624)
XLA Ops:
  0.0 0.5 %collective-permute-start = (bf16[512,1536]{1,0:T(8,128)(2,1)}, bf16[512,1536]{1,0:T(8,128)(2,1)}, u32[]{:S(2)}, u32[]{:S(2)}) collective-permute-start(bf16[512,1536]{1,0:T(8,128)(2,1)} %refs_0_.1), channel_id=1, source_target_pairs={{0,1},{1,0},{2,3},{3,2},{4,5},{5,4},{6,7},{7,6},{8,9},{9,8},{10,11... | collective-permute-start | bytes 4718600 | tf_op jit(solution)/shard_map/ppermute | solution.py:54
  0.5 1.1 %constant_dynamic-slice_fusion.1 = bf16[128,1024]{1,0:T(8,128)(2,1)S(1)} fusion(bf16[512,1536]{1,0:T(8,128)(2,1)} %refs_0_.1, s32[]{:T(128)S(6)} %select_n.73), kind=kLoop, calls=%fused_computation.7 | loop fusion | bytes 524292 | tf_op jit(solution)/shard_map/dynamic_slice | solution.py:372
  1.6 2.6 %collective-permute-start.2 = (bf16[128,1024]{1,0:T(8,128)(2,1)S(1)}, bf16[128,1024]{1,0:T(8,128)(2,1)S(1)}, u32[]{:S(2)}, u32[]{:S(2)}) collective-permute-start(bf16[128,1024]{1,0:T(8,128)(2,1)S(1)} %constant_dynamic-slice_fusion.1), channel_id=1, source_target_pairs={{0,2},{1,3},{2,0},{3,1},{4,6},{5,7},{6,4},{7,5},{8,10},{9,11},{10,... | collective-permute-start | bytes 786440 | tf_op jit(solution)/shard_map/ppermute | solution.py:54
  4.2 1.6 %constant_dynamic-slice_fusion = bf16[64,1024]{1,0:T(8,128)(2,1)} fusion(bf16[512,1536]{1,0:T(8,128)(2,1)} %refs_0_.1, s32[]{:T(128)S(6)} %select_n.74), kind=kLoop, calls=%fused_computation.6 | loop fusion | bytes 262148 | tf_op jit(solution)/shard_map/dynamic_slice | solution.py:372
  5.8 1.7 %slice.6 = bf16[128,1024]{1,0:T(8,128)(2,1)} slice(bf16[512,1536]{1,0:T(8,128)(2,1)} %refs_0_.1), slice={[384:512], [512:1536]} | slice | bytes 524288 | tf_op jit(solution)/shard_map/slice | solution.py:386
  7.5 2.0 %collective-permute-start.6 = (bf16[128,1024]{1,0:T(8,128)(2,1)}, bf16[128,1024]{1,0:T(8,128)(2,1)S(1)}, u32[]{:S(2)}, u32[]{:S(2)}) collective-permute-start(bf16[128,1024]{1,0:T(8,128)(2,1)} %slice.6), channel_id=1, source_target_pairs={{0,2},{1,3},{2,0},{3,1},{4,6},{5,7},{6,4},{7,5},{8,10},{9,11},{10,... | collective-permute-start | bytes 786440 | tf_op jit(solution)/shard_map/ppermute | solution.py:54
  9.5 1.9 %slice.7 = bf16[512,512]{1,0:T(8,128)(2,1)} slice(bf16[512,1536]{1,0:T(8,128)(2,1)} %refs_0_.1), slice={[0:512], [0:512]} | slice | bytes 1048576 | tf_op jit(solution)/shard_map/slice | solution.py:393
  11.4 2.0 %collective-permute-start.3 = (bf16[128,1024]{1,0:T(8,128)(2,1)S(1)}, bf16[128,1024]{1,0:T(8,128)(2,1)S(1)}, u32[]{:S(2)}, u32[]{:S(2)}) collective-permute-start(bf16[128,1024]{1,0:T(8,128)(2,1)S(1)} %collective-permute-done.2.refs_0_), channel_id=1, source_target_pairs={{0,4},{4,0},{8,12},{12,8},{16,20},{20,16},{24,28},{28,24},{1,5},{5... | collective-permute-start | bytes 786440 | tf_op jit(solution)/shard_map/ppermute | solution.py:54
  13.5 0.6 %collective-permute-done.4.refs_2_ = bf16[64,1024]{1,0:T(8,128)(2,1)S(1)} collective-permute-done((bf16[64,1024]{1,0:T(8,128)(2,1)}, bf16[64,1024]{1,0:T(8,128)(2,1)S(1)}, u32[]{:S(2)}, u32[]{:S(2)}) %collective-permute-start.4) | collective-permute-done | bytes 131104 | tf_op jit(solution)/shard_map/ppermute | solution.py:54
  14.1 2.1 %collective-permute-start.5 = (bf16[64,1024]{1,0:T(8,128)(2,1)S(1)}, bf16[64,1024]{1,0:T(8,128)(2,1)}, u32[]{:S(2)}, u32[]{:S(2)}) collective-permute-start(bf16[64,1024]{1,0:T(8,128)(2,1)S(1)} %collective-permute-done.4.refs_2_), channel_id=1, source_target_pairs={{0,8},{4,12},{8,0},{12,4},{16,24},{20,28},{24,16},{28,20},{1,9},{5... | collective-permute-start | bytes 393224 | tf_op jit(solution)/shard_map/ppermute | solution.py:54
  16.5 1.4 %copy-done.1 = bf16[512,1536]{1,0:T(8,128)(2,1)S(1)} copy-done((bf16[512,1536]{1,0:T(8,128)(2,1)S(1)}, bf16[512,1536]{1,0:T(8,128)(2,1)}, u32[]{:S(2)}) %copy-start.1) | copy-done | bytes 1572888
  17.9 3.2 %project_own.1.partial = f32[512,1536]{1,0:T(8,128)S(1)} custom-call(s32[25]{0:T(128)S(1)} %concatenate.3.meta, bf16[512,2048]{1,0:T(8,128)(2,1)S(1)} %bitcast.13, bf16[512,1536]{1,0:T(8,128)(2,1)S(1)} %copy-done.1, bf16[512,1536]{1,0:T(8,128)(2,1)} %collective-permute-done.refs_1_), custom_call_target="tpu_custom_call" | custom-call | flops 3680000 | bytes 1000 | tf_op jit(solution)/shard_map/project_own/pallas_call | solution.py:342
  21.1 0.6 %collective-permute-start.7 = (bf16[128,1024]{1,0:T(8,128)(2,1)S(1)}, bf16[128,1024]{1,0:T(8,128)(2,1)S(1)}, u32[]{:S(2)}, u32[]{:S(2)}) collective-permute-start(bf16[128,1024]{1,0:T(8,128)(2,1)S(1)} %collective-permute-done.2.refs_0_), channel_id=1, source_target_pairs={{0,1},{1,0},{2,3},{3,2},{4,5},{5,4},{6,7},{7,6},{8,9},{9,8},{10,11... | collective-permute-start | bytes 786440 | tf_op jit(solution)/shard_map/ppermute | solution.py:54
  22.3 1.3 %project_first.1 = (f32[128,1024]{1,0:T(8,128)S(1)}, bf16[512,1024]{1,0:T(8,128)(2,1)S(1)}) custom-call(s32[25]{0:T(128)S(1)} %concatenate.3.meta, bf16[512,2048]{1,0:T(8,128)(2,1)S(1)} %bitcast.14, f32[512,1536]{1,0:T(8,128)S(1)} %project_own.1.partial, bf16[128,1024]{1,0:T(8,128)(2,1)S(1)} %collective-permute-done.2.refs_0_, ...), custom_call_target="tpu_custom_call" | custom-call | flops 689999 | bytes 1000 | tf_op jit(solution)/shard_map/project_first/pallas_call | solution.py:342
  24.0 1.0 %project_pack.1 = (bf16[128,1024]{1,0:T(8,128)(2,1)S(1)}, bf16[512,1024]{1,0:T(8,128)(2,1)S(1)}) custom-call(s32[25]{0:T(128)S(1)} %concatenate.3.meta, bf16[512,2048]{1,0:T(8,128)(2,1)S(1)} %bitcast.15, f32[128,1024]{1,0:T(8,128)S(1)} %get-tuple-element.26.refs_0_, bf16[128,1024]{1,0:T(8,128)(2,1)S(1)} %collective-permute-done.7.refs_1_, ...), custom_call_target="tpu_custom_call" | custom-call | flops 689999 | bytes 1000 | tf_op jit(solution)/shard_map/project_pack/pallas_call | solution.py:342
  24.9 1.6 %collective-permute-start.12 = (bf16[128,1024]{1,0:T(8,128)(2,1)S(1)}, bf16[128,1024]{1,0:T(8,128)(2,1)S(1)}, u32[]{:S(2)}, u32[]{:S(2)}) collective-permute-start(bf16[128,1024]{1,0:T(8,128)(2,1)S(1)} %get-tuple-element.27), channel_id=1, source_target_pairs={{0,12},{4,8},{8,4},{12,0},{16,28},{20,24},{24,20},{28,16},{1,13},{... | collective-permute-start | bytes 786440 | tf_op jit(solution)/shard_map/ppermute | solution.py:431
  26.5 1.4 %collective-permute-start.13 = (bf16[128,1024]{1,0:T(8,128)(2,1)S(1)}, bf16[128,1024]{1,0:T(8,128)(2,1)S(1)}, u32[]{:S(2)}, u32[]{:S(2)}) collective-permute-start(bf16[128,1024]{1,0:T(8,128)(2,1)S(1)} %get-tuple-element.27), channel_id=1, source_target_pairs={{0,8},{4,12},{8,0},{12,4},{16,24},{20,28},{24,16},{28,20},{1,9},{5... | collective-permute-start | bytes 786440 | tf_op jit(solution)/shard_map/ppermute | solution.py:431
  28.0 0.5 %collective-permute-start.14 = (bf16[128,1024]{1,0:T(8,128)(2,1)S(1)}, bf16[128,1024]{1,0:T(8,128)(2,1)S(1)}, u32[]{:S(2)}, u32[]{:S(2)}) collective-permute-start(bf16[128,1024]{1,0:T(8,128)(2,1)S(1)} %get-tuple-element.27), channel_id=1, source_target_pairs={{0,4},{4,0},{8,12},{12,8},{16,20},{20,16},{24,28},{28,24},{1,5},{5... | collective-permute-start | bytes 786440 | tf_op jit(solution)/shard_map/ppermute | solution.py:431
  28.5 1.8 %project_kv.1.refs_2_ = bf16[512,1024]{1,0:T(8,128)(2,1)S(1)} custom-call(s32[25]{0:T(128)S(1)} %concatenate.3.meta, bf16[512,2048]{1,0:T(8,128)(2,1)S(1)} %bitcast.16, f32[512,1536]{1,0:T(8,128)S(1)} %project_own.1.partial, bf16[512,1024]{1,0:T(8,128)(2,1)S(1)} %get-tuple-element.29.refs_0_, bf16[512,1024]{1,0:T(8,128)(2,1)S(1)} %get-tuple-element.30.refs_1_), custom_call_target="tpu_custom_call" | custom-call | flops 2990000 | bytes 1000 | tf_op jit(solution)/shard_map/project_kv/pallas_call | solution.py:342
  30.7 0.6 %slot_queries.1 = bf16[2,512,512]{2,1,0:T(8,128)(2,1)S(1)} custom-call(s32[25]{0:T(128)S(1)} %concatenate.3.meta, bf16[512,512]{1,0:T(8,128)(2,1)S(1)} %collective-permute-done.1.source.refs_0_), custom_call_target="tpu_custom_call" | custom-call | flops 575000 | bytes 1000 | tf_op jit(solution)/shard_map/slot_queries/pallas_call | solution.py:342
  31.3 4.6 %all_to_all.5.refs_1_ = bf16[2,512,512]{2,1,0:T(8,128)(2,1)S(1)} all-to-all(bf16[2,512,512]{2,1,0:T(8,128)(2,1)S(1)} %slot_queries.1), channel_id=1, replica_groups={{0,1},{2,3},{4,5},{6,7},{8,9},{10,11},{12,13},{14,15},{16,17},{18,19},{..., dimensions={0} | all-to-all | bytes 2097152 | tf_op jit(solution)/shard_map/all_to_all | solution.py:441
  35.9 3.4 %attend_local.1 = (bf16[512,512]{1,0:T(8,128)(2,1)}, bf16[128,512]{1,0:T(8,128)(2,1)S(1)}, f32[128,512]{1,0:T(8,128)S(1)}, f32[128,512]{1,0:T(8,128)S(1)}, f32[128,512]{1,0:T(8,128)S(1)}) custom-call(s32[25]{0:T(128)S(1)} %concatenate.3.meta, bf16[512,2048]{1,0:T(8,128)(2,1)S(1)} %bitcast.17, f32[512,1536]{1,0:T(8,128)S(1)} %project_own.1.partial, ...), custom_call_target="tpu_custom_call" | custom-call | flops 6325000 | bytes 1000 | tf_op jit(solution)/shard_map/attend_local/pallas_call | solution.py:342
  39.3 0.7 %collective-permute-done.13.refs_5_ = bf16[128,1024]{1,0:T(8,128)(2,1)S(1)} collective-permute-done((bf16[128,1024]{1,0:T(8,128)(2,1)S(1)}, bf16[128,1024]{1,0:T(8,128)(2,1)S(1)}, u32[]{:S(2)}, u32[]{:S(2)}) %collective-permute-start.13) | collective-permute-done | bytes 262176 | tf_op jit(solution)/shard_map/ppermute | solution.py:431
  40.0 0.6 %merge_near.1 = bf16[512,512]{1,0:T(8,128)(2,1)} custom-call(s32[25]{0:T(128)S(1)} %concatenate.3.meta, bf16[128,512]{1,0:T(8,128)(2,1)S(1)} %get-tuple-element.32.refs_0_, f32[128,512]{1,0:T(8,128)S(1)} %get-tuple-element.33.refs_1_, f32[128,512]{1,0:T(8,128)S(1)} %get-tuple-element.34.refs_2_, ...), custom_call_target="tpu_custom_call", output_to_operand_aliasing={{}: (8, {})} | custom-call | flops 2990000 | bytes 1000 | tf_op jit(solution)/shard_map/merge_near/pallas_call | solution.py:455
  (29 shorter events, 1.7 us)
Async XLA Ops:
  0.0 13.4 %copy-start.3 = (s32[4]{0:T(128)S(1)}, s32[4]{0:T(128)}, u32[]{:S(2)}) copy-start(s32[4]{0:T(128)} %param.7) | copy-start | bytes 52
  0.0 16.3 %copy-start.2 = (s32[4]{0:T(128)S(1)}, s32[4]{0:T(128)}, u32[]{:S(2)}) copy-start(s32[4]{0:T(128)} %param.6) | copy-start | bytes 52
  0.0 16.5 %copy-start = (bf16[1,512,2048]{2,1,0:T(8,128)(2,1)S(1)}, bf16[1,512,2048]{2,1,0:T(8,128)(2,1)}, u32[]{:S(2)}) copy-start(bf16[1,512,2048]{2,1,0:T(8,128)(2,1)} %param.4) | copy-start | bytes 6291460
  0.0 16.4 %collective-permute-start = (bf16[512,1536]{1,0:T(8,128)(2,1)}, bf16[512,1536]{1,0:T(8,128)(2,1)}, u32[]{:S(2)}, u32[]{:S(2)}) collective-permute-start(bf16[512,1536]{1,0:T(8,128)(2,1)} %refs_0_.1), channel_id=1, source_target_pairs={{0,1},{1,0},{2,3},{3,2},{4,5},{5,4},{6,7},{7,6},{8,9},{9,8},{10,11... | collective-permute-start | bytes 4718600 | tf_op jit(solution)/shard_map/ppermute | solution.py:54
  1.6 9.8 %collective-permute-start.2 = (bf16[128,1024]{1,0:T(8,128)(2,1)S(1)}, bf16[128,1024]{1,0:T(8,128)(2,1)S(1)}, u32[]{:S(2)}, u32[]{:S(2)}) collective-permute-start(bf16[128,1024]{1,0:T(8,128)(2,1)S(1)} %constant_dynamic-slice_fusion.1), channel_id=1, source_target_pairs={{0,2},{1,3},{2,0},{3,1},{4,6},{5,7},{6,4},{7,5},{8,10},{9,11},{10,... | collective-permute-start | bytes 786440 | tf_op jit(solution)/shard_map/ppermute | solution.py:54
  5.8 8.3 %collective-permute-start.4 = (bf16[64,1024]{1,0:T(8,128)(2,1)}, bf16[64,1024]{1,0:T(8,128)(2,1)S(1)}, u32[]{:S(2)}, u32[]{:S(2)}) collective-permute-start(bf16[64,1024]{1,0:T(8,128)(2,1)} %constant_dynamic-slice_fusion), channel_id=1, source_target_pairs={{0,2},{1,3},{2,0},{3,1},{4,6},{5,7},{6,4},{7,5},{8,10},{9,11},{10,... | collective-permute-start | bytes 393224 | tf_op jit(solution)/shard_map/ppermute | solution.py:54
  7.5 13.6 %collective-permute-start.6 = (bf16[128,1024]{1,0:T(8,128)(2,1)}, bf16[128,1024]{1,0:T(8,128)(2,1)S(1)}, u32[]{:S(2)}, u32[]{:S(2)}) collective-permute-start(bf16[128,1024]{1,0:T(8,128)(2,1)} %slice.6), channel_id=1, source_target_pairs={{0,2},{1,3},{2,0},{3,1},{4,6},{5,7},{6,4},{7,5},{8,10},{9,11},{10,... | collective-permute-start | bytes 786440 | tf_op jit(solution)/shard_map/ppermute | solution.py:54
  11.3 19.3 %collective-permute-start.1 = (bf16[512,512]{1,0:T(8,128)(2,1)}, bf16[512,512]{1,0:T(8,128)(2,1)S(1)}, u32[]{:S(2)}, u32[]{:S(2)}) collective-permute-start(bf16[512,512]{1,0:T(8,128)(2,1)} %slice.7), channel_id=1, source_target_pairs={{0,2},{1,3},{2,0},{3,1},{4,6},{5,7},{6,4},{7,5},{8,10},{9,11},{10,... | collective-permute-start | bytes 1572872 | tf_op jit(solution)/shard_map/ppermute | solution.py:54
  11.4 10.2 %collective-permute-start.3 = (bf16[128,1024]{1,0:T(8,128)(2,1)S(1)}, bf16[128,1024]{1,0:T(8,128)(2,1)S(1)}, u32[]{:S(2)}, u32[]{:S(2)}) collective-permute-start(bf16[128,1024]{1,0:T(8,128)(2,1)S(1)} %collective-permute-done.2.refs_0_), channel_id=1, source_target_pairs={{0,4},{4,0},{8,12},{12,8},{16,20},{20,16},{24,28},{28,24},{1,5},{5... | collective-permute-start | bytes 786440 | tf_op jit(solution)/shard_map/ppermute | solution.py:54
  14.1 7.6 %collective-permute-start.5 = (bf16[64,1024]{1,0:T(8,128)(2,1)S(1)}, bf16[64,1024]{1,0:T(8,128)(2,1)}, u32[]{:S(2)}, u32[]{:S(2)}) collective-permute-start(bf16[64,1024]{1,0:T(8,128)(2,1)S(1)} %collective-permute-done.4.refs_2_), channel_id=1, source_target_pairs={{0,8},{4,12},{8,0},{12,4},{16,24},{20,28},{24,16},{28,20},{1,9},{5... | collective-permute-start | bytes 393224 | tf_op jit(solution)/shard_map/ppermute | solution.py:54
  16.4 5.8 %collective-permute-start.9 = (bf16[64,1024]{1,0:T(8,128)(2,1)S(1)}, bf16[64,1024]{1,0:T(8,128)(2,1)S(1)}, u32[]{:S(2)}, u32[]{:S(2)}) collective-permute-start(bf16[64,1024]{1,0:T(8,128)(2,1)S(1)} %collective-permute-done.4.refs_2_), channel_id=1, source_target_pairs={{0,1},{1,0},{2,3},{3,2},{4,5},{5,4},{6,7},{7,6},{8,9},{9,8},{10,11... | collective-permute-start | bytes 393224 | tf_op jit(solution)/shard_map/ppermute | solution.py:54
  16.5 1.4 %copy-start.1 = (bf16[512,1536]{1,0:T(8,128)(2,1)S(1)}, bf16[512,1536]{1,0:T(8,128)(2,1)}, u32[]{:S(2)}) copy-start(bf16[512,1536]{1,0:T(8,128)(2,1)} %refs_0_.1) | copy-start | bytes 4718596
  21.1 2.5 %collective-permute-start.7 = (bf16[128,1024]{1,0:T(8,128)(2,1)S(1)}, bf16[128,1024]{1,0:T(8,128)(2,1)S(1)}, u32[]{:S(2)}, u32[]{:S(2)}) collective-permute-start(bf16[128,1024]{1,0:T(8,128)(2,1)S(1)} %collective-permute-done.2.refs_0_), channel_id=1, source_target_pairs={{0,1},{1,0},{2,3},{3,2},{4,5},{5,4},{6,7},{7,6},{8,9},{9,8},{10,11... | collective-permute-start | bytes 786440 | tf_op jit(solution)/shard_map/ppermute | solution.py:54
  21.6 1.9 %collective-permute-start.11 = (bf16[128,1024]{1,0:T(8,128)(2,1)S(1)}, bf16[128,1024]{1,0:T(8,128)(2,1)S(1)}, u32[]{:S(2)}, u32[]{:S(2)}) collective-permute-start(bf16[128,1024]{1,0:T(8,128)(2,1)S(1)} %collective-permute-done.6.refs_4_), channel_id=1, source_target_pairs={{0,1},{1,0},{2,3},{3,2},{4,5},{5,4},{6,7},{7,6},{8,9},{9,8},{10,11... | collective-permute-start | bytes 786440 | tf_op jit(solution)/shard_map/ppermute | solution.py:54
  21.7 2.2 %collective-permute-start.8 = (bf16[128,1024]{1,0:T(8,128)(2,1)S(1)}, bf16[128,1024]{1,0:T(8,128)(2,1)S(1)}, u32[]{:S(2)}, u32[]{:S(2)}) collective-permute-start(bf16[128,1024]{1,0:T(8,128)(2,1)S(1)} %collective-permute-done.3.refs_1_), channel_id=1, source_target_pairs={{0,1},{1,0},{2,3},{3,2},{4,5},{5,4},{6,7},{7,6},{8,9},{9,8},{10,11... | collective-permute-start | bytes 786440 | tf_op jit(solution)/shard_map/ppermute | solution.py:54
  22.2 1.8 %collective-permute-start.10 = (bf16[64,1024]{1,0:T(8,128)(2,1)}, bf16[64,1024]{1,0:T(8,128)(2,1)S(1)}, u32[]{:S(2)}, u32[]{:S(2)}) collective-permute-start(bf16[64,1024]{1,0:T(8,128)(2,1)} %collective-permute-done.5.refs_3_), channel_id=1, source_target_pairs={{0,1},{1,0},{2,3},{3,2},{4,5},{5,4},{6,7},{7,6},{8,9},{9,8},{10,11... | collective-permute-start | bytes 393224 | tf_op jit(solution)/shard_map/ppermute | solution.py:54
  24.9 14.3 %collective-permute-start.12 = (bf16[128,1024]{1,0:T(8,128)(2,1)S(1)}, bf16[128,1024]{1,0:T(8,128)(2,1)S(1)}, u32[]{:S(2)}, u32[]{:S(2)}) collective-permute-start(bf16[128,1024]{1,0:T(8,128)(2,1)S(1)} %get-tuple-element.27), channel_id=1, source_target_pairs={{0,12},{4,8},{8,4},{12,0},{16,28},{20,24},{24,20},{28,16},{1,13},{... | collective-permute-start | bytes 786440 | tf_op jit(solution)/shard_map/ppermute | solution.py:431
  26.5 13.4 %collective-permute-start.13 = (bf16[128,1024]{1,0:T(8,128)(2,1)S(1)}, bf16[128,1024]{1,0:T(8,128)(2,1)S(1)}, u32[]{:S(2)}, u32[]{:S(2)}) collective-permute-start(bf16[128,1024]{1,0:T(8,128)(2,1)S(1)} %get-tuple-element.27), channel_id=1, source_target_pairs={{0,8},{4,12},{8,0},{12,4},{16,24},{20,28},{24,16},{28,20},{1,9},{5... | collective-permute-start | bytes 786440 | tf_op jit(solution)/shard_map/ppermute | solution.py:431
  28.0 12.0 %collective-permute-start.14 = (bf16[128,1024]{1,0:T(8,128)(2,1)S(1)}, bf16[128,1024]{1,0:T(8,128)(2,1)S(1)}, u32[]{:S(2)}, u32[]{:S(2)}) collective-permute-start(bf16[128,1024]{1,0:T(8,128)(2,1)S(1)} %get-tuple-element.27), channel_id=1, source_target_pairs={{0,4},{4,0},{8,12},{12,8},{16,20},{20,16},{24,28},{28,24},{1,5},{5... | collective-permute-start | bytes 786440 | tf_op jit(solution)/shard_map/ppermute | solution.py:431
